TPU v7x, 32 devices: a whole 2x2x4 slice. The times are simulated.
32 devices in a mesh: grp: 2 (over y), row: 8 (over z, x), layer: 2 (over core).
Axes of the slice: x: 2, y: 2, z: 4, core: 2. Of those that a mesh axis runs over, the one named last changes fastest.
Arguments:
- train_grads: bfloat16 [4096, 2, 4096], P(('grp', 'row'), 'layer'), parts along dimension 0, may hold values from -0.015991211 to 0.015991211
- query_grads: bfloat16 [3, 16, 2, 4096], P(None, 'row', 'layer'), may hold values from -6 to 6
- out_basis: float32 [2, 64, 64], P('layer')
- in_basis: float32 [2, 64, 64], P('layer')
- eigenvalues: float32 [2, 4096], P('layer'), may hold values from 0.05 to 5
- block_order: int32 [3], replicated, may hold values from 0 to 2, each once
- row_ids: int32 [16, 256], P(('grp', 'row')), parts along dimension 0, may hold values from 0 to 255, each once within a row
Outputs:
- scores: bfloat16 [3, 4096, 16], P(None, ('grp', 'row'), 'layer'), parts along dimension 1
There are 2 independent parts, one for each index of `grp`. A program takes and returns all parts, laid end to end along the dimension named above; an argument that names none is the same for every part. Nothing has to cross between parts.
Inputs may be any that keep to these rules, and one draw needn't show every extreme that they name: Each row of row_ids holds every number of 0 to 255 once. block_order holds every number of 0 to 2 once.
All inputs are finite; a program needn't handle non-finite values.
Results may differ from a plain program's by a relative error of at most 0.0051.
Values may be sent and summed in bfloat16 or wider, within the bound.
No kernel may reach another device: no remote copies, remote signals or barrier semaphores. Data moves between devices by JAX's collectives and lax.ppermute only.
A program may use at most 64 MiB of HBM per device.

v0:
```python
import jax
import jax.numpy as jnp
from jax import lax
from jax.sharding import PartitionSpec as P

DAMPING = 0.01


def precondition(raw, out_basis, in_basis, eigenvalues):
    count, layers, width = raw.shape
    side = out_basis.shape[1]
    grads = raw.astype(jnp.float32).reshape(count, layers, side, side)
    highest = lax.Precision.HIGHEST
    half = jnp.einsum("lao,nlab->nlob", out_basis, grads, precision=highest)
    rotated = jnp.einsum("nlob,lbi->nloi", half, in_basis, precision=highest)
    scaled = rotated / (eigenvalues.reshape(layers, side, side) + DAMPING)
    half_back = jnp.einsum("lao,nloi->nlai", out_basis, scaled, precision=highest)
    back = jnp.einsum("nlai,lbi->nlab", half_back, in_basis, precision=highest)
    return back.reshape(count, layers, width).astype(jnp.bfloat16)


def body(train_grads, query_grads, out_basis, in_basis, eigenvalues, block_order, row_ids):
    blocks, qdev, layers, width = query_grads.shape
    ordered_rows = jnp.take(train_grads, row_ids[0], axis=0)
    outgoing = precondition(
        query_grads.reshape(blocks * qdev, layers, width), out_basis, in_basis, eigenvalues
    )
    outgoing = outgoing.reshape(blocks, qdev, layers, width)
    results = []
    for j in range(blocks):
        chosen = lax.dynamic_index_in_dim(outgoing, block_order[j], 0, keepdims=False)
        flat = lax.all_gather(chosen, "row", axis=0, tiled=True)
        terms = jnp.einsum("rlp,qlp->rq", ordered_rows, flat, preferred_element_type=jnp.float32)
        results.append(
            lax.psum_scatter(terms, "layer", scatter_dimension=1, tiled=True).astype(jnp.bfloat16)
        )
    return jnp.stack(results, axis=0)


def solution(mesh):
    in_specs = (
        P(("grp", "row"), "layer", None),
        P(None, "row", "layer", None),
        P("layer", None, None),
        P("layer", None, None),
        P("layer", None),
        P(),
        P(("grp", "row"), None),
    )
    out_specs = P(None, ("grp", "row"), "layer")
    return jax.shard_map(body, mesh=mesh, in_specs=in_specs, out_specs=out_specs, check_vma=False)
```

profile of v0, /device:TPU:0, one launch (start us, length us, event | category | flops | bytes accessed | tf_op | source)
XLA Modules:
  0.0 143.2 jit_solution(6415681909086268523)
XLA Ops:
  6.5 0.0 copy-start
  6.5 0.0 copy-start.1
  6.5 0.0 reduce-scatter.6.cloned.1.call-start
  6.5 1.5 %fusion.22 = (s32[1]{0:T(128)}, s32[1]{0:T(128)}, s32[1]{0:T(128)}) fusion(s32[3]{0:T(128)} %param.12), kind=kLoop, calls=%fused_computation.40 | loop fusion | bytes 24 | tf_op jit(solution)/shard_map/slice | solution.py:31
  11.9 0.9 reshape.165
  12.8 0.8 add_reduce_fusion
  13.6 0.1 add.58
  13.6 1.0 convolution_bitcast_fusion.2
  14.7 1.2 fusion.8
  15.9 1.2 convolution_bitcast_fusion
  17.2 1.2 fusion.6
  18.4 0.1 convert_element_type.38
  20.6 32.5 %all-gather.1 = bf16[1,16,1,4096]{3,2,0,1:T(2,128)(2,1)S(1)} all-gather(bf16[1,2,1,4096]{3,2,0,1:T(2,128)(2,1)S(1)} %copy.38), channel_id=3, replica_groups=mesh['grp'=2,'row'=8,'layer'=2] {'row'}, dimensions={1}, use_global_device_ids=true | all-gather | bytes 147456 | tf_op jit(solution)/shard_map/all_gather | solution.py:32
  53.1 0.0 copy-done.1
  53.1 0.0 copy-done
  53.2 3.2 %gather_fusion = bf16[256,4096]{1,0:T(8,128)(2,1)} fusion(bf16[256,4096]{1,0:T(8,128)(2,1)S(1)} %bitcast.93, s32[1024]{0:T(1024)S(1)} %pad_clamp_fusion), kind=kCustom, calls=%fused_computation | custom fusion | bytes 4195328 | tf_op jit(solution)/shard_map/jit(_take)/gather | solution.py:24
  56.4 2.9 %fusion.2 = f32[256,16]{0,1:T(8,128)} fusion(bf16[256,4096]{1,0:T(8,128)(2,1)} %gather_fusion, pred[256]{0:T(512)(128)(4,1)S(1)} %compare_and_fusion, bf16[1,16,1,4096]{3,2,0,1:T(2,128)(2,1)S(1)} %all-gather.1), kind=kOutput, calls=%fused_computation.3 | convolution fusion | flops 34603008 | bytes 2244864 | tf_op jit(solution)/shard_map/rlp,qlp->rq/dot_general | solution.py:33
  59.3 0.0 reduce-scatter.6.cloned.1.call-update
  59.3 0.0 reduce-scatter.4.cloned.1.call-start
  59.4 30.7 %all-gather = bf16[1,16,1,4096]{3,2,0,1:T(2,128)(2,1)S(1)} all-gather(bf16[1,2,1,4096]{3,2,0,1:T(2,128)(2,1)S(1)} %copy.37), channel_id=2, replica_groups=mesh['grp'=2,'row'=8,'layer'=2] {'row'}, dimensions={1}, use_global_device_ids=true | all-gather | bytes 147456 | tf_op jit(solution)/shard_map/all_gather | solution.py:32
  90.1 2.9 %fusion.4 = f32[256,16]{0,1:T(8,128)} fusion(bf16[256,4096]{1,0:T(8,128)(2,1)} %gather_fusion, pred[256]{0:T(512)(128)(4,1)S(1)} %compare_and_fusion, bf16[1,16,1,4096]{3,2,0,1:T(2,128)(2,1)S(1)} %all-gather), kind=kOutput, calls=%fused_computation.5 | convolution fusion | flops 34603008 | bytes 2244864 | tf_op jit(solution)/shard_map/rlp,qlp->rq/dot_general | solution.py:33
  93.0 0.0 reduce-scatter.4.cloned.1.call-update
  93.1 0.0 reduce-scatter.8.cloned.1.call-start
  93.2 30.8 %all-gather.2 = bf16[1,16,1,4096]{3,2,0,1:T(2,128)(2,1)S(1)} all-gather(bf16[1,2,1,4096]{3,2,0,1:T(2,128)(2,1)S(1)} %copy.39), channel_id=4, replica_groups=mesh['grp'=2,'row'=8,'layer'=2] {'row'}, dimensions={1}, use_global_device_ids=true | all-gather | bytes 147456 | tf_op jit(solution)/shard_map/all_gather | solution.py:32
  124.0 2.9 %fusion = f32[256,16]{0,1:T(8,128)} fusion(bf16[256,4096]{1,0:T(8,128)(2,1)} %gather_fusion, pred[256]{0:T(512)(128)(4,1)S(1)} %compare_and_fusion, bf16[1,16,1,4096]{3,2,0,1:T(2,128)(2,1)S(1)} %all-gather.2), kind=kOutput, calls=%fused_computation.1 | convolution fusion | flops 34603008 | bytes 2244864 | tf_op jit(solution)/shard_map/rlp,qlp->rq/dot_general | solution.py:33
  126.9 0.0 reduce-scatter.8.cloned.1.call-update
  126.9 0.0 reduce-scatter.6.cloned.1.call-done
  127.0 0.7 convert_bitcast_fusion.1
  127.7 0.0 reduce-scatter.4.cloned.1.call-done
  127.7 0.7 convert_bitcast_fusion.2
  128.4 7.0 %reduce-scatter.8.cloned.1.call-done = f32[256,8]{0,1:T(8,128)} async-done(((f32[256,16]{0,1:T(8,128)}), f32[256,8]{0,1:T(8,128)}) %reduce-scatter.8.cloned.1.call-update) | async-done | bytes 8208 | tf_op jit(solution)/shard_map/reduce_scatter | solution.py:35
  135.4 0.7 convert_bitcast_fusion
  136.1 0.6 pad_maximum_fusion
  (7 shorter events, 0.1 us)
Async XLA Ops:
  6.5 46.6 %copy-start = (bf16[256,1,4096]{2,0,1:T(8,128)(2,1)S(1)}, bf16[256,1,4096]{2,0,1:T(8,128)(2,1)}, u32[]{:S(2)}) copy-start(bf16[256,1,4096]{2,0,1:T(8,128)(2,1)} %param.7) | copy-start | bytes 6291460
  6.5 46.6 %copy-start.1 = (s32[1,256]{1,0:T(1,128)S(1)}, s32[1,256]{1,0:T(1,128)}, u32[]{:S(2)}) copy-start(s32[1,256]{1,0:T(1,128)} %param.13) | copy-start | bytes 3076
  6.5 120.4 %reduce-scatter.6.cloned.1.call-start = ((), (), s32[]{:S(2)}) async-start(), calls=%async_computation.4 | async-start | bytes 24576 | tf_op jit(solution)/shard_map/reduce_scatter | solution.py:35
  59.3 68.4 %reduce-scatter.4.cloned.1.call-start = ((), (), s32[]{:S(2)}) async-start(), calls=%async_computation.3 | async-start | bytes 24576 | tf_op jit(solution)/shard_map/reduce_scatter | solution.py:35
  93.1 42.3 %reduce-scatter.8.cloned.1.call-start = ((), (), s32[]{:S(2)}) async-start(), calls=%async_computation.5 | async-start | bytes 24576 | tf_op jit(solution)/shard_map/reduce_scatter | solution.py:35
Sparse Core Ops, SparseCore 0:
  59.4 8.3 reduce-scatter.5
  93.2 8.3 reduce-scatter.3
  127.0 8.3 reduce-scatter.7
where the time goes:
time: 144 us; the launch traced here: 143 us
  blocking collectives  94.1 us (65%)
  between operations  19 us (13%)
  matrix products  13.5 us (9%)
  waiting for transfers between devices  7.11 us (5%)
  local copies, waits for them, and re-layouts  5.96 us (4%)
  other arithmetic  3.48 us (2%)
    all_gather x3, blocking collectives, body(): flat = lax.all_gather(chosen, 'row', axis=0, tiled=True)  94.1 us
    dot_general x3, matrix products, body(): jnp.einsum('rlp,qlp->rq', ordered_rows, flat, preferred_element_type=jnp....  8.76 us
    reduce_scatter x3, waiting for transfers between devices, body(): lax.psum_scatter(terms, 'layer', scatter_dimension=1, tiled=True)  7.06 us
    gather x1, local copies, waits for them, and re-layouts, body(): ordered_rows = jnp.take(train_grads, row_ids[0], axis=0)  3.19 us
  transfers between devices with their start and end apart: 3, of which 1 were waited for; matrix products, arithmetic and copies ran while one was open for 5% of the time, Pallas kernels for 0%

commit v1 on v0

v1 whole, which is shorter than its diff:
```python
import jax
import jax.numpy as jnp
from jax import lax
from jax.sharding import PartitionSpec as P

DAMPING = 0.01


def precondition(raw, out_basis, in_basis, eigenvalues):
    count, layers, width = raw.shape
    side = out_basis.shape[1]
    grads = raw.astype(jnp.float32).reshape(count, layers, side, side)
    highest = lax.Precision.HIGHEST
    half = jnp.einsum("lao,nlab->nlob", out_basis, grads, precision=highest)
    rotated = jnp.einsum("nlob,lbi->nloi", half, in_basis, precision=highest)
    scaled = rotated / (eigenvalues.reshape(layers, side, side) + DAMPING)
    half_back = jnp.einsum("lao,nloi->nlai", out_basis, scaled, precision=highest)
    back = jnp.einsum("nlai,lbi->nlab", half_back, in_basis, precision=highest)
    return back.reshape(count, layers, width).astype(jnp.bfloat16)


def make_body(n_row, n_layer):
    def body(train_grads, query_grads, out_basis, in_basis, eigenvalues, block_order, row_ids):
        blocks, qdev, layers, width = query_grads.shape
        rows = train_grads.shape[0]
        own = precondition(
            query_grads.reshape(blocks * qdev, layers, width), out_basis, in_basis, eigenvalues
        )
        own = own.reshape(blocks * qdev, width)
        me = lax.axis_index("row")
        parts = [own]
        for m in range(1, n_row):
            parts.append(lax.ppermute(own, "row", [(i, i ^ m) for i in range(n_row)]))
        flat = jnp.concatenate(parts, axis=0)
        terms = jnp.dot(train_grads[:, 0, :], flat.T, preferred_element_type=jnp.float32)
        terms = terms.reshape(rows, n_row, blocks, qdev)
        source = jnp.arange(n_row, dtype=jnp.int32) ^ me
        terms = jnp.take(terms, source, axis=1)
        terms = terms.transpose(2, 0, 1, 3).reshape(blocks, rows, n_layer, n_row * qdev // n_layer)
        core = lax.axis_index("layer")
        mine = lax.dynamic_index_in_dim(terms, core, 2, keepdims=False)
        theirs = lax.dynamic_index_in_dim(terms, 1 - core, 2, keepdims=False)
        got = lax.ppermute(theirs, "layer", [(0, 1), (1, 0)])
        total = (mine + got).astype(jnp.bfloat16)
        return jnp.take(jnp.take(total, block_order, axis=0), row_ids[0], axis=1)

    return body


def solution(mesh):
    in_specs = (
        P(("grp", "row"), "layer", None),
        P(None, "row", "layer", None),
        P("layer", None, None),
        P("layer", None, None),
        P("layer", None),
        P(),
        P(("grp", "row"), None),
    )
    out_specs = P(None, ("grp", "row"), "layer")
    body = make_body(mesh.shape["row"], mesh.shape["layer"])
    return jax.shard_map(body, mesh=mesh, in_specs=in_specs, out_specs=out_specs, check_vma=False)
```

time: 144 us -> 33.6 us (0.23)
  blocking collectives: 94.1 us -> 0 us
  between operations: 19 us -> 0.23 us
  starting transfers between devices: 0.09 us -> 12.7 us
  matrix products: 13.5 us -> 5.53 us
  other arithmetic: 3.48 us -> 1.33 us
    all_gather x3 -> x0, blocking collectives: 94.1 us -> none  [body(): flat = lax.all_gather(chosen, 'row', axis=0, tiled=True)]
    ppermute x0 -> x8, starting transfers between devices: none -> 12.7 us  [the longest x7 12.6 us: body(): parts.append(lax.ppermute(own, 'row', [(i, i ^ m) for i in range(n_row)]))]
    ppermute x0 -> x8, waiting for transfers between devices: none -> 8.16 us  [the longest x7 6.99 us: body(): parts.append(lax.ppermute(own, 'row', [(i, i ^ m) for i in range(n_row)]))]
    dot_general x3 -> x1, matrix products: 8.76 us -> 0.75 us  [body(): jnp.dot(train_grads[:, 0, :], flat.T, preferred_element_type=jnp.float32)]
    reduce_scatter x3 -> x0, waiting for transfers between devices: 7.06 us -> none  [body(): lax.psum_scatter(terms, 'layer', scatter_dimension=1, tiled=True)]
    another operation x4 -> x0, other arithmetic: 2.7 us -> none  [body(): return jnp.stack(results, axis=0)]
    slice x1 -> x0, local copies, waits for them, and re-layouts: 1.5 us -> none  [body(): block_order[j]]
    gather x1 -> x3, local copies, waits for them, and re-layouts: 3.19 us -> 2.13 us  [the longest x2 1.53 us: body(): return jnp.take(jnp.take(total, block_order, axis=0), row_ids[0], axis=1)]
  transfers between devices with their start and end apart: 3 -> 8, of which waited for: 1 -> 3; matrix products, arithmetic and copies ran while one was open for 5% -> 0% of each run, Pallas kernels for 0% -> 0%
where the time goes in v1:
time: 33.6 us; the launch traced here: 33.2 us
  starting transfers between devices  12.7 us (38%)
  waiting for transfers between devices  8.16 us (24%)
  matrix products  5.53 us (16%)
  local copies, waits for them, and re-layouts  5.27 us (16%)
  other arithmetic  1.33 us (4%)
    ppermute x7, starting transfers between devices, body(): parts.append(lax.ppermute(own, 'row', [(i, i ^ m) for i in range(n_row)]))  12.6 us
    ppermute x7, waiting for transfers between devices, body(): parts.append(lax.ppermute(own, 'row', [(i, i ^ m) for i in range(n_row)]))  6.99 us
    gather x2, local copies, waits for them, and re-layouts, body(): return jnp.take(jnp.take(total, block_order, axis=0), row_ids[0], axis=1)  1.53 us
    dot_general x1, matrix products, precondition(): back = jnp.einsum('nlai,lbi->nlab', half_back, in_basis, precision=highest)  1.25 us
    dot_general x1, matrix products, precondition(): rotated = jnp.einsum('nlob,lbi->nloi', half, in_basis, precision=highest)  1.25 us
    dot_general x1, matrix products, precondition(): jnp.einsum('lao,nloi->nlai', out_basis, scaled, precision=highest)  1.25 us
    ppermute x1, waiting for transfers between devices, body(): got = lax.ppermute(theirs, 'layer', [(0, 1), (1, 0)])  1.17 us
    another operation x1, local copies, waits for them, and re-layouts  1.07 us
  transfers between devices with their start and end apart: 8, of which 3 were waited for; matrix products, arithmetic and copies ran while one was open for 0% of the time, Pallas kernels for 0%

profile of v1, /device:TPU:0, one launch (start us, length us, event | category | flops | bytes accessed | tf_op | source)
XLA Modules:
  0.0 33.2 jit_solution(17611382328415812474)
XLA Ops:
  0.0 0.0 copy-start
  0.0 0.0 copy-start.2
  0.0 0.0 copy-start.1
  0.0 1.1 %reshape.115 = bf16[6,64,64]{2,1,0:T(8,128)(2,1)S(1)} reshape(bf16[3,2,1,4096]{3,1,2,0:T(2,128)(2,1)} %param.8) | data formatting | bytes 98304 | tf_op jit(solution)/shard_map/reshape.4
  1.1 0.8 %add_reduce_fusion = f32[4096]{0:T(1024)S(1)} fusion(f32[1,4096]{1,0:T(1,128)} %param.11), kind=kLoop, calls=%fused_computation.22 | loop fusion | flops 4096 | bytes 32768 | tf_op jit(solution)/shard_map/add | solution.py:16
  1.8 0.1 add.72
  1.9 1.0 %convolution_bitcast_fusion.2 = f32[6,64,64]{1,2,0:T(8,128)S(1)} fusion(bf16[6,64,64]{2,1,0:T(8,128)(2,1)S(1)} %reshape.115, f32[1,64,64]{2,1,0:T(8,128)} %param.9), kind=kOutput, calls=%fused_computation.7 | convolution fusion | flops 18874368 | bytes 163840 | tf_op jit(solution)/shard_map/lao,nlab->nlob/dot_general | solution.py:14
  3.0 1.2 %fusion.7 = f32[6,64,64]{2,1,0:T(8,128)S(1)} fusion(f32[6,64,64]{1,2,0:T(8,128)S(1)} %convolution_bitcast_fusion.2, f32[64,64]{1,0:T(8,128)S(1)} %add.72, f32[1,64,64]{2,1,0:T(8,128)} %param.10), kind=kOutput, calls=%fused_computation.12 | convolution fusion | flops 18898944 | bytes 229376 | tf_op jit(solution)/shard_map/nlob,lbi->nloi/dot_general | solution.py:15
  4.2 1.2 %convolution_bitcast_fusion = f32[6,64,64]{1,2,0:T(8,128)S(1)} fusion(f32[6,64,64]{2,1,0:T(8,128)S(1)} %fusion.7, f32[1,64,64]{2,1,0:T(8,128)} %param.9), kind=kOutput, calls=%fused_computation.5 | convolution fusion | flops 18874368 | bytes 212992 | tf_op jit(solution)/shard_map/lao,nloi->nlai/dot_general | solution.py:17
  5.5 1.2 %fusion.2 = bf16[6,1,64,64]{3,2,0,1:T(8,128)(2,1)S(1)} fusion(f32[6,64,64]{1,2,0:T(8,128)S(1)} %convolution_bitcast_fusion, f32[1,64,64]{2,1,0:T(8,128)} %param.10), kind=kOutput, calls=%fused_computation.9 | convolution fusion | flops 18898944 | bytes 163840 | tf_op jit(solution)/shard_map/nlai,lbi->nlab/dot_general | solution.py:18
  6.7 0.1 convert_element_type.26
  6.9 3.0 %collective-permute-start = (bf16[6,4096]{1,0:T(8,128)(2,1)S(1)}, bf16[6,4096]{1,0:T(8,128)(2,1)S(1)}, u32[]{:S(2)}, u32[]{:S(2)}) collective-permute-start(bf16[6,4096]{1,0:T(8,128)(2,1)S(1)} %convert_element_type.26), channel_id=1, source_target_pairs={{0,2},{2,0},{4,6},{6,4},{8,10},{10,8},{12,14},{14,12},{1,3},{3,1},... | collective-permute-start | bytes 147464 | tf_op jit(solution)/shard_map/ppermute | solution.py:33
  9.9 1.6 %collective-permute-start.1 = (bf16[6,4096]{1,0:T(8,128)(2,1)S(1)}, bf16[6,4096]{1,0:T(8,128)(2,1)S(1)}, u32[]{:S(2)}, u32[]{:S(2)}) collective-permute-start(bf16[6,4096]{1,0:T(8,128)(2,1)S(1)} %convert_element_type.26), channel_id=1, source_target_pairs={{0,4},{2,6},{4,0},{6,2},{8,12},{10,14},{12,8},{14,10},{1,5},{3,7},... | collective-permute-start | bytes 147464 | tf_op jit(solution)/shard_map/ppermute | solution.py:33
  11.5 0.0 collective-permute-start.2
  11.5 3.0 %collective-permute-start.3 = (bf16[6,4096]{1,0:T(8,128)(2,1)S(1)}, bf16[6,4096]{1,0:T(8,128)(2,1)S(1)}, u32[]{:S(2)}, u32[]{:S(2)}) collective-permute-start(bf16[6,4096]{1,0:T(8,128)(2,1)S(1)} %convert_element_type.26), channel_id=1, source_target_pairs={{0,8},{2,10},{4,12},{6,14},{8,0},{10,2},{12,4},{14,6},{1,9},{3,11}... | collective-permute-start | bytes 147464 | tf_op jit(solution)/shard_map/ppermute | solution.py:33
  14.5 1.3 %collective-permute-start.4 = (bf16[6,4096]{1,0:T(8,128)(2,1)S(1)}, bf16[6,4096]{1,0:T(8,128)(2,1)S(1)}, u32[]{:S(2)}, u32[]{:S(2)}) collective-permute-start(bf16[6,4096]{1,0:T(8,128)(2,1)S(1)} %convert_element_type.26), channel_id=1, source_target_pairs={{0,10},{2,8},{4,14},{6,12},{8,2},{10,0},{12,6},{14,4},{1,11},{3,9}... | collective-permute-start | bytes 147464 | tf_op jit(solution)/shard_map/ppermute | solution.py:33
  15.7 0.0 copy-done.2
  15.8 0.0 copy-done.1
  15.8 0.0 collective-permute-done
  15.8 3.7 %collective-permute-start.5 = (bf16[6,4096]{1,0:T(8,128)(2,1)S(1)}, bf16[6,4096]{1,0:T(8,128)(2,1)S(1)}, u32[]{:S(2)}, u32[]{:S(2)}) collective-permute-start(bf16[6,4096]{1,0:T(8,128)(2,1)S(1)} %convert_element_type.26), channel_id=1, source_target_pairs={{0,12},{2,14},{4,8},{6,10},{8,4},{10,6},{12,0},{14,2},{1,13},{3,15... | collective-permute-start | bytes 147464 | tf_op jit(solution)/shard_map/ppermute | solution.py:33
  19.5 0.0 collective-permute-done.1
  19.5 0.1 collective-permute-start.6
  19.6 0.0 collective-permute-done.2
  19.6 0.0 collective-permute-done.3
  19.6 5.1 %collective-permute-done.4 = bf16[6,4096]{1,0:T(8,128)(2,1)S(1)} collective-permute-done((bf16[6,4096]{1,0:T(8,128)(2,1)S(1)}, bf16[6,4096]{1,0:T(8,128)(2,1)S(1)}, u32[]{:S(2)}, u32[]{:S(2)}) %collective-permute-start.4) | collective-permute-done | bytes 49184 | tf_op jit(solution)/shard_map/ppermute | solution.py:33
  24.6 0.0 collective-permute-done.5
  24.6 1.9 %collective-permute-done.6 = bf16[6,4096]{1,0:T(8,128)(2,1)S(1)} collective-permute-done((bf16[6,4096]{1,0:T(8,128)(2,1)S(1)}, bf16[6,4096]{1,0:T(8,128)(2,1)S(1)}, u32[]{:S(2)}, u32[]{:S(2)}) %collective-permute-start.6) | collective-permute-done | bytes 49184 | tf_op jit(solution)/shard_map/ppermute | solution.py:33
  26.6 0.8 %concatenate.3 = bf16[48,4096]{1,0:T(8,128)(2,1)S(1)} concatenate(bf16[6,4096]{1,0:T(8,128)(2,1)S(1)} %convert_element_type.26, bf16[6,4096]{1,0:T(8,128)(2,1)S(1)} %collective-permute-done, bf16[6,4096]{1,0:T(8,128)(2,1)S(1)} %collective-permute-done.1, bf16[6,4096]{1,0:T(8,128)(2,1)S(1)} %collective-permute-done.2, bf16[6,4096]{1,0:T(8,128)(2,1)S(1)} %collective-permute-done.3, ...), dimensions={0} | concatenate | bytes 786432 | tf_op jit(solution)/shard_map/concatenate | solution.py:34
  27.4 0.0 copy-done
  27.4 0.7 %fusion.3 = f32[256,48]{0,1:T(8,128)S(1)} fusion(bf16[48,4096]{1,0:T(8,128)(2,1)S(1)} %concatenate.3, bf16[256,1,4096]{2,0,1:T(8,128)(2,1)S(1)} %copy-done), kind=kOutput, calls=%fused_computation.10 | convolution fusion | flops 100663296 | bytes 2539520 | tf_op jit(solution)/shard_map/dot_general | solution.py:35
  28.2 0.6 %gather_fusion = f32[8,256,3,2]{1,3,2,0:T(2,128)S(1)} fusion(f32[256,8,3,2]{0,3,2,1:T(2,128)S(1)} %reshape.121, s32[1024]{0:T(1024)S(1)} %pad_clamp_fusion.2), kind=kCustom, calls=%fused_computation | custom fusion | bytes 98336 | tf_op jit(solution)/shard_map/jit(_take)/gather | solution.py:38
  28.8 0.1 select_bitcast_fusion.1
  29.0 0.1 collective-permute-start.7
  29.1 1.2 %collective-permute-done.7 = f32[3,256,8]{1,2,0:T(8,128)S(1)} collective-permute-done((f32[3,256,8]{1,2,0:T(8,128)S(1)}, f32[3,256,8]{1,2,0:T(8,128)S(1)}, u32[]{:S(2)}, u32[]{:S(2)}) %collective-permute-start.7) | collective-permute-done | bytes 24608 | tf_op jit(solution)/shard_map/ppermute | solution.py:43
  30.3 0.5 %gather_fusion.1 = bf16[3,256,8]{1,2,0:T(8,128)(2,1)S(1)} fusion(bf16[3,256,8]{1,2,0:T(8,128)(2,1)S(1)} %fusion.12, s32[1024]{0:T(1024)S(1)} %pad_clamp_fusion.1), kind=kCustom, calls=%fused_computation.1 | custom fusion | bytes 24588 | tf_op jit(solution)/shard_map/jit(_take)/gather | solution.py:45
  30.8 0.1 broadcast_select_fusion
  30.9 0.2 copy.22
  31.1 1.0 %gather_fusion.2 = bf16[256,3,8]{2,1,0:T(4,128)(2,1)S(1)} fusion(bf16[3,256,8]{2,0,1:T(4,128)(2,1)S(1)} %copy.22, s32[1024]{0:T(1024)S(1)} %pad_clamp_fusion), kind=kCustom, calls=%fused_computation.2 | custom fusion | bytes 25600 | tf_op jit(solution)/shard_map/jit(_take)/gather | solution.py:45
  32.1 0.3 %select_bitcast_fusion = bf16[3,256,8]{2,0,1:T(4,128)(2,1)S(1)} fusion(bf16[256,3,8]{2,1,0:T(4,128)(2,1)S(1)} %gather_fusion.2, pred[256]{0:T(512)(128)(4,1)S(1)} %compare_and_fusion.2), kind=kLoop, calls=%fused_computation.13 | loop fusion | flops 6144 | bytes 24832 | tf_op jit(solution)/shard_map/jit(_take)/select_n | solution.py:45
  32.4 0.7 %copy.23 = bf16[3,256,8]{1,2,0:T(8,128)(2,1)} copy(bf16[3,256,8]{2,0,1:T(4,128)(2,1)S(1)} %select_bitcast_fusion) | data formatting | bytes 24576 | tf_op jit(solution)/shard_map/jit(_take)/select_n | solution.py:45
  (14 shorter events, 0.1 us)
Async XLA Ops:
  0.0 27.4 %copy-start = (bf16[256,1,4096]{2,0,1:T(8,128)(2,1)S(1)}, bf16[256,1,4096]{2,0,1:T(8,128)(2,1)}, u32[]{:S(2)}) copy-start(bf16[256,1,4096]{2,0,1:T(8,128)(2,1)} %param.7) | copy-start | bytes 6291460
  0.0 15.7 %copy-start.2 = (s32[3]{0:T(128)S(1)}, s32[3]{0:T(128)}, u32[]{:S(2)}) copy-start(s32[3]{0:T(128)} %param.12) | copy-start | bytes 40
  0.0 15.8 %copy-start.1 = (s32[1,256]{1,0:T(1,128)S(1)}, s32[1,256]{1,0:T(1,128)}, u32[]{:S(2)}) copy-start(s32[1,256]{1,0:T(1,128)} %param.13) | copy-start | bytes 3076
  6.9 9.0 %collective-permute-start = (bf16[6,4096]{1,0:T(8,128)(2,1)S(1)}, bf16[6,4096]{1,0:T(8,128)(2,1)S(1)}, u32[]{:S(2)}, u32[]{:S(2)}) collective-permute-start(bf16[6,4096]{1,0:T(8,128)(2,1)S(1)} %convert_element_type.26), channel_id=1, source_target_pairs={{0,2},{2,0},{4,6},{6,4},{8,10},{10,8},{12,14},{14,12},{1,3},{3,1},... | collective-permute-start | bytes 147464 | tf_op jit(solution)/shard_map/ppermute | solution.py:33
  9.9 9.6 %collective-permute-start.1 = (bf16[6,4096]{1,0:T(8,128)(2,1)S(1)}, bf16[6,4096]{1,0:T(8,128)(2,1)S(1)}, u32[]{:S(2)}, u32[]{:S(2)}) collective-permute-start(bf16[6,4096]{1,0:T(8,128)(2,1)S(1)} %convert_element_type.26), channel_id=1, source_target_pairs={{0,4},{2,6},{4,0},{6,2},{8,12},{10,14},{12,8},{14,10},{1,5},{3,7},... | collective-permute-start | bytes 147464 | tf_op jit(solution)/shard_map/ppermute | solution.py:33
  11.5 8.1 %collective-permute-start.2 = (bf16[6,4096]{1,0:T(8,128)(2,1)S(1)}, bf16[6,4096]{1,0:T(8,128)(2,1)S(1)}, u32[]{:S(2)}, u32[]{:S(2)}) collective-permute-start(bf16[6,4096]{1,0:T(8,128)(2,1)S(1)} %convert_element_type.26), channel_id=1, source_target_pairs={{0,6},{2,4},{4,2},{6,0},{8,14},{10,12},{12,10},{14,8},{1,7},{3,5},... | collective-permute-start | bytes 147464 | tf_op jit(solution)/shard_map/ppermute | solution.py:33
  11.5 8.1 %collective-permute-start.3 = (bf16[6,4096]{1,0:T(8,128)(2,1)S(1)}, bf16[6,4096]{1,0:T(8,128)(2,1)S(1)}, u32[]{:S(2)}, u32[]{:S(2)}) collective-permute-start(bf16[6,4096]{1,0:T(8,128)(2,1)S(1)} %convert_element_type.26), channel_id=1, source_target_pairs={{0,8},{2,10},{4,12},{6,14},{8,0},{10,2},{12,4},{14,6},{1,9},{3,11}... | collective-permute-start | bytes 147464 | tf_op jit(solution)/shard_map/ppermute | solution.py:33
  14.5 10.2 %collective-permute-start.4 = (bf16[6,4096]{1,0:T(8,128)(2,1)S(1)}, bf16[6,4096]{1,0:T(8,128)(2,1)S(1)}, u32[]{:S(2)}, u32[]{:S(2)}) collective-permute-start(bf16[6,4096]{1,0:T(8,128)(2,1)S(1)} %convert_element_type.26), channel_id=1, source_target_pairs={{0,10},{2,8},{4,14},{6,12},{8,2},{10,0},{12,6},{14,4},{1,11},{3,9}... | collective-permute-start | bytes 147464 | tf_op jit(solution)/shard_map/ppermute | solution.py:33
  15.8 8.8 %collective-permute-start.5 = (bf16[6,4096]{1,0:T(8,128)(2,1)S(1)}, bf16[6,4096]{1,0:T(8,128)(2,1)S(1)}, u32[]{:S(2)}, u32[]{:S(2)}) collective-permute-start(bf16[6,4096]{1,0:T(8,128)(2,1)S(1)} %convert_element_type.26), channel_id=1, source_target_pairs={{0,12},{2,14},{4,8},{6,10},{8,4},{10,6},{12,0},{14,2},{1,13},{3,15... | collective-permute-start | bytes 147464 | tf_op jit(solution)/shard_map/ppermute | solution.py:33
  19.5 7.1 %collective-permute-start.6 = (bf16[6,4096]{1,0:T(8,128)(2,1)S(1)}, bf16[6,4096]{1,0:T(8,128)(2,1)S(1)}, u32[]{:S(2)}, u32[]{:S(2)}) collective-permute-start(bf16[6,4096]{1,0:T(8,128)(2,1)S(1)} %convert_element_type.26), channel_id=1, source_target_pairs={{0,14},{2,12},{4,10},{6,8},{8,6},{10,4},{12,2},{14,0},{1,15},{3,13... | collective-permute-start | bytes 147464 | tf_op jit(solution)/shard_map/ppermute | solution.py:33
  29.0 1.3 %collective-permute-start.7 = (f32[3,256,8]{1,2,0:T(8,128)S(1)}, f32[3,256,8]{1,2,0:T(8,128)S(1)}, u32[]{:S(2)}, u32[]{:S(2)}) collective-permute-start(f32[3,256,8]{1,2,0:T(8,128)S(1)} %dynamic-slice_bitcast_fusion), channel_id=1, source_target_pairs={{0,1},{1,0},{2,3},{3,2},{4,5},{5,4},{6,7},{7,6},{8,9},{9,8},{10,11... | collective-permute-start | bytes 73736 | tf_op jit(solution)/shard_map/ppermute | solution.py:43

commit v2 on v0

v2 whole, which is shorter than its diff:
```python
import functools

import jax
import jax.numpy as jnp
from jax import lax
from jax.experimental import pallas as pl
from jax.experimental.pallas import tpu as pltpu
from jax.sharding import PartitionSpec as P

DAMPING = 0.01
LANES = 128
SEGMENTS = 4
F32, BF16 = jnp.float32, jnp.bfloat16
NT = (((1,), (1,)), ((), ()))


def split2(x):
    high = x.astype(BF16)
    return high, (x - high.astype(F32)).astype(BF16)


def mm(a, b):
    return jnp.dot(a, b, preferred_element_type=F32)


def mm_nt(a, b):
    return lax.dot_general(a, b, NT, preferred_element_type=F32)


def precondition_kernel(q_ref, out_basis_ref, in_basis_ref, eig_ref, sent_ref, x_scr, o_scr, eig_scr):
    blocks, qdev, width = q_ref.shape
    side = out_basis_ref.shape[1]
    half = side // 2
    count = blocks * qdev
    chunks = width // LANES
    for blk in range(blocks):
        flat = q_ref[blk].astype(F32)
        for k in range(chunks):
            x_scr[pl.ds(blk * qdev * chunks + k, qdev, stride=chunks), :] = flat[:, k * LANES:(k + 1) * LANES]
    scale = 1.0 / (eig_ref[...] + DAMPING)
    for k in range(chunks):
        for odd in range(2):
            at = k * LANES + odd * side
            eig_scr[2 * k + odd:2 * k + odd + 1, :side] = scale[:, at:at + side]
    scale = eig_scr[:, :side]
    o_scr[:, :side] = out_basis_ref[0]
    basis = jnp.concatenate(
        [o_scr[pl.ds(0, half, stride=2), :side], o_scr[pl.ds(1, half, stride=2), :side]], axis=0
    )
    b_hi, b_lo = split2(basis)
    t_hi, t_lo = split2(basis.T)
    left = jnp.concatenate([t_hi, t_hi, t_lo], axis=1)
    back = jnp.concatenate([b_hi, b_hi, b_lo], axis=1)
    i_hi, i_lo = split2(in_basis_ref[0])
    none = jnp.zeros_like(i_hi)
    raw = x_scr[...].astype(BF16)
    raw2 = jnp.concatenate([raw, raw], axis=1)
    even = mm(raw2, jnp.concatenate([i_hi, none, i_lo, none], axis=0))
    odd = mm(raw2, jnp.concatenate([none, i_hi, none, i_lo], axis=0))
    evens, odds = [], []
    for q in range(count):
        rows = slice(q * half, (q + 1) * half)
        hi, lo = split2(jnp.concatenate([even[rows], odd[rows]], axis=0))
        rotated = mm(left, jnp.concatenate([hi, lo, hi], axis=0))
        hi, lo = split2(rotated * scale)
        again = mm(back, jnp.concatenate([hi, lo, hi], axis=0))
        evens.append(again[:half])
        odds.append(again[half:])
    total = None
    for rows, lower in ((evens, False), (odds, True)):
        hi, lo = split2(jnp.concatenate(rows, axis=0))
        w_hi = jnp.concatenate([none, i_hi] if lower else [i_hi, none], axis=0)
        w_lo = jnp.concatenate([none, i_lo] if lower else [i_lo, none], axis=0)
        term = mm_nt(hi, w_hi) + mm_nt(lo, w_hi) + mm_nt(hi, w_lo)
        total = term if total is None else total + term
    x_scr[...] = total
    per = chunks // SEGMENTS
    for c in range(per):
        piece = x_scr[pl.ds(c, count * SEGMENTS, stride=per), :].astype(BF16)
        for d in range(sent_ref.shape[0]):
            sent_ref[d, :, c * LANES:(c + 1) * LANES] = piece


def precondition(query_grads, out_basis, in_basis, eigenvalues, copies):
    blocks, qdev, _, width = query_grads.shape
    count = blocks * qdev
    side = out_basis.shape[1]
    return pl.pallas_call(
        precondition_kernel,
        out_shape=jax.ShapeDtypeStruct((copies, count * SEGMENTS, width // SEGMENTS), BF16),
        in_specs=[pl.BlockSpec(memory_space=pltpu.VMEM)] * 4,
        out_specs=pl.BlockSpec(memory_space=pltpu.VMEM),
        scratch_shapes=[
            pltpu.VMEM((count * width // LANES, LANES), F32),
            pltpu.VMEM((side, LANES), F32),
            pltpu.VMEM((side, LANES), F32),
        ],
        name="precondition",
    )(query_grads.reshape(blocks, qdev, width), out_basis, in_basis, eigenvalues)


def exact_rows(pick, x):
    hi = x.astype(BF16)
    rest = x - hi.astype(F32)
    mid = rest.astype(BF16)
    low = (rest - mid.astype(F32)).astype(BF16)
    return hi, mid, low


def scores_kernel(n_row, blocks, qdev, core_ref, order_ref, train_ref, gathered_ref, ids_ref, mine_ref, other_ref):
    count = blocks * qdev
    seg = gathered_ref.shape[1]
    rows = train_ref.shape[0]
    queries = gathered_ref[...]
    lines = queries.shape[0]
    segment = lax.broadcasted_iota(jnp.int32, (lines, rows), 0) % SEGMENTS
    terms = jnp.zeros((lines, rows), F32)
    for j in range(SEGMENTS):
        terms = jnp.where(segment == j, mm_nt(queries, train_ref[:, j * seg:(j + 1) * seg]), terms)
    here = lax.broadcasted_iota(jnp.int32, (rows, rows), 0)
    place = (here == ids_ref[...]).astype(BF16)
    per = n_row * qdev // 2
    line = lax.broadcasted_iota(jnp.int32, (blocks * per, lines), 0)
    source = lax.broadcasted_iota(jnp.int32, (blocks * per, lines), 1) // SEGMENTS
    block = jnp.zeros_like(line)
    for j in range(blocks):
        block = jnp.where(line // per == j, order_ref[j], block)
    parts = exact_rows(None, terms)
    for which, ref in ((core_ref[0], mine_ref), (1 - core_ref[0], other_ref)):
        query = line % per + which * per
        pick = (source == (query // qdev) * count + block * qdev + query % qdev).astype(BF16)
        chosen = mm(pick, parts[0]) + mm(pick, parts[1]) + mm(pick, parts[2])
        a, b, c = exact_rows(None, chosen)
        ref[...] = mm(a, place) + mm(b, place) + mm(c, place)


def scores(n_row, core, block_order, train, gathered, row_ids, blocks, qdev):
    rows = train.shape[0]
    out = jax.ShapeDtypeStruct((blocks * n_row * qdev // 2, rows), F32)
    return pl.pallas_call(
        functools.partial(scores_kernel, n_row, blocks, qdev),
        out_shape=(out, out),
        in_specs=[pl.BlockSpec(memory_space=pltpu.SMEM)] * 2 + [pl.BlockSpec(memory_space=pltpu.VMEM)] * 3,
        out_specs=(pl.BlockSpec(memory_space=pltpu.VMEM),) * 2,
        compiler_params=pltpu.CompilerParams(vmem_limit_bytes=32 * 2**20),
        name="scores",
    )(core, block_order, train, gathered, row_ids)


def make_body(n_row):
    def body(train_grads, query_grads, out_basis, in_basis, eigenvalues, block_order, row_ids):
        blocks, qdev, _, width = query_grads.shape
        rows = train_grads.shape[0]
        sent = precondition(query_grads, out_basis, in_basis, eigenvalues, n_row)
        gathered = lax.all_to_all(sent, "row", 0, 0)
        gathered = gathered.reshape(-1, gathered.shape[-1])
        core = lax.axis_index("layer").reshape(1).astype(jnp.int32)
        mine, other = scores(
            n_row, core, block_order, train_grads.reshape(rows, width), gathered, row_ids, blocks, qdev
        )
        got = lax.ppermute(other, "layer", [(0, 1), (1, 0)])
        total = (mine + got).astype(BF16)
        return total.reshape(blocks, -1, rows).transpose(0, 2, 1)

    return body


def solution(mesh):
    in_specs = (
        P(("grp", "row"), "layer", None),
        P(None, "row", "layer", None),
        P("layer", None, None),
        P("layer", None, None),
        P("layer", None),
        P(),
        P(("grp", "row"), None),
    )
    out_specs = P(None, ("grp", "row"), "layer")
    body = make_body(mesh.shape["row"])
    return jax.shard_map(body, mesh=mesh, in_specs=in_specs, out_specs=out_specs, check_vma=False)
```

time: 144 us -> 28.5 us (0.20)
  blocking collectives: 94.1 us -> 0 us
  between operations: 19 us -> 0.01 us
  matrix products: 13.5 us -> 0 us
  starting transfers between devices: 0.09 us -> 7.26 us
  waiting for transfers between devices: 7.11 us -> 12.9 us
  Pallas kernels: 0 us -> 4.47 us
  local copies, waits for them, and re-layouts: 5.96 us -> 2.92 us
  other arithmetic: 3.48 us -> 0.6 us
    all_gather x3 -> x0, blocking collectives: 94.1 us -> none  [body(): flat = lax.all_gather(chosen, 'row', axis=0, tiled=True)]
    dot_general x7 -> x0, matrix products: 13.5 us -> none  [the longest x3 8.76 us: body(): jnp.einsum('rlp,qlp->rq', ordered_rows, flat, preferred_element_type=jnp....]
    all_to_all x0 -> x1, waiting for transfers between devices: none -> 11.7 us  [body(): gathered = lax.all_to_all(sent, 'row', 0, 0)]
    all_to_all x0 -> x1, starting transfers between devices: none -> 7.25 us  [body(): gathered = lax.all_to_all(sent, 'row', 0, 0)]
    reduce_scatter x3 -> x0, waiting for transfers between devices: 7.06 us -> none  [body(): lax.psum_scatter(terms, 'layer', scatter_dimension=1, tiled=True)]
    pallas_call x0 -> x2, Pallas kernels: none -> 4.47 us  [the longest x1 2.53 us: precondition(): pl.pallas_call(precondition_kernel, out_shape=jax.ShapeDtypeStruct((copie...]
    gather x1 -> x0, local copies, waits for them, and re-layouts: 3.19 us -> none  [body(): ordered_rows = jnp.take(train_grads, row_ids[0], axis=0)]
    unnamed x7 -> x6, local copies, waits for them, and re-layouts: 0.09 us -> 2.92 us
  transfers between devices with their start and end apart: 3 -> 2, of which waited for: 1 -> 2; matrix products, arithmetic and copies ran while one was open for 5% -> 0% of each run, Pallas kernels for 0% -> 0%
where the time goes in v2:
time: 28.5 us; the launch traced here: 28.2 us
  waiting for transfers between devices  12.9 us (45%)
  starting transfers between devices  7.26 us (25%)
  Pallas kernels  4.47 us (16%)
  local copies, waits for them, and re-layouts  2.92 us (10%)
  other arithmetic  0.6 us (2%)
    all_to_all x1, waiting for transfers between devices, body(): gathered = lax.all_to_all(sent, 'row', 0, 0)  11.7 us
    all_to_all x1, starting transfers between devices, body(): gathered = lax.all_to_all(sent, 'row', 0, 0)  7.25 us
    unnamed x6, local copies, waits for them, and re-layouts  2.92 us
    pallas_call x1, Pallas kernels, precondition(): pl.pallas_call(precondition_kernel, out_shape=jax.ShapeDtypeStruct((copie...  2.53 us
    pallas_call x1, Pallas kernels, scores(): pl.pallas_call(functools.partial(scores_kernel, n_row, blocks, qdev), out...  1.94 us
    ppermute x1, waiting for transfers between devices, body(): got = lax.ppermute(other, 'layer', [(0, 1), (1, 0)])  1.21 us
    transpose x1, other arithmetic, body(): return total.reshape(blocks, -1, rows).transpose(0, 2, 1)  0.6 us
  transfers between devices with their start and end apart: 2, of which 2 were waited for; matrix products, arithmetic and copies ran while one was open for 0% of the time, Pallas kernels for 0%

profile of v2, /device:TPU:0, one launch (start us, length us, event | category | flops | bytes accessed | tf_op | source)
XLA Modules:
  0.0 28.2 jit_solution(16987792514070560996)
XLA Ops:
  0.0 2.5 %precondition.1 = bf16[8,24,1024]{2,1,0:T(8,128)(2,1)} custom-call(bf16[3,2,4096]{2,1,0:T(2,128)(2,1)} %bitcast.10, f32[1,64,64]{2,1,0:T(8,128)} %out_basis_ref.1, f32[1,64,64]{2,1,0:T(8,128)} %in_basis_ref.1, f32[1,4096]{1,0:T(1,128)} %eig_ref.1), custom_call_target="tpu_custom_call" | custom-call | tf_op jit(solution)/shard_map/precondition/pallas_call | solution.py:88
  2.5 7.3 %all-to-all-start = ((bf16[8,24,1024]{2,1,0:T(8,128)(2,1)}), bf16[8,24,1024]{2,1,0:T(8,128)(2,1)S(1)}, u32[]{:S(2)}, u32[]{:S(2)}) async-start(bf16[8,24,1024]{2,1,0:T(8,128)(2,1)} %precondition.1), calls=%async_computation | async-start | bytes 786432 | tf_op jit(solution)/shard_map/all_to_all | solution.py:155
  9.8 11.7 %all-to-all-done = bf16[8,24,1024]{2,1,0:T(8,128)(2,1)S(1)} async-done(((bf16[8,24,1024]{2,1,0:T(8,128)(2,1)}), bf16[8,24,1024]{2,1,0:T(8,128)(2,1)S(1)}, u32[]{:S(2)}, u32[]{:S(2)}) %all-to-all-start) | async-done | bytes 393248 | tf_op jit(solution)/shard_map/all_to_all | solution.py:155
  21.5 0.0 copy-start
  21.5 1.6 %copy-done = bf16[256,1,4096]{2,0,1:T(8,128)(2,1)S(1)} copy-done((bf16[256,1,4096]{2,0,1:T(8,128)(2,1)S(1)}, bf16[256,1,4096]{2,0,1:T(8,128)(2,1)}, u32[]{:S(2)}) %copy-start) | copy-done | bytes 2097176
  23.1 0.0 copy-start.1
  23.1 0.7 %copy-done.1 = s32[1,256]{1,0:T(1,128)S(1)} copy-done((s32[1,256]{1,0:T(1,128)S(1)}, s32[1,256]{1,0:T(1,128)}, u32[]{:S(2)}) %copy-start.1) | copy-done | bytes 1048
  23.7 0.0 copy-start.2
  23.8 0.7 %copy-done.2 = s32[3]{0:T(128)S(1)} copy-done((s32[3]{0:T(128)S(1)}, s32[3]{0:T(128)}, u32[]{:S(2)}) %copy-start.2) | copy-done | bytes 36
  24.4 1.9 %scores.1 = (f32[24,256]{1,0:T(8,128)S(1)}, f32[24,256]{1,0:T(8,128)S(1)}) custom-call(s32[1]{0:T(128)} %bitcast.core_ref, s32[3]{0:T(128)S(1)} %copy-done.2, bf16[256,4096]{1,0:T(8,128)(2,1)S(1)} %bitcast.8, bf16[192,1024]{1,0:T(8,128)(2,1)S(1)} %bitcast.9, s32[1,256]{1,0:T(1,128)S(1)} %copy-done.1), custom_call_target="tpu_custom_call" | custom-call | tf_op jit(solution)/shard_map/scores/pallas_call | solution.py:140
  26.3 0.0 collective-permute-start
  26.3 1.2 %collective-permute-done = f32[24,256]{1,0:T(8,128)S(1)} collective-permute-done((f32[24,256]{1,0:T(8,128)S(1)}, f32[24,256]{1,0:T(8,128)S(1)}, u32[]{:S(2)}, u32[]{:S(2)}) %collective-permute-start) | collective-permute-done | bytes 24608 | tf_op jit(solution)/shard_map/ppermute | solution.py:161
  27.6 0.6 %fusion = bf16[3,256,8]{1,2,0:T(8,128)(2,1)} fusion(f32[24,256]{1,0:T(8,128)S(1)} %get-tuple-element.7, f32[24,256]{1,0:T(8,128)S(1)} %collective-permute-done), kind=kLoop, calls=%fused_computation.1 | loop fusion | flops 12288 | bytes 61440 | tf_op jit(solution)/shard_map/transpose | solution.py:163
Async XLA Ops:
  2.5 18.9 %all-to-all-start = ((bf16[8,24,1024]{2,1,0:T(8,128)(2,1)}), bf16[8,24,1024]{2,1,0:T(8,128)(2,1)S(1)}, u32[]{:S(2)}, u32[]{:S(2)}) async-start(bf16[8,24,1024]{2,1,0:T(8,128)(2,1)} %precondition.1), calls=%async_computation | async-start | bytes 786432 | tf_op jit(solution)/shard_map/all_to_all | solution.py:155
  21.5 1.6 %copy-start = (bf16[256,1,4096]{2,0,1:T(8,128)(2,1)S(1)}, bf16[256,1,4096]{2,0,1:T(8,128)(2,1)}, u32[]{:S(2)}) copy-start(bf16[256,1,4096]{2,0,1:T(8,128)(2,1)} %param.7) | copy-start | bytes 6291460
  23.1 0.7 %copy-start.1 = (s32[1,256]{1,0:T(1,128)S(1)}, s32[1,256]{1,0:T(1,128)}, u32[]{:S(2)}) copy-start(s32[1,256]{1,0:T(1,128)} %ids_ref.1) | copy-start | bytes 3076
  23.7 0.7 %copy-start.2 = (s32[3]{0:T(128)S(1)}, s32[3]{0:T(128)}, u32[]{:S(2)}) copy-start(s32[3]{0:T(128)} %order_ref.1) | copy-start | bytes 40
  26.3 1.2 %collective-permute-start = (f32[24,256]{1,0:T(8,128)S(1)}, f32[24,256]{1,0:T(8,128)S(1)}, u32[]{:S(2)}, u32[]{:S(2)}) collective-permute-start(f32[24,256]{1,0:T(8,128)S(1)} %get-tuple-element.8), channel_id=1, source_target_pairs={{0,1},{1,0},{2,3},{3,2},{4,5},{5,4},{6,7},{7,6},{8,9},{9,8},{10,11... | collective-permute-start | bytes 73736 | tf_op jit(solution)/shard_map/ppermute | solution.py:161

commit v3 on v2

v3 whole, which is shorter than its diff:
```python
import functools

import jax
import jax.numpy as jnp
from jax import lax
from jax.experimental import pallas as pl
from jax.experimental.pallas import tpu as pltpu
from jax.sharding import PartitionSpec as P

DAMPING = 0.01
LANES = 128
SEGMENTS = 4
F32, BF16 = jnp.float32, jnp.bfloat16
NT = (((1,), (1,)), ((), ()))


def split2(x):
    high = x.astype(BF16)
    return high, (x - high.astype(F32)).astype(BF16)


def mm(a, b):
    return jnp.dot(a, b, preferred_element_type=F32)


def mm_nt(a, b):
    return lax.dot_general(a, b, NT, preferred_element_type=F32)


def precondition_kernel(
    order_hbm, q_hbm, out_basis_hbm, in_basis_hbm, eig_hbm, ids_hbm, train_hbm,
    sent_ref, ids_out_ref, train_out_ref,
    order_ref, q_ref, out_basis_ref, in_basis_ref, eig_ref, x_scr, o_scr, eig_scr, sems,
):
    copies = [
        pltpu.make_async_copy(src, dst, sems.at[n])
        for n, (src, dst) in enumerate((
            (order_hbm, order_ref), (q_hbm, q_ref), (in_basis_hbm, in_basis_ref), (out_basis_hbm, out_basis_ref), (eig_hbm, eig_ref),
            (ids_hbm, ids_out_ref), (train_hbm, train_out_ref),
        ))
    ]
    for copy in copies:
        copy.start()
    for copy in copies[:5]:
        copy.wait()
    blocks, qdev, width = q_ref.shape
    side = out_basis_ref.shape[1]
    half = side // 2
    count = blocks * qdev
    chunks = width // LANES
    for j in range(blocks):
        flat = q_ref[order_ref[j]].astype(F32)
        for k in range(chunks):
            x_scr[pl.ds(j * qdev * chunks + k, qdev, stride=chunks), :] = flat[:, k * LANES:(k + 1) * LANES]
    scale = 1.0 / (eig_ref[...] + DAMPING)
    for k in range(chunks):
        for odd in range(2):
            at = k * LANES + odd * side
            eig_scr[2 * k + odd:2 * k + odd + 1, :side] = scale[:, at:at + side]
    scale = eig_scr[:, :side]
    o_scr[:, :side] = out_basis_ref[0]
    basis = jnp.concatenate(
        [o_scr[pl.ds(0, half, stride=2), :side], o_scr[pl.ds(1, half, stride=2), :side]], axis=0
    )
    b_hi, b_lo = split2(basis)
    t_hi, t_lo = split2(basis.T)
    left = jnp.concatenate([t_hi, t_hi, t_lo], axis=1)
    back = jnp.concatenate([b_hi, b_hi, b_lo], axis=1)
    i_hi, i_lo = split2(in_basis_ref[0])
    none = jnp.zeros_like(i_hi)
    raw = x_scr[...].astype(BF16)
    raw2 = jnp.concatenate([raw, raw], axis=1)
    even = mm(raw2, jnp.concatenate([i_hi, none, i_lo, none], axis=0))
    odd = mm(raw2, jnp.concatenate([none, i_hi, none, i_lo], axis=0))
    evens, odds = [], []
    for q in range(count):
        rows = slice(q * half, (q + 1) * half)
        hi, lo = split2(jnp.concatenate([even[rows], odd[rows]], axis=0))
        rotated = mm(left, jnp.concatenate([hi, lo, hi], axis=0))
        hi, lo = split2(rotated * scale)
        again = mm(back, jnp.concatenate([hi, lo, hi], axis=0))
        evens.append(again[:half])
        odds.append(again[half:])
    total = None
    for rows, lower in ((evens, False), (odds, True)):
        hi, lo = split2(jnp.concatenate(rows, axis=0))
        w_hi = jnp.concatenate([none, i_hi] if lower else [i_hi, none], axis=0)
        w_lo = jnp.concatenate([none, i_lo] if lower else [i_lo, none], axis=0)
        term = mm_nt(hi, w_hi) + mm_nt(lo, w_hi) + mm_nt(hi, w_lo)
        total = term if total is None else total + term
    x_scr[...] = total
    per = chunks // SEGMENTS
    for c in range(per):
        piece = x_scr[pl.ds(c, count * SEGMENTS, stride=per), :].astype(BF16)
        sent_ref[:, c * LANES:(c + 1) * LANES] = piece
    for copy in copies[5:]:
        copy.wait()


def precondition(block_order, query_grads, out_basis, in_basis, eigenvalues, row_ids, train):
    blocks, qdev, width = query_grads.shape
    count = blocks * qdev
    side = out_basis.shape[1]
    vmem = pl.BlockSpec(memory_space=pltpu.VMEM)
    hbm = pl.BlockSpec(memory_space=pltpu.HBM)
    free = pl.BlockSpec(memory_space=pl.ANY)
    return pl.pallas_call(
        precondition_kernel,
        out_shape=(
            jax.ShapeDtypeStruct((count * SEGMENTS, width // SEGMENTS), BF16),
            jax.ShapeDtypeStruct(row_ids.shape, row_ids.dtype),
            jax.ShapeDtypeStruct(train.shape, train.dtype),
        ),
        in_specs=[hbm] * 7,
        out_specs=(vmem, free, free),
        scratch_shapes=[
            pltpu.SMEM(block_order.shape, block_order.dtype),
            pltpu.VMEM(query_grads.shape, BF16),
            pltpu.VMEM(out_basis.shape, F32),
            pltpu.VMEM(in_basis.shape, F32),
            pltpu.VMEM(eigenvalues.shape, F32),
            pltpu.VMEM((count * width // LANES, LANES), F32),
            pltpu.VMEM((side, LANES), F32),
            pltpu.VMEM((side, LANES), F32),
            pltpu.SemaphoreType.DMA((7,)),
        ],
        compiler_params=pltpu.CompilerParams(vmem_limit_bytes=4 * 2**20),
        name="precondition",
    )(*(
        pltpu.with_memory_space_constraint(x, pltpu.HBM)
        for x in (block_order, query_grads, out_basis, in_basis, eigenvalues, row_ids, train)
    ))


def split3(x):
    hi = x.astype(BF16)
    rest = x - hi.astype(F32)
    mid = rest.astype(BF16)
    return hi, mid, (rest - mid.astype(F32)).astype(BF16)


def scores_kernel(masks, blocks, qdev, place_ref, train_ref, ids_ref, *refs):
    n_row = len(masks)
    parts, (mine_ref, other_ref, flat_scr, out_scr) = refs[:n_row], refs[n_row:]
    lines, seg = parts[0].shape
    rows = train_ref.shape[0]
    slot = 8
    per_seg = seg // LANES
    for b, part in enumerate(parts):
        flat = part[...].astype(F32)
        for c in range(per_seg):
            flat_scr[b, c, :lines, :] = flat[:, c * LANES:(c + 1) * LANES]
    terms = None
    for j in range(SEGMENTS):
        queries = jnp.concatenate([
            jnp.concatenate([flat_scr[b, c, pl.ds(j, slot, stride=SEGMENTS), :] for b in range(n_row)], axis=0)
            for c in range(per_seg)
        ], axis=1)
        term = mm_nt(queries.astype(BF16), train_ref[:, j * seg:(j + 1) * seg])
        terms = term if terms is None else terms + term
    here = lax.broadcasted_iota(jnp.int32, (rows, rows), 0)
    place = (here == ids_ref[...]).astype(BF16)
    a, b, c = split3(terms)
    ordered = mm(a, place) + mm(b, place) + mm(c, place)
    me, core = place_ref[0], place_ref[1]
    per = n_row // 2
    for b, mask in enumerate(masks):
        source = me ^ mask
        which = jnp.where(source // per == core, 0, 1)
        first = which * (blocks * per) + source % per
        for j in range(blocks):
            at = b * slot + j * qdev
            out_scr[first + j * per] = ordered[at:at + qdev]
    for i in range(blocks * per):
        mine_ref[i * qdev:(i + 1) * qdev, :] = out_scr[i]
        other_ref[i * qdev:(i + 1) * qdev, :] = out_scr[blocks * per + i]


def scores(masks, place, train, row_ids, parts, blocks, qdev):
    rows = train.shape[0]
    n_row = len(masks)
    lines, seg = parts[0].shape
    out = jax.ShapeDtypeStruct((blocks * n_row * qdev // 2, rows), F32)
    vmem = pl.BlockSpec(memory_space=pltpu.VMEM)
    return pl.pallas_call(
        functools.partial(scores_kernel, masks, blocks, qdev),
        out_shape=(out, out),
        in_specs=[pl.BlockSpec(memory_space=pltpu.SMEM)] + [vmem] * (2 + n_row),
        out_specs=(vmem, vmem),
        scratch_shapes=[
            pltpu.VMEM((n_row, seg // LANES, 8 * SEGMENTS, LANES), F32),
            pltpu.VMEM((blocks * n_row, qdev, rows), F32),
        ],
        compiler_params=pltpu.CompilerParams(vmem_limit_bytes=(16 if n_row <= 16 else 48) * 2**20),
        cost_estimate=pl.CostEstimate(flops=2 * n_row * 8 * rows * seg * SEGMENTS, bytes_accessed=train.size * 2 + n_row * lines * seg * 2, transcendentals=0),
        name="scores",
    )(place, train, row_ids, *parts)


def make_body(n_row):
    def swap(x, mask):
        return lax.ppermute(x, "row", [(i, i ^ mask) for i in range(n_row)])

    def body(train_grads, query_grads, out_basis, in_basis, eigenvalues, block_order, row_ids):
        blocks, qdev, _, width = query_grads.shape
        rows = train_grads.shape[0]
        own, row_ids, train = precondition(
            block_order, query_grads.reshape(blocks, qdev, width), out_basis, in_basis, eigenvalues, row_ids,
            train_grads.reshape(rows, width),
        )
        near = {0: own}
        for mask in [4, 6, 2] if n_row == 8 else range(2, n_row, 2):
            near[mask] = swap(own, mask)
        far = {mask ^ 1: swap(x, 1) for mask, x in near.items()}
        both = {**near, **far}
        place = jnp.stack([lax.axis_index("row"), lax.axis_index("layer")]).astype(jnp.int32)
        mine, other = scores(
            tuple(both), place, train, row_ids, tuple(both.values()), blocks, qdev
        )
        got = lax.ppermute(other, "layer", [(0, 1), (1, 0)])
        total = (mine + got).astype(BF16)
        return total.reshape(blocks, -1, rows).transpose(0, 2, 1)

    return body


def solution(mesh):
    in_specs = (
        P(("grp", "row"), "layer", None),
        P(None, "row", "layer", None),
        P("layer", None, None),
        P("layer", None, None),
        P("layer", None),
        P(),
        P(("grp", "row"), None),
    )
    out_specs = P(None, ("grp", "row"), "layer")
    body = make_body(mesh.shape["row"])
    return jax.shard_map(body, mesh=mesh, in_specs=in_specs, out_specs=out_specs, check_vma=False)
```

time: 28.5 us -> 20.6 us (0.72)
  waiting for transfers between devices: 12.9 us -> 5.61 us
  starting transfers between devices: 7.26 us -> 10.7 us
  local copies, waits for them, and re-layouts: 2.92 us -> 0 us
  Pallas kernels: 4.47 us -> 3.37 us
    all_to_all x1 -> x0, waiting for transfers between devices: 11.7 us -> none  [body(): gathered = lax.all_to_all(sent, 'row', 0, 0)]
    ppermute x0 -> x7, starting transfers between devices: none -> 10.7 us  [swap(): return lax.ppermute(x, 'row', [(i, i ^ mask) for i in range(n_row)])]
    all_to_all x1 -> x0, starting transfers between devices: 7.25 us -> none  [body(): gathered = lax.all_to_all(sent, 'row', 0, 0)]
    ppermute x0 -> x7, waiting for transfers between devices: none -> 4.43 us  [swap(): return lax.ppermute(x, 'row', [(i, i ^ mask) for i in range(n_row)])]
    unnamed x6 -> x0, local copies, waits for them, and re-layouts: 2.92 us -> none
    pallas_call x2, Pallas kernels: 4.47 us -> 3.37 us  [the longest x1 1.78 us: precondition(): pl.pallas_call(precondition_kernel, out_shape=(jax.ShapeDtypeStruct((coun...]
  transfers between devices with their start and end apart: 2 -> 8, of which waited for: 2 -> 4; matrix products, arithmetic and copies ran while one was open for 0% -> 0% of each run, Pallas kernels for 0% -> 0%
where the time goes in v3:
time: 20.6 us; the launch traced here: 20.4 us
  starting transfers between devices  10.7 us (52%)
  waiting for transfers between devices  5.61 us (27%)
  Pallas kernels  3.37 us (16%)
  other arithmetic  0.68 us (3%)
    ppermute x7, starting transfers between devices, swap(): return lax.ppermute(x, 'row', [(i, i ^ mask) for i in range(n_row)])  10.7 us
    ppermute x7, waiting for transfers between devices, swap(): return lax.ppermute(x, 'row', [(i, i ^ mask) for i in range(n_row)])  4.43 us
    pallas_call x1, Pallas kernels, precondition(): pl.pallas_call(precondition_kernel, out_shape=(jax.ShapeDtypeStruct((coun...  1.78 us
    pallas_call x1, Pallas kernels, scores(): pl.pallas_call(functools.partial(scores_kernel, masks, blocks, qdev), out...  1.59 us
    ppermute x1, waiting for transfers between devices, body(): got = lax.ppermute(other, 'layer', [(0, 1), (1, 0)])  1.18 us
    transpose x1, other arithmetic, body(): return total.reshape(blocks, -1, rows).transpose(0, 2, 1)  0.6 us
  transfers between devices with their start and end apart: 8, of which 4 were waited for; matrix products, arithmetic and copies ran while one was open for 0% of the time, Pallas kernels for 0%

profile of v3, /device:TPU:0, one launch (start us, length us, event | category | flops | bytes accessed | tf_op | source)
XLA Modules:
  0.0 20.4 jit_solution(3080812679860069087)
XLA Ops:
  0.0 1.8 %precondition.1 = (bf16[24,1024]{1,0:T(8,128)(2,1)S(1)}, s32[1,256]{1,0:T(1,128)S(1)}, bf16[256,4096]{1,0:T(8,128)(2,1)S(1)}) custom-call(s32[3]{0:T(128)} %order_hbm.1, bf16[3,2,4096]{2,1,0:T(2,128)(2,1)} %bitcast.9, f32[1,64,64]{2,1,0:T(8,128)} %out_basis_hbm.1, f32[1,64,64]{2,1,0:T(8,128)} %in_basis_hbm.1, f32[1,4096]{1,0:T(1,128)} %eig_hbm.1, ...), custom_call_target="tpu_custom_call" | custom-call | tf_op jit(solution)/shard_map/precondition/pallas_call | solution.py:107
  1.8 3.1 %collective-permute-start.2 = (bf16[24,1024]{1,0:T(8,128)(2,1)S(1)}, bf16[24,1024]{1,0:T(8,128)(2,1)S(1)}, u32[]{:S(2)}, u32[]{:S(2)}) collective-permute-start(bf16[24,1024]{1,0:T(8,128)(2,1)S(1)} %get-tuple-element.12.refs_0_), channel_id=1, source_target_pairs={{0,4},{2,6},{4,0},{6,2},{8,12},{10,14},{12,8},{14,10},{1,5},{3,7},... | collective-permute-start | bytes 147464 | tf_op jit(solution)/shard_map/ppermute | solution.py:202
  4.9 2.5 %collective-permute-start.1 = (bf16[24,1024]{1,0:T(8,128)(2,1)S(1)}, bf16[24,1024]{1,0:T(8,128)(2,1)S(1)}, u32[]{:S(2)}, u32[]{:S(2)}) collective-permute-start(bf16[24,1024]{1,0:T(8,128)(2,1)S(1)} %get-tuple-element.12.refs_0_), channel_id=1, source_target_pairs={{0,12},{2,14},{4,8},{6,10},{8,4},{10,6},{12,0},{14,2},{1,13},{3,15... | collective-permute-start | bytes 147464 | tf_op jit(solution)/shard_map/ppermute | solution.py:202
  7.3 0.1 collective-permute-start
  7.5 1.5 %collective-permute-start.3 = (bf16[24,1024]{1,0:T(8,128)(2,1)S(1)}, bf16[24,1024]{1,0:T(8,128)(2,1)S(1)}, u32[]{:S(2)}, u32[]{:S(2)}) collective-permute-start(bf16[24,1024]{1,0:T(8,128)(2,1)S(1)} %get-tuple-element.12.refs_0_), channel_id=1, source_target_pairs={{0,2},{2,0},{4,6},{6,4},{8,10},{10,8},{12,14},{14,12},{1,3},{3,1},... | collective-permute-start | bytes 147464 | tf_op jit(solution)/shard_map/ppermute | solution.py:202
  9.0 0.0 collective-permute-done.2.refs_3_
  9.0 0.5 %collective-permute-start.6 = (bf16[24,1024]{1,0:T(8,128)(2,1)S(1)}, bf16[24,1024]{1,0:T(8,128)(2,1)S(1)}, u32[]{:S(2)}, u32[]{:S(2)}) collective-permute-start(bf16[24,1024]{1,0:T(8,128)(2,1)S(1)} %collective-permute-done.2.refs_3_), channel_id=1, source_target_pairs={{0,2},{2,0},{4,6},{6,4},{8,10},{10,8},{12,14},{14,12},{1,3},{3,1},... | collective-permute-start | bytes 147464 | tf_op jit(solution)/shard_map/ppermute | solution.py:202
  9.5 1.9 %collective-permute-done.1.refs_2_ = bf16[24,1024]{1,0:T(8,128)(2,1)S(1)} collective-permute-done((bf16[24,1024]{1,0:T(8,128)(2,1)S(1)}, bf16[24,1024]{1,0:T(8,128)(2,1)S(1)}, u32[]{:S(2)}, u32[]{:S(2)}) %collective-permute-start.1) | collective-permute-done | bytes 49184 | tf_op jit(solution)/shard_map/ppermute | solution.py:202
  11.4 1.5 %collective-permute-start.5 = (bf16[24,1024]{1,0:T(8,128)(2,1)S(1)}, bf16[24,1024]{1,0:T(8,128)(2,1)S(1)}, u32[]{:S(2)}, u32[]{:S(2)}) collective-permute-start(bf16[24,1024]{1,0:T(8,128)(2,1)S(1)} %collective-permute-done.1.refs_2_), channel_id=1, source_target_pairs={{0,2},{2,0},{4,6},{6,4},{8,10},{10,8},{12,14},{14,12},{1,3},{3,1},... | collective-permute-start | bytes 147464 | tf_op jit(solution)/shard_map/ppermute | solution.py:202
  12.9 0.0 collective-permute-done.refs_1_
  12.9 1.5 %collective-permute-start.4 = (bf16[24,1024]{1,0:T(8,128)(2,1)S(1)}, bf16[24,1024]{1,0:T(8,128)(2,1)S(1)}, u32[]{:S(2)}, u32[]{:S(2)}) collective-permute-start(bf16[24,1024]{1,0:T(8,128)(2,1)S(1)} %collective-permute-done.refs_1_), channel_id=1, source_target_pairs={{0,2},{2,0},{4,6},{6,4},{8,10},{10,8},{12,14},{14,12},{1,3},{3,1},... | collective-permute-start | bytes 147464 | tf_op jit(solution)/shard_map/ppermute | solution.py:202
  14.4 0.1 pad_add_fusion.place_ref
  14.4 0.0 collective-permute-done.3.refs_4_
  14.4 0.0 collective-permute-done.6.refs_7_
  14.4 1.0 %collective-permute-done.5.refs_6_ = bf16[24,1024]{1,0:T(8,128)(2,1)S(1)} collective-permute-done((bf16[24,1024]{1,0:T(8,128)(2,1)S(1)}, bf16[24,1024]{1,0:T(8,128)(2,1)S(1)}, u32[]{:S(2)}, u32[]{:S(2)}) %collective-permute-start.5) | collective-permute-done | bytes 49184 | tf_op jit(solution)/shard_map/ppermute | solution.py:202
  15.5 1.5 %collective-permute-done.4.refs_5_ = bf16[24,1024]{1,0:T(8,128)(2,1)S(1)} collective-permute-done((bf16[24,1024]{1,0:T(8,128)(2,1)S(1)}, bf16[24,1024]{1,0:T(8,128)(2,1)S(1)}, u32[]{:S(2)}, u32[]{:S(2)}) %collective-permute-start.4) | collective-permute-done | bytes 49184 | tf_op jit(solution)/shard_map/ppermute | solution.py:202
  17.0 1.6 %scores.1 = (f32[24,256]{1,0:T(8,128)S(1)}, f32[24,256]{1,0:T(8,128)S(1)}) custom-call(s32[2]{0:T(128)S(1)} %pad_add_fusion.place_ref, bf16[256,4096]{1,0:T(8,128)(2,1)S(1)} %get-tuple-element.10.train_ref, s32[1,256]{1,0:T(1,128)S(1)} %get-tuple-element.11.ids_ref, bf16[24,1024]{1,0:T(8,128)(2,1)S(1)} %get-tuple-element.12.refs_0_, ...), custom_call_target="tpu_custom_call" | custom-call | flops 134217728 | bytes 2490368 | tf_op jit(solution)/shard_map/scores/pallas_call | solution.py:185
  18.6 0.1 collective-permute-start.7
  18.7 1.2 %collective-permute-done.7 = f32[24,256]{1,0:T(8,128)S(1)} collective-permute-done((f32[24,256]{1,0:T(8,128)S(1)}, f32[24,256]{1,0:T(8,128)S(1)}, u32[]{:S(2)}, u32[]{:S(2)}) %collective-permute-start.7) | collective-permute-done | bytes 24608 | tf_op jit(solution)/shard_map/ppermute | solution.py:220
  19.8 0.6 %fusion = bf16[3,256,8]{1,2,0:T(8,128)(2,1)} fusion(f32[24,256]{1,0:T(8,128)S(1)} %get-tuple-element.13, f32[24,256]{1,0:T(8,128)S(1)} %collective-permute-done.7), kind=kLoop, calls=%fused_computation.1 | loop fusion | flops 12288 | bytes 61440 | tf_op jit(solution)/shard_map/transpose | solution.py:222
Async XLA Ops:
  1.8 7.2 %collective-permute-start.2 = (bf16[24,1024]{1,0:T(8,128)(2,1)S(1)}, bf16[24,1024]{1,0:T(8,128)(2,1)S(1)}, u32[]{:S(2)}, u32[]{:S(2)}) collective-permute-start(bf16[24,1024]{1,0:T(8,128)(2,1)S(1)} %get-tuple-element.12.refs_0_), channel_id=1, source_target_pairs={{0,4},{2,6},{4,0},{6,2},{8,12},{10,14},{12,8},{14,10},{1,5},{3,7},... | collective-permute-start | bytes 147464 | tf_op jit(solution)/shard_map/ppermute | solution.py:202
  4.9 6.5 %collective-permute-start.1 = (bf16[24,1024]{1,0:T(8,128)(2,1)S(1)}, bf16[24,1024]{1,0:T(8,128)(2,1)S(1)}, u32[]{:S(2)}, u32[]{:S(2)}) collective-permute-start(bf16[24,1024]{1,0:T(8,128)(2,1)S(1)} %get-tuple-element.12.refs_0_), channel_id=1, source_target_pairs={{0,12},{2,14},{4,8},{6,10},{8,4},{10,6},{12,0},{14,2},{1,13},{3,15... | collective-permute-start | bytes 147464 | tf_op jit(solution)/shard_map/ppermute | solution.py:202
  7.3 5.5 %collective-permute-start = (bf16[24,1024]{1,0:T(8,128)(2,1)S(1)}, bf16[24,1024]{1,0:T(8,128)(2,1)S(1)}, u32[]{:S(2)}, u32[]{:S(2)}) collective-permute-start(bf16[24,1024]{1,0:T(8,128)(2,1)S(1)} %get-tuple-element.12.refs_0_), channel_id=1, source_target_pairs={{0,8},{2,10},{4,12},{6,14},{8,0},{10,2},{12,4},{14,6},{1,9},{3,11}... | collective-permute-start | bytes 147464 | tf_op jit(solution)/shard_map/ppermute | solution.py:202
  7.5 7.0 %collective-permute-start.3 = (bf16[24,1024]{1,0:T(8,128)(2,1)S(1)}, bf16[24,1024]{1,0:T(8,128)(2,1)S(1)}, u32[]{:S(2)}, u32[]{:S(2)}) collective-permute-start(bf16[24,1024]{1,0:T(8,128)(2,1)S(1)} %get-tuple-element.12.refs_0_), channel_id=1, source_target_pairs={{0,2},{2,0},{4,6},{6,4},{8,10},{10,8},{12,14},{14,12},{1,3},{3,1},... | collective-permute-start | bytes 147464 | tf_op jit(solution)/shard_map/ppermute | solution.py:202
  9.0 5.5 %collective-permute-start.6 = (bf16[24,1024]{1,0:T(8,128)(2,1)S(1)}, bf16[24,1024]{1,0:T(8,128)(2,1)S(1)}, u32[]{:S(2)}, u32[]{:S(2)}) collective-permute-start(bf16[24,1024]{1,0:T(8,128)(2,1)S(1)} %collective-permute-done.2.refs_3_), channel_id=1, source_target_pairs={{0,2},{2,0},{4,6},{6,4},{8,10},{10,8},{12,14},{14,12},{1,3},{3,1},... | collective-permute-start | bytes 147464 | tf_op jit(solution)/shard_map/ppermute | solution.py:202
  11.4 4.1 %collective-permute-start.5 = (bf16[24,1024]{1,0:T(8,128)(2,1)S(1)}, bf16[24,1024]{1,0:T(8,128)(2,1)S(1)}, u32[]{:S(2)}, u32[]{:S(2)}) collective-permute-start(bf16[24,1024]{1,0:T(8,128)(2,1)S(1)} %collective-permute-done.1.refs_2_), channel_id=1, source_target_pairs={{0,2},{2,0},{4,6},{6,4},{8,10},{10,8},{12,14},{14,12},{1,3},{3,1},... | collective-permute-start | bytes 147464 | tf_op jit(solution)/shard_map/ppermute | solution.py:202
  12.9 4.1 %collective-permute-start.4 = (bf16[24,1024]{1,0:T(8,128)(2,1)S(1)}, bf16[24,1024]{1,0:T(8,128)(2,1)S(1)}, u32[]{:S(2)}, u32[]{:S(2)}) collective-permute-start(bf16[24,1024]{1,0:T(8,128)(2,1)S(1)} %collective-permute-done.refs_1_), channel_id=1, source_target_pairs={{0,2},{2,0},{4,6},{6,4},{8,10},{10,8},{12,14},{14,12},{1,3},{3,1},... | collective-permute-start | bytes 147464 | tf_op jit(solution)/shard_map/ppermute | solution.py:202
  18.6 1.3 %collective-permute-start.7 = (f32[24,256]{1,0:T(8,128)S(1)}, f32[24,256]{1,0:T(8,128)S(1)}, u32[]{:S(2)}, u32[]{:S(2)}) collective-permute-start(f32[24,256]{1,0:T(8,128)S(1)} %get-tuple-element.14), channel_id=1, source_target_pairs={{0,1},{1,0},{2,3},{3,2},{4,5},{5,4},{6,7},{7,6},{8,9},{9,8},{10,11... | collective-permute-start | bytes 73736 | tf_op jit(solution)/shard_map/ppermute | solution.py:220

commit v4 on v3

--- a/solution.py
+++ b/solution.py
@@ -209,9 +209,19 @@
             train_grads.reshape(rows, width),
         )
         near = {0: own}
-        for mask in [4, 6, 2] if n_row == 8 else range(2, n_row, 2):
-            near[mask] = swap(own, mask)
-        far = {mask ^ 1: swap(x, 1) for mask, x in near.items()}
+        far = {}
+        if n_row == 8:
+            near[2] = swap(own, 2)
+            far[1] = swap(own, 1)
+            near[4] = swap(own, 4)
+            near[2], far[1], near[4] = lax.optimization_barrier((near[2], far[1], near[4]))
+            near[6] = swap(near[4], 2)
+        else:
+            for mask in range(2, n_row, 2):
+                near[mask] = swap(own, mask)
+        for mask in near:
+            if mask ^ 1 not in far:
+                far[mask ^ 1] = swap(near[mask], 1)
         both = {**near, **far}
         place = jnp.stack([lax.axis_index("row"), lax.axis_index("layer")]).astype(jnp.int32)
         mine, other = scores(

time: 20.6 us -> 23.3 us (1.13)
  waiting for transfers between devices: 5.61 us -> 7.66 us
  starting transfers between devices: 10.7 us -> 11.4 us
    ppermute x7, waiting for transfers between devices: 4.43 us -> 6.48 us  [swap(): return lax.ppermute(x, 'row', [(i, i ^ mask) for i in range(n_row)])]
    ppermute x7, starting transfers between devices: 10.7 us -> 11.3 us  [swap(): return lax.ppermute(x, 'row', [(i, i ^ mask) for i in range(n_row)])]
  transfers between devices with their start and end apart: 8 -> 8, of which waited for: 4 -> 6; matrix products, arithmetic and copies ran while one was open for 0% -> 0% of each run, Pallas kernels for 0% -> 0%
where the time goes in v4:
time: 23.3 us; the launch traced here: 23.1 us
  starting transfers between devices  11.4 us (49%)
  waiting for transfers between devices  7.66 us (33%)
  Pallas kernels  3.37 us (14%)
  other arithmetic  0.68 us (3%)
    ppermute x7, starting transfers between devices, swap(): return lax.ppermute(x, 'row', [(i, i ^ mask) for i in range(n_row)])  11.3 us
    ppermute x7, waiting for transfers between devices, swap(): return lax.ppermute(x, 'row', [(i, i ^ mask) for i in range(n_row)])  6.48 us
    pallas_call x1, Pallas kernels, precondition(): pl.pallas_call(precondition_kernel, out_shape=(jax.ShapeDtypeStruct((coun...  1.78 us
    pallas_call x1, Pallas kernels, scores(): pl.pallas_call(functools.partial(scores_kernel, masks, blocks, qdev), out...  1.59 us
    ppermute x1, waiting for transfers between devices, body(): got = lax.ppermute(other, 'layer', [(0, 1), (1, 0)])  1.18 us
    transpose x1, other arithmetic, body(): return total.reshape(blocks, -1, rows).transpose(0, 2, 1)  0.6 us
  transfers between devices with their start and end apart: 8, of which 6 were waited for; matrix products, arithmetic and copies ran while one was open for 0% of the time, Pallas kernels for 0%

profile of v4, /device:TPU:0, one launch (start us, length us, event | category | flops | bytes accessed | tf_op | source)
XLA Modules:
  0.0 23.1 jit_solution(2896842502717915839)
XLA Ops:
  0.0 1.8 %precondition.1 = (bf16[24,1024]{1,0:T(8,128)(2,1)S(1)}, s32[1,256]{1,0:T(1,128)S(1)}, bf16[256,4096]{1,0:T(8,128)(2,1)S(1)}) custom-call(s32[3]{0:T(128)} %order_hbm.1, bf16[3,2,4096]{2,1,0:T(2,128)(2,1)} %bitcast.9, f32[1,64,64]{2,1,0:T(8,128)} %out_basis_hbm.1, f32[1,64,64]{2,1,0:T(8,128)} %in_basis_hbm.1, f32[1,4096]{1,0:T(1,128)} %eig_hbm.1, ...), custom_call_target="tpu_custom_call" | custom-call | tf_op jit(solution)/shard_map/precondition/pallas_call | solution.py:107
  1.8 4.1 %collective-permute-start.2 = (bf16[24,1024]{1,0:T(8,128)(2,1)S(1)}, bf16[24,1024]{1,0:T(8,128)(2,1)S(1)}, u32[]{:S(2)}, u32[]{:S(2)}) collective-permute-start(bf16[24,1024]{1,0:T(8,128)(2,1)S(1)} %get-tuple-element.15.refs_0_), channel_id=1, source_target_pairs={{0,8},{2,10},{4,12},{6,14},{8,0},{10,2},{12,4},{14,6},{1,9},{3,11}... | collective-permute-start | bytes 147464 | tf_op jit(solution)/shard_map/ppermute | solution.py:202
  5.9 1.5 %collective-permute-start.1 = (bf16[24,1024]{1,0:T(8,128)(2,1)S(1)}, bf16[24,1024]{1,0:T(8,128)(2,1)S(1)}, u32[]{:S(2)}, u32[]{:S(2)}) collective-permute-start(bf16[24,1024]{1,0:T(8,128)(2,1)S(1)} %get-tuple-element.15.refs_0_), channel_id=1, source_target_pairs={{0,2},{2,0},{4,6},{6,4},{8,10},{10,8},{12,14},{14,12},{1,3},{3,1},... | collective-permute-start | bytes 147464 | tf_op jit(solution)/shard_map/ppermute | solution.py:202
  7.4 1.6 %collective-permute-start = (bf16[24,1024]{1,0:T(8,128)(2,1)S(1)}, bf16[24,1024]{1,0:T(8,128)(2,1)S(1)}, u32[]{:S(2)}, u32[]{:S(2)}) collective-permute-start(bf16[24,1024]{1,0:T(8,128)(2,1)S(1)} %get-tuple-element.15.refs_0_), channel_id=1, source_target_pairs={{0,4},{2,6},{4,0},{6,2},{8,12},{10,14},{12,8},{14,10},{1,5},{3,7},... | collective-permute-start | bytes 147464 | tf_op jit(solution)/shard_map/ppermute | solution.py:202
  9.0 0.0 collective-permute-done.2.refs_2_
  9.0 1.0 %collective-permute-done.1.refs_4_ = bf16[24,1024]{1,0:T(8,128)(2,1)S(1)} collective-permute-done((bf16[24,1024]{1,0:T(8,128)(2,1)S(1)}, bf16[24,1024]{1,0:T(8,128)(2,1)S(1)}, u32[]{:S(2)}, u32[]{:S(2)}) %collective-permute-start.1) | collective-permute-done | bytes 49184 | tf_op jit(solution)/shard_map/ppermute | solution.py:202
  10.0 1.5 %collective-permute-done.refs_1_ = bf16[24,1024]{1,0:T(8,128)(2,1)S(1)} collective-permute-done((bf16[24,1024]{1,0:T(8,128)(2,1)S(1)}, bf16[24,1024]{1,0:T(8,128)(2,1)S(1)}, u32[]{:S(2)}, u32[]{:S(2)}) %collective-permute-start) | collective-permute-done | bytes 49184 | tf_op jit(solution)/shard_map/ppermute | solution.py:202
  11.5 1.6 %collective-permute-start.3 = (bf16[24,1024]{1,0:T(8,128)(2,1)S(1)}, bf16[24,1024]{1,0:T(8,128)(2,1)S(1)}, u32[]{:S(2)}, u32[]{:S(2)}) collective-permute-start(bf16[24,1024]{1,0:T(8,128)(2,1)S(1)} %collective-permute-done.2.refs_2_), channel_id=1, source_target_pairs={{0,4},{2,6},{4,0},{6,2},{8,12},{10,14},{12,8},{14,10},{1,5},{3,7},... | collective-permute-start | bytes 147464 | tf_op jit(solution)/shard_map/ppermute | solution.py:202
  13.0 0.5 %collective-permute-start.5 = (bf16[24,1024]{1,0:T(8,128)(2,1)S(1)}, bf16[24,1024]{1,0:T(8,128)(2,1)S(1)}, u32[]{:S(2)}, u32[]{:S(2)}) collective-permute-start(bf16[24,1024]{1,0:T(8,128)(2,1)S(1)} %collective-permute-done.2.refs_2_), channel_id=1, source_target_pairs={{0,2},{2,0},{4,6},{6,4},{8,10},{10,8},{12,14},{14,12},{1,3},{3,1},... | collective-permute-start | bytes 147464 | tf_op jit(solution)/shard_map/ppermute | solution.py:202
  13.6 1.5 %collective-permute-start.4 = (bf16[24,1024]{1,0:T(8,128)(2,1)S(1)}, bf16[24,1024]{1,0:T(8,128)(2,1)S(1)}, u32[]{:S(2)}, u32[]{:S(2)}) collective-permute-start(bf16[24,1024]{1,0:T(8,128)(2,1)S(1)} %collective-permute-done.refs_1_), channel_id=1, source_target_pairs={{0,2},{2,0},{4,6},{6,4},{8,10},{10,8},{12,14},{14,12},{1,3},{3,1},... | collective-permute-start | bytes 147464 | tf_op jit(solution)/shard_map/ppermute | solution.py:202
  15.1 0.5 %collective-permute-done.3.refs_3_ = bf16[24,1024]{1,0:T(8,128)(2,1)S(1)} collective-permute-done((bf16[24,1024]{1,0:T(8,128)(2,1)S(1)}, bf16[24,1024]{1,0:T(8,128)(2,1)S(1)}, u32[]{:S(2)}, u32[]{:S(2)}) %collective-permute-start.3) | collective-permute-done | bytes 49184 | tf_op jit(solution)/shard_map/ppermute | solution.py:202
  15.6 0.5 %collective-permute-start.6 = (bf16[24,1024]{1,0:T(8,128)(2,1)S(1)}, bf16[24,1024]{1,0:T(8,128)(2,1)S(1)}, u32[]{:S(2)}, u32[]{:S(2)}) collective-permute-start(bf16[24,1024]{1,0:T(8,128)(2,1)S(1)} %collective-permute-done.3.refs_3_), channel_id=1, source_target_pairs={{0,2},{2,0},{4,6},{6,4},{8,10},{10,8},{12,14},{14,12},{1,3},{3,1},... | collective-permute-start | bytes 147464 | tf_op jit(solution)/shard_map/ppermute | solution.py:202
  16.1 0.1 pad_add_fusion.place_ref
  16.2 1.5 %collective-permute-done.4.refs_5_ = bf16[24,1024]{1,0:T(8,128)(2,1)S(1)} collective-permute-done((bf16[24,1024]{1,0:T(8,128)(2,1)S(1)}, bf16[24,1024]{1,0:T(8,128)(2,1)S(1)}, u32[]{:S(2)}, u32[]{:S(2)}) %collective-permute-start.4) | collective-permute-done | bytes 49184 | tf_op jit(solution)/shard_map/ppermute | solution.py:202
  17.7 0.0 collective-permute-done.5.refs_6_
  17.7 2.0 %collective-permute-done.6.refs_7_ = bf16[24,1024]{1,0:T(8,128)(2,1)S(1)} collective-permute-done((bf16[24,1024]{1,0:T(8,128)(2,1)S(1)}, bf16[24,1024]{1,0:T(8,128)(2,1)S(1)}, u32[]{:S(2)}, u32[]{:S(2)}) %collective-permute-start.6) | collective-permute-done | bytes 49184 | tf_op jit(solution)/shard_map/ppermute | solution.py:202
  19.6 1.6 %scores.1 = (f32[24,256]{1,0:T(8,128)S(1)}, f32[24,256]{1,0:T(8,128)S(1)}) custom-call(s32[2]{0:T(128)S(1)} %pad_add_fusion.place_ref, bf16[256,4096]{1,0:T(8,128)(2,1)S(1)} %get-tuple-element.13.train_ref, s32[1,256]{1,0:T(1,128)S(1)} %get-tuple-element.14.ids_ref, bf16[24,1024]{1,0:T(8,128)(2,1)S(1)} %get-tuple-element.15.refs_0_, ...), custom_call_target="tpu_custom_call" | custom-call | flops 134217728 | bytes 2490368 | tf_op jit(solution)/shard_map/scores/pallas_call | solution.py:185
  21.3 0.1 collective-permute-start.7
  21.3 1.2 %collective-permute-done.7 = f32[24,256]{1,0:T(8,128)S(1)} collective-permute-done((f32[24,256]{1,0:T(8,128)S(1)}, f32[24,256]{1,0:T(8,128)S(1)}, u32[]{:S(2)}, u32[]{:S(2)}) %collective-permute-start.7) | collective-permute-done | bytes 24608 | tf_op jit(solution)/shard_map/ppermute | solution.py:230
  22.5 0.6 %fusion = bf16[3,256,8]{1,2,0:T(8,128)(2,1)} fusion(f32[24,256]{1,0:T(8,128)S(1)} %get-tuple-element.19, f32[24,256]{1,0:T(8,128)S(1)} %collective-permute-done.7), kind=kLoop, calls=%fused_computation.1 | loop fusion | flops 12288 | bytes 61440 | tf_op jit(solution)/shard_map/transpose | solution.py:232
Async XLA Ops:
  1.8 7.2 %collective-permute-start.2 = (bf16[24,1024]{1,0:T(8,128)(2,1)S(1)}, bf16[24,1024]{1,0:T(8,128)(2,1)S(1)}, u32[]{:S(2)}, u32[]{:S(2)}) collective-permute-start(bf16[24,1024]{1,0:T(8,128)(2,1)S(1)} %get-tuple-element.15.refs_0_), channel_id=1, source_target_pairs={{0,8},{2,10},{4,12},{6,14},{8,0},{10,2},{12,4},{14,6},{1,9},{3,11}... | collective-permute-start | bytes 147464 | tf_op jit(solution)/shard_map/ppermute | solution.py:202
  5.9 4.1 %collective-permute-start.1 = (bf16[24,1024]{1,0:T(8,128)(2,1)S(1)}, bf16[24,1024]{1,0:T(8,128)(2,1)S(1)}, u32[]{:S(2)}, u32[]{:S(2)}) collective-permute-start(bf16[24,1024]{1,0:T(8,128)(2,1)S(1)} %get-tuple-element.15.refs_0_), channel_id=1, source_target_pairs={{0,2},{2,0},{4,6},{6,4},{8,10},{10,8},{12,14},{14,12},{1,3},{3,1},... | collective-permute-start | bytes 147464 | tf_op jit(solution)/shard_map/ppermute | solution.py:202
  7.4 4.1 %collective-permute-start = (bf16[24,1024]{1,0:T(8,128)(2,1)S(1)}, bf16[24,1024]{1,0:T(8,128)(2,1)S(1)}, u32[]{:S(2)}, u32[]{:S(2)}) collective-permute-start(bf16[24,1024]{1,0:T(8,128)(2,1)S(1)} %get-tuple-element.15.refs_0_), channel_id=1, source_target_pairs={{0,4},{2,6},{4,0},{6,2},{8,12},{10,14},{12,8},{14,10},{1,5},{3,7},... | collective-permute-start | bytes 147464 | tf_op jit(solution)/shard_map/ppermute | solution.py:202
  11.5 4.1 %collective-permute-start.3 = (bf16[24,1024]{1,0:T(8,128)(2,1)S(1)}, bf16[24,1024]{1,0:T(8,128)(2,1)S(1)}, u32[]{:S(2)}, u32[]{:S(2)}) collective-permute-start(bf16[24,1024]{1,0:T(8,128)(2,1)S(1)} %collective-permute-done.2.refs_2_), channel_id=1, source_target_pairs={{0,4},{2,6},{4,0},{6,2},{8,12},{10,14},{12,8},{14,10},{1,5},{3,7},... | collective-permute-start | bytes 147464 | tf_op jit(solution)/shard_map/ppermute | solution.py:202
  13.0 4.6 %collective-permute-start.5 = (bf16[24,1024]{1,0:T(8,128)(2,1)S(1)}, bf16[24,1024]{1,0:T(8,128)(2,1)S(1)}, u32[]{:S(2)}, u32[]{:S(2)}) collective-permute-start(bf16[24,1024]{1,0:T(8,128)(2,1)S(1)} %collective-permute-done.2.refs_2_), channel_id=1, source_target_pairs={{0,2},{2,0},{4,6},{6,4},{8,10},{10,8},{12,14},{14,12},{1,3},{3,1},... | collective-permute-start | bytes 147464 | tf_op jit(solution)/shard_map/ppermute | solution.py:202
  13.6 4.1 %collective-permute-start.4 = (bf16[24,1024]{1,0:T(8,128)(2,1)S(1)}, bf16[24,1024]{1,0:T(8,128)(2,1)S(1)}, u32[]{:S(2)}, u32[]{:S(2)}) collective-permute-start(bf16[24,1024]{1,0:T(8,128)(2,1)S(1)} %collective-permute-done.refs_1_), channel_id=1, source_target_pairs={{0,2},{2,0},{4,6},{6,4},{8,10},{10,8},{12,14},{14,12},{1,3},{3,1},... | collective-permute-start | bytes 147464 | tf_op jit(solution)/shard_map/ppermute | solution.py:202
  15.6 4.1 %collective-permute-start.6 = (bf16[24,1024]{1,0:T(8,128)(2,1)S(1)}, bf16[24,1024]{1,0:T(8,128)(2,1)S(1)}, u32[]{:S(2)}, u32[]{:S(2)}) collective-permute-start(bf16[24,1024]{1,0:T(8,128)(2,1)S(1)} %collective-permute-done.3.refs_3_), channel_id=1, source_target_pairs={{0,2},{2,0},{4,6},{6,4},{8,10},{10,8},{12,14},{14,12},{1,3},{3,1},... | collective-permute-start | bytes 147464 | tf_op jit(solution)/shard_map/ppermute | solution.py:202
  21.3 1.3 %collective-permute-start.7 = (f32[24,256]{1,0:T(8,128)S(1)}, f32[24,256]{1,0:T(8,128)S(1)}, u32[]{:S(2)}, u32[]{:S(2)}) collective-permute-start(f32[24,256]{1,0:T(8,128)S(1)} %get-tuple-element.20), channel_id=1, source_target_pairs={{0,1},{1,0},{2,3},{3,2},{4,5},{5,4},{6,7},{7,6},{8,9},{9,8},{10,11... | collective-permute-start | bytes 73736 | tf_op jit(solution)/shard_map/ppermute | solution.py:230

commit v5 on v3

--- a/solution.py
+++ b/solution.py
@@ -139,7 +139,7 @@
     return hi, mid, (rest - mid.astype(F32)).astype(BF16)
 
 
-def scores_kernel(masks, blocks, qdev, place_ref, train_ref, ids_ref, *refs):
+def scores_kernel(masks, flips, blocks, qdev, place_ref, train_ref, ids_ref, *refs):
     n_row = len(masks)
     parts, (mine_ref, other_ref, flat_scr, out_scr) = refs[:n_row], refs[n_row:]
     lines, seg = parts[0].shape
@@ -162,10 +162,10 @@
     place = (here == ids_ref[...]).astype(BF16)
     a, b, c = split3(terms)
     ordered = mm(a, place) + mm(b, place) + mm(c, place)
-    me, core = place_ref[0], place_ref[1]
+    me, core, group = place_ref[0], place_ref[1], place_ref[2]
     per = n_row // 2
-    for b, mask in enumerate(masks):
-        source = me ^ mask
+    for b, (mask, flip) in enumerate(zip(masks, flips)):
+        source = me ^ mask ^ (group * flip)
         which = jnp.where(source // per == core, 0, 1)
         first = which * (blocks * per) + source % per
         for j in range(blocks):
@@ -176,14 +176,14 @@
         other_ref[i * qdev:(i + 1) * qdev, :] = out_scr[blocks * per + i]
 
 
-def scores(masks, place, train, row_ids, parts, blocks, qdev):
+def scores(masks, flips, place, train, row_ids, parts, blocks, qdev):
     rows = train.shape[0]
     n_row = len(masks)
     lines, seg = parts[0].shape
     out = jax.ShapeDtypeStruct((blocks * n_row * qdev // 2, rows), F32)
     vmem = pl.BlockSpec(memory_space=pltpu.VMEM)
     return pl.pallas_call(
-        functools.partial(scores_kernel, masks, blocks, qdev),
+        functools.partial(scores_kernel, masks, flips, blocks, qdev),
         out_shape=(out, out),
         in_specs=[pl.BlockSpec(memory_space=pltpu.SMEM)] + [vmem] * (2 + n_row),
         out_specs=(vmem, vmem),
@@ -197,9 +197,26 @@
     )(place, train, row_ids, *parts)
 
 
-def make_body(n_row):
-    def swap(x, mask):
-        return lax.ppermute(x, "row", [(i, i ^ mask) for i in range(n_row)])
+def make_body(n_grp, n_row):
+    def swap(x, mask, other_mask=None, cross=0):
+        pairs = []
+        for g in range(n_grp):
+            for r in range(n_row):
+                to = r ^ (mask if g == 0 or other_mask is None else other_mask)
+                pairs.append((g * n_row + r, (g ^ cross) * n_row + to))
+        return lax.ppermute(x, ("grp", "row"), pairs)
+
+    def gather(own):
+        if n_row != 8 or n_grp != 2:
+            near = [(0, 0, own)] + [(m, 0, swap(own, m)) for m in range(2, n_row, 2)]
+            return near + [(m ^ 1, 0, swap(x, 1)) for m, _, x in near]
+        far = swap(own, 4, 6)
+        parts = [(0, 0, own)] + [(m, 0, swap(own, m)) for m in (1, 2, 3)]
+        parts.append((4, 2, far))
+        parts.append((6, 2, swap(far, 0, cross=1)))
+        parts.append((5, 2, swap(far, 1)))
+        parts.append((7, 2, swap(far, 1, cross=1)))
+        return parts
 
     def body(train_grads, query_grads, out_basis, in_basis, eigenvalues, block_order, row_ids):
         blocks, qdev, _, width = query_grads.shape
@@ -208,15 +225,9 @@
             block_order, query_grads.reshape(blocks, qdev, width), out_basis, in_basis, eigenvalues, row_ids,
             train_grads.reshape(rows, width),
         )
-        near = {0: own}
-        for mask in [4, 6, 2] if n_row == 8 else range(2, n_row, 2):
-            near[mask] = swap(own, mask)
-        far = {mask ^ 1: swap(x, 1) for mask, x in near.items()}
-        both = {**near, **far}
-        place = jnp.stack([lax.axis_index("row"), lax.axis_index("layer")]).astype(jnp.int32)
-        mine, other = scores(
-            tuple(both), place, train, row_ids, tuple(both.values()), blocks, qdev
-        )
+        masks, flips, parts = zip(*gather(own))
+        place = jnp.stack([lax.axis_index(name) for name in ("row", "layer", "grp")]).astype(jnp.int32)
+        mine, other = scores(masks, flips, place, train, row_ids, parts, blocks, qdev)
         got = lax.ppermute(other, "layer", [(0, 1), (1, 0)])
         total = (mine + got).astype(BF16)
         return total.reshape(blocks, -1, rows).transpose(0, 2, 1)
@@ -235,5 +246,5 @@
         P(("grp", "row"), None),
     )
     out_specs = P(None, ("grp", "row"), "layer")
-    body = make_body(mesh.shape["row"])
+    body = make_body(mesh.shape["grp"], mesh.shape["row"])
     return jax.shard_map(body, mesh=mesh, in_specs=in_specs, out_specs=out_specs, check_vma=False)

time: 20.6 us -> 21.1 us (1.024)
  starting transfers between devices: 10.7 us -> 11.7 us
  waiting for transfers between devices: 5.61 us -> 5.13 us
    ppermute x7, starting transfers between devices: 10.7 us -> 11.7 us  [swap(): return lax.ppermute(x, ('grp', 'row'), pairs)]
    ppermute x7, waiting for transfers between devices: 4.43 us -> 3.94 us  [swap(): return lax.ppermute(x, ('grp', 'row'), pairs)]
where the time goes in v5:
time: 21.1 us; the launch traced here: 20.9 us
  starting transfers between devices  11.7 us (55%)
  waiting for transfers between devices  5.13 us (24%)
  Pallas kernels  3.37 us (16%)
  other arithmetic  0.68 us (3%)
    ppermute x7, starting transfers between devices, swap(): return lax.ppermute(x, ('grp', 'row'), pairs)  11.7 us
    ppermute x7, waiting for transfers between devices, swap(): return lax.ppermute(x, ('grp', 'row'), pairs)  3.94 us
    pallas_call x1, Pallas kernels, precondition(): pl.pallas_call(precondition_kernel, out_shape=(jax.ShapeDtypeStruct((coun...  1.78 us
    pallas_call x1, Pallas kernels, scores(): pl.pallas_call(functools.partial(scores_kernel, masks, flips, blocks, qde...  1.59 us
    ppermute x1, waiting for transfers between devices, body(): got = lax.ppermute(other, 'layer', [(0, 1), (1, 0)])  1.18 us
    transpose x1, other arithmetic, body(): return total.reshape(blocks, -1, rows).transpose(0, 2, 1)  0.6 us
  transfers between devices with their start and end apart: 8, of which 4 were waited for; matrix products, arithmetic and copies ran while one was open for 0% of the time, Pallas kernels for 0%

profile of v5, /device:TPU:0, one launch (start us, length us, event | category | flops | bytes accessed | tf_op | source)
XLA Modules:
  0.0 20.9 jit_solution(7680823938681888252)
XLA Ops:
  0.0 1.8 %precondition.1 = (bf16[24,1024]{1,0:T(8,128)(2,1)S(1)}, s32[1,256]{1,0:T(1,128)S(1)}, bf16[256,4096]{1,0:T(8,128)(2,1)S(1)}) custom-call(s32[3]{0:T(128)} %order_hbm.1, bf16[3,2,4096]{2,1,0:T(2,128)(2,1)} %bitcast.10, f32[1,64,64]{2,1,0:T(8,128)} %out_basis_hbm.1, f32[1,64,64]{2,1,0:T(8,128)} %in_basis_hbm.1, f32[1,4096]{1,0:T(1,128)} %eig_hbm.1, ...), custom_call_target="tpu_custom_call" | custom-call | tf_op jit(solution)/shard_map/precondition/pallas_call | solution.py:107
  1.8 4.1 %collective-permute-start.3 = (bf16[24,1024]{1,0:T(8,128)(2,1)S(1)}, bf16[24,1024]{1,0:T(8,128)(2,1)S(1)}, u32[]{:S(2)}, u32[]{:S(2)}) collective-permute-start(bf16[24,1024]{1,0:T(8,128)(2,1)S(1)} %get-tuple-element.12.refs_0_), channel_id=1, source_target_pairs={{0,8},{2,10},{4,12},{6,14},{8,0},{10,2},{12,4},{14,6},{16,28},{18,... | collective-permute-start | bytes 147464 | tf_op jit(solution)/shard_map/ppermute | solution.py:207
  5.9 2.5 %collective-permute-start.2 = (bf16[24,1024]{1,0:T(8,128)(2,1)S(1)}, bf16[24,1024]{1,0:T(8,128)(2,1)S(1)}, u32[]{:S(2)}, u32[]{:S(2)}) collective-permute-start(bf16[24,1024]{1,0:T(8,128)(2,1)S(1)} %get-tuple-element.12.refs_0_), channel_id=1, source_target_pairs={{0,6},{2,4},{4,2},{6,0},{8,14},{10,12},{12,10},{14,8},{16,22},{18,... | collective-permute-start | bytes 147464 | tf_op jit(solution)/shard_map/ppermute | solution.py:207
  8.4 0.4 %collective-permute-start.1 = (bf16[24,1024]{1,0:T(8,128)(2,1)S(1)}, bf16[24,1024]{1,0:T(8,128)(2,1)S(1)}, u32[]{:S(2)}, u32[]{:S(2)}) collective-permute-start(bf16[24,1024]{1,0:T(8,128)(2,1)S(1)} %get-tuple-element.12.refs_0_), channel_id=1, source_target_pairs={{0,4},{2,6},{4,0},{6,2},{8,12},{10,14},{12,8},{14,10},{16,20},{18,... | collective-permute-start | bytes 147464 | tf_op jit(solution)/shard_map/ppermute | solution.py:207
  8.8 0.5 %collective-permute-start = (bf16[24,1024]{1,0:T(8,128)(2,1)S(1)}, bf16[24,1024]{1,0:T(8,128)(2,1)S(1)}, u32[]{:S(2)}, u32[]{:S(2)}) collective-permute-start(bf16[24,1024]{1,0:T(8,128)(2,1)S(1)} %get-tuple-element.12.refs_0_), channel_id=1, source_target_pairs={{0,2},{2,0},{4,6},{6,4},{8,10},{10,8},{12,14},{14,12},{16,18},{18,... | collective-permute-start | bytes 147464 | tf_op jit(solution)/shard_map/ppermute | solution.py:207
  9.4 0.0 collective-permute-done.3.refs_4_
  9.4 3.5 %collective-permute-start.6 = (bf16[24,1024]{1,0:T(8,128)(2,1)S(1)}, bf16[24,1024]{1,0:T(8,128)(2,1)S(1)}, u32[]{:S(2)}, u32[]{:S(2)}) collective-permute-start(bf16[24,1024]{1,0:T(8,128)(2,1)S(1)} %collective-permute-done.3.refs_4_), channel_id=1, source_target_pairs={{0,18},{2,16},{4,22},{6,20},{8,26},{10,24},{12,30},{14,28},{16,2},... | collective-permute-start | bytes 147464 | tf_op jit(solution)/shard_map/ppermute | solution.py:207
  12.8 0.5 %collective-permute-start.5 = (bf16[24,1024]{1,0:T(8,128)(2,1)S(1)}, bf16[24,1024]{1,0:T(8,128)(2,1)S(1)}, u32[]{:S(2)}, u32[]{:S(2)}) collective-permute-start(bf16[24,1024]{1,0:T(8,128)(2,1)S(1)} %collective-permute-done.3.refs_4_), channel_id=1, source_target_pairs={{0,2},{2,0},{4,6},{6,4},{8,10},{10,8},{12,14},{14,12},{16,18},{18,... | collective-permute-start | bytes 147464 | tf_op jit(solution)/shard_map/ppermute | solution.py:207
  13.4 0.0 collective-permute-done.2.refs_3_
  13.4 0.1 collective-permute-start.4
  13.5 0.1 pad_add_fusion.place_ref
  13.5 0.0 collective-permute-done.1.refs_2_
  13.5 0.0 collective-permute-done.refs_1_
  13.5 1.9 %collective-permute-done.6.refs_7_ = bf16[24,1024]{1,0:T(8,128)(2,1)S(1)} collective-permute-done((bf16[24,1024]{1,0:T(8,128)(2,1)S(1)}, bf16[24,1024]{1,0:T(8,128)(2,1)S(1)}, u32[]{:S(2)}, u32[]{:S(2)}) %collective-permute-start.6) | collective-permute-done | bytes 49184 | tf_op jit(solution)/shard_map/ppermute | solution.py:207
  15.5 1.5 %collective-permute-done.5.refs_6_ = bf16[24,1024]{1,0:T(8,128)(2,1)S(1)} collective-permute-done((bf16[24,1024]{1,0:T(8,128)(2,1)S(1)}, bf16[24,1024]{1,0:T(8,128)(2,1)S(1)}, u32[]{:S(2)}, u32[]{:S(2)}) %collective-permute-start.5) | collective-permute-done | bytes 49184 | tf_op jit(solution)/shard_map/ppermute | solution.py:207
  16.9 0.5 %collective-permute-done.4.refs_5_ = bf16[24,1024]{1,0:T(8,128)(2,1)S(1)} collective-permute-done((bf16[24,1024]{1,0:T(8,128)(2,1)S(1)}, bf16[24,1024]{1,0:T(8,128)(2,1)S(1)}, u32[]{:S(2)}, u32[]{:S(2)}) %collective-permute-start.4) | collective-permute-done | bytes 49184 | tf_op jit(solution)/shard_map/ppermute | solution.py:207
  17.5 1.6 %scores.1 = (f32[24,256]{1,0:T(8,128)S(1)}, f32[24,256]{1,0:T(8,128)S(1)}) custom-call(s32[3]{0:T(128)S(1)} %pad_add_fusion.place_ref, bf16[256,4096]{1,0:T(8,128)(2,1)S(1)} %get-tuple-element.10.train_ref, s32[1,256]{1,0:T(1,128)S(1)} %get-tuple-element.11.ids_ref, bf16[24,1024]{1,0:T(8,128)(2,1)S(1)} %get-tuple-element.12.refs_0_, ...), custom_call_target="tpu_custom_call" | custom-call | flops 134217728 | bytes 2490368 | tf_op jit(solution)/shard_map/scores/pallas_call | solution.py:185
  19.1 0.1 collective-permute-start.7
  19.1 1.2 %collective-permute-done.7 = f32[24,256]{1,0:T(8,128)S(1)} collective-permute-done((f32[24,256]{1,0:T(8,128)S(1)}, f32[24,256]{1,0:T(8,128)S(1)}, u32[]{:S(2)}, u32[]{:S(2)}) %collective-permute-start.7) | collective-permute-done | bytes 24608 | tf_op jit(solution)/shard_map/ppermute | solution.py:231
  20.3 0.6 %fusion = bf16[3,256,8]{1,2,0:T(8,128)(2,1)} fusion(f32[24,256]{1,0:T(8,128)S(1)} %get-tuple-element.13, f32[24,256]{1,0:T(8,128)S(1)} %collective-permute-done.7), kind=kLoop, calls=%fused_computation.1 | loop fusion | flops 12288 | bytes 61440 | tf_op jit(solution)/shard_map/transpose | solution.py:233
Async XLA Ops:
  1.8 7.6 %collective-permute-start.3 = (bf16[24,1024]{1,0:T(8,128)(2,1)S(1)}, bf16[24,1024]{1,0:T(8,128)(2,1)S(1)}, u32[]{:S(2)}, u32[]{:S(2)}) collective-permute-start(bf16[24,1024]{1,0:T(8,128)(2,1)S(1)} %get-tuple-element.12.refs_0_), channel_id=1, source_target_pairs={{0,8},{2,10},{4,12},{6,14},{8,0},{10,2},{12,4},{14,6},{16,28},{18,... | collective-permute-start | bytes 147464 | tf_op jit(solution)/shard_map/ppermute | solution.py:207
  5.9 7.5 %collective-permute-start.2 = (bf16[24,1024]{1,0:T(8,128)(2,1)S(1)}, bf16[24,1024]{1,0:T(8,128)(2,1)S(1)}, u32[]{:S(2)}, u32[]{:S(2)}) collective-permute-start(bf16[24,1024]{1,0:T(8,128)(2,1)S(1)} %get-tuple-element.12.refs_0_), channel_id=1, source_target_pairs={{0,6},{2,4},{4,2},{6,0},{8,14},{10,12},{12,10},{14,8},{16,22},{18,... | collective-permute-start | bytes 147464 | tf_op jit(solution)/shard_map/ppermute | solution.py:207
  8.4 5.1 %collective-permute-start.1 = (bf16[24,1024]{1,0:T(8,128)(2,1)S(1)}, bf16[24,1024]{1,0:T(8,128)(2,1)S(1)}, u32[]{:S(2)}, u32[]{:S(2)}) collective-permute-start(bf16[24,1024]{1,0:T(8,128)(2,1)S(1)} %get-tuple-element.12.refs_0_), channel_id=1, source_target_pairs={{0,4},{2,6},{4,0},{6,2},{8,12},{10,14},{12,8},{14,10},{16,20},{18,... | collective-permute-start | bytes 147464 | tf_op jit(solution)/shard_map/ppermute | solution.py:207
  8.8 4.7 %collective-permute-start = (bf16[24,1024]{1,0:T(8,128)(2,1)S(1)}, bf16[24,1024]{1,0:T(8,128)(2,1)S(1)}, u32[]{:S(2)}, u32[]{:S(2)}) collective-permute-start(bf16[24,1024]{1,0:T(8,128)(2,1)S(1)} %get-tuple-element.12.refs_0_), channel_id=1, source_target_pairs={{0,2},{2,0},{4,6},{6,4},{8,10},{10,8},{12,14},{14,12},{16,18},{18,... | collective-permute-start | bytes 147464 | tf_op jit(solution)/shard_map/ppermute | solution.py:207
  9.4 6.1 %collective-permute-start.6 = (bf16[24,1024]{1,0:T(8,128)(2,1)S(1)}, bf16[24,1024]{1,0:T(8,128)(2,1)S(1)}, u32[]{:S(2)}, u32[]{:S(2)}) collective-permute-start(bf16[24,1024]{1,0:T(8,128)(2,1)S(1)} %collective-permute-done.3.refs_4_), channel_id=1, source_target_pairs={{0,18},{2,16},{4,22},{6,20},{8,26},{10,24},{12,30},{14,28},{16,2},... | collective-permute-start | bytes 147464 | tf_op jit(solution)/shard_map/ppermute | solution.py:207
  12.8 4.1 %collective-permute-start.5 = (bf16[24,1024]{1,0:T(8,128)(2,1)S(1)}, bf16[24,1024]{1,0:T(8,128)(2,1)S(1)}, u32[]{:S(2)}, u32[]{:S(2)}) collective-permute-start(bf16[24,1024]{1,0:T(8,128)(2,1)S(1)} %collective-permute-done.3.refs_4_), channel_id=1, source_target_pairs={{0,2},{2,0},{4,6},{6,4},{8,10},{10,8},{12,14},{14,12},{16,18},{18,... | collective-permute-start | bytes 147464 | tf_op jit(solution)/shard_map/ppermute | solution.py:207
  13.4 4.1 %collective-permute-start.4 = (bf16[24,1024]{1,0:T(8,128)(2,1)S(1)}, bf16[24,1024]{1,0:T(8,128)(2,1)S(1)}, u32[]{:S(2)}, u32[]{:S(2)}) collective-permute-start(bf16[24,1024]{1,0:T(8,128)(2,1)S(1)} %collective-permute-done.3.refs_4_), channel_id=1, source_target_pairs={{0,16},{2,18},{4,20},{6,22},{8,24},{10,26},{12,28},{14,30},{16,0},... | collective-permute-start | bytes 147464 | tf_op jit(solution)/shard_map/ppermute | solution.py:207
  19.1 1.3 %collective-permute-start.7 = (f32[24,256]{1,0:T(8,128)S(1)}, f32[24,256]{1,0:T(8,128)S(1)}, u32[]{:S(2)}, u32[]{:S(2)}) collective-permute-start(f32[24,256]{1,0:T(8,128)S(1)} %get-tuple-element.14), channel_id=1, source_target_pairs={{0,1},{1,0},{2,3},{3,2},{4,5},{5,4},{6,7},{7,6},{8,9},{9,8},{10,11... | collective-permute-start | bytes 73736 | tf_op jit(solution)/shard_map/ppermute | solution.py:231

commit v6 on v5

--- a/solution.py
+++ b/solution.py
@@ -210,12 +210,10 @@
         if n_row != 8 or n_grp != 2:
             near = [(0, 0, own)] + [(m, 0, swap(own, m)) for m in range(2, n_row, 2)]
             return near + [(m ^ 1, 0, swap(x, 1)) for m, _, x in near]
-        far = swap(own, 4, 6)
-        parts = [(0, 0, own)] + [(m, 0, swap(own, m)) for m in (1, 2, 3)]
-        parts.append((4, 2, far))
-        parts.append((6, 2, swap(far, 0, cross=1)))
-        parts.append((5, 2, swap(far, 1)))
-        parts.append((7, 2, swap(far, 1, cross=1)))
+        far = {m: swap(own, m) for m in (4, 6)}
+        parts = [(0, 0, own)] + [(m, 0, swap(own, m)) for m in (3, 1, 2)]
+        parts += [(m, 0, x) for m, x in far.items()]
+        parts += [(m ^ 1, 0, swap(x, 1)) for m, x in far.items()]
         return parts
 
     def body(train_grads, query_grads, out_basis, in_basis, eigenvalues, block_order, row_ids):

time: 21.1 us -> 19.6 us (0.929)
  waiting for transfers between devices: 5.13 us -> 3.71 us
    ppermute x7, waiting for transfers between devices: 3.94 us -> 2.53 us  [swap(): return lax.ppermute(x, ('grp', 'row'), pairs)]
where the time goes in v6:
time: 19.6 us; the launch traced here: 19.5 us
  starting transfers between devices  11.7 us (60%)
  waiting for transfers between devices  3.71 us (19%)
  Pallas kernels  3.37 us (17%)
  other arithmetic  0.68 us (3%)
    ppermute x7, starting transfers between devices, swap(): return lax.ppermute(x, ('grp', 'row'), pairs)  11.6 us
    ppermute x7, waiting for transfers between devices, swap(): return lax.ppermute(x, ('grp', 'row'), pairs)  2.53 us
    pallas_call x1, Pallas kernels, precondition(): pl.pallas_call(precondition_kernel, out_shape=(jax.ShapeDtypeStruct((coun...  1.78 us
    pallas_call x1, Pallas kernels, scores(): pl.pallas_call(functools.partial(scores_kernel, masks, flips, blocks, qde...  1.59 us
    ppermute x1, waiting for transfers between devices, body(): got = lax.ppermute(other, 'layer', [(0, 1), (1, 0)])  1.18 us
    transpose x1, other arithmetic, body(): return total.reshape(blocks, -1, rows).transpose(0, 2, 1)  0.6 us
  transfers between devices with their start and end apart: 8, of which 4 were waited for; matrix products, arithmetic and copies ran while one was open for 0% of the time, Pallas kernels for 0%

profile of v6, /device:TPU:0, one launch (start us, length us, event | category | flops | bytes accessed | tf_op | source)
XLA Modules:
  0.0 19.5 jit_solution(16330849623381641861)
XLA Ops:
  0.0 1.8 %precondition.1 = (bf16[24,1024]{1,0:T(8,128)(2,1)S(1)}, s32[1,256]{1,0:T(1,128)S(1)}, bf16[256,4096]{1,0:T(8,128)(2,1)S(1)}) custom-call(s32[3]{0:T(128)} %order_hbm.1, bf16[3,2,4096]{2,1,0:T(2,128)(2,1)} %bitcast.10, f32[1,64,64]{2,1,0:T(8,128)} %out_basis_hbm.1, f32[1,64,64]{2,1,0:T(8,128)} %in_basis_hbm.1, f32[1,4096]{1,0:T(1,128)} %eig_hbm.1, ...), custom_call_target="tpu_custom_call" | custom-call | tf_op jit(solution)/shard_map/precondition/pallas_call | solution.py:107
  1.8 5.1 %collective-permute-start.4 = (bf16[24,1024]{1,0:T(8,128)(2,1)S(1)}, bf16[24,1024]{1,0:T(8,128)(2,1)S(1)}, u32[]{:S(2)}, u32[]{:S(2)}) collective-permute-start(bf16[24,1024]{1,0:T(8,128)(2,1)S(1)} %get-tuple-element.12.refs_0_), channel_id=1, source_target_pairs={{0,12},{2,14},{4,8},{6,10},{8,4},{10,6},{12,0},{14,2},{16,28},{18,... | collective-permute-start | bytes 147464 | tf_op jit(solution)/shard_map/ppermute | solution.py:207
  6.9 0.0 collective-permute-start.3
  6.9 0.6 %collective-permute-start.2 = (bf16[24,1024]{1,0:T(8,128)(2,1)S(1)}, bf16[24,1024]{1,0:T(8,128)(2,1)S(1)}, u32[]{:S(2)}, u32[]{:S(2)}) collective-permute-start(bf16[24,1024]{1,0:T(8,128)(2,1)S(1)} %get-tuple-element.12.refs_0_), channel_id=1, source_target_pairs={{0,4},{2,6},{4,0},{6,2},{8,12},{10,14},{12,8},{14,10},{16,20},{18,... | collective-permute-start | bytes 147464 | tf_op jit(solution)/shard_map/ppermute | solution.py:207
  7.5 1.6 %collective-permute-start.1 = (bf16[24,1024]{1,0:T(8,128)(2,1)S(1)}, bf16[24,1024]{1,0:T(8,128)(2,1)S(1)}, u32[]{:S(2)}, u32[]{:S(2)}) collective-permute-start(bf16[24,1024]{1,0:T(8,128)(2,1)S(1)} %get-tuple-element.12.refs_0_), channel_id=1, source_target_pairs={{0,2},{2,0},{4,6},{6,4},{8,10},{10,8},{12,14},{14,12},{16,18},{18,... | collective-permute-start | bytes 147464 | tf_op jit(solution)/shard_map/ppermute | solution.py:207
  9.2 1.2 %collective-permute-start = (bf16[24,1024]{1,0:T(8,128)(2,1)S(1)}, bf16[24,1024]{1,0:T(8,128)(2,1)S(1)}, u32[]{:S(2)}, u32[]{:S(2)}) collective-permute-start(bf16[24,1024]{1,0:T(8,128)(2,1)S(1)} %get-tuple-element.12.refs_0_), channel_id=1, source_target_pairs={{0,6},{2,4},{4,2},{6,0},{8,14},{10,12},{12,10},{14,8},{16,22},{18,... | collective-permute-start | bytes 147464 | tf_op jit(solution)/shard_map/ppermute | solution.py:207
  10.4 0.0 collective-permute-done.4.refs_5_
  10.4 1.5 %collective-permute-start.6 = (bf16[24,1024]{1,0:T(8,128)(2,1)S(1)}, bf16[24,1024]{1,0:T(8,128)(2,1)S(1)}, u32[]{:S(2)}, u32[]{:S(2)}) collective-permute-start(bf16[24,1024]{1,0:T(8,128)(2,1)S(1)} %collective-permute-done.4.refs_5_), channel_id=1, source_target_pairs={{0,2},{2,0},{4,6},{6,4},{8,10},{10,8},{12,14},{14,12},{16,18},{18,... | collective-permute-start | bytes 147464 | tf_op jit(solution)/shard_map/ppermute | solution.py:207
  11.9 0.0 collective-permute-done.3.refs_4_
  11.9 1.5 %collective-permute-start.5 = (bf16[24,1024]{1,0:T(8,128)(2,1)S(1)}, bf16[24,1024]{1,0:T(8,128)(2,1)S(1)}, u32[]{:S(2)}, u32[]{:S(2)}) collective-permute-start(bf16[24,1024]{1,0:T(8,128)(2,1)S(1)} %collective-permute-done.3.refs_4_), channel_id=1, source_target_pairs={{0,2},{2,0},{4,6},{6,4},{8,10},{10,8},{12,14},{14,12},{16,18},{18,... | collective-permute-start | bytes 147464 | tf_op jit(solution)/shard_map/ppermute | solution.py:207
  13.4 0.1 pad_add_fusion.place_ref
  13.5 0.0 collective-permute-done.2.refs_3_
  13.5 0.0 collective-permute-done.1.refs_2_
  13.5 0.8 %collective-permute-done.refs_1_ = bf16[24,1024]{1,0:T(8,128)(2,1)S(1)} collective-permute-done((bf16[24,1024]{1,0:T(8,128)(2,1)S(1)}, bf16[24,1024]{1,0:T(8,128)(2,1)S(1)}, u32[]{:S(2)}, u32[]{:S(2)}) %collective-permute-start) | collective-permute-done | bytes 49184 | tf_op jit(solution)/shard_map/ppermute | solution.py:207
  14.3 0.8 %collective-permute-done.6.refs_7_ = bf16[24,1024]{1,0:T(8,128)(2,1)S(1)} collective-permute-done((bf16[24,1024]{1,0:T(8,128)(2,1)S(1)}, bf16[24,1024]{1,0:T(8,128)(2,1)S(1)}, u32[]{:S(2)}, u32[]{:S(2)}) %collective-permute-start.6) | collective-permute-done | bytes 49184 | tf_op jit(solution)/shard_map/ppermute | solution.py:207
  15.1 0.9 %collective-permute-done.5.refs_6_ = bf16[24,1024]{1,0:T(8,128)(2,1)S(1)} collective-permute-done((bf16[24,1024]{1,0:T(8,128)(2,1)S(1)}, bf16[24,1024]{1,0:T(8,128)(2,1)S(1)}, u32[]{:S(2)}, u32[]{:S(2)}) %collective-permute-start.5) | collective-permute-done | bytes 49184 | tf_op jit(solution)/shard_map/ppermute | solution.py:207
  16.0 1.6 %scores.1 = (f32[24,256]{1,0:T(8,128)S(1)}, f32[24,256]{1,0:T(8,128)S(1)}) custom-call(s32[3]{0:T(128)S(1)} %pad_add_fusion.place_ref, bf16[256,4096]{1,0:T(8,128)(2,1)S(1)} %get-tuple-element.10.train_ref, s32[1,256]{1,0:T(1,128)S(1)} %get-tuple-element.11.ids_ref, bf16[24,1024]{1,0:T(8,128)(2,1)S(1)} %get-tuple-element.12.refs_0_, ...), custom_call_target="tpu_custom_call" | custom-call | flops 134217728 | bytes 2490368 | tf_op jit(solution)/shard_map/scores/pallas_call | solution.py:185
  17.6 0.1 collective-permute-start.7
  17.7 1.2 %collective-permute-done.7 = f32[24,256]{1,0:T(8,128)S(1)} collective-permute-done((f32[24,256]{1,0:T(8,128)S(1)}, f32[24,256]{1,0:T(8,128)S(1)}, u32[]{:S(2)}, u32[]{:S(2)}) %collective-permute-start.7) | collective-permute-done | bytes 24608 | tf_op jit(solution)/shard_map/ppermute | solution.py:229
  18.8 0.6 %fusion = bf16[3,256,8]{1,2,0:T(8,128)(2,1)} fusion(f32[24,256]{1,0:T(8,128)S(1)} %get-tuple-element.13, f32[24,256]{1,0:T(8,128)S(1)} %collective-permute-done.7), kind=kLoop, calls=%fused_computation.1 | loop fusion | flops 12288 | bytes 61440 | tf_op jit(solution)/shard_map/transpose | solution.py:231
Async XLA Ops:
  1.8 8.6 %collective-permute-start.4 = (bf16[24,1024]{1,0:T(8,128)(2,1)S(1)}, bf16[24,1024]{1,0:T(8,128)(2,1)S(1)}, u32[]{:S(2)}, u32[]{:S(2)}) collective-permute-start(bf16[24,1024]{1,0:T(8,128)(2,1)S(1)} %get-tuple-element.12.refs_0_), channel_id=1, source_target_pairs={{0,12},{2,14},{4,8},{6,10},{8,4},{10,6},{12,0},{14,2},{16,28},{18,... | collective-permute-start | bytes 147464 | tf_op jit(solution)/shard_map/ppermute | solution.py:207
  6.9 5.0 %collective-permute-start.3 = (bf16[24,1024]{1,0:T(8,128)(2,1)S(1)}, bf16[24,1024]{1,0:T(8,128)(2,1)S(1)}, u32[]{:S(2)}, u32[]{:S(2)}) collective-permute-start(bf16[24,1024]{1,0:T(8,128)(2,1)S(1)} %get-tuple-element.12.refs_0_), channel_id=1, source_target_pairs={{0,8},{2,10},{4,12},{6,14},{8,0},{10,2},{12,4},{14,6},{16,24},{18,... | collective-permute-start | bytes 147464 | tf_op jit(solution)/shard_map/ppermute | solution.py:207
  6.9 6.6 %collective-permute-start.2 = (bf16[24,1024]{1,0:T(8,128)(2,1)S(1)}, bf16[24,1024]{1,0:T(8,128)(2,1)S(1)}, u32[]{:S(2)}, u32[]{:S(2)}) collective-permute-start(bf16[24,1024]{1,0:T(8,128)(2,1)S(1)} %get-tuple-element.12.refs_0_), channel_id=1, source_target_pairs={{0,4},{2,6},{4,0},{6,2},{8,12},{10,14},{12,8},{14,10},{16,20},{18,... | collective-permute-start | bytes 147464 | tf_op jit(solution)/shard_map/ppermute | solution.py:207
  7.5 5.9 %collective-permute-start.1 = (bf16[24,1024]{1,0:T(8,128)(2,1)S(1)}, bf16[24,1024]{1,0:T(8,128)(2,1)S(1)}, u32[]{:S(2)}, u32[]{:S(2)}) collective-permute-start(bf16[24,1024]{1,0:T(8,128)(2,1)S(1)} %get-tuple-element.12.refs_0_), channel_id=1, source_target_pairs={{0,2},{2,0},{4,6},{6,4},{8,10},{10,8},{12,14},{14,12},{16,18},{18,... | collective-permute-start | bytes 147464 | tf_op jit(solution)/shard_map/ppermute | solution.py:207
  9.2 5.1 %collective-permute-start = (bf16[24,1024]{1,0:T(8,128)(2,1)S(1)}, bf16[24,1024]{1,0:T(8,128)(2,1)S(1)}, u32[]{:S(2)}, u32[]{:S(2)}) collective-permute-start(bf16[24,1024]{1,0:T(8,128)(2,1)S(1)} %get-tuple-element.12.refs_0_), channel_id=1, source_target_pairs={{0,6},{2,4},{4,2},{6,0},{8,14},{10,12},{12,10},{14,8},{16,22},{18,... | collective-permute-start | bytes 147464 | tf_op jit(solution)/shard_map/ppermute | solution.py:207
  10.4 4.7 %collective-permute-start.6 = (bf16[24,1024]{1,0:T(8,128)(2,1)S(1)}, bf16[24,1024]{1,0:T(8,128)(2,1)S(1)}, u32[]{:S(2)}, u32[]{:S(2)}) collective-permute-start(bf16[24,1024]{1,0:T(8,128)(2,1)S(1)} %collective-permute-done.4.refs_5_), channel_id=1, source_target_pairs={{0,2},{2,0},{4,6},{6,4},{8,10},{10,8},{12,14},{14,12},{16,18},{18,... | collective-permute-start | bytes 147464 | tf_op jit(solution)/shard_map/ppermute | solution.py:207
  11.9 4.1 %collective-permute-start.5 = (bf16[24,1024]{1,0:T(8,128)(2,1)S(1)}, bf16[24,1024]{1,0:T(8,128)(2,1)S(1)}, u32[]{:S(2)}, u32[]{:S(2)}) collective-permute-start(bf16[24,1024]{1,0:T(8,128)(2,1)S(1)} %collective-permute-done.3.refs_4_), channel_id=1, source_target_pairs={{0,2},{2,0},{4,6},{6,4},{8,10},{10,8},{12,14},{14,12},{16,18},{18,... | collective-permute-start | bytes 147464 | tf_op jit(solution)/shard_map/ppermute | solution.py:207
  17.6 1.3 %collective-permute-start.7 = (f32[24,256]{1,0:T(8,128)S(1)}, f32[24,256]{1,0:T(8,128)S(1)}, u32[]{:S(2)}, u32[]{:S(2)}) collective-permute-start(f32[24,256]{1,0:T(8,128)S(1)} %get-tuple-element.14), channel_id=1, source_target_pairs={{0,1},{1,0},{2,3},{3,2},{4,5},{5,4},{6,7},{7,6},{8,9},{9,8},{10,11... | collective-permute-start | bytes 73736 | tf_op jit(solution)/shard_map/ppermute | solution.py:229

commit v7 on v3

--- a/solution.py
+++ b/solution.py
@@ -10,6 +10,7 @@
 DAMPING = 0.01
 LANES = 128
 SEGMENTS = 4
+SLOT = 8
 F32, BF16 = jnp.float32, jnp.bfloat16
 NT = (((1,), (1,)), ((), ()))
 
@@ -139,12 +140,8 @@
     return hi, mid, (rest - mid.astype(F32)).astype(BF16)
 
 
-def scores_kernel(masks, blocks, qdev, place_ref, train_ref, ids_ref, *refs):
-    n_row = len(masks)
-    parts, (mine_ref, other_ref, flat_scr, out_scr) = refs[:n_row], refs[n_row:]
+def placed_terms(parts, train_ref, place, flat_scr):
     lines, seg = parts[0].shape
-    rows = train_ref.shape[0]
-    slot = 8
     per_seg = seg // LANES
     for b, part in enumerate(parts):
         flat = part[...].astype(F32)
@@ -153,53 +150,99 @@
     terms = None
     for j in range(SEGMENTS):
         queries = jnp.concatenate([
-            jnp.concatenate([flat_scr[b, c, pl.ds(j, slot, stride=SEGMENTS), :] for b in range(n_row)], axis=0)
+            jnp.concatenate([flat_scr[b, c, pl.ds(j, SLOT, stride=SEGMENTS), :] for b in range(len(parts))], axis=0)
             for c in range(per_seg)
         ], axis=1)
         term = mm_nt(queries.astype(BF16), train_ref[:, j * seg:(j + 1) * seg])
         terms = term if terms is None else terms + term
+    a, b, c = split3(terms)
+    return mm(a, place) + mm(b, place) + mm(c, place)
+
+
+def early_kernel(train_ref, ids_ref, *refs):
+    parts, (terms_ref, place_ref, flat_scr) = refs[:-3], refs[-3:]
+    rows = train_ref.shape[0]
     here = lax.broadcasted_iota(jnp.int32, (rows, rows), 0)
     place = (here == ids_ref[...]).astype(BF16)
-    a, b, c = split3(terms)
-    ordered = mm(a, place) + mm(b, place) + mm(c, place)
-    me, core = place_ref[0], place_ref[1]
+    place_ref[...] = place
+    terms_ref[...] = placed_terms(parts, train_ref, place, flat_scr)
+
+
+def late_kernel(masks, blocks, qdev, where_ref, train_ref, place_ref, early_ref, *refs):
+    parts, (mine_ref, other_ref, flat_scr, out_scr) = refs[:-4], refs[-4:]
+    n_row = len(masks)
+    ordered = jnp.concatenate(
+        [early_ref[...], placed_terms(parts, train_ref, place_ref[...], flat_scr)], axis=0
+    )
+    me, core = where_ref[0], where_ref[1]
     per = n_row // 2
     for b, mask in enumerate(masks):
         source = me ^ mask
         which = jnp.where(source // per == core, 0, 1)
         first = which * (blocks * per) + source % per
         for j in range(blocks):
-            at = b * slot + j * qdev
+            at = b * SLOT + j * qdev
             out_scr[first + j * per] = ordered[at:at + qdev]
     for i in range(blocks * per):
         mine_ref[i * qdev:(i + 1) * qdev, :] = out_scr[i]
         other_ref[i * qdev:(i + 1) * qdev, :] = out_scr[blocks * per + i]
 
 
-def scores(masks, place, train, row_ids, parts, blocks, qdev):
-    rows = train.shape[0]
+def scores(masks, early, where, train, row_ids, parts, blocks, qdev):
+    rows, width = train.shape
     n_row = len(masks)
     lines, seg = parts[0].shape
+    vmem = pl.BlockSpec(memory_space=pltpu.VMEM)
+    params = pltpu.CompilerParams(vmem_limit_bytes=(16 if n_row <= 16 else 24) * 2**20)
+
+    def flat(count):
+        return pltpu.VMEM((count, seg // LANES, SLOT * SEGMENTS, LANES), F32)
+
+    def cost(count):
+        return pl.CostEstimate(
+            flops=2 * count * SLOT * rows * width, bytes_accessed=2 * (rows * width + count * lines * seg),
+            transcendentals=0,
+        )
+
+    terms, place = pl.pallas_call(
+        early_kernel,
+        out_shape=(
+            jax.ShapeDtypeStruct((early * SLOT, rows), F32),
+            jax.ShapeDtypeStruct((rows, rows), BF16),
+        ),
+        in_specs=[vmem] * (2 + early),
+        out_specs=(vmem, vmem),
+        scratch_shapes=[flat(early)],
+        compiler_params=params,
+        cost_estimate=cost(early),
+        name="scores_early",
+    )(train, row_ids, *parts[:early])
+    late = n_row - early
     out = jax.ShapeDtypeStruct((blocks * n_row * qdev // 2, rows), F32)
-    vmem = pl.BlockSpec(memory_space=pltpu.VMEM)
     return pl.pallas_call(
-        functools.partial(scores_kernel, masks, blocks, qdev),
+        functools.partial(late_kernel, masks, blocks, qdev),
         out_shape=(out, out),
-        in_specs=[pl.BlockSpec(memory_space=pltpu.SMEM)] + [vmem] * (2 + n_row),
+        in_specs=[pl.BlockSpec(memory_space=pltpu.SMEM)] + [vmem] * (3 + late),
         out_specs=(vmem, vmem),
-        scratch_shapes=[
-            pltpu.VMEM((n_row, seg // LANES, 8 * SEGMENTS, LANES), F32),
-            pltpu.VMEM((blocks * n_row, qdev, rows), F32),
-        ],
-        compiler_params=pltpu.CompilerParams(vmem_limit_bytes=(16 if n_row <= 16 else 48) * 2**20),
-        cost_estimate=pl.CostEstimate(flops=2 * n_row * 8 * rows * seg * SEGMENTS, bytes_accessed=train.size * 2 + n_row * lines * seg * 2, transcendentals=0),
-        name="scores",
-    )(place, train, row_ids, *parts)
+        scratch_shapes=[flat(late), pltpu.VMEM((blocks * n_row, qdev, rows), F32)],
+        compiler_params=params,
+        cost_estimate=cost(late),
+        name="scores_late",
+    )(where, train, place, terms, *parts[early:])
 
 
 def make_body(n_row):
     def swap(x, mask):
-        return lax.ppermute(x, "row", [(i, i ^ mask) for i in range(n_row)])
+        return lax.ppermute(x, "row", [(r, r ^ mask) for r in range(n_row)])
+
+    def gather(own):
+        if n_row != 8:
+            near = {0: own, **{m: swap(own, m) for m in range(2, n_row, 2)}}
+            return {**near, **{m ^ 1: swap(x, 1) for m, x in near.items()}}, n_row // 2
+        far = {m: swap(own, m) for m in (6, 4)}
+        diagonal = {3: swap(own, 3)}
+        near = {m: swap(own, m) for m in (2, 1)}
+        return {0: own, **near, **far, **diagonal, **{m ^ 1: swap(x, 1) for m, x in far.items()}}, 5
 
     def body(train_grads, query_grads, out_basis, in_basis, eigenvalues, block_order, row_ids):
         blocks, qdev, _, width = query_grads.shape
@@ -208,14 +251,10 @@
             block_order, query_grads.reshape(blocks, qdev, width), out_basis, in_basis, eigenvalues, row_ids,
             train_grads.reshape(rows, width),
         )
-        near = {0: own}
-        for mask in [4, 6, 2] if n_row == 8 else range(2, n_row, 2):
-            near[mask] = swap(own, mask)
-        far = {mask ^ 1: swap(x, 1) for mask, x in near.items()}
-        both = {**near, **far}
-        place = jnp.stack([lax.axis_index("row"), lax.axis_index("layer")]).astype(jnp.int32)
+        parts, early = gather(own)
+        where = jnp.stack([lax.axis_index(name) for name in ("row", "layer")]).astype(jnp.int32)
         mine, other = scores(
-            tuple(both), place, train, row_ids, tuple(both.values()), blocks, qdev
+            tuple(parts), early, where, train, row_ids, tuple(parts.values()), blocks, qdev
         )
         got = lax.ppermute(other, "layer", [(0, 1), (1, 0)])
         total = (mine + got).astype(BF16)

time: 20.6 us -> 19.5 us (0.947)
  waiting for transfers between devices: 5.61 us -> 2.72 us
  starting transfers between devices: 10.7 us -> 11.7 us
  Pallas kernels: 3.37 us -> 4.28 us
    ppermute x7, waiting for transfers between devices: 4.43 us -> 1.54 us  [swap(): return lax.ppermute(x, 'row', [(r, r ^ mask) for r in range(n_row)])]
    ppermute x7, starting transfers between devices: 10.7 us -> 11.6 us  [swap(): return lax.ppermute(x, 'row', [(r, r ^ mask) for r in range(n_row)])]
    pallas_call x1 -> x2, Pallas kernels: 1.59 us -> 2.51 us  [the longest x1 1.53 us: scores(): pl.pallas_call(functools.partial(late_kernel, masks, blocks, qdev), out_s...]
  transfers between devices with their start and end apart: 8 -> 8, of which waited for: 4 -> 3; matrix products, arithmetic and copies ran while one was open for 0% -> 0% of each run, Pallas kernels for 0% -> 5%
where the time goes in v7:
time: 19.5 us; the launch traced here: 19.4 us
  starting transfers between devices  11.7 us (60%)
  Pallas kernels  4.28 us (22%)
  waiting for transfers between devices  2.72 us (14%)
  other arithmetic  0.68 us (3%)
    ppermute x7, starting transfers between devices, swap(): return lax.ppermute(x, 'row', [(r, r ^ mask) for r in range(n_row)])  11.6 us
    pallas_call x1, Pallas kernels, precondition(): pl.pallas_call(precondition_kernel, out_shape=(jax.ShapeDtypeStruct((coun...  1.78 us
    ppermute x7, waiting for transfers between devices, swap(): return lax.ppermute(x, 'row', [(r, r ^ mask) for r in range(n_row)])  1.54 us
    pallas_call x1, Pallas kernels, scores(): pl.pallas_call(functools.partial(late_kernel, masks, blocks, qdev), out_s...  1.53 us
    ppermute x1, waiting for transfers between devices, body(): got = lax.ppermute(other, 'layer', [(0, 1), (1, 0)])  1.18 us
    pallas_call x1, Pallas kernels, scores(): pl.pallas_call(early_kernel, out_shape=(jax.ShapeDtypeStruct((early * SLO...  0.98 us
    transpose x1, other arithmetic, body(): return total.reshape(blocks, -1, rows).transpose(0, 2, 1)  0.6 us
  transfers between devices with their start and end apart: 8, of which 3 were waited for; matrix products, arithmetic and copies ran while one was open for 0% of the time, Pallas kernels for 5%

profile of v7, /device:TPU:0, one launch (start us, length us, event | category | flops | bytes accessed | tf_op | source)
XLA Modules:
  0.0 19.4 jit_solution(17699196417376591906)
XLA Ops:
  0.0 1.8 %precondition.1 = (bf16[24,1024]{1,0:T(8,128)(2,1)S(1)}, s32[1,256]{1,0:T(1,128)S(1)}, bf16[256,4096]{1,0:T(8,128)(2,1)S(1)}) custom-call(s32[3]{0:T(128)} %order_hbm.1, bf16[3,2,4096]{2,1,0:T(2,128)(2,1)} %bitcast.9, f32[1,64,64]{2,1,0:T(8,128)} %out_basis_hbm.1, f32[1,64,64]{2,1,0:T(8,128)} %in_basis_hbm.1, f32[1,4096]{1,0:T(1,128)} %eig_hbm.1, ...), custom_call_target="tpu_custom_call" | custom-call | tf_op jit(solution)/shard_map/precondition/pallas_call | solution.py:108
  1.8 5.1 %collective-permute-start.2 = (bf16[24,1024]{1,0:T(8,128)(2,1)S(1)}, bf16[24,1024]{1,0:T(8,128)(2,1)S(1)}, u32[]{:S(2)}, u32[]{:S(2)}) collective-permute-start(bf16[24,1024]{1,0:T(8,128)(2,1)S(1)} %get-tuple-element.14.refs_0_), channel_id=1, source_target_pairs={{0,12},{2,14},{4,8},{6,10},{8,4},{10,6},{12,0},{14,2},{1,13},{3,15... | collective-permute-start | bytes 147464 | tf_op jit(solution)/shard_map/ppermute | solution.py:236
  6.9 0.0 collective-permute-start.3
  6.9 0.6 %collective-permute-start = (bf16[24,1024]{1,0:T(8,128)(2,1)S(1)}, bf16[24,1024]{1,0:T(8,128)(2,1)S(1)}, u32[]{:S(2)}, u32[]{:S(2)}) collective-permute-start(bf16[24,1024]{1,0:T(8,128)(2,1)S(1)} %get-tuple-element.14.refs_0_), channel_id=1, source_target_pairs={{0,4},{2,6},{4,0},{6,2},{8,12},{10,14},{12,8},{14,10},{1,5},{3,7},... | collective-permute-start | bytes 147464 | tf_op jit(solution)/shard_map/ppermute | solution.py:236
  7.5 1.6 %collective-permute-start.1 = (bf16[24,1024]{1,0:T(8,128)(2,1)S(1)}, bf16[24,1024]{1,0:T(8,128)(2,1)S(1)}, u32[]{:S(2)}, u32[]{:S(2)}) collective-permute-start(bf16[24,1024]{1,0:T(8,128)(2,1)S(1)} %get-tuple-element.14.refs_0_), channel_id=1, source_target_pairs={{0,2},{2,0},{4,6},{6,4},{8,10},{10,8},{12,14},{14,12},{1,3},{3,1},... | collective-permute-start | bytes 147464 | tf_op jit(solution)/shard_map/ppermute | solution.py:236
  9.2 1.2 %collective-permute-start.4 = (bf16[24,1024]{1,0:T(8,128)(2,1)S(1)}, bf16[24,1024]{1,0:T(8,128)(2,1)S(1)}, u32[]{:S(2)}, u32[]{:S(2)}) collective-permute-start(bf16[24,1024]{1,0:T(8,128)(2,1)S(1)} %get-tuple-element.14.refs_0_), channel_id=1, source_target_pairs={{0,6},{2,4},{4,2},{6,0},{8,14},{10,12},{12,10},{14,8},{1,7},{3,5},... | collective-permute-start | bytes 147464 | tf_op jit(solution)/shard_map/ppermute | solution.py:236
  10.4 0.0 collective-permute-done.2.refs_3_
  10.4 1.5 %collective-permute-start.5 = (bf16[24,1024]{1,0:T(8,128)(2,1)S(1)}, bf16[24,1024]{1,0:T(8,128)(2,1)S(1)}, u32[]{:S(2)}, u32[]{:S(2)}) collective-permute-start(bf16[24,1024]{1,0:T(8,128)(2,1)S(1)} %collective-permute-done.2.refs_3_), channel_id=1, source_target_pairs={{0,2},{2,0},{4,6},{6,4},{8,10},{10,8},{12,14},{14,12},{1,3},{3,1},... | collective-permute-start | bytes 147464 | tf_op jit(solution)/shard_map/ppermute | solution.py:236
  11.9 0.0 collective-permute-done.3.refs_4_
  11.9 1.5 %collective-permute-start.6 = (bf16[24,1024]{1,0:T(8,128)(2,1)S(1)}, bf16[24,1024]{1,0:T(8,128)(2,1)S(1)}, u32[]{:S(2)}, u32[]{:S(2)}) collective-permute-start(bf16[24,1024]{1,0:T(8,128)(2,1)S(1)} %collective-permute-done.3.refs_4_), channel_id=1, source_target_pairs={{0,2},{2,0},{4,6},{6,4},{8,10},{10,8},{12,14},{14,12},{1,3},{3,1},... | collective-permute-start | bytes 147464 | tf_op jit(solution)/shard_map/ppermute | solution.py:236
  13.4 0.1 pad_add_fusion.where_ref
  13.5 0.0 collective-permute-done.refs_1_
  13.5 0.0 collective-permute-done.1.refs_2_
  13.5 1.0 %scores_early.1 = (f32[40,256]{1,0:T(8,128)S(1)}, bf16[256,256]{1,0:T(8,128)(2,1)S(1)}) custom-call(bf16[256,4096]{1,0:T(8,128)(2,1)S(1)} %get-tuple-element.12.train_ref, s32[1,256]{1,0:T(1,128)S(1)} %get-tuple-element.13.ids_ref, bf16[24,1024]{1,0:T(8,128)(2,1)S(1)} %get-tuple-element.14.refs_0_, bf16[24,1024]{1,0:T(8,128)(2,1)S(1)} %collective-permute-done.refs_1_, ...), custom_call_target="tpu_custom_call" | custom-call | flops 83886080 | bytes 2342912 | tf_op jit(solution)/shard_map/scores_early/pallas_call | solution.py:207
  14.4 0.0 collective-permute-done.4.refs_0_
  14.5 0.6 %collective-permute-done.5.refs_1_ = bf16[24,1024]{1,0:T(8,128)(2,1)S(1)} collective-permute-done((bf16[24,1024]{1,0:T(8,128)(2,1)S(1)}, bf16[24,1024]{1,0:T(8,128)(2,1)S(1)}, u32[]{:S(2)}, u32[]{:S(2)}) %collective-permute-start.5) | collective-permute-done | bytes 49184 | tf_op jit(solution)/shard_map/ppermute | solution.py:236
  15.1 0.9 %collective-permute-done.6.refs_2_ = bf16[24,1024]{1,0:T(8,128)(2,1)S(1)} collective-permute-done((bf16[24,1024]{1,0:T(8,128)(2,1)S(1)}, bf16[24,1024]{1,0:T(8,128)(2,1)S(1)}, u32[]{:S(2)}, u32[]{:S(2)}) %collective-permute-start.6) | collective-permute-done | bytes 49184 | tf_op jit(solution)/shard_map/ppermute | solution.py:236
  16.0 1.5 %scores_late.1 = (f32[24,256]{1,0:T(8,128)S(1)}, f32[24,256]{1,0:T(8,128)S(1)}) custom-call(s32[2]{0:T(128)S(1)} %pad_add_fusion.where_ref, bf16[256,4096]{1,0:T(8,128)(2,1)S(1)} %get-tuple-element.12.train_ref, bf16[256,256]{1,0:T(8,128)(2,1)S(1)} %get-tuple-element.15.place_ref, f32[40,256]{1,0:T(8,128)S(1)} %get-tuple-element.16.early_ref, ...), custom_call_target="tpu_custom_call" | custom-call | flops 50331648 | bytes 2244608 | tf_op jit(solution)/shard_map/scores_late/pallas_call | solution.py:222
  17.5 0.1 collective-permute-start.7
  17.6 1.2 %collective-permute-done.7 = f32[24,256]{1,0:T(8,128)S(1)} collective-permute-done((f32[24,256]{1,0:T(8,128)S(1)}, f32[24,256]{1,0:T(8,128)S(1)}, u32[]{:S(2)}, u32[]{:S(2)}) %collective-permute-start.7) | collective-permute-done | bytes 24608 | tf_op jit(solution)/shard_map/ppermute | solution.py:259
  18.8 0.6 %fusion = bf16[3,256,8]{1,2,0:T(8,128)(2,1)} fusion(f32[24,256]{1,0:T(8,128)S(1)} %get-tuple-element.17, f32[24,256]{1,0:T(8,128)S(1)} %collective-permute-done.7), kind=kLoop, calls=%fused_computation.1 | loop fusion | flops 12288 | bytes 61440 | tf_op jit(solution)/shard_map/transpose | solution.py:261
Async XLA Ops:
  1.8 8.6 %collective-permute-start.2 = (bf16[24,1024]{1,0:T(8,128)(2,1)S(1)}, bf16[24,1024]{1,0:T(8,128)(2,1)S(1)}, u32[]{:S(2)}, u32[]{:S(2)}) collective-permute-start(bf16[24,1024]{1,0:T(8,128)(2,1)S(1)} %get-tuple-element.14.refs_0_), channel_id=1, source_target_pairs={{0,12},{2,14},{4,8},{6,10},{8,4},{10,6},{12,0},{14,2},{1,13},{3,15... | collective-permute-start | bytes 147464 | tf_op jit(solution)/shard_map/ppermute | solution.py:236
  6.9 5.0 %collective-permute-start.3 = (bf16[24,1024]{1,0:T(8,128)(2,1)S(1)}, bf16[24,1024]{1,0:T(8,128)(2,1)S(1)}, u32[]{:S(2)}, u32[]{:S(2)}) collective-permute-start(bf16[24,1024]{1,0:T(8,128)(2,1)S(1)} %get-tuple-element.14.refs_0_), channel_id=1, source_target_pairs={{0,8},{2,10},{4,12},{6,14},{8,0},{10,2},{12,4},{14,6},{1,9},{3,11}... | collective-permute-start | bytes 147464 | tf_op jit(solution)/shard_map/ppermute | solution.py:236
  6.9 6.6 %collective-permute-start = (bf16[24,1024]{1,0:T(8,128)(2,1)S(1)}, bf16[24,1024]{1,0:T(8,128)(2,1)S(1)}, u32[]{:S(2)}, u32[]{:S(2)}) collective-permute-start(bf16[24,1024]{1,0:T(8,128)(2,1)S(1)} %get-tuple-element.14.refs_0_), channel_id=1, source_target_pairs={{0,4},{2,6},{4,0},{6,2},{8,12},{10,14},{12,8},{14,10},{1,5},{3,7},... | collective-permute-start | bytes 147464 | tf_op jit(solution)/shard_map/ppermute | solution.py:236
  7.5 5.9 %collective-permute-start.1 = (bf16[24,1024]{1,0:T(8,128)(2,1)S(1)}, bf16[24,1024]{1,0:T(8,128)(2,1)S(1)}, u32[]{:S(2)}, u32[]{:S(2)}) collective-permute-start(bf16[24,1024]{1,0:T(8,128)(2,1)S(1)} %get-tuple-element.14.refs_0_), channel_id=1, source_target_pairs={{0,2},{2,0},{4,6},{6,4},{8,10},{10,8},{12,14},{14,12},{1,3},{3,1},... | collective-permute-start | bytes 147464 | tf_op jit(solution)/shard_map/ppermute | solution.py:236
  9.2 5.3 %collective-permute-start.4 = (bf16[24,1024]{1,0:T(8,128)(2,1)S(1)}, bf16[24,1024]{1,0:T(8,128)(2,1)S(1)}, u32[]{:S(2)}, u32[]{:S(2)}) collective-permute-start(bf16[24,1024]{1,0:T(8,128)(2,1)S(1)} %get-tuple-element.14.refs_0_), channel_id=1, source_target_pairs={{0,6},{2,4},{4,2},{6,0},{8,14},{10,12},{12,10},{14,8},{1,7},{3,5},... | collective-permute-start | bytes 147464 | tf_op jit(solution)/shard_map/ppermute | solution.py:236
  10.4 4.7 %collective-permute-start.5 = (bf16[24,1024]{1,0:T(8,128)(2,1)S(1)}, bf16[24,1024]{1,0:T(8,128)(2,1)S(1)}, u32[]{:S(2)}, u32[]{:S(2)}) collective-permute-start(bf16[24,1024]{1,0:T(8,128)(2,1)S(1)} %collective-permute-done.2.refs_3_), channel_id=1, source_target_pairs={{0,2},{2,0},{4,6},{6,4},{8,10},{10,8},{12,14},{14,12},{1,3},{3,1},... | collective-permute-start | bytes 147464 | tf_op jit(solution)/shard_map/ppermute | solution.py:236
  11.9 4.1 %collective-permute-start.6 = (bf16[24,1024]{1,0:T(8,128)(2,1)S(1)}, bf16[24,1024]{1,0:T(8,128)(2,1)S(1)}, u32[]{:S(2)}, u32[]{:S(2)}) collective-permute-start(bf16[24,1024]{1,0:T(8,128)(2,1)S(1)} %collective-permute-done.3.refs_4_), channel_id=1, source_target_pairs={{0,2},{2,0},{4,6},{6,4},{8,10},{10,8},{12,14},{14,12},{1,3},{3,1},... | collective-permute-start | bytes 147464 | tf_op jit(solution)/shard_map/ppermute | solution.py:236
  17.5 1.3 %collective-permute-start.7 = (f32[24,256]{1,0:T(8,128)S(1)}, f32[24,256]{1,0:T(8,128)S(1)}, u32[]{:S(2)}, u32[]{:S(2)}) collective-permute-start(f32[24,256]{1,0:T(8,128)S(1)} %get-tuple-element.18), channel_id=1, source_target_pairs={{0,1},{1,0},{2,3},{3,2},{4,5},{5,4},{6,7},{7,6},{8,9},{9,8},{10,11... | collective-permute-start | bytes 73736 | tf_op jit(solution)/shard_map/ppermute | solution.py:259

commit v8 on v7

--- a/solution.py
+++ b/solution.py
@@ -10,7 +10,6 @@
 DAMPING = 0.01
 LANES = 128
 SEGMENTS = 4
-SLOT = 8
 F32, BF16 = jnp.float32, jnp.bfloat16
 NT = (((1,), (1,)), ((), ()))
 
@@ -140,17 +139,26 @@
     return hi, mid, (rest - mid.astype(F32)).astype(BF16)
 
 
-def placed_terms(parts, train_ref, place, flat_scr):
+def slot_of(where_ref, n_row, mask):
+    source, per = where_ref[0] ^ mask, n_row // 2
+    return jnp.where(source // per == where_ref[1], 0, per) + source % per
+
+
+def placed_terms(where_ref, masks, parts, train_ref, place, flat_scr):
     lines, seg = parts[0].shape
+    n_row = len(masks)
     per_seg = seg // LANES
-    for b, part in enumerate(parts):
-        flat = part[...].astype(F32)
+    for b, mask in enumerate(masks):
+        at = pl.ds(pl.multiple_of(slot_of(where_ref, n_row, mask) * lines, lines), lines)
+        flat = parts[b][...].astype(F32) if b < len(parts) else jnp.zeros((lines, seg), F32)
         for c in range(per_seg):
-            flat_scr[b, c, :lines, :] = flat[:, c * LANES:(c + 1) * LANES]
+            flat_scr[c, at, :] = flat[:, c * LANES:(c + 1) * LANES]
     terms = None
     for j in range(SEGMENTS):
         queries = jnp.concatenate([
-            jnp.concatenate([flat_scr[b, c, pl.ds(j, SLOT, stride=SEGMENTS), :] for b in range(len(parts))], axis=0)
+            jnp.concatenate(
+                [flat_scr[c, pl.ds(t + j, n_row, stride=lines), :] for t in range(0, lines, SEGMENTS)], axis=0
+            )
             for c in range(per_seg)
         ], axis=1)
         term = mm_nt(queries.astype(BF16), train_ref[:, j * seg:(j + 1) * seg])
@@ -159,74 +167,68 @@
     return mm(a, place) + mm(b, place) + mm(c, place)
 
 
-def early_kernel(train_ref, ids_ref, *refs):
+def early_kernel(masks, where_ref, train_ref, ids_ref, *refs):
     parts, (terms_ref, place_ref, flat_scr) = refs[:-3], refs[-3:]
     rows = train_ref.shape[0]
     here = lax.broadcasted_iota(jnp.int32, (rows, rows), 0)
     place = (here == ids_ref[...]).astype(BF16)
     place_ref[...] = place
-    terms_ref[...] = placed_terms(parts, train_ref, place, flat_scr)
+    terms_ref[...] = placed_terms(where_ref, masks, parts, train_ref, place, flat_scr)
 
 
 def late_kernel(masks, blocks, qdev, where_ref, train_ref, place_ref, early_ref, *refs):
     parts, (mine_ref, other_ref, flat_scr, out_scr) = refs[:-4], refs[-4:]
     n_row = len(masks)
-    ordered = jnp.concatenate(
-        [early_ref[...], placed_terms(parts, train_ref, place_ref[...], flat_scr)], axis=0
-    )
-    me, core = where_ref[0], where_ref[1]
     per = n_row // 2
-    for b, mask in enumerate(masks):
-        source = me ^ mask
-        which = jnp.where(source // per == core, 0, 1)
-        first = which * (blocks * per) + source % per
-        for j in range(blocks):
-            at = b * SLOT + j * qdev
-            out_scr[first + j * per] = ordered[at:at + qdev]
-    for i in range(blocks * per):
-        mine_ref[i * qdev:(i + 1) * qdev, :] = out_scr[i]
-        other_ref[i * qdev:(i + 1) * qdev, :] = out_scr[blocks * per + i]
+    terms = early_ref[...] + placed_terms(where_ref, masks, parts, train_ref, place_ref[...], flat_scr)
+    halves = terms.shape[1] // LANES
+    half_rows = blocks * per * qdev
+    for q in range(blocks * qdev):
+        for which in range(2):
+            first = which * half_rows + (q // qdev) * per * qdev + q % qdev
+            at = q * n_row + which * per
+            for h in range(halves):
+                out_scr[h, pl.ds(first, per, stride=qdev), :] = terms[at:at + per, h * LANES:(h + 1) * LANES]
+    for h in range(halves):
+        mine_ref[:, h * LANES:(h + 1) * LANES] = out_scr[h, :half_rows]
+        other_ref[:, h * LANES:(h + 1) * LANES] = out_scr[h, half_rows:]
 
 
 def scores(masks, early, where, train, row_ids, parts, blocks, qdev):
     rows, width = train.shape
     n_row = len(masks)
     lines, seg = parts[0].shape
+    queries = blocks * n_row * qdev
     vmem = pl.BlockSpec(memory_space=pltpu.VMEM)
-    params = pltpu.CompilerParams(vmem_limit_bytes=(16 if n_row <= 16 else 24) * 2**20)
-
-    def flat(count):
-        return pltpu.VMEM((count, seg // LANES, SLOT * SEGMENTS, LANES), F32)
-
-    def cost(count):
-        return pl.CostEstimate(
-            flops=2 * count * SLOT * rows * width, bytes_accessed=2 * (rows * width + count * lines * seg),
-            transcendentals=0,
-        )
-
+    smem = pl.BlockSpec(memory_space=pltpu.SMEM)
+    params = pltpu.CompilerParams(vmem_limit_bytes=(16 if n_row <= 16 else 40) * 2**20)
+    cost = pl.CostEstimate(
+        flops=2 * queries * rows * width, bytes_accessed=2 * (rows * width + n_row * lines * seg // 2),
+        transcendentals=0,
+    )
+    flat_scr = pltpu.VMEM((seg // LANES, n_row * lines, LANES), F32)
     terms, place = pl.pallas_call(
-        early_kernel,
+        functools.partial(early_kernel, masks),
         out_shape=(
-            jax.ShapeDtypeStruct((early * SLOT, rows), F32),
+            jax.ShapeDtypeStruct((queries, rows), F32),
             jax.ShapeDtypeStruct((rows, rows), BF16),
         ),
-        in_specs=[vmem] * (2 + early),
+        in_specs=[smem] + [vmem] * (2 + early),
         out_specs=(vmem, vmem),
-        scratch_shapes=[flat(early)],
+        scratch_shapes=[flat_scr],
         compiler_params=params,
-        cost_estimate=cost(early),
+        cost_estimate=cost,
         name="scores_early",
-    )(train, row_ids, *parts[:early])
-    late = n_row - early
-    out = jax.ShapeDtypeStruct((blocks * n_row * qdev // 2, rows), F32)
+    )(where, train, row_ids, *parts[:early])
+    out = jax.ShapeDtypeStruct((queries // 2, rows), F32)
     return pl.pallas_call(
-        functools.partial(late_kernel, masks, blocks, qdev),
+        functools.partial(late_kernel, masks[early:] + masks[:early], blocks, qdev),
         out_shape=(out, out),
-        in_specs=[pl.BlockSpec(memory_space=pltpu.SMEM)] + [vmem] * (3 + late),
+        in_specs=[smem] + [vmem] * (3 + n_row - early),
         out_specs=(vmem, vmem),
-        scratch_shapes=[flat(late), pltpu.VMEM((blocks * n_row, qdev, rows), F32)],
+        scratch_shapes=[flat_scr, pltpu.VMEM((rows // LANES, queries, LANES), F32)],
         compiler_params=params,
-        cost_estimate=cost(late),
+        cost_estimate=cost,
         name="scores_late",
     )(where, train, place, terms, *parts[early:])
 

time: 19.5 us -> 19.6 us (level)
  Pallas kernels: 4.28 us -> 4.85 us
  waiting for transfers between devices: 2.72 us -> 2.18 us
    pallas_call x2, Pallas kernels: 2.51 us -> 3.08 us  [the longest x1 1.55 us: scores(): pl.pallas_call(functools.partial(late_kernel, masks[early:] + masks[:earl...]
    ppermute x7, waiting for transfers between devices: 1.54 us -> 0.99 us  [swap(): return lax.ppermute(x, 'row', [(r, r ^ mask) for r in range(n_row)])]
  transfers between devices with their start and end apart: 8 -> 8, of which waited for: 3 -> 3; matrix products, arithmetic and copies ran while one was open for 0% -> 0% of each run, Pallas kernels for 5% -> 8%
where the time goes in v8:
time: 19.6 us; the launch traced here: 19.4 us
  starting transfers between devices  11.7 us (60%)
  Pallas kernels  4.85 us (25%)
  waiting for transfers between devices  2.18 us (11%)
  other arithmetic  0.68 us (3%)
    ppermute x7, starting transfers between devices, swap(): return lax.ppermute(x, 'row', [(r, r ^ mask) for r in range(n_row)])  11.6 us
    pallas_call x1, Pallas kernels, precondition(): pl.pallas_call(precondition_kernel, out_shape=(jax.ShapeDtypeStruct((coun...  1.78 us
    pallas_call x1, Pallas kernels, scores(): pl.pallas_call(functools.partial(late_kernel, masks[early:] + masks[:earl...  1.55 us
    pallas_call x1, Pallas kernels, scores(): pl.pallas_call(functools.partial(early_kernel, masks), out_shape=(jax.Sha...  1.53 us
    ppermute x1, waiting for transfers between devices, body(): got = lax.ppermute(other, 'layer', [(0, 1), (1, 0)])  1.18 us
    ppermute x7, waiting for transfers between devices, swap(): return lax.ppermute(x, 'row', [(r, r ^ mask) for r in range(n_row)])  0.99 us
    transpose x1, other arithmetic, body(): return total.reshape(blocks, -1, rows).transpose(0, 2, 1)  0.6 us
  transfers between devices with their start and end apart: 8, of which 3 were waited for; matrix products, arithmetic and copies ran while one was open for 0% of the time, Pallas kernels for 8%

profile of v8, /device:TPU:0, one launch (start us, length us, event | category | flops | bytes accessed | tf_op | source)
XLA Modules:
  0.0 19.4 jit_solution(3022099507120737023)
XLA Ops:
  0.0 1.8 %precondition.1 = (bf16[24,1024]{1,0:T(8,128)(2,1)S(1)}, s32[1,256]{1,0:T(1,128)S(1)}, bf16[256,4096]{1,0:T(8,128)(2,1)S(1)}) custom-call(s32[3]{0:T(128)} %order_hbm.1, bf16[3,2,4096]{2,1,0:T(2,128)(2,1)} %bitcast.9, f32[1,64,64]{2,1,0:T(8,128)} %out_basis_hbm.1, f32[1,64,64]{2,1,0:T(8,128)} %in_basis_hbm.1, f32[1,4096]{1,0:T(1,128)} %eig_hbm.1, ...), custom_call_target="tpu_custom_call" | custom-call | tf_op jit(solution)/shard_map/precondition/pallas_call | solution.py:107
  1.8 5.1 %collective-permute-start.2 = (bf16[24,1024]{1,0:T(8,128)(2,1)S(1)}, bf16[24,1024]{1,0:T(8,128)(2,1)S(1)}, u32[]{:S(2)}, u32[]{:S(2)}) collective-permute-start(bf16[24,1024]{1,0:T(8,128)(2,1)S(1)} %get-tuple-element.14.refs_0_), channel_id=1, source_target_pairs={{0,12},{2,14},{4,8},{6,10},{8,4},{10,6},{12,0},{14,2},{1,13},{3,15... | collective-permute-start | bytes 147464 | tf_op jit(solution)/shard_map/ppermute | solution.py:238
  6.9 0.0 collective-permute-start.3
  6.9 0.6 %collective-permute-start = (bf16[24,1024]{1,0:T(8,128)(2,1)S(1)}, bf16[24,1024]{1,0:T(8,128)(2,1)S(1)}, u32[]{:S(2)}, u32[]{:S(2)}) collective-permute-start(bf16[24,1024]{1,0:T(8,128)(2,1)S(1)} %get-tuple-element.14.refs_0_), channel_id=1, source_target_pairs={{0,4},{2,6},{4,0},{6,2},{8,12},{10,14},{12,8},{14,10},{1,5},{3,7},... | collective-permute-start | bytes 147464 | tf_op jit(solution)/shard_map/ppermute | solution.py:238
  7.5 1.6 %collective-permute-start.1 = (bf16[24,1024]{1,0:T(8,128)(2,1)S(1)}, bf16[24,1024]{1,0:T(8,128)(2,1)S(1)}, u32[]{:S(2)}, u32[]{:S(2)}) collective-permute-start(bf16[24,1024]{1,0:T(8,128)(2,1)S(1)} %get-tuple-element.14.refs_0_), channel_id=1, source_target_pairs={{0,2},{2,0},{4,6},{6,4},{8,10},{10,8},{12,14},{14,12},{1,3},{3,1},... | collective-permute-start | bytes 147464 | tf_op jit(solution)/shard_map/ppermute | solution.py:238
  9.2 1.2 %collective-permute-start.4 = (bf16[24,1024]{1,0:T(8,128)(2,1)S(1)}, bf16[24,1024]{1,0:T(8,128)(2,1)S(1)}, u32[]{:S(2)}, u32[]{:S(2)}) collective-permute-start(bf16[24,1024]{1,0:T(8,128)(2,1)S(1)} %get-tuple-element.14.refs_0_), channel_id=1, source_target_pairs={{0,6},{2,4},{4,2},{6,0},{8,14},{10,12},{12,10},{14,8},{1,7},{3,5},... | collective-permute-start | bytes 147464 | tf_op jit(solution)/shard_map/ppermute | solution.py:238
  10.4 0.0 collective-permute-done.2.refs_3_
  10.4 1.5 %collective-permute-start.5 = (bf16[24,1024]{1,0:T(8,128)(2,1)S(1)}, bf16[24,1024]{1,0:T(8,128)(2,1)S(1)}, u32[]{:S(2)}, u32[]{:S(2)}) collective-permute-start(bf16[24,1024]{1,0:T(8,128)(2,1)S(1)} %collective-permute-done.2.refs_3_), channel_id=1, source_target_pairs={{0,2},{2,0},{4,6},{6,4},{8,10},{10,8},{12,14},{14,12},{1,3},{3,1},... | collective-permute-start | bytes 147464 | tf_op jit(solution)/shard_map/ppermute | solution.py:238
  11.9 0.0 collective-permute-done.3.refs_4_
  11.9 1.5 %collective-permute-start.6 = (bf16[24,1024]{1,0:T(8,128)(2,1)S(1)}, bf16[24,1024]{1,0:T(8,128)(2,1)S(1)}, u32[]{:S(2)}, u32[]{:S(2)}) collective-permute-start(bf16[24,1024]{1,0:T(8,128)(2,1)S(1)} %collective-permute-done.3.refs_4_), channel_id=1, source_target_pairs={{0,2},{2,0},{4,6},{6,4},{8,10},{10,8},{12,14},{14,12},{1,3},{3,1},... | collective-permute-start | bytes 147464 | tf_op jit(solution)/shard_map/ppermute | solution.py:238
  13.4 0.1 pad_add_fusion.where_ref
  13.5 0.0 collective-permute-done.refs_1_
  13.5 0.0 collective-permute-done.1.refs_2_
  13.5 1.5 %scores_early.1 = (f32[48,256]{1,0:T(8,128)S(1)}, bf16[256,256]{1,0:T(8,128)(2,1)S(1)}) custom-call(s32[2]{0:T(128)S(1)} %pad_add_fusion.where_ref, bf16[256,4096]{1,0:T(8,128)(2,1)S(1)} %get-tuple-element.12.train_ref, s32[1,256]{1,0:T(1,128)S(1)} %get-tuple-element.13.ids_ref, bf16[24,1024]{1,0:T(8,128)(2,1)S(1)} %get-tuple-element.14.refs_0_, ...), custom_call_target="tpu_custom_call" | custom-call | flops 100663296 | bytes 2293760 | tf_op jit(solution)/shard_map/scores_early/pallas_call | solution.py:210
  15.0 0.0 collective-permute-done.4.refs_0_
  15.0 0.1 collective-permute-done.5.refs_1_
  15.1 0.9 %collective-permute-done.6.refs_2_ = bf16[24,1024]{1,0:T(8,128)(2,1)S(1)} collective-permute-done((bf16[24,1024]{1,0:T(8,128)(2,1)S(1)}, bf16[24,1024]{1,0:T(8,128)(2,1)S(1)}, u32[]{:S(2)}, u32[]{:S(2)}) %collective-permute-start.6) | collective-permute-done | bytes 49184 | tf_op jit(solution)/shard_map/ppermute | solution.py:238
  16.0 1.6 %scores_late.1 = (f32[24,256]{1,0:T(8,128)S(1)}, f32[24,256]{1,0:T(8,128)S(1)}) custom-call(s32[2]{0:T(128)S(1)} %pad_add_fusion.where_ref, bf16[256,4096]{1,0:T(8,128)(2,1)S(1)} %get-tuple-element.12.train_ref, bf16[256,256]{1,0:T(8,128)(2,1)S(1)} %get-tuple-element.15.place_ref, f32[48,256]{1,0:T(8,128)S(1)} %get-tuple-element.16.early_ref, ...), custom_call_target="tpu_custom_call" | custom-call | flops 100663296 | bytes 2293760 | tf_op jit(solution)/shard_map/scores_late/pallas_call | solution.py:224
  17.5 0.1 collective-permute-start.7
  17.6 1.2 %collective-permute-done.7 = f32[24,256]{1,0:T(8,128)S(1)} collective-permute-done((f32[24,256]{1,0:T(8,128)S(1)}, f32[24,256]{1,0:T(8,128)S(1)}, u32[]{:S(2)}, u32[]{:S(2)}) %collective-permute-start.7) | collective-permute-done | bytes 24608 | tf_op jit(solution)/shard_map/ppermute | solution.py:261
  18.8 0.6 %fusion = bf16[3,256,8]{1,2,0:T(8,128)(2,1)} fusion(f32[24,256]{1,0:T(8,128)S(1)} %get-tuple-element.17, f32[24,256]{1,0:T(8,128)S(1)} %collective-permute-done.7), kind=kLoop, calls=%fused_computation.1 | loop fusion | flops 12288 | bytes 61440 | tf_op jit(solution)/shard_map/transpose | solution.py:263
Async XLA Ops:
  1.8 8.6 %collective-permute-start.2 = (bf16[24,1024]{1,0:T(8,128)(2,1)S(1)}, bf16[24,1024]{1,0:T(8,128)(2,1)S(1)}, u32[]{:S(2)}, u32[]{:S(2)}) collective-permute-start(bf16[24,1024]{1,0:T(8,128)(2,1)S(1)} %get-tuple-element.14.refs_0_), channel_id=1, source_target_pairs={{0,12},{2,14},{4,8},{6,10},{8,4},{10,6},{12,0},{14,2},{1,13},{3,15... | collective-permute-start | bytes 147464 | tf_op jit(solution)/shard_map/ppermute | solution.py:238
  6.9 5.0 %collective-permute-start.3 = (bf16[24,1024]{1,0:T(8,128)(2,1)S(1)}, bf16[24,1024]{1,0:T(8,128)(2,1)S(1)}, u32[]{:S(2)}, u32[]{:S(2)}) collective-permute-start(bf16[24,1024]{1,0:T(8,128)(2,1)S(1)} %get-tuple-element.14.refs_0_), channel_id=1, source_target_pairs={{0,8},{2,10},{4,12},{6,14},{8,0},{10,2},{12,4},{14,6},{1,9},{3,11}... | collective-permute-start | bytes 147464 | tf_op jit(solution)/shard_map/ppermute | solution.py:238
  6.9 6.6 %collective-permute-start = (bf16[24,1024]{1,0:T(8,128)(2,1)S(1)}, bf16[24,1024]{1,0:T(8,128)(2,1)S(1)}, u32[]{:S(2)}, u32[]{:S(2)}) collective-permute-start(bf16[24,1024]{1,0:T(8,128)(2,1)S(1)} %get-tuple-element.14.refs_0_), channel_id=1, source_target_pairs={{0,4},{2,6},{4,0},{6,2},{8,12},{10,14},{12,8},{14,10},{1,5},{3,7},... | collective-permute-start | bytes 147464 | tf_op jit(solution)/shard_map/ppermute | solution.py:238
  7.5 5.9 %collective-permute-start.1 = (bf16[24,1024]{1,0:T(8,128)(2,1)S(1)}, bf16[24,1024]{1,0:T(8,128)(2,1)S(1)}, u32[]{:S(2)}, u32[]{:S(2)}) collective-permute-start(bf16[24,1024]{1,0:T(8,128)(2,1)S(1)} %get-tuple-element.14.refs_0_), channel_id=1, source_target_pairs={{0,2},{2,0},{4,6},{6,4},{8,10},{10,8},{12,14},{14,12},{1,3},{3,1},... | collective-permute-start | bytes 147464 | tf_op jit(solution)/shard_map/ppermute | solution.py:238
  9.2 5.8 %collective-permute-start.4 = (bf16[24,1024]{1,0:T(8,128)(2,1)S(1)}, bf16[24,1024]{1,0:T(8,128)(2,1)S(1)}, u32[]{:S(2)}, u32[]{:S(2)}) collective-permute-start(bf16[24,1024]{1,0:T(8,128)(2,1)S(1)} %get-tuple-element.14.refs_0_), channel_id=1, source_target_pairs={{0,6},{2,4},{4,2},{6,0},{8,14},{10,12},{12,10},{14,8},{1,7},{3,5},... | collective-permute-start | bytes 147464 | tf_op jit(solution)/shard_map/ppermute | solution.py:238
  10.4 4.7 %collective-permute-start.5 = (bf16[24,1024]{1,0:T(8,128)(2,1)S(1)}, bf16[24,1024]{1,0:T(8,128)(2,1)S(1)}, u32[]{:S(2)}, u32[]{:S(2)}) collective-permute-start(bf16[24,1024]{1,0:T(8,128)(2,1)S(1)} %collective-permute-done.2.refs_3_), channel_id=1, source_target_pairs={{0,2},{2,0},{4,6},{6,4},{8,10},{10,8},{12,14},{14,12},{1,3},{3,1},... | collective-permute-start | bytes 147464 | tf_op jit(solution)/shard_map/ppermute | solution.py:238
  11.9 4.1 %collective-permute-start.6 = (bf16[24,1024]{1,0:T(8,128)(2,1)S(1)}, bf16[24,1024]{1,0:T(8,128)(2,1)S(1)}, u32[]{:S(2)}, u32[]{:S(2)}) collective-permute-start(bf16[24,1024]{1,0:T(8,128)(2,1)S(1)} %collective-permute-done.3.refs_4_), channel_id=1, source_target_pairs={{0,2},{2,0},{4,6},{6,4},{8,10},{10,8},{12,14},{14,12},{1,3},{3,1},... | collective-permute-start | bytes 147464 | tf_op jit(solution)/shard_map/ppermute | solution.py:238
  17.5 1.3 %collective-permute-start.7 = (f32[24,256]{1,0:T(8,128)S(1)}, f32[24,256]{1,0:T(8,128)S(1)}, u32[]{:S(2)}, u32[]{:S(2)}) collective-permute-start(f32[24,256]{1,0:T(8,128)S(1)} %get-tuple-element.18), channel_id=1, source_target_pairs={{0,1},{1,0},{2,3},{3,2},{4,5},{5,4},{6,7},{7,6},{8,9},{9,8},{10,11... | collective-permute-start | bytes 73736 | tf_op jit(solution)/shard_map/ppermute | solution.py:261

commit v9 on v8

--- a/solution.py
+++ b/solution.py
@@ -139,17 +139,17 @@
     return hi, mid, (rest - mid.astype(F32)).astype(BF16)
 
 
-def slot_of(where_ref, n_row, mask):
-    source, per = where_ref[0] ^ mask, n_row // 2
-    return jnp.where(source // per == where_ref[1], 0, per) + source % per
-
-
-def placed_terms(where_ref, masks, parts, train_ref, place, flat_scr):
+def slot_of(n_row, mask):
+    source, per = lax.axis_index("row") ^ mask, n_row // 2
+    return source ^ (lax.axis_index("layer") * per)
+
+
+def placed_terms(masks, parts, train_ref, place, flat_scr):
     lines, seg = parts[0].shape
     n_row = len(masks)
     per_seg = seg // LANES
     for b, mask in enumerate(masks):
-        at = pl.ds(pl.multiple_of(slot_of(where_ref, n_row, mask) * lines, lines), lines)
+        at = pl.ds(pl.multiple_of(slot_of(n_row, mask) * lines, lines), lines)
         flat = parts[b][...].astype(F32) if b < len(parts) else jnp.zeros((lines, seg), F32)
         for c in range(per_seg):
             flat_scr[c, at, :] = flat[:, c * LANES:(c + 1) * LANES]
@@ -167,20 +167,20 @@
     return mm(a, place) + mm(b, place) + mm(c, place)
 
 
-def early_kernel(masks, where_ref, train_ref, ids_ref, *refs):
+def early_kernel(masks, train_ref, ids_ref, *refs):
     parts, (terms_ref, place_ref, flat_scr) = refs[:-3], refs[-3:]
     rows = train_ref.shape[0]
     here = lax.broadcasted_iota(jnp.int32, (rows, rows), 0)
     place = (here == ids_ref[...]).astype(BF16)
     place_ref[...] = place
-    terms_ref[...] = placed_terms(where_ref, masks, parts, train_ref, place, flat_scr)
-
-
-def late_kernel(masks, blocks, qdev, where_ref, train_ref, place_ref, early_ref, *refs):
+    terms_ref[...] = placed_terms(masks, parts, train_ref, place, flat_scr)
+
+
+def late_kernel(masks, blocks, qdev, train_ref, place_ref, early_ref, *refs):
     parts, (mine_ref, other_ref, flat_scr, out_scr) = refs[:-4], refs[-4:]
     n_row = len(masks)
     per = n_row // 2
-    terms = early_ref[...] + placed_terms(where_ref, masks, parts, train_ref, place_ref[...], flat_scr)
+    terms = early_ref[...] + placed_terms(masks, parts, train_ref, place_ref[...], flat_scr)
     halves = terms.shape[1] // LANES
     half_rows = blocks * per * qdev
     for q in range(blocks * qdev):
@@ -194,13 +194,12 @@
         other_ref[:, h * LANES:(h + 1) * LANES] = out_scr[h, half_rows:]
 
 
-def scores(masks, early, where, train, row_ids, parts, blocks, qdev):
+def scores(masks, early, train, row_ids, parts, blocks, qdev):
     rows, width = train.shape
     n_row = len(masks)
     lines, seg = parts[0].shape
     queries = blocks * n_row * qdev
     vmem = pl.BlockSpec(memory_space=pltpu.VMEM)
-    smem = pl.BlockSpec(memory_space=pltpu.SMEM)
     params = pltpu.CompilerParams(vmem_limit_bytes=(16 if n_row <= 16 else 40) * 2**20)
     cost = pl.CostEstimate(
         flops=2 * queries * rows * width, bytes_accessed=2 * (rows * width + n_row * lines * seg // 2),
@@ -213,24 +212,24 @@
             jax.ShapeDtypeStruct((queries, rows), F32),
             jax.ShapeDtypeStruct((rows, rows), BF16),
         ),
-        in_specs=[smem] + [vmem] * (2 + early),
+        in_specs=[vmem] * (2 + early),
         out_specs=(vmem, vmem),
         scratch_shapes=[flat_scr],
         compiler_params=params,
         cost_estimate=cost,
         name="scores_early",
-    )(where, train, row_ids, *parts[:early])
+    )(train, row_ids, *parts[:early])
     out = jax.ShapeDtypeStruct((queries // 2, rows), F32)
     return pl.pallas_call(
         functools.partial(late_kernel, masks[early:] + masks[:early], blocks, qdev),
         out_shape=(out, out),
-        in_specs=[smem] + [vmem] * (3 + n_row - early),
+        in_specs=[vmem] * (3 + n_row - early),
         out_specs=(vmem, vmem),
         scratch_shapes=[flat_scr, pltpu.VMEM((rows // LANES, queries, LANES), F32)],
         compiler_params=params,
         cost_estimate=cost,
         name="scores_late",
-    )(where, train, place, terms, *parts[early:])
+    )(train, place, terms, *parts[early:])
 
 
 def make_body(n_row):
@@ -254,10 +253,7 @@
             train_grads.reshape(rows, width),
         )
         parts, early = gather(own)
-        where = jnp.stack([lax.axis_index(name) for name in ("row", "layer")]).astype(jnp.int32)
-        mine, other = scores(
-            tuple(parts), early, where, train, row_ids, tuple(parts.values()), blocks, qdev
-        )
+        mine, other = scores(tuple(parts), early, train, row_ids, tuple(parts.values()), blocks, qdev)
         got = lax.ppermute(other, "layer", [(0, 1), (1, 0)])
         total = (mine + got).astype(BF16)
         return total.reshape(blocks, -1, rows).transpose(0, 2, 1)

time: 19.6 us -> 19 us (0.969)
  Pallas kernels: 4.85 us -> 3.77 us
  waiting for transfers between devices: 2.18 us -> 2.78 us
    ppermute x7, waiting for transfers between devices: 0.99 us -> 1.6 us  [swap(): return lax.ppermute(x, 'row', [(r, r ^ mask) for r in range(n_row)])]
    pallas_call x1, Pallas kernels: 1.55 us -> 1.01 us  [scores(): pl.pallas_call(functools.partial(late_kernel, masks[early:] + masks[:earl...]
    pallas_call x1, Pallas kernels: 1.53 us -> 0.99 us  [scores(): pl.pallas_call(functools.partial(early_kernel, masks), out_shape=(jax.Sha...]
  transfers between devices with their start and end apart: 8 -> 8, of which waited for: 3 -> 3; matrix products, arithmetic and copies ran while one was open for 0% -> 0% of each run, Pallas kernels for 8% -> 5%
where the time goes in v9:
time: 19 us; the launch traced here: 18.9 us
  starting transfers between devices  11.7 us (62%)
  Pallas kernels  3.77 us (20%)
  waiting for transfers between devices  2.78 us (15%)
  other arithmetic  0.6 us (3%)
    ppermute x7, starting transfers between devices, swap(): return lax.ppermute(x, 'row', [(r, r ^ mask) for r in range(n_row)])  11.6 us
    pallas_call x1, Pallas kernels, precondition(): pl.pallas_call(precondition_kernel, out_shape=(jax.ShapeDtypeStruct((coun...  1.78 us
    ppermute x7, waiting for transfers between devices, swap(): return lax.ppermute(x, 'row', [(r, r ^ mask) for r in range(n_row)])  1.6 us
    ppermute x1, waiting for transfers between devices, body(): got = lax.ppermute(other, 'layer', [(0, 1), (1, 0)])  1.18 us
    pallas_call x1, Pallas kernels, scores(): pl.pallas_call(functools.partial(late_kernel, masks[early:] + masks[:earl...  1.01 us
    pallas_call x1, Pallas kernels, scores(): pl.pallas_call(functools.partial(early_kernel, masks), out_shape=(jax.Sha...  0.99 us
    transpose x1, other arithmetic, body(): return total.reshape(blocks, -1, rows).transpose(0, 2, 1)  0.6 us
  transfers between devices with their start and end apart: 8, of which 3 were waited for; matrix products, arithmetic and copies ran while one was open for 0% of the time, Pallas kernels for 5%

profile of v9, /device:TPU:0, one launch (start us, length us, event | category | flops | bytes accessed | tf_op | source)
XLA Modules:
  0.0 18.9 jit_solution(17057388477078167042)
XLA Ops:
  0.0 1.8 %precondition.1 = (bf16[24,1024]{1,0:T(8,128)(2,1)S(1)}, s32[1,256]{1,0:T(1,128)S(1)}, bf16[256,4096]{1,0:T(8,128)(2,1)S(1)}) custom-call(s32[3]{0:T(128)} %order_hbm.1, bf16[3,2,4096]{2,1,0:T(2,128)(2,1)} %bitcast.7, f32[1,64,64]{2,1,0:T(8,128)} %out_basis_hbm.1, f32[1,64,64]{2,1,0:T(8,128)} %in_basis_hbm.1, f32[1,4096]{1,0:T(1,128)} %eig_hbm.1, ...), custom_call_target="tpu_custom_call" | custom-call | tf_op jit(solution)/shard_map/precondition/pallas_call | solution.py:107
  1.8 5.1 %collective-permute-start.2 = (bf16[24,1024]{1,0:T(8,128)(2,1)S(1)}, bf16[24,1024]{1,0:T(8,128)(2,1)S(1)}, u32[]{:S(2)}, u32[]{:S(2)}) collective-permute-start(bf16[24,1024]{1,0:T(8,128)(2,1)S(1)} %get-tuple-element.14.refs_0_), channel_id=1, source_target_pairs={{0,12},{2,14},{4,8},{6,10},{8,4},{10,6},{12,0},{14,2},{1,13},{3,15... | collective-permute-start | bytes 147464 | tf_op jit(solution)/shard_map/ppermute | solution.py:237
  6.9 0.0 collective-permute-start.3
  6.9 0.6 %collective-permute-start = (bf16[24,1024]{1,0:T(8,128)(2,1)S(1)}, bf16[24,1024]{1,0:T(8,128)(2,1)S(1)}, u32[]{:S(2)}, u32[]{:S(2)}) collective-permute-start(bf16[24,1024]{1,0:T(8,128)(2,1)S(1)} %get-tuple-element.14.refs_0_), channel_id=1, source_target_pairs={{0,4},{2,6},{4,0},{6,2},{8,12},{10,14},{12,8},{14,10},{1,5},{3,7},... | collective-permute-start | bytes 147464 | tf_op jit(solution)/shard_map/ppermute | solution.py:237
  7.5 1.6 %collective-permute-start.1 = (bf16[24,1024]{1,0:T(8,128)(2,1)S(1)}, bf16[24,1024]{1,0:T(8,128)(2,1)S(1)}, u32[]{:S(2)}, u32[]{:S(2)}) collective-permute-start(bf16[24,1024]{1,0:T(8,128)(2,1)S(1)} %get-tuple-element.14.refs_0_), channel_id=1, source_target_pairs={{0,2},{2,0},{4,6},{6,4},{8,10},{10,8},{12,14},{14,12},{1,3},{3,1},... | collective-permute-start | bytes 147464 | tf_op jit(solution)/shard_map/ppermute | solution.py:237
  9.2 1.2 %collective-permute-start.4 = (bf16[24,1024]{1,0:T(8,128)(2,1)S(1)}, bf16[24,1024]{1,0:T(8,128)(2,1)S(1)}, u32[]{:S(2)}, u32[]{:S(2)}) collective-permute-start(bf16[24,1024]{1,0:T(8,128)(2,1)S(1)} %get-tuple-element.14.refs_0_), channel_id=1, source_target_pairs={{0,6},{2,4},{4,2},{6,0},{8,14},{10,12},{12,10},{14,8},{1,7},{3,5},... | collective-permute-start | bytes 147464 | tf_op jit(solution)/shard_map/ppermute | solution.py:237
  10.4 0.0 collective-permute-done.2.refs_3_
  10.4 1.5 %collective-permute-start.5 = (bf16[24,1024]{1,0:T(8,128)(2,1)S(1)}, bf16[24,1024]{1,0:T(8,128)(2,1)S(1)}, u32[]{:S(2)}, u32[]{:S(2)}) collective-permute-start(bf16[24,1024]{1,0:T(8,128)(2,1)S(1)} %collective-permute-done.2.refs_3_), channel_id=1, source_target_pairs={{0,2},{2,0},{4,6},{6,4},{8,10},{10,8},{12,14},{14,12},{1,3},{3,1},... | collective-permute-start | bytes 147464 | tf_op jit(solution)/shard_map/ppermute | solution.py:237
  11.9 0.0 collective-permute-done.3.refs_4_
  11.9 1.5 %collective-permute-start.6 = (bf16[24,1024]{1,0:T(8,128)(2,1)S(1)}, bf16[24,1024]{1,0:T(8,128)(2,1)S(1)}, u32[]{:S(2)}, u32[]{:S(2)}) collective-permute-start(bf16[24,1024]{1,0:T(8,128)(2,1)S(1)} %collective-permute-done.3.refs_4_), channel_id=1, source_target_pairs={{0,2},{2,0},{4,6},{6,4},{8,10},{10,8},{12,14},{14,12},{1,3},{3,1},... | collective-permute-start | bytes 147464 | tf_op jit(solution)/shard_map/ppermute | solution.py:237
  13.4 0.0 collective-permute-done.refs_1_
  13.4 0.0 collective-permute-done.1.refs_2_
  13.4 1.0 %scores_early.1 = (f32[48,256]{1,0:T(8,128)S(1)}, bf16[256,256]{1,0:T(8,128)(2,1)S(1)}) custom-call(bf16[256,4096]{1,0:T(8,128)(2,1)S(1)} %get-tuple-element.12.train_ref, s32[1,256]{1,0:T(1,128)S(1)} %get-tuple-element.13.ids_ref, bf16[24,1024]{1,0:T(8,128)(2,1)S(1)} %get-tuple-element.14.refs_0_, bf16[24,1024]{1,0:T(8,128)(2,1)S(1)} %collective-permute-done.refs_1_, ...), custom_call_target="tpu_custom_call" | custom-call | flops 100663296 | bytes 2293760 | tf_op jit(solution)/shard_map/scores_early/pallas_call | solution.py:209
  14.4 0.0 collective-permute-done.4.refs_0_
  14.4 0.7 %collective-permute-done.5.refs_1_ = bf16[24,1024]{1,0:T(8,128)(2,1)S(1)} collective-permute-done((bf16[24,1024]{1,0:T(8,128)(2,1)S(1)}, bf16[24,1024]{1,0:T(8,128)(2,1)S(1)}, u32[]{:S(2)}, u32[]{:S(2)}) %collective-permute-start.5) | collective-permute-done | bytes 49184 | tf_op jit(solution)/shard_map/ppermute | solution.py:237
  15.1 0.9 %collective-permute-done.6.refs_2_ = bf16[24,1024]{1,0:T(8,128)(2,1)S(1)} collective-permute-done((bf16[24,1024]{1,0:T(8,128)(2,1)S(1)}, bf16[24,1024]{1,0:T(8,128)(2,1)S(1)}, u32[]{:S(2)}, u32[]{:S(2)}) %collective-permute-start.6) | collective-permute-done | bytes 49184 | tf_op jit(solution)/shard_map/ppermute | solution.py:237
  16.0 1.0 %scores_late.1 = (f32[24,256]{1,0:T(8,128)S(1)}, f32[24,256]{1,0:T(8,128)S(1)}) custom-call(bf16[256,4096]{1,0:T(8,128)(2,1)S(1)} %get-tuple-element.12.train_ref, bf16[256,256]{1,0:T(8,128)(2,1)S(1)} %get-tuple-element.15.place_ref, f32[48,256]{1,0:T(8,128)S(1)} %get-tuple-element.16.early_ref, bf16[24,1024]{1,0:T(8,128)(2,1)S(1)} %collective-permute-done.4.refs_0_, ...), custom_call_target="tpu_custom_call" | custom-call | flops 100663296 | bytes 2293760 | tf_op jit(solution)/shard_map/scores_late/pallas_call | solution.py:223
  17.0 0.1 collective-permute-start.7
  17.1 1.2 %collective-permute-done.7 = f32[24,256]{1,0:T(8,128)S(1)} collective-permute-done((f32[24,256]{1,0:T(8,128)S(1)}, f32[24,256]{1,0:T(8,128)S(1)}, u32[]{:S(2)}, u32[]{:S(2)}) %collective-permute-start.7) | collective-permute-done | bytes 24608 | tf_op jit(solution)/shard_map/ppermute | solution.py:257
  18.3 0.6 %fusion = bf16[3,256,8]{1,2,0:T(8,128)(2,1)} fusion(f32[24,256]{1,0:T(8,128)S(1)} %get-tuple-element.17, f32[24,256]{1,0:T(8,128)S(1)} %collective-permute-done.7), kind=kLoop, calls=%fused_computation.1 | loop fusion | flops 12288 | bytes 61440 | tf_op jit(solution)/shard_map/transpose | solution.py:259
Async XLA Ops:
  1.8 8.6 %collective-permute-start.2 = (bf16[24,1024]{1,0:T(8,128)(2,1)S(1)}, bf16[24,1024]{1,0:T(8,128)(2,1)S(1)}, u32[]{:S(2)}, u32[]{:S(2)}) collective-permute-start(bf16[24,1024]{1,0:T(8,128)(2,1)S(1)} %get-tuple-element.14.refs_0_), channel_id=1, source_target_pairs={{0,12},{2,14},{4,8},{6,10},{8,4},{10,6},{12,0},{14,2},{1,13},{3,15... | collective-permute-start | bytes 147464 | tf_op jit(solution)/shard_map/ppermute | solution.py:237
  6.9 5.0 %collective-permute-start.3 = (bf16[24,1024]{1,0:T(8,128)(2,1)S(1)}, bf16[24,1024]{1,0:T(8,128)(2,1)S(1)}, u32[]{:S(2)}, u32[]{:S(2)}) collective-permute-start(bf16[24,1024]{1,0:T(8,128)(2,1)S(1)} %get-tuple-element.14.refs_0_), channel_id=1, source_target_pairs={{0,8},{2,10},{4,12},{6,14},{8,0},{10,2},{12,4},{14,6},{1,9},{3,11}... | collective-permute-start | bytes 147464 | tf_op jit(solution)/shard_map/ppermute | solution.py:237
  6.9 6.5 %collective-permute-start = (bf16[24,1024]{1,0:T(8,128)(2,1)S(1)}, bf16[24,1024]{1,0:T(8,128)(2,1)S(1)}, u32[]{:S(2)}, u32[]{:S(2)}) collective-permute-start(bf16[24,1024]{1,0:T(8,128)(2,1)S(1)} %get-tuple-element.14.refs_0_), channel_id=1, source_target_pairs={{0,4},{2,6},{4,0},{6,2},{8,12},{10,14},{12,8},{14,10},{1,5},{3,7},... | collective-permute-start | bytes 147464 | tf_op jit(solution)/shard_map/ppermute | solution.py:237
  7.5 5.8 %collective-permute-start.1 = (bf16[24,1024]{1,0:T(8,128)(2,1)S(1)}, bf16[24,1024]{1,0:T(8,128)(2,1)S(1)}, u32[]{:S(2)}, u32[]{:S(2)}) collective-permute-start(bf16[24,1024]{1,0:T(8,128)(2,1)S(1)} %get-tuple-element.14.refs_0_), channel_id=1, source_target_pairs={{0,2},{2,0},{4,6},{6,4},{8,10},{10,8},{12,14},{14,12},{1,3},{3,1},... | collective-permute-start | bytes 147464 | tf_op jit(solution)/shard_map/ppermute | solution.py:237
  9.2 5.2 %collective-permute-start.4 = (bf16[24,1024]{1,0:T(8,128)(2,1)S(1)}, bf16[24,1024]{1,0:T(8,128)(2,1)S(1)}, u32[]{:S(2)}, u32[]{:S(2)}) collective-permute-start(bf16[24,1024]{1,0:T(8,128)(2,1)S(1)} %get-tuple-element.14.refs_0_), channel_id=1, source_target_pairs={{0,6},{2,4},{4,2},{6,0},{8,14},{10,12},{12,10},{14,8},{1,7},{3,5},... | collective-permute-start | bytes 147464 | tf_op jit(solution)/shard_map/ppermute | solution.py:237
  10.4 4.7 %collective-permute-start.5 = (bf16[24,1024]{1,0:T(8,128)(2,1)S(1)}, bf16[24,1024]{1,0:T(8,128)(2,1)S(1)}, u32[]{:S(2)}, u32[]{:S(2)}) collective-permute-start(bf16[24,1024]{1,0:T(8,128)(2,1)S(1)} %collective-permute-done.2.refs_3_), channel_id=1, source_target_pairs={{0,2},{2,0},{4,6},{6,4},{8,10},{10,8},{12,14},{14,12},{1,3},{3,1},... | collective-permute-start | bytes 147464 | tf_op jit(solution)/shard_map/ppermute | solution.py:237
  11.9 4.1 %collective-permute-start.6 = (bf16[24,1024]{1,0:T(8,128)(2,1)S(1)}, bf16[24,1024]{1,0:T(8,128)(2,1)S(1)}, u32[]{:S(2)}, u32[]{:S(2)}) collective-permute-start(bf16[24,1024]{1,0:T(8,128)(2,1)S(1)} %collective-permute-done.3.refs_4_), channel_id=1, source_target_pairs={{0,2},{2,0},{4,6},{6,4},{8,10},{10,8},{12,14},{14,12},{1,3},{3,1},... | collective-permute-start | bytes 147464 | tf_op jit(solution)/shard_map/ppermute | solution.py:237
  17.0 1.3 %collective-permute-start.7 = (f32[24,256]{1,0:T(8,128)S(1)}, f32[24,256]{1,0:T(8,128)S(1)}, u32[]{:S(2)}, u32[]{:S(2)}) collective-permute-start(f32[24,256]{1,0:T(8,128)S(1)} %get-tuple-element.18), channel_id=1, source_target_pairs={{0,1},{1,0},{2,3},{3,2},{4,5},{5,4},{6,7},{7,6},{8,9},{9,8},{10,11... | collective-permute-start | bytes 73736 | tf_op jit(solution)/shard_map/ppermute | solution.py:257

commit v10 on v9

--- a/solution.py
+++ b/solution.py
@@ -241,9 +241,10 @@
             near = {0: own, **{m: swap(own, m) for m in range(2, n_row, 2)}}
             return {**near, **{m ^ 1: swap(x, 1) for m, x in near.items()}}, n_row // 2
         far = {m: swap(own, m) for m in (6, 4)}
-        diagonal = {3: swap(own, 3)}
-        near = {m: swap(own, m) for m in (2, 1)}
-        return {0: own, **near, **far, **diagonal, **{m ^ 1: swap(x, 1) for m, x in far.items()}}, 5
+        across = {m: swap(own, m) for m in (3, 1)}
+        far[6], across[1] = lax.optimization_barrier((far[6], across[1]))
+        near = {2: swap(own, 2)}
+        return {0: own, **across, **far, **near, **{m ^ 1: swap(x, 1) for m, x in far.items()}}, 5
 
     def body(train_grads, query_grads, out_basis, in_basis, eigenvalues, block_order, row_ids):
         blocks, qdev, _, width = query_grads.shape

time: 19 us -> 20.6 us (1.084)
  waiting for transfers between devices: 2.78 us -> 5.12 us
  starting transfers between devices: 11.7 us -> 10.9 us
    ppermute x7, waiting for transfers between devices: 1.6 us -> 3.94 us  [swap(): return lax.ppermute(x, 'row', [(r, r ^ mask) for r in range(n_row)])]
    ppermute x7, starting transfers between devices: 11.6 us -> 10.8 us  [swap(): return lax.ppermute(x, 'row', [(r, r ^ mask) for r in range(n_row)])]
  transfers between devices with their start and end apart: 8 -> 8, of which waited for: 3 -> 5; matrix products, arithmetic and copies ran while one was open for 0% -> 0% of each run, Pallas kernels for 5% -> 5%
where the time goes in v10:
time: 20.6 us; the launch traced here: 20.5 us
  starting transfers between devices  10.9 us (53%)
  waiting for transfers between devices  5.12 us (25%)
  Pallas kernels  3.77 us (18%)
  other arithmetic  0.6 us (3%)
    ppermute x7, starting transfers between devices, swap(): return lax.ppermute(x, 'row', [(r, r ^ mask) for r in range(n_row)])  10.8 us
    ppermute x7, waiting for transfers between devices, swap(): return lax.ppermute(x, 'row', [(r, r ^ mask) for r in range(n_row)])  3.94 us
    pallas_call x1, Pallas kernels, precondition(): pl.pallas_call(precondition_kernel, out_shape=(jax.ShapeDtypeStruct((coun...  1.78 us
    ppermute x1, waiting for transfers between devices, body(): got = lax.ppermute(other, 'layer', [(0, 1), (1, 0)])  1.18 us
    pallas_call x1, Pallas kernels, scores(): pl.pallas_call(functools.partial(late_kernel, masks[early:] + masks[:earl...  1 us
    pallas_call x1, Pallas kernels, scores(): pl.pallas_call(functools.partial(early_kernel, masks), out_shape=(jax.Sha...  0.99 us
    transpose x1, other arithmetic, body(): return total.reshape(blocks, -1, rows).transpose(0, 2, 1)  0.6 us
  transfers between devices with their start and end apart: 8, of which 5 were waited for; matrix products, arithmetic and copies ran while one was open for 0% of the time, Pallas kernels for 5%

profile of v10, /device:TPU:0, one launch (start us, length us, event | category | flops | bytes accessed | tf_op | source)
XLA Modules:
  0.0 20.5 jit_solution(16833299569891917221)
XLA Ops:
  0.0 1.8 %precondition.1 = (bf16[24,1024]{1,0:T(8,128)(2,1)S(1)}, s32[1,256]{1,0:T(1,128)S(1)}, bf16[256,4096]{1,0:T(8,128)(2,1)S(1)}) custom-call(s32[3]{0:T(128)} %order_hbm.1, bf16[3,2,4096]{2,1,0:T(2,128)(2,1)} %bitcast.7, f32[1,64,64]{2,1,0:T(8,128)} %out_basis_hbm.1, f32[1,64,64]{2,1,0:T(8,128)} %in_basis_hbm.1, f32[1,4096]{1,0:T(1,128)} %eig_hbm.1, ...), custom_call_target="tpu_custom_call" | custom-call | tf_op jit(solution)/shard_map/precondition/pallas_call | solution.py:107
  1.8 5.1 %collective-permute-start.1 = (bf16[24,1024]{1,0:T(8,128)(2,1)S(1)}, bf16[24,1024]{1,0:T(8,128)(2,1)S(1)}, u32[]{:S(2)}, u32[]{:S(2)}) collective-permute-start(bf16[24,1024]{1,0:T(8,128)(2,1)S(1)} %get-tuple-element.16.refs_0_), channel_id=1, source_target_pairs={{0,12},{2,14},{4,8},{6,10},{8,4},{10,6},{12,0},{14,2},{1,13},{3,15... | collective-permute-start | bytes 147464 | tf_op jit(solution)/shard_map/ppermute | solution.py:237
  6.9 1.5 %collective-permute-start.2 = (bf16[24,1024]{1,0:T(8,128)(2,1)S(1)}, bf16[24,1024]{1,0:T(8,128)(2,1)S(1)}, u32[]{:S(2)}, u32[]{:S(2)}) collective-permute-start(bf16[24,1024]{1,0:T(8,128)(2,1)S(1)} %get-tuple-element.16.refs_0_), channel_id=1, source_target_pairs={{0,2},{2,0},{4,6},{6,4},{8,10},{10,8},{12,14},{14,12},{1,3},{3,1},... | collective-permute-start | bytes 147464 | tf_op jit(solution)/shard_map/ppermute | solution.py:237
  8.4 0.0 collective-permute-start.3
  8.4 0.6 %collective-permute-start = (bf16[24,1024]{1,0:T(8,128)(2,1)S(1)}, bf16[24,1024]{1,0:T(8,128)(2,1)S(1)}, u32[]{:S(2)}, u32[]{:S(2)}) collective-permute-start(bf16[24,1024]{1,0:T(8,128)(2,1)S(1)} %get-tuple-element.16.refs_0_), channel_id=1, source_target_pairs={{0,6},{2,4},{4,2},{6,0},{8,14},{10,12},{12,10},{14,8},{1,7},{3,5},... | collective-permute-start | bytes 147464 | tf_op jit(solution)/shard_map/ppermute | solution.py:237
  9.0 1.4 %collective-permute-start.4 = (bf16[24,1024]{1,0:T(8,128)(2,1)S(1)}, bf16[24,1024]{1,0:T(8,128)(2,1)S(1)}, u32[]{:S(2)}, u32[]{:S(2)}) collective-permute-start(bf16[24,1024]{1,0:T(8,128)(2,1)S(1)} %get-tuple-element.16.refs_0_), channel_id=1, source_target_pairs={{0,4},{2,6},{4,0},{6,2},{8,12},{10,14},{12,8},{14,10},{1,5},{3,7},... | collective-permute-start | bytes 147464 | tf_op jit(solution)/shard_map/ppermute | solution.py:237
  10.4 0.0 collective-permute-done.1.refs_3_
  10.4 0.6 %collective-permute-done.2.refs_2_ = bf16[24,1024]{1,0:T(8,128)(2,1)S(1)} collective-permute-done((bf16[24,1024]{1,0:T(8,128)(2,1)S(1)}, bf16[24,1024]{1,0:T(8,128)(2,1)S(1)}, u32[]{:S(2)}, u32[]{:S(2)}) %collective-permute-start.2) | collective-permute-done | bytes 49184 | tf_op jit(solution)/shard_map/ppermute | solution.py:237
  11.0 1.8 %collective-permute-start.5 = (bf16[24,1024]{1,0:T(8,128)(2,1)S(1)}, bf16[24,1024]{1,0:T(8,128)(2,1)S(1)}, u32[]{:S(2)}, u32[]{:S(2)}) collective-permute-start(bf16[24,1024]{1,0:T(8,128)(2,1)S(1)} %collective-permute-done.1.refs_3_), channel_id=1, source_target_pairs={{0,2},{2,0},{4,6},{6,4},{8,10},{10,8},{12,14},{14,12},{1,3},{3,1},... | collective-permute-start | bytes 147464 | tf_op jit(solution)/shard_map/ppermute | solution.py:237
  12.7 0.7 %collective-permute-done.3.refs_4_ = bf16[24,1024]{1,0:T(8,128)(2,1)S(1)} collective-permute-done((bf16[24,1024]{1,0:T(8,128)(2,1)S(1)}, bf16[24,1024]{1,0:T(8,128)(2,1)S(1)}, u32[]{:S(2)}, u32[]{:S(2)}) %collective-permute-start.3) | collective-permute-done | bytes 49184 | tf_op jit(solution)/shard_map/ppermute | solution.py:237
  13.5 0.5 %collective-permute-start.6 = (bf16[24,1024]{1,0:T(8,128)(2,1)S(1)}, bf16[24,1024]{1,0:T(8,128)(2,1)S(1)}, u32[]{:S(2)}, u32[]{:S(2)}) collective-permute-start(bf16[24,1024]{1,0:T(8,128)(2,1)S(1)} %collective-permute-done.3.refs_4_), channel_id=1, source_target_pairs={{0,2},{2,0},{4,6},{6,4},{8,10},{10,8},{12,14},{14,12},{1,3},{3,1},... | collective-permute-start | bytes 147464 | tf_op jit(solution)/shard_map/ppermute | solution.py:237
  14.0 0.0 collective-permute-done.refs_1_
  14.0 1.0 %scores_early.1 = (f32[48,256]{1,0:T(8,128)S(1)}, bf16[256,256]{1,0:T(8,128)(2,1)S(1)}) custom-call(bf16[256,4096]{1,0:T(8,128)(2,1)S(1)} %get-tuple-element.14.train_ref, s32[1,256]{1,0:T(1,128)S(1)} %get-tuple-element.15.ids_ref, bf16[24,1024]{1,0:T(8,128)(2,1)S(1)} %get-tuple-element.16.refs_0_, bf16[24,1024]{1,0:T(8,128)(2,1)S(1)} %collective-permute-done.refs_1_, ...), custom_call_target="tpu_custom_call" | custom-call | flops 100663296 | bytes 2293760 | tf_op jit(solution)/shard_map/scores_early/pallas_call | solution.py:209
  15.0 0.0 collective-permute-done.4.refs_0_
  15.0 0.3 %collective-permute-done.5.refs_1_ = bf16[24,1024]{1,0:T(8,128)(2,1)S(1)} collective-permute-done((bf16[24,1024]{1,0:T(8,128)(2,1)S(1)}, bf16[24,1024]{1,0:T(8,128)(2,1)S(1)}, u32[]{:S(2)}, u32[]{:S(2)}) %collective-permute-start.5) | collective-permute-done | bytes 49184 | tf_op jit(solution)/shard_map/ppermute | solution.py:237
  15.3 2.3 %collective-permute-done.6.refs_2_ = bf16[24,1024]{1,0:T(8,128)(2,1)S(1)} collective-permute-done((bf16[24,1024]{1,0:T(8,128)(2,1)S(1)}, bf16[24,1024]{1,0:T(8,128)(2,1)S(1)}, u32[]{:S(2)}, u32[]{:S(2)}) %collective-permute-start.6) | collective-permute-done | bytes 49184 | tf_op jit(solution)/shard_map/ppermute | solution.py:237
  17.6 1.0 %scores_late.1 = (f32[24,256]{1,0:T(8,128)S(1)}, f32[24,256]{1,0:T(8,128)S(1)}) custom-call(bf16[256,4096]{1,0:T(8,128)(2,1)S(1)} %get-tuple-element.14.train_ref, bf16[256,256]{1,0:T(8,128)(2,1)S(1)} %get-tuple-element.19.place_ref, f32[48,256]{1,0:T(8,128)S(1)} %get-tuple-element.20.early_ref, bf16[24,1024]{1,0:T(8,128)(2,1)S(1)} %collective-permute-done.4.refs_0_, ...), custom_call_target="tpu_custom_call" | custom-call | flops 100663296 | bytes 2293760 | tf_op jit(solution)/shard_map/scores_late/pallas_call | solution.py:223
  18.6 0.1 collective-permute-start.7
  18.7 1.2 %collective-permute-done.7 = f32[24,256]{1,0:T(8,128)S(1)} collective-permute-done((f32[24,256]{1,0:T(8,128)S(1)}, f32[24,256]{1,0:T(8,128)S(1)}, u32[]{:S(2)}, u32[]{:S(2)}) %collective-permute-start.7) | collective-permute-done | bytes 24608 | tf_op jit(solution)/shard_map/ppermute | solution.py:258
  19.8 0.6 %fusion = bf16[3,256,8]{1,2,0:T(8,128)(2,1)} fusion(f32[24,256]{1,0:T(8,128)S(1)} %get-tuple-element.21, f32[24,256]{1,0:T(8,128)S(1)} %collective-permute-done.7), kind=kLoop, calls=%fused_computation.1 | loop fusion | flops 12288 | bytes 61440 | tf_op jit(solution)/shard_map/transpose | solution.py:260
Async XLA Ops:
  1.8 8.6 %collective-permute-start.1 = (bf16[24,1024]{1,0:T(8,128)(2,1)S(1)}, bf16[24,1024]{1,0:T(8,128)(2,1)S(1)}, u32[]{:S(2)}, u32[]{:S(2)}) collective-permute-start(bf16[24,1024]{1,0:T(8,128)(2,1)S(1)} %get-tuple-element.16.refs_0_), channel_id=1, source_target_pairs={{0,12},{2,14},{4,8},{6,10},{8,4},{10,6},{12,0},{14,2},{1,13},{3,15... | collective-permute-start | bytes 147464 | tf_op jit(solution)/shard_map/ppermute | solution.py:237
  6.9 4.1 %collective-permute-start.2 = (bf16[24,1024]{1,0:T(8,128)(2,1)S(1)}, bf16[24,1024]{1,0:T(8,128)(2,1)S(1)}, u32[]{:S(2)}, u32[]{:S(2)}) collective-permute-start(bf16[24,1024]{1,0:T(8,128)(2,1)S(1)} %get-tuple-element.16.refs_0_), channel_id=1, source_target_pairs={{0,2},{2,0},{4,6},{6,4},{8,10},{10,8},{12,14},{14,12},{1,3},{3,1},... | collective-permute-start | bytes 147464 | tf_op jit(solution)/shard_map/ppermute | solution.py:237
  8.4 5.1 %collective-permute-start.3 = (bf16[24,1024]{1,0:T(8,128)(2,1)S(1)}, bf16[24,1024]{1,0:T(8,128)(2,1)S(1)}, u32[]{:S(2)}, u32[]{:S(2)}) collective-permute-start(bf16[24,1024]{1,0:T(8,128)(2,1)S(1)} %get-tuple-element.16.refs_0_), channel_id=1, source_target_pairs={{0,8},{2,10},{4,12},{6,14},{8,0},{10,2},{12,4},{14,6},{1,9},{3,11}... | collective-permute-start | bytes 147464 | tf_op jit(solution)/shard_map/ppermute | solution.py:237
  8.4 5.6 %collective-permute-start = (bf16[24,1024]{1,0:T(8,128)(2,1)S(1)}, bf16[24,1024]{1,0:T(8,128)(2,1)S(1)}, u32[]{:S(2)}, u32[]{:S(2)}) collective-permute-start(bf16[24,1024]{1,0:T(8,128)(2,1)S(1)} %get-tuple-element.16.refs_0_), channel_id=1, source_target_pairs={{0,6},{2,4},{4,2},{6,0},{8,14},{10,12},{12,10},{14,8},{1,7},{3,5},... | collective-permute-start | bytes 147464 | tf_op jit(solution)/shard_map/ppermute | solution.py:237
  9.0 6.0 %collective-permute-start.4 = (bf16[24,1024]{1,0:T(8,128)(2,1)S(1)}, bf16[24,1024]{1,0:T(8,128)(2,1)S(1)}, u32[]{:S(2)}, u32[]{:S(2)}) collective-permute-start(bf16[24,1024]{1,0:T(8,128)(2,1)S(1)} %get-tuple-element.16.refs_0_), channel_id=1, source_target_pairs={{0,4},{2,6},{4,0},{6,2},{8,12},{10,14},{12,8},{14,10},{1,5},{3,7},... | collective-permute-start | bytes 147464 | tf_op jit(solution)/shard_map/ppermute | solution.py:237
  11.0 4.3 %collective-permute-start.5 = (bf16[24,1024]{1,0:T(8,128)(2,1)S(1)}, bf16[24,1024]{1,0:T(8,128)(2,1)S(1)}, u32[]{:S(2)}, u32[]{:S(2)}) collective-permute-start(bf16[24,1024]{1,0:T(8,128)(2,1)S(1)} %collective-permute-done.1.refs_3_), channel_id=1, source_target_pairs={{0,2},{2,0},{4,6},{6,4},{8,10},{10,8},{12,14},{14,12},{1,3},{3,1},... | collective-permute-start | bytes 147464 | tf_op jit(solution)/shard_map/ppermute | solution.py:237
  13.5 4.1 %collective-permute-start.6 = (bf16[24,1024]{1,0:T(8,128)(2,1)S(1)}, bf16[24,1024]{1,0:T(8,128)(2,1)S(1)}, u32[]{:S(2)}, u32[]{:S(2)}) collective-permute-start(bf16[24,1024]{1,0:T(8,128)(2,1)S(1)} %collective-permute-done.3.refs_4_), channel_id=1, source_target_pairs={{0,2},{2,0},{4,6},{6,4},{8,10},{10,8},{12,14},{14,12},{1,3},{3,1},... | collective-permute-start | bytes 147464 | tf_op jit(solution)/shard_map/ppermute | solution.py:237
  18.6 1.3 %collective-permute-start.7 = (f32[24,256]{1,0:T(8,128)S(1)}, f32[24,256]{1,0:T(8,128)S(1)}, u32[]{:S(2)}, u32[]{:S(2)}) collective-permute-start(f32[24,256]{1,0:T(8,128)S(1)} %get-tuple-element.22), channel_id=1, source_target_pairs={{0,1},{1,0},{2,3},{3,2},{4,5},{5,4},{6,7},{7,6},{8,9},{9,8},{10,11... | collective-permute-start | bytes 73736 | tf_op jit(solution)/shard_map/ppermute | solution.py:258

commit v11 on v9

--- a/solution.py
+++ b/solution.py
@@ -140,7 +140,8 @@
 
 
 def slot_of(n_row, mask):
-    source, per = lax.axis_index("row") ^ mask, n_row // 2
+    mask, flip = mask
+    source, per = lax.axis_index("row") ^ mask ^ (lax.axis_index("grp") * flip), n_row // 2
     return source ^ (lax.axis_index("layer") * per)
 
 
@@ -232,18 +233,23 @@
     )(train, place, terms, *parts[early:])
 
 
-def make_body(n_row):
-    def swap(x, mask):
-        return lax.ppermute(x, "row", [(r, r ^ mask) for r in range(n_row)])
+def make_body(n_grp, n_row):
+    def swap(x, mask, flip=0, cross=0):
+        pairs = [
+            (g * n_row + r, (g ^ cross) * n_row + (r ^ mask ^ (g * flip))) for g in range(n_grp) for r in range(n_row)
+        ]
+        return lax.ppermute(x, ("grp", "row"), pairs)
 
     def gather(own):
-        if n_row != 8:
+        if (n_grp, n_row) != (2, 8):
             near = {0: own, **{m: swap(own, m) for m in range(2, n_row, 2)}}
-            return {**near, **{m ^ 1: swap(x, 1) for m, x in near.items()}}, n_row // 2
-        far = {m: swap(own, m) for m in (6, 4)}
-        diagonal = {3: swap(own, 3)}
-        near = {m: swap(own, m) for m in (2, 1)}
-        return {0: own, **near, **far, **diagonal, **{m ^ 1: swap(x, 1) for m, x in far.items()}}, 5
+            parts = {**near, **{m ^ 1: swap(x, 1) for m, x in near.items()}}
+            return {(m, 0): x for m, x in parts.items()}, n_row // 2
+        far = swap(own, 4, 2)
+        return {
+            (0, 0): own, (7, 2): swap(own, 7, 2), (2, 0): swap(own, 2), (1, 0): swap(own, 1), (4, 2): far,
+            (3, 0): swap(own, 3), (5, 2): swap(far, 1), (6, 2): swap(far, 0, cross=1),
+        }, 5
 
     def body(train_grads, query_grads, out_basis, in_basis, eigenvalues, block_order, row_ids):
         blocks, qdev, _, width = query_grads.shape
@@ -272,5 +278,5 @@
         P(("grp", "row"), None),
     )
     out_specs = P(None, ("grp", "row"), "layer")
-    body = make_body(mesh.shape["row"])
+    body = make_body(mesh.shape["grp"], mesh.shape["row"])
     return jax.shard_map(body, mesh=mesh, in_specs=in_specs, out_specs=out_specs, check_vma=False)

time: 19 us -> 19.9 us (1.047)
  waiting for transfers between devices: 2.78 us -> 3.38 us
  starting transfers between devices: 11.7 us -> 12 us
    ppermute x7, waiting for transfers between devices: 1.6 us -> 2.2 us  [swap(): return lax.ppermute(x, ('grp', 'row'), pairs)]
    ppermute x7, starting transfers between devices: 11.6 us -> 11.9 us  [swap(): return lax.ppermute(x, ('grp', 'row'), pairs)]
  transfers between devices with their start and end apart: 8 -> 8, of which waited for: 3 -> 4; matrix products, arithmetic and copies ran while one was open for 0% -> 0% of each run, Pallas kernels for 5% -> 5%
where the time goes in v11:
time: 19.9 us; the launch traced here: 19.8 us
  starting transfers between devices  12 us (60%)
  Pallas kernels  3.77 us (19%)
  waiting for transfers between devices  3.38 us (17%)
  other arithmetic  0.6 us (3%)
    ppermute x7, starting transfers between devices, swap(): return lax.ppermute(x, ('grp', 'row'), pairs)  11.9 us
    ppermute x7, waiting for transfers between devices, swap(): return lax.ppermute(x, ('grp', 'row'), pairs)  2.2 us
    pallas_call x1, Pallas kernels, precondition(): pl.pallas_call(precondition_kernel, out_shape=(jax.ShapeDtypeStruct((coun...  1.78 us
    ppermute x1, waiting for transfers between devices, body(): got = lax.ppermute(other, 'layer', [(0, 1), (1, 0)])  1.18 us
    pallas_call x1, Pallas kernels, scores(): pl.pallas_call(functools.partial(late_kernel, masks[early:] + masks[:earl...  1 us
    pallas_call x1, Pallas kernels, scores(): pl.pallas_call(functools.partial(early_kernel, masks), out_shape=(jax.Sha...  0.99 us
    transpose x1, other arithmetic, body(): return total.reshape(blocks, -1, rows).transpose(0, 2, 1)  0.6 us
  transfers between devices with their start and end apart: 8, of which 4 were waited for; matrix products, arithmetic and copies ran while one was open for 0% of the time, Pallas kernels for 5%

profile of v11, /device:TPU:0, one launch (start us, length us, event | category | flops | bytes accessed | tf_op | source)
XLA Modules:
  0.0 19.8 jit_solution(9044480825554642815)
XLA Ops:
  0.0 1.8 %precondition.1 = (bf16[24,1024]{1,0:T(8,128)(2,1)S(1)}, s32[1,256]{1,0:T(1,128)S(1)}, bf16[256,4096]{1,0:T(8,128)(2,1)S(1)}) custom-call(s32[3]{0:T(128)} %order_hbm.1, bf16[3,2,4096]{2,1,0:T(2,128)(2,1)} %bitcast.7, f32[1,64,64]{2,1,0:T(8,128)} %out_basis_hbm.1, f32[1,64,64]{2,1,0:T(8,128)} %in_basis_hbm.1, f32[1,4096]{1,0:T(1,128)} %eig_hbm.1, ...), custom_call_target="tpu_custom_call" | custom-call | tf_op jit(solution)/shard_map/precondition/pallas_call | solution.py:107
  1.8 4.1 %collective-permute-start.3 = (bf16[24,1024]{1,0:T(8,128)(2,1)S(1)}, bf16[24,1024]{1,0:T(8,128)(2,1)S(1)}, u32[]{:S(2)}, u32[]{:S(2)}) collective-permute-start(bf16[24,1024]{1,0:T(8,128)(2,1)S(1)} %get-tuple-element.14.refs_0_), channel_id=1, source_target_pairs={{0,8},{2,10},{4,12},{6,14},{8,0},{10,2},{12,4},{14,6},{16,28},{18,... | collective-permute-start | bytes 147464 | tf_op jit(solution)/shard_map/ppermute | solution.py:241
  5.9 2.3 %collective-permute-start = (bf16[24,1024]{1,0:T(8,128)(2,1)S(1)}, bf16[24,1024]{1,0:T(8,128)(2,1)S(1)}, u32[]{:S(2)}, u32[]{:S(2)}) collective-permute-start(bf16[24,1024]{1,0:T(8,128)(2,1)S(1)} %get-tuple-element.14.refs_0_), channel_id=1, source_target_pairs={{0,14},{2,12},{4,10},{6,8},{8,6},{10,4},{12,2},{14,0},{16,26},{18,... | collective-permute-start | bytes 147464 | tf_op jit(solution)/shard_map/ppermute | solution.py:241
  8.2 0.0 collective-permute-start.1
  8.2 0.8 %collective-permute-start.2 = (bf16[24,1024]{1,0:T(8,128)(2,1)S(1)}, bf16[24,1024]{1,0:T(8,128)(2,1)S(1)}, u32[]{:S(2)}, u32[]{:S(2)}) collective-permute-start(bf16[24,1024]{1,0:T(8,128)(2,1)S(1)} %get-tuple-element.14.refs_0_), channel_id=1, source_target_pairs={{0,2},{2,0},{4,6},{6,4},{8,10},{10,8},{12,14},{14,12},{16,18},{18,... | collective-permute-start | bytes 147464 | tf_op jit(solution)/shard_map/ppermute | solution.py:241
  9.0 2.7 %collective-permute-start.4 = (bf16[24,1024]{1,0:T(8,128)(2,1)S(1)}, bf16[24,1024]{1,0:T(8,128)(2,1)S(1)}, u32[]{:S(2)}, u32[]{:S(2)}) collective-permute-start(bf16[24,1024]{1,0:T(8,128)(2,1)S(1)} %get-tuple-element.14.refs_0_), channel_id=1, source_target_pairs={{0,6},{2,4},{4,2},{6,0},{8,14},{10,12},{12,10},{14,8},{16,22},{18,... | collective-permute-start | bytes 147464 | tf_op jit(solution)/shard_map/ppermute | solution.py:241
  11.7 0.0 collective-permute-done.3.refs_4_
  11.7 0.5 %collective-permute-start.5 = (bf16[24,1024]{1,0:T(8,128)(2,1)S(1)}, bf16[24,1024]{1,0:T(8,128)(2,1)S(1)}, u32[]{:S(2)}, u32[]{:S(2)}) collective-permute-start(bf16[24,1024]{1,0:T(8,128)(2,1)S(1)} %collective-permute-done.3.refs_4_), channel_id=1, source_target_pairs={{0,2},{2,0},{4,6},{6,4},{8,10},{10,8},{12,14},{14,12},{16,18},{18,... | collective-permute-start | bytes 147464 | tf_op jit(solution)/shard_map/ppermute | solution.py:241
  12.2 0.6 %collective-permute-done.refs_1_ = bf16[24,1024]{1,0:T(8,128)(2,1)S(1)} collective-permute-done((bf16[24,1024]{1,0:T(8,128)(2,1)S(1)}, bf16[24,1024]{1,0:T(8,128)(2,1)S(1)}, u32[]{:S(2)}, u32[]{:S(2)}) %collective-permute-start) | collective-permute-done | bytes 49184 | tf_op jit(solution)/shard_map/ppermute | solution.py:241
  12.8 1.5 %collective-permute-start.6 = (bf16[24,1024]{1,0:T(8,128)(2,1)S(1)}, bf16[24,1024]{1,0:T(8,128)(2,1)S(1)}, u32[]{:S(2)}, u32[]{:S(2)}) collective-permute-start(bf16[24,1024]{1,0:T(8,128)(2,1)S(1)} %collective-permute-done.3.refs_4_), channel_id=1, source_target_pairs={{0,16},{2,18},{4,20},{6,22},{8,24},{10,26},{12,28},{14,30},{16,0},... | collective-permute-start | bytes 147464 | tf_op jit(solution)/shard_map/ppermute | solution.py:241
  14.4 0.0 collective-permute-done.1.refs_2_
  14.4 0.0 collective-permute-done.2.refs_3_
  14.4 1.0 %scores_early.1 = (f32[48,256]{1,0:T(8,128)S(1)}, bf16[256,256]{1,0:T(8,128)(2,1)S(1)}) custom-call(bf16[256,4096]{1,0:T(8,128)(2,1)S(1)} %get-tuple-element.12.train_ref, s32[1,256]{1,0:T(1,128)S(1)} %get-tuple-element.13.ids_ref, bf16[24,1024]{1,0:T(8,128)(2,1)S(1)} %get-tuple-element.14.refs_0_, bf16[24,1024]{1,0:T(8,128)(2,1)S(1)} %collective-permute-done.refs_1_, ...), custom_call_target="tpu_custom_call" | custom-call | flops 100663296 | bytes 2293760 | tf_op jit(solution)/shard_map/scores_early/pallas_call | solution.py:210
  15.4 0.0 collective-permute-done.4.refs_0_
  15.4 0.4 %collective-permute-done.5.refs_1_ = bf16[24,1024]{1,0:T(8,128)(2,1)S(1)} collective-permute-done((bf16[24,1024]{1,0:T(8,128)(2,1)S(1)}, bf16[24,1024]{1,0:T(8,128)(2,1)S(1)}, u32[]{:S(2)}, u32[]{:S(2)}) %collective-permute-start.5) | collective-permute-done | bytes 49184 | tf_op jit(solution)/shard_map/ppermute | solution.py:241
  15.7 1.2 %collective-permute-done.6.refs_2_ = bf16[24,1024]{1,0:T(8,128)(2,1)S(1)} collective-permute-done((bf16[24,1024]{1,0:T(8,128)(2,1)S(1)}, bf16[24,1024]{1,0:T(8,128)(2,1)S(1)}, u32[]{:S(2)}, u32[]{:S(2)}) %collective-permute-start.6) | collective-permute-done | bytes 49184 | tf_op jit(solution)/shard_map/ppermute | solution.py:241
  16.9 1.0 %scores_late.1 = (f32[24,256]{1,0:T(8,128)S(1)}, f32[24,256]{1,0:T(8,128)S(1)}) custom-call(bf16[256,4096]{1,0:T(8,128)(2,1)S(1)} %get-tuple-element.12.train_ref, bf16[256,256]{1,0:T(8,128)(2,1)S(1)} %get-tuple-element.15.place_ref, f32[48,256]{1,0:T(8,128)S(1)} %get-tuple-element.16.early_ref, bf16[24,1024]{1,0:T(8,128)(2,1)S(1)} %collective-permute-done.4.refs_0_, ...), custom_call_target="tpu_custom_call" | custom-call | flops 100663296 | bytes 2293760 | tf_op jit(solution)/shard_map/scores_late/pallas_call | solution.py:224
  17.9 0.1 collective-permute-start.7
  18.0 1.2 %collective-permute-done.7 = f32[24,256]{1,0:T(8,128)S(1)} collective-permute-done((f32[24,256]{1,0:T(8,128)S(1)}, f32[24,256]{1,0:T(8,128)S(1)}, u32[]{:S(2)}, u32[]{:S(2)}) %collective-permute-start.7) | collective-permute-done | bytes 24608 | tf_op jit(solution)/shard_map/ppermute | solution.py:263
  19.2 0.6 %fusion = bf16[3,256,8]{1,2,0:T(8,128)(2,1)} fusion(f32[24,256]{1,0:T(8,128)S(1)} %get-tuple-element.17, f32[24,256]{1,0:T(8,128)S(1)} %collective-permute-done.7), kind=kLoop, calls=%fused_computation.1 | loop fusion | flops 12288 | bytes 61440 | tf_op jit(solution)/shard_map/transpose | solution.py:265
Async XLA Ops:
  1.8 9.9 %collective-permute-start.3 = (bf16[24,1024]{1,0:T(8,128)(2,1)S(1)}, bf16[24,1024]{1,0:T(8,128)(2,1)S(1)}, u32[]{:S(2)}, u32[]{:S(2)}) collective-permute-start(bf16[24,1024]{1,0:T(8,128)(2,1)S(1)} %get-tuple-element.14.refs_0_), channel_id=1, source_target_pairs={{0,8},{2,10},{4,12},{6,14},{8,0},{10,2},{12,4},{14,6},{16,28},{18,... | collective-permute-start | bytes 147464 | tf_op jit(solution)/shard_map/ppermute | solution.py:241
  5.9 6.9 %collective-permute-start = (bf16[24,1024]{1,0:T(8,128)(2,1)S(1)}, bf16[24,1024]{1,0:T(8,128)(2,1)S(1)}, u32[]{:S(2)}, u32[]{:S(2)}) collective-permute-start(bf16[24,1024]{1,0:T(8,128)(2,1)S(1)} %get-tuple-element.14.refs_0_), channel_id=1, source_target_pairs={{0,14},{2,12},{4,10},{6,8},{8,6},{10,4},{12,2},{14,0},{16,26},{18,... | collective-permute-start | bytes 147464 | tf_op jit(solution)/shard_map/ppermute | solution.py:241
  8.2 6.2 %collective-permute-start.1 = (bf16[24,1024]{1,0:T(8,128)(2,1)S(1)}, bf16[24,1024]{1,0:T(8,128)(2,1)S(1)}, u32[]{:S(2)}, u32[]{:S(2)}) collective-permute-start(bf16[24,1024]{1,0:T(8,128)(2,1)S(1)} %get-tuple-element.14.refs_0_), channel_id=1, source_target_pairs={{0,4},{2,6},{4,0},{6,2},{8,12},{10,14},{12,8},{14,10},{16,20},{18,... | collective-permute-start | bytes 147464 | tf_op jit(solution)/shard_map/ppermute | solution.py:241
  8.2 6.2 %collective-permute-start.2 = (bf16[24,1024]{1,0:T(8,128)(2,1)S(1)}, bf16[24,1024]{1,0:T(8,128)(2,1)S(1)}, u32[]{:S(2)}, u32[]{:S(2)}) collective-permute-start(bf16[24,1024]{1,0:T(8,128)(2,1)S(1)} %get-tuple-element.14.refs_0_), channel_id=1, source_target_pairs={{0,2},{2,0},{4,6},{6,4},{8,10},{10,8},{12,14},{14,12},{16,18},{18,... | collective-permute-start | bytes 147464 | tf_op jit(solution)/shard_map/ppermute | solution.py:241
  9.0 6.4 %collective-permute-start.4 = (bf16[24,1024]{1,0:T(8,128)(2,1)S(1)}, bf16[24,1024]{1,0:T(8,128)(2,1)S(1)}, u32[]{:S(2)}, u32[]{:S(2)}) collective-permute-start(bf16[24,1024]{1,0:T(8,128)(2,1)S(1)} %get-tuple-element.14.refs_0_), channel_id=1, source_target_pairs={{0,6},{2,4},{4,2},{6,0},{8,14},{10,12},{12,10},{14,8},{16,22},{18,... | collective-permute-start | bytes 147464 | tf_op jit(solution)/shard_map/ppermute | solution.py:241
  11.7 4.1 %collective-permute-start.5 = (bf16[24,1024]{1,0:T(8,128)(2,1)S(1)}, bf16[24,1024]{1,0:T(8,128)(2,1)S(1)}, u32[]{:S(2)}, u32[]{:S(2)}) collective-permute-start(bf16[24,1024]{1,0:T(8,128)(2,1)S(1)} %collective-permute-done.3.refs_4_), channel_id=1, source_target_pairs={{0,2},{2,0},{4,6},{6,4},{8,10},{10,8},{12,14},{14,12},{16,18},{18,... | collective-permute-start | bytes 147464 | tf_op jit(solution)/shard_map/ppermute | solution.py:241
  12.8 4.1 %collective-permute-start.6 = (bf16[24,1024]{1,0:T(8,128)(2,1)S(1)}, bf16[24,1024]{1,0:T(8,128)(2,1)S(1)}, u32[]{:S(2)}, u32[]{:S(2)}) collective-permute-start(bf16[24,1024]{1,0:T(8,128)(2,1)S(1)} %collective-permute-done.3.refs_4_), channel_id=1, source_target_pairs={{0,16},{2,18},{4,20},{6,22},{8,24},{10,26},{12,28},{14,30},{16,0},... | collective-permute-start | bytes 147464 | tf_op jit(solution)/shard_map/ppermute | solution.py:241
  17.9 1.3 %collective-permute-start.7 = (f32[24,256]{1,0:T(8,128)S(1)}, f32[24,256]{1,0:T(8,128)S(1)}, u32[]{:S(2)}, u32[]{:S(2)}) collective-permute-start(f32[24,256]{1,0:T(8,128)S(1)} %get-tuple-element.18), channel_id=1, source_target_pairs={{0,1},{1,0},{2,3},{3,2},{4,5},{5,4},{6,7},{7,6},{8,9},{9,8},{10,11... | collective-permute-start | bytes 73736 | tf_op jit(solution)/shard_map/ppermute | solution.py:263

commit v12 on v9

--- a/solution.py
+++ b/solution.py
@@ -30,7 +30,7 @@
 def precondition_kernel(
     order_hbm, q_hbm, out_basis_hbm, in_basis_hbm, eig_hbm, ids_hbm, train_hbm,
     sent_ref, ids_out_ref, train_out_ref,
-    order_ref, q_ref, out_basis_ref, in_basis_ref, eig_ref, x_scr, o_scr, eig_scr, sems,
+    order_ref, q_ref, out_basis_ref, in_basis_ref, eig_ref, x_scr, even_scr, odd_scr, o_scr, eig_scr, sems,
 ):
     copies = [
         pltpu.make_async_copy(src, dst, sems.at[n])
@@ -43,20 +43,15 @@
         copy.start()
     for copy in copies[:5]:
         copy.wait()
-    blocks, qdev, width = q_ref.shape
+    blocks, lines, _ = q_ref.shape
+    chunks = eig_ref.shape[0]
     side = out_basis_ref.shape[1]
     half = side // 2
+    qdev = lines // chunks
     count = blocks * qdev
-    chunks = width // LANES
-    for j in range(blocks):
-        flat = q_ref[order_ref[j]].astype(F32)
-        for k in range(chunks):
-            x_scr[pl.ds(j * qdev * chunks + k, qdev, stride=chunks), :] = flat[:, k * LANES:(k + 1) * LANES]
     scale = 1.0 / (eig_ref[...] + DAMPING)
-    for k in range(chunks):
-        for odd in range(2):
-            at = k * LANES + odd * side
-            eig_scr[2 * k + odd:2 * k + odd + 1, :side] = scale[:, at:at + side]
+    eig_scr[pl.ds(0, half, stride=2), :side] = scale[:, :side]
+    eig_scr[pl.ds(1, half, stride=2), :side] = scale[:, side:]
     scale = eig_scr[:, :side]
     o_scr[:, :side] = out_basis_ref[0]
     basis = jnp.concatenate(
@@ -68,14 +63,16 @@
     back = jnp.concatenate([b_hi, b_hi, b_lo], axis=1)
     i_hi, i_lo = split2(in_basis_ref[0])
     none = jnp.zeros_like(i_hi)
-    raw = x_scr[...].astype(BF16)
+    raw = jnp.concatenate([q_ref[order_ref[j]] for j in range(blocks)], axis=0)
     raw2 = jnp.concatenate([raw, raw], axis=1)
     even = mm(raw2, jnp.concatenate([i_hi, none, i_lo, none], axis=0))
     odd = mm(raw2, jnp.concatenate([none, i_hi, none, i_lo], axis=0))
+    even_scr[:, :side] = even
+    odd_scr[:, :side] = odd
     evens, odds = [], []
     for q in range(count):
-        rows = slice(q * half, (q + 1) * half)
-        hi, lo = split2(jnp.concatenate([even[rows], odd[rows]], axis=0))
+        rows = pl.ds(q // qdev * lines + q % qdev, half, stride=qdev)
+        hi, lo = split2(jnp.concatenate([even_scr[rows, :side], odd_scr[rows, :side]], axis=0))
         rotated = mm(left, jnp.concatenate([hi, lo, hi], axis=0))
         hi, lo = split2(rotated * scale)
         again = mm(back, jnp.concatenate([hi, lo, hi], axis=0))
@@ -101,9 +98,13 @@
     blocks, qdev, width = query_grads.shape
     count = blocks * qdev
     side = out_basis.shape[1]
+    chunks = width // LANES
+    query_grads = query_grads.reshape(blocks, qdev, chunks, LANES).swapaxes(1, 2).reshape(blocks, -1, LANES)
+    eigenvalues = eigenvalues.reshape(chunks, LANES)
     vmem = pl.BlockSpec(memory_space=pltpu.VMEM)
     hbm = pl.BlockSpec(memory_space=pltpu.HBM)
     free = pl.BlockSpec(memory_space=pl.ANY)
+    rows = pltpu.VMEM((count * chunks, LANES), F32)
     return pl.pallas_call(
         precondition_kernel,
         out_shape=(
@@ -119,7 +120,7 @@
             pltpu.VMEM(out_basis.shape, F32),
             pltpu.VMEM(in_basis.shape, F32),
             pltpu.VMEM(eigenvalues.shape, F32),
-            pltpu.VMEM((count * width // LANES, LANES), F32),
+            rows, rows, rows,
             pltpu.VMEM((side, LANES), F32),
             pltpu.VMEM((side, LANES), F32),
             pltpu.SemaphoreType.DMA((7,)),

time: 19 us -> 19 us (level)
  no operation moved by 1% of the time
where the time goes in v12:
time: 19 us; the launch traced here: 18.9 us
  starting transfers between devices  11.7 us (62%)
  Pallas kernels  3.76 us (20%)
  waiting for transfers between devices  2.79 us (15%)
  other arithmetic  0.6 us (3%)
    ppermute x7, starting transfers between devices, swap(): return lax.ppermute(x, 'row', [(r, r ^ mask) for r in range(n_row)])  11.6 us
    pallas_call x1, Pallas kernels, precondition(): pl.pallas_call(precondition_kernel, out_shape=(jax.ShapeDtypeStruct((coun...  1.76 us
    ppermute x7, waiting for transfers between devices, swap(): return lax.ppermute(x, 'row', [(r, r ^ mask) for r in range(n_row)])  1.61 us
    ppermute x1, waiting for transfers between devices, body(): got = lax.ppermute(other, 'layer', [(0, 1), (1, 0)])  1.18 us
    pallas_call x1, Pallas kernels, scores(): pl.pallas_call(functools.partial(late_kernel, masks[early:] + masks[:earl...  1 us
    pallas_call x1, Pallas kernels, scores(): pl.pallas_call(functools.partial(early_kernel, masks), out_shape=(jax.Sha...  0.99 us
    transpose x1, other arithmetic, body(): return total.reshape(blocks, -1, rows).transpose(0, 2, 1)  0.6 us
  transfers between devices with their start and end apart: 8, of which 3 were waited for; matrix products, arithmetic and copies ran while one was open for 0% of the time, Pallas kernels for 5%

profile of v12, /device:TPU:0, one launch (start us, length us, event | category | flops | bytes accessed | tf_op | source)
XLA Modules:
  0.0 18.9 jit_solution(8797853589374262914)
XLA Ops:
  0.0 1.8 %precondition.1 = (bf16[24,1024]{1,0:T(8,128)(2,1)S(1)}, s32[1,256]{1,0:T(1,128)S(1)}, bf16[256,4096]{1,0:T(8,128)(2,1)S(1)}) custom-call(s32[3]{0:T(128)} %order_hbm.1, bf16[3,64,128]{2,1,0:T(8,128)(2,1)} %bitcast.12, f32[1,64,64]{2,1,0:T(8,128)} %out_basis_hbm.1, f32[1,64,64]{2,1,0:T(8,128)} %in_basis_hbm.1, f32[32,128]{1,0:T(8,128)} %bitcast.13, ...), custom_call_target="tpu_custom_call" | custom-call | tf_op jit(solution)/shard_map/precondition/pallas_call | solution.py:108
  1.8 5.1 %collective-permute-start.2 = (bf16[24,1024]{1,0:T(8,128)(2,1)S(1)}, bf16[24,1024]{1,0:T(8,128)(2,1)S(1)}, u32[]{:S(2)}, u32[]{:S(2)}) collective-permute-start(bf16[24,1024]{1,0:T(8,128)(2,1)S(1)} %get-tuple-element.14.refs_0_), channel_id=1, source_target_pairs={{0,12},{2,14},{4,8},{6,10},{8,4},{10,6},{12,0},{14,2},{1,13},{3,15... | collective-permute-start | bytes 147464 | tf_op jit(solution)/shard_map/ppermute | solution.py:238
  6.9 0.0 collective-permute-start.3
  6.9 0.6 %collective-permute-start = (bf16[24,1024]{1,0:T(8,128)(2,1)S(1)}, bf16[24,1024]{1,0:T(8,128)(2,1)S(1)}, u32[]{:S(2)}, u32[]{:S(2)}) collective-permute-start(bf16[24,1024]{1,0:T(8,128)(2,1)S(1)} %get-tuple-element.14.refs_0_), channel_id=1, source_target_pairs={{0,4},{2,6},{4,0},{6,2},{8,12},{10,14},{12,8},{14,10},{1,5},{3,7},... | collective-permute-start | bytes 147464 | tf_op jit(solution)/shard_map/ppermute | solution.py:238
  7.5 1.6 %collective-permute-start.1 = (bf16[24,1024]{1,0:T(8,128)(2,1)S(1)}, bf16[24,1024]{1,0:T(8,128)(2,1)S(1)}, u32[]{:S(2)}, u32[]{:S(2)}) collective-permute-start(bf16[24,1024]{1,0:T(8,128)(2,1)S(1)} %get-tuple-element.14.refs_0_), channel_id=1, source_target_pairs={{0,2},{2,0},{4,6},{6,4},{8,10},{10,8},{12,14},{14,12},{1,3},{3,1},... | collective-permute-start | bytes 147464 | tf_op jit(solution)/shard_map/ppermute | solution.py:238
  9.2 1.2 %collective-permute-start.4 = (bf16[24,1024]{1,0:T(8,128)(2,1)S(1)}, bf16[24,1024]{1,0:T(8,128)(2,1)S(1)}, u32[]{:S(2)}, u32[]{:S(2)}) collective-permute-start(bf16[24,1024]{1,0:T(8,128)(2,1)S(1)} %get-tuple-element.14.refs_0_), channel_id=1, source_target_pairs={{0,6},{2,4},{4,2},{6,0},{8,14},{10,12},{12,10},{14,8},{1,7},{3,5},... | collective-permute-start | bytes 147464 | tf_op jit(solution)/shard_map/ppermute | solution.py:238
  10.4 0.0 collective-permute-done.2.refs_3_
  10.4 1.5 %collective-permute-start.5 = (bf16[24,1024]{1,0:T(8,128)(2,1)S(1)}, bf16[24,1024]{1,0:T(8,128)(2,1)S(1)}, u32[]{:S(2)}, u32[]{:S(2)}) collective-permute-start(bf16[24,1024]{1,0:T(8,128)(2,1)S(1)} %collective-permute-done.2.refs_3_), channel_id=1, source_target_pairs={{0,2},{2,0},{4,6},{6,4},{8,10},{10,8},{12,14},{14,12},{1,3},{3,1},... | collective-permute-start | bytes 147464 | tf_op jit(solution)/shard_map/ppermute | solution.py:238
  11.9 0.0 collective-permute-done.3.refs_4_
  11.9 1.5 %collective-permute-start.6 = (bf16[24,1024]{1,0:T(8,128)(2,1)S(1)}, bf16[24,1024]{1,0:T(8,128)(2,1)S(1)}, u32[]{:S(2)}, u32[]{:S(2)}) collective-permute-start(bf16[24,1024]{1,0:T(8,128)(2,1)S(1)} %collective-permute-done.3.refs_4_), channel_id=1, source_target_pairs={{0,2},{2,0},{4,6},{6,4},{8,10},{10,8},{12,14},{14,12},{1,3},{3,1},... | collective-permute-start | bytes 147464 | tf_op jit(solution)/shard_map/ppermute | solution.py:238
  13.4 0.0 collective-permute-done.refs_1_
  13.4 0.0 collective-permute-done.1.refs_2_
  13.4 1.0 %scores_early.1 = (f32[48,256]{1,0:T(8,128)S(1)}, bf16[256,256]{1,0:T(8,128)(2,1)S(1)}) custom-call(bf16[256,4096]{1,0:T(8,128)(2,1)S(1)} %get-tuple-element.12.train_ref, s32[1,256]{1,0:T(1,128)S(1)} %get-tuple-element.13.ids_ref, bf16[24,1024]{1,0:T(8,128)(2,1)S(1)} %get-tuple-element.14.refs_0_, bf16[24,1024]{1,0:T(8,128)(2,1)S(1)} %collective-permute-done.refs_1_, ...), custom_call_target="tpu_custom_call" | custom-call | flops 100663296 | bytes 2293760 | tf_op jit(solution)/shard_map/scores_early/pallas_call | solution.py:210
  14.4 0.0 collective-permute-done.4.refs_0_
  14.4 0.7 %collective-permute-done.5.refs_1_ = bf16[24,1024]{1,0:T(8,128)(2,1)S(1)} collective-permute-done((bf16[24,1024]{1,0:T(8,128)(2,1)S(1)}, bf16[24,1024]{1,0:T(8,128)(2,1)S(1)}, u32[]{:S(2)}, u32[]{:S(2)}) %collective-permute-start.5) | collective-permute-done | bytes 49184 | tf_op jit(solution)/shard_map/ppermute | solution.py:238
  15.1 0.9 %collective-permute-done.6.refs_2_ = bf16[24,1024]{1,0:T(8,128)(2,1)S(1)} collective-permute-done((bf16[24,1024]{1,0:T(8,128)(2,1)S(1)}, bf16[24,1024]{1,0:T(8,128)(2,1)S(1)}, u32[]{:S(2)}, u32[]{:S(2)}) %collective-permute-start.6) | collective-permute-done | bytes 49184 | tf_op jit(solution)/shard_map/ppermute | solution.py:238
  16.0 1.0 %scores_late.1 = (f32[24,256]{1,0:T(8,128)S(1)}, f32[24,256]{1,0:T(8,128)S(1)}) custom-call(bf16[256,4096]{1,0:T(8,128)(2,1)S(1)} %get-tuple-element.12.train_ref, bf16[256,256]{1,0:T(8,128)(2,1)S(1)} %get-tuple-element.15.place_ref, f32[48,256]{1,0:T(8,128)S(1)} %get-tuple-element.16.early_ref, bf16[24,1024]{1,0:T(8,128)(2,1)S(1)} %collective-permute-done.4.refs_0_, ...), custom_call_target="tpu_custom_call" | custom-call | flops 100663296 | bytes 2293760 | tf_op jit(solution)/shard_map/scores_late/pallas_call | solution.py:224
  17.0 0.1 collective-permute-start.7
  17.1 1.2 %collective-permute-done.7 = f32[24,256]{1,0:T(8,128)S(1)} collective-permute-done((f32[24,256]{1,0:T(8,128)S(1)}, f32[24,256]{1,0:T(8,128)S(1)}, u32[]{:S(2)}, u32[]{:S(2)}) %collective-permute-start.7) | collective-permute-done | bytes 24608 | tf_op jit(solution)/shard_map/ppermute | solution.py:258
  18.2 0.6 %fusion = bf16[3,256,8]{1,2,0:T(8,128)(2,1)} fusion(f32[24,256]{1,0:T(8,128)S(1)} %get-tuple-element.17, f32[24,256]{1,0:T(8,128)S(1)} %collective-permute-done.7), kind=kLoop, calls=%fused_computation.1 | loop fusion | flops 12288 | bytes 61440 | tf_op jit(solution)/shard_map/transpose | solution.py:260
Async XLA Ops:
  1.8 8.6 %collective-permute-start.2 = (bf16[24,1024]{1,0:T(8,128)(2,1)S(1)}, bf16[24,1024]{1,0:T(8,128)(2,1)S(1)}, u32[]{:S(2)}, u32[]{:S(2)}) collective-permute-start(bf16[24,1024]{1,0:T(8,128)(2,1)S(1)} %get-tuple-element.14.refs_0_), channel_id=1, source_target_pairs={{0,12},{2,14},{4,8},{6,10},{8,4},{10,6},{12,0},{14,2},{1,13},{3,15... | collective-permute-start | bytes 147464 | tf_op jit(solution)/shard_map/ppermute | solution.py:238
  6.9 5.0 %collective-permute-start.3 = (bf16[24,1024]{1,0:T(8,128)(2,1)S(1)}, bf16[24,1024]{1,0:T(8,128)(2,1)S(1)}, u32[]{:S(2)}, u32[]{:S(2)}) collective-permute-start(bf16[24,1024]{1,0:T(8,128)(2,1)S(1)} %get-tuple-element.14.refs_0_), channel_id=1, source_target_pairs={{0,8},{2,10},{4,12},{6,14},{8,0},{10,2},{12,4},{14,6},{1,9},{3,11}... | collective-permute-start | bytes 147464 | tf_op jit(solution)/shard_map/ppermute | solution.py:238
  6.9 6.5 %collective-permute-start = (bf16[24,1024]{1,0:T(8,128)(2,1)S(1)}, bf16[24,1024]{1,0:T(8,128)(2,1)S(1)}, u32[]{:S(2)}, u32[]{:S(2)}) collective-permute-start(bf16[24,1024]{1,0:T(8,128)(2,1)S(1)} %get-tuple-element.14.refs_0_), channel_id=1, source_target_pairs={{0,4},{2,6},{4,0},{6,2},{8,12},{10,14},{12,8},{14,10},{1,5},{3,7},... | collective-permute-start | bytes 147464 | tf_op jit(solution)/shard_map/ppermute | solution.py:238
  7.5 5.8 %collective-permute-start.1 = (bf16[24,1024]{1,0:T(8,128)(2,1)S(1)}, bf16[24,1024]{1,0:T(8,128)(2,1)S(1)}, u32[]{:S(2)}, u32[]{:S(2)}) collective-permute-start(bf16[24,1024]{1,0:T(8,128)(2,1)S(1)} %get-tuple-element.14.refs_0_), channel_id=1, source_target_pairs={{0,2},{2,0},{4,6},{6,4},{8,10},{10,8},{12,14},{14,12},{1,3},{3,1},... | collective-permute-start | bytes 147464 | tf_op jit(solution)/shard_map/ppermute | solution.py:238
  9.2 5.2 %collective-permute-start.4 = (bf16[24,1024]{1,0:T(8,128)(2,1)S(1)}, bf16[24,1024]{1,0:T(8,128)(2,1)S(1)}, u32[]{:S(2)}, u32[]{:S(2)}) collective-permute-start(bf16[24,1024]{1,0:T(8,128)(2,1)S(1)} %get-tuple-element.14.refs_0_), channel_id=1, source_target_pairs={{0,6},{2,4},{4,2},{6,0},{8,14},{10,12},{12,10},{14,8},{1,7},{3,5},... | collective-permute-start | bytes 147464 | tf_op jit(solution)/shard_map/ppermute | solution.py:238
  10.4 4.7 %collective-permute-start.5 = (bf16[24,1024]{1,0:T(8,128)(2,1)S(1)}, bf16[24,1024]{1,0:T(8,128)(2,1)S(1)}, u32[]{:S(2)}, u32[]{:S(2)}) collective-permute-start(bf16[24,1024]{1,0:T(8,128)(2,1)S(1)} %collective-permute-done.2.refs_3_), channel_id=1, source_target_pairs={{0,2},{2,0},{4,6},{6,4},{8,10},{10,8},{12,14},{14,12},{1,3},{3,1},... | collective-permute-start | bytes 147464 | tf_op jit(solution)/shard_map/ppermute | solution.py:238
  11.9 4.1 %collective-permute-start.6 = (bf16[24,1024]{1,0:T(8,128)(2,1)S(1)}, bf16[24,1024]{1,0:T(8,128)(2,1)S(1)}, u32[]{:S(2)}, u32[]{:S(2)}) collective-permute-start(bf16[24,1024]{1,0:T(8,128)(2,1)S(1)} %collective-permute-done.3.refs_4_), channel_id=1, source_target_pairs={{0,2},{2,0},{4,6},{6,4},{8,10},{10,8},{12,14},{14,12},{1,3},{3,1},... | collective-permute-start | bytes 147464 | tf_op jit(solution)/shard_map/ppermute | solution.py:238
  17.0 1.3 %collective-permute-start.7 = (f32[24,256]{1,0:T(8,128)S(1)}, f32[24,256]{1,0:T(8,128)S(1)}, u32[]{:S(2)}, u32[]{:S(2)}) collective-permute-start(f32[24,256]{1,0:T(8,128)S(1)} %get-tuple-element.18), channel_id=1, source_target_pairs={{0,1},{1,0},{2,3},{3,2},{4,5},{5,4},{6,7},{7,6},{8,9},{9,8},{10,11... | collective-permute-start | bytes 73736 | tf_op jit(solution)/shard_map/ppermute | solution.py:258

commit v13 on v12

--- a/solution.py
+++ b/solution.py
@@ -28,15 +28,15 @@
 
 
 def precondition_kernel(
-    order_hbm, q_hbm, out_basis_hbm, in_basis_hbm, eig_hbm, ids_hbm, train_hbm,
-    sent_ref, ids_out_ref, train_out_ref,
+    order_hbm, q_hbm, out_basis_hbm, in_basis_hbm, eig_hbm, ids_hbm,
+    sent_ref, ids_out_ref,
     order_ref, q_ref, out_basis_ref, in_basis_ref, eig_ref, x_scr, even_scr, odd_scr, o_scr, eig_scr, sems,
 ):
     copies = [
         pltpu.make_async_copy(src, dst, sems.at[n])
         for n, (src, dst) in enumerate((
             (order_hbm, order_ref), (q_hbm, q_ref), (in_basis_hbm, in_basis_ref), (out_basis_hbm, out_basis_ref), (eig_hbm, eig_ref),
-            (ids_hbm, ids_out_ref), (train_hbm, train_out_ref),
+            (ids_hbm, ids_out_ref),
         ))
     ]
     for copy in copies:
@@ -94,7 +94,7 @@
         copy.wait()
 
 
-def precondition(block_order, query_grads, out_basis, in_basis, eigenvalues, row_ids, train):
+def precondition(block_order, query_grads, out_basis, in_basis, eigenvalues, row_ids):
     blocks, qdev, width = query_grads.shape
     count = blocks * qdev
     side = out_basis.shape[1]
@@ -110,10 +110,9 @@
         out_shape=(
             jax.ShapeDtypeStruct((count * SEGMENTS, width // SEGMENTS), BF16),
             jax.ShapeDtypeStruct(row_ids.shape, row_ids.dtype),
-            jax.ShapeDtypeStruct(train.shape, train.dtype),
         ),
-        in_specs=[hbm] * 7,
-        out_specs=(vmem, free, free),
+        in_specs=[hbm] * 6,
+        out_specs=(vmem, free),
         scratch_shapes=[
             pltpu.SMEM(block_order.shape, block_order.dtype),
             pltpu.VMEM(query_grads.shape, BF16),
@@ -123,13 +122,13 @@
             rows, rows, rows,
             pltpu.VMEM((side, LANES), F32),
             pltpu.VMEM((side, LANES), F32),
-            pltpu.SemaphoreType.DMA((7,)),
+            pltpu.SemaphoreType.DMA((6,)),
         ],
         compiler_params=pltpu.CompilerParams(vmem_limit_bytes=4 * 2**20),
         name="precondition",
     )(*(
         pltpu.with_memory_space_constraint(x, pltpu.HBM)
-        for x in (block_order, query_grads, out_basis, in_basis, eigenvalues, row_ids, train)
+        for x in (block_order, query_grads, out_basis, in_basis, eigenvalues, row_ids)
     ))
 
 
@@ -145,7 +144,7 @@
     return source ^ (lax.axis_index("layer") * per)
 
 
-def placed_terms(masks, parts, train_ref, place, flat_scr):
+def placed_terms(masks, parts, train_ref, place, flat_scr, copies=()):
     lines, seg = parts[0].shape
     n_row = len(masks)
     per_seg = seg // LANES
@@ -162,19 +161,27 @@
             )
             for c in range(per_seg)
         ], axis=1)
+        if copies:
+            copies[j].wait()
         term = mm_nt(queries.astype(BF16), train_ref[:, j * seg:(j + 1) * seg])
         terms = term if terms is None else terms + term
     a, b, c = split3(terms)
     return mm(a, place) + mm(b, place) + mm(c, place)
 
 
-def early_kernel(masks, train_ref, ids_ref, *refs):
-    parts, (terms_ref, place_ref, flat_scr) = refs[:-3], refs[-3:]
-    rows = train_ref.shape[0]
+def early_kernel(masks, train_hbm, ids_ref, *refs):
+    parts, (terms_ref, place_ref, train_ref, flat_scr, sems) = refs[:-5], refs[-5:]
+    rows, width = train_ref.shape
+    seg = width // SEGMENTS
+    copies = []
+    for j in range(SEGMENTS):
+        columns = (slice(None), pl.ds(j * seg, seg))
+        copies.append(pltpu.make_async_copy(train_hbm.at[columns], train_ref.at[columns], sems.at[j]))
+        copies[j].start()
     here = lax.broadcasted_iota(jnp.int32, (rows, rows), 0)
     place = (here == ids_ref[...]).astype(BF16)
     place_ref[...] = place
-    terms_ref[...] = placed_terms(masks, parts, train_ref, place, flat_scr)
+    terms_ref[...] = placed_terms(masks, parts, train_ref, place, flat_scr, copies)
 
 
 def late_kernel(masks, blocks, qdev, train_ref, place_ref, early_ref, *refs):
@@ -207,19 +214,20 @@
         transcendentals=0,
     )
     flat_scr = pltpu.VMEM((seg // LANES, n_row * lines, LANES), F32)
-    terms, place = pl.pallas_call(
+    terms, place, train = pl.pallas_call(
         functools.partial(early_kernel, masks),
         out_shape=(
             jax.ShapeDtypeStruct((queries, rows), F32),
             jax.ShapeDtypeStruct((rows, rows), BF16),
+            jax.ShapeDtypeStruct(train.shape, train.dtype),
         ),
-        in_specs=[vmem] * (2 + early),
-        out_specs=(vmem, vmem),
-        scratch_shapes=[flat_scr],
+        in_specs=[pl.BlockSpec(memory_space=pltpu.HBM)] + [vmem] * (1 + early),
+        out_specs=(vmem, vmem, vmem),
+        scratch_shapes=[flat_scr, pltpu.SemaphoreType.DMA((SEGMENTS,))],
         compiler_params=params,
         cost_estimate=cost,
         name="scores_early",
-    )(train, row_ids, *parts[:early])
+    )(pltpu.with_memory_space_constraint(train, pltpu.HBM), row_ids, *parts[:early])
     out = jax.ShapeDtypeStruct((queries // 2, rows), F32)
     return pl.pallas_call(
         functools.partial(late_kernel, masks[early:] + masks[:early], blocks, qdev),
@@ -249,10 +257,10 @@
     def body(train_grads, query_grads, out_basis, in_basis, eigenvalues, block_order, row_ids):
         blocks, qdev, _, width = query_grads.shape
         rows = train_grads.shape[0]
-        own, row_ids, train = precondition(
-            block_order, query_grads.reshape(blocks, qdev, width), out_basis, in_basis, eigenvalues, row_ids,
-            train_grads.reshape(rows, width),
+        own, row_ids = precondition(
+            block_order, query_grads.reshape(blocks, qdev, width), out_basis, in_basis, eigenvalues, row_ids
         )
+        train = train_grads.reshape(rows, width)
         parts, early = gather(own)
         mine, other = scores(tuple(parts), early, train, row_ids, tuple(parts.values()), blocks, qdev)
         got = lax.ppermute(other, "layer", [(0, 1), (1, 0)])

time: 19 us -> 19.2 us (1.011)
  Pallas kernels: 3.76 us -> 5.53 us
  waiting for transfers between devices: 2.79 us -> 1.2 us
    pallas_call x1, Pallas kernels: 0.99 us -> 2.77 us  [scores(): pl.pallas_call(functools.partial(early_kernel, masks), out_shape=(jax.Sha...]
    ppermute x7, waiting for transfers between devices: 1.61 us -> 0.02 us  [swap(): return lax.ppermute(x, 'row', [(r, r ^ mask) for r in range(n_row)])]
  transfers between devices with their start and end apart: 8 -> 8, of which waited for: 3 -> 1; matrix products, arithmetic and copies ran while one was open for 0% -> 0% of each run, Pallas kernels for 5% -> 14%
where the time goes in v13:
time: 19.2 us; the launch traced here: 19.1 us
  starting transfers between devices  11.7 us (61%)
  Pallas kernels  5.53 us (29%)
  waiting for transfers between devices  1.2 us (6%)
  other arithmetic  0.6 us (3%)
    ppermute x7, starting transfers between devices, swap(): return lax.ppermute(x, 'row', [(r, r ^ mask) for r in range(n_row)])  11.6 us
    pallas_call x1, Pallas kernels, scores(): pl.pallas_call(functools.partial(early_kernel, masks), out_shape=(jax.Sha...  2.77 us
    pallas_call x1, Pallas kernels, precondition(): pl.pallas_call(precondition_kernel, out_shape=(jax.ShapeDtypeStruct((coun...  1.75 us
    ppermute x1, waiting for transfers between devices, body(): got = lax.ppermute(other, 'layer', [(0, 1), (1, 0)])  1.18 us
    pallas_call x1, Pallas kernels, scores(): pl.pallas_call(functools.partial(late_kernel, masks[early:] + masks[:earl...  1 us
    transpose x1, other arithmetic, body(): return total.reshape(blocks, -1, rows).transpose(0, 2, 1)  0.6 us
  transfers between devices with their start and end apart: 8, of which 1 were waited for; matrix products, arithmetic and copies ran while one was open for 0% of the time, Pallas kernels for 14%

profile of v13, /device:TPU:0, one launch (start us, length us, event | category | flops | bytes accessed | tf_op | source)
XLA Modules:
  0.0 19.1 jit_solution(5181480036843705276)
XLA Ops:
  0.0 1.8 %precondition.1 = (bf16[24,1024]{1,0:T(8,128)(2,1)S(1)}, s32[1,256]{1,0:T(1,128)S(1)}) custom-call(s32[3]{0:T(128)} %order_hbm.1, bf16[3,64,128]{2,1,0:T(8,128)(2,1)} %bitcast.12, f32[1,64,64]{2,1,0:T(8,128)} %out_basis_hbm.1, f32[1,64,64]{2,1,0:T(8,128)} %in_basis_hbm.1, f32[32,128]{1,0:T(8,128)} %bitcast.13, s32[1,256]{1,0:T(1,128)} %ids_hbm.1), custom_call_target="tpu_custom_call" | custom-call | tf_op jit(solution)/shard_map/precondition/pallas_call | solution.py:108
  1.8 5.1 %collective-permute-start.2 = (bf16[24,1024]{1,0:T(8,128)(2,1)S(1)}, bf16[24,1024]{1,0:T(8,128)(2,1)S(1)}, u32[]{:S(2)}, u32[]{:S(2)}) collective-permute-start(bf16[24,1024]{1,0:T(8,128)(2,1)S(1)} %get-tuple-element.13.refs_0_), channel_id=1, source_target_pairs={{0,12},{2,14},{4,8},{6,10},{8,4},{10,6},{12,0},{14,2},{1,13},{3,15... | collective-permute-start | bytes 147464 | tf_op jit(solution)/shard_map/ppermute | solution.py:246
  6.9 0.0 collective-permute-start.3
  6.9 0.6 %collective-permute-start = (bf16[24,1024]{1,0:T(8,128)(2,1)S(1)}, bf16[24,1024]{1,0:T(8,128)(2,1)S(1)}, u32[]{:S(2)}, u32[]{:S(2)}) collective-permute-start(bf16[24,1024]{1,0:T(8,128)(2,1)S(1)} %get-tuple-element.13.refs_0_), channel_id=1, source_target_pairs={{0,4},{2,6},{4,0},{6,2},{8,12},{10,14},{12,8},{14,10},{1,5},{3,7},... | collective-permute-start | bytes 147464 | tf_op jit(solution)/shard_map/ppermute | solution.py:246
  7.5 1.6 %collective-permute-start.1 = (bf16[24,1024]{1,0:T(8,128)(2,1)S(1)}, bf16[24,1024]{1,0:T(8,128)(2,1)S(1)}, u32[]{:S(2)}, u32[]{:S(2)}) collective-permute-start(bf16[24,1024]{1,0:T(8,128)(2,1)S(1)} %get-tuple-element.13.refs_0_), channel_id=1, source_target_pairs={{0,2},{2,0},{4,6},{6,4},{8,10},{10,8},{12,14},{14,12},{1,3},{3,1},... | collective-permute-start | bytes 147464 | tf_op jit(solution)/shard_map/ppermute | solution.py:246
  9.2 1.2 %collective-permute-start.4 = (bf16[24,1024]{1,0:T(8,128)(2,1)S(1)}, bf16[24,1024]{1,0:T(8,128)(2,1)S(1)}, u32[]{:S(2)}, u32[]{:S(2)}) collective-permute-start(bf16[24,1024]{1,0:T(8,128)(2,1)S(1)} %get-tuple-element.13.refs_0_), channel_id=1, source_target_pairs={{0,6},{2,4},{4,2},{6,0},{8,14},{10,12},{12,10},{14,8},{1,7},{3,5},... | collective-permute-start | bytes 147464 | tf_op jit(solution)/shard_map/ppermute | solution.py:246
  10.4 0.0 collective-permute-done.2.refs_3_
  10.4 1.5 %collective-permute-start.5 = (bf16[24,1024]{1,0:T(8,128)(2,1)S(1)}, bf16[24,1024]{1,0:T(8,128)(2,1)S(1)}, u32[]{:S(2)}, u32[]{:S(2)}) collective-permute-start(bf16[24,1024]{1,0:T(8,128)(2,1)S(1)} %collective-permute-done.2.refs_3_), channel_id=1, source_target_pairs={{0,2},{2,0},{4,6},{6,4},{8,10},{10,8},{12,14},{14,12},{1,3},{3,1},... | collective-permute-start | bytes 147464 | tf_op jit(solution)/shard_map/ppermute | solution.py:246
  11.9 0.0 collective-permute-done.3.refs_4_
  11.9 1.5 %collective-permute-start.6 = (bf16[24,1024]{1,0:T(8,128)(2,1)S(1)}, bf16[24,1024]{1,0:T(8,128)(2,1)S(1)}, u32[]{:S(2)}, u32[]{:S(2)}) collective-permute-start(bf16[24,1024]{1,0:T(8,128)(2,1)S(1)} %collective-permute-done.3.refs_4_), channel_id=1, source_target_pairs={{0,2},{2,0},{4,6},{6,4},{8,10},{10,8},{12,14},{14,12},{1,3},{3,1},... | collective-permute-start | bytes 147464 | tf_op jit(solution)/shard_map/ppermute | solution.py:246
  13.4 0.0 collective-permute-done.refs_1_
  13.4 0.0 collective-permute-done.1.refs_2_
  13.4 2.8 %scores_early.1 = (f32[48,256]{1,0:T(8,128)S(1)}, bf16[256,256]{1,0:T(8,128)(2,1)S(1)}, bf16[256,4096]{1,0:T(8,128)(2,1)S(1)}) custom-call(bf16[256,4096]{1,0:T(8,128)(2,1)} %bitcast.11, s32[1,256]{1,0:T(1,128)S(1)} %get-tuple-element.12.ids_ref, bf16[24,1024]{1,0:T(8,128)(2,1)S(1)} %get-tuple-element.13.refs_0_, ...), custom_call_target="tpu_custom_call" | custom-call | flops 100663296 | bytes 2293760 | tf_op jit(solution)/shard_map/scores_early/pallas_call | solution.py:217
  16.1 0.0 collective-permute-done.4.refs_0_
  16.2 0.0 collective-permute-done.5.refs_1_
  16.2 0.0 collective-permute-done.6.refs_2_
  16.2 1.0 %scores_late.1 = (f32[24,256]{1,0:T(8,128)S(1)}, f32[24,256]{1,0:T(8,128)S(1)}) custom-call(bf16[256,4096]{1,0:T(8,128)(2,1)S(1)} %get-tuple-element.14.train_ref, bf16[256,256]{1,0:T(8,128)(2,1)S(1)} %get-tuple-element.15.place_ref, f32[48,256]{1,0:T(8,128)S(1)} %get-tuple-element.16.early_ref, bf16[24,1024]{1,0:T(8,128)(2,1)S(1)} %collective-permute-done.4.refs_0_, ...), custom_call_target="tpu_custom_call" | custom-call | flops 100663296 | bytes 2293760 | tf_op jit(solution)/shard_map/scores_late/pallas_call | solution.py:232
  17.2 0.1 collective-permute-start.7
  17.3 1.2 %collective-permute-done.7 = f32[24,256]{1,0:T(8,128)S(1)} collective-permute-done((f32[24,256]{1,0:T(8,128)S(1)}, f32[24,256]{1,0:T(8,128)S(1)}, u32[]{:S(2)}, u32[]{:S(2)}) %collective-permute-start.7) | collective-permute-done | bytes 24608 | tf_op jit(solution)/shard_map/ppermute | solution.py:266
  18.5 0.6 %fusion = bf16[3,256,8]{1,2,0:T(8,128)(2,1)} fusion(f32[24,256]{1,0:T(8,128)S(1)} %get-tuple-element.17, f32[24,256]{1,0:T(8,128)S(1)} %collective-permute-done.7), kind=kLoop, calls=%fused_computation.1 | loop fusion | flops 12288 | bytes 61440 | tf_op jit(solution)/shard_map/transpose | solution.py:268
Async XLA Ops:
  1.8 8.6 %collective-permute-start.2 = (bf16[24,1024]{1,0:T(8,128)(2,1)S(1)}, bf16[24,1024]{1,0:T(8,128)(2,1)S(1)}, u32[]{:S(2)}, u32[]{:S(2)}) collective-permute-start(bf16[24,1024]{1,0:T(8,128)(2,1)S(1)} %get-tuple-element.13.refs_0_), channel_id=1, source_target_pairs={{0,12},{2,14},{4,8},{6,10},{8,4},{10,6},{12,0},{14,2},{1,13},{3,15... | collective-permute-start | bytes 147464 | tf_op jit(solution)/shard_map/ppermute | solution.py:246
  6.9 5.0 %collective-permute-start.3 = (bf16[24,1024]{1,0:T(8,128)(2,1)S(1)}, bf16[24,1024]{1,0:T(8,128)(2,1)S(1)}, u32[]{:S(2)}, u32[]{:S(2)}) collective-permute-start(bf16[24,1024]{1,0:T(8,128)(2,1)S(1)} %get-tuple-element.13.refs_0_), channel_id=1, source_target_pairs={{0,8},{2,10},{4,12},{6,14},{8,0},{10,2},{12,4},{14,6},{1,9},{3,11}... | collective-permute-start | bytes 147464 | tf_op jit(solution)/shard_map/ppermute | solution.py:246
  6.9 6.5 %collective-permute-start = (bf16[24,1024]{1,0:T(8,128)(2,1)S(1)}, bf16[24,1024]{1,0:T(8,128)(2,1)S(1)}, u32[]{:S(2)}, u32[]{:S(2)}) collective-permute-start(bf16[24,1024]{1,0:T(8,128)(2,1)S(1)} %get-tuple-element.13.refs_0_), channel_id=1, source_target_pairs={{0,4},{2,6},{4,0},{6,2},{8,12},{10,14},{12,8},{14,10},{1,5},{3,7},... | collective-permute-start | bytes 147464 | tf_op jit(solution)/shard_map/ppermute | solution.py:246
  7.5 5.8 %collective-permute-start.1 = (bf16[24,1024]{1,0:T(8,128)(2,1)S(1)}, bf16[24,1024]{1,0:T(8,128)(2,1)S(1)}, u32[]{:S(2)}, u32[]{:S(2)}) collective-permute-start(bf16[24,1024]{1,0:T(8,128)(2,1)S(1)} %get-tuple-element.13.refs_0_), channel_id=1, source_target_pairs={{0,2},{2,0},{4,6},{6,4},{8,10},{10,8},{12,14},{14,12},{1,3},{3,1},... | collective-permute-start | bytes 147464 | tf_op jit(solution)/shard_map/ppermute | solution.py:246
  9.2 7.0 %collective-permute-start.4 = (bf16[24,1024]{1,0:T(8,128)(2,1)S(1)}, bf16[24,1024]{1,0:T(8,128)(2,1)S(1)}, u32[]{:S(2)}, u32[]{:S(2)}) collective-permute-start(bf16[24,1024]{1,0:T(8,128)(2,1)S(1)} %get-tuple-element.13.refs_0_), channel_id=1, source_target_pairs={{0,6},{2,4},{4,2},{6,0},{8,14},{10,12},{12,10},{14,8},{1,7},{3,5},... | collective-permute-start | bytes 147464 | tf_op jit(solution)/shard_map/ppermute | solution.py:246
  10.4 5.8 %collective-permute-start.5 = (bf16[24,1024]{1,0:T(8,128)(2,1)S(1)}, bf16[24,1024]{1,0:T(8,128)(2,1)S(1)}, u32[]{:S(2)}, u32[]{:S(2)}) collective-permute-start(bf16[24,1024]{1,0:T(8,128)(2,1)S(1)} %collective-permute-done.2.refs_3_), channel_id=1, source_target_pairs={{0,2},{2,0},{4,6},{6,4},{8,10},{10,8},{12,14},{14,12},{1,3},{3,1},... | collective-permute-start | bytes 147464 | tf_op jit(solution)/shard_map/ppermute | solution.py:246
  11.9 4.3 %collective-permute-start.6 = (bf16[24,1024]{1,0:T(8,128)(2,1)S(1)}, bf16[24,1024]{1,0:T(8,128)(2,1)S(1)}, u32[]{:S(2)}, u32[]{:S(2)}) collective-permute-start(bf16[24,1024]{1,0:T(8,128)(2,1)S(1)} %collective-permute-done.3.refs_4_), channel_id=1, source_target_pairs={{0,2},{2,0},{4,6},{6,4},{8,10},{10,8},{12,14},{14,12},{1,3},{3,1},... | collective-permute-start | bytes 147464 | tf_op jit(solution)/shard_map/ppermute | solution.py:246
  17.2 1.3 %collective-permute-start.7 = (f32[24,256]{1,0:T(8,128)S(1)}, f32[24,256]{1,0:T(8,128)S(1)}, u32[]{:S(2)}, u32[]{:S(2)}) collective-permute-start(f32[24,256]{1,0:T(8,128)S(1)} %get-tuple-element.18), channel_id=1, source_target_pairs={{0,1},{1,0},{2,3},{3,2},{4,5},{5,4},{6,7},{7,6},{8,9},{9,8},{10,11... | collective-permute-start | bytes 73736 | tf_op jit(solution)/shard_map/ppermute | solution.py:266

commit v14 on v12

--- a/solution.py
+++ b/solution.py
@@ -35,13 +35,13 @@
     copies = [
         pltpu.make_async_copy(src, dst, sems.at[n])
         for n, (src, dst) in enumerate((
-            (order_hbm, order_ref), (q_hbm, q_ref), (in_basis_hbm, in_basis_ref), (out_basis_hbm, out_basis_ref), (eig_hbm, eig_ref),
-            (ids_hbm, ids_out_ref), (train_hbm, train_out_ref),
+            (in_basis_hbm, in_basis_ref), (q_hbm, q_ref), (out_basis_hbm, out_basis_ref), (eig_hbm, eig_ref),
+            (order_hbm, order_ref), (ids_hbm, ids_out_ref), (train_hbm, train_out_ref),
         ))
     ]
     for copy in copies:
         copy.start()
-    for copy in copies[:5]:
+    for copy in copies[:2]:
         copy.wait()
     blocks, lines, _ = q_ref.shape
     chunks = eig_ref.shape[0]
@@ -49,6 +49,16 @@
     half = side // 2
     qdev = lines // chunks
     count = blocks * qdev
+    i_hi, i_lo = split2(in_basis_ref[0])
+    none = jnp.zeros_like(i_hi)
+    raw = jnp.concatenate([q_ref[b] for b in range(blocks)], axis=0)
+    raw2 = jnp.concatenate([raw, raw], axis=1)
+    even = mm(raw2, jnp.concatenate([i_hi, none, i_lo, none], axis=0))
+    odd = mm(raw2, jnp.concatenate([none, i_hi, none, i_lo], axis=0))
+    even_scr[:, :side] = even
+    odd_scr[:, :side] = odd
+    for copy in copies[2:4]:
+        copy.wait()
     scale = 1.0 / (eig_ref[...] + DAMPING)
     eig_scr[pl.ds(0, half, stride=2), :side] = scale[:, :side]
     eig_scr[pl.ds(1, half, stride=2), :side] = scale[:, side:]
@@ -61,14 +71,6 @@
     t_hi, t_lo = split2(basis.T)
     left = jnp.concatenate([t_hi, t_hi, t_lo], axis=1)
     back = jnp.concatenate([b_hi, b_hi, b_lo], axis=1)
-    i_hi, i_lo = split2(in_basis_ref[0])
-    none = jnp.zeros_like(i_hi)
-    raw = jnp.concatenate([q_ref[order_ref[j]] for j in range(blocks)], axis=0)
-    raw2 = jnp.concatenate([raw, raw], axis=1)
-    even = mm(raw2, jnp.concatenate([i_hi, none, i_lo, none], axis=0))
-    odd = mm(raw2, jnp.concatenate([none, i_hi, none, i_lo], axis=0))
-    even_scr[:, :side] = even
-    odd_scr[:, :side] = odd
     evens, odds = [], []
     for q in range(count):
         rows = pl.ds(q // qdev * lines + q % qdev, half, stride=qdev)
@@ -85,11 +87,13 @@
         w_lo = jnp.concatenate([none, i_lo] if lower else [i_lo, none], axis=0)
         term = mm_nt(hi, w_hi) + mm_nt(lo, w_hi) + mm_nt(hi, w_lo)
         total = term if total is None else total + term
-    x_scr[...] = total
+    x_scr[...] = total.reshape(x_scr.shape)
+    copies[4].wait()
     per = chunks // SEGMENTS
+    lines = qdev * SEGMENTS
     for c in range(per):
-        piece = x_scr[pl.ds(c, count * SEGMENTS, stride=per), :].astype(BF16)
-        sent_ref[:, c * LANES:(c + 1) * LANES] = piece
+        piece = [x_scr[order_ref[j], pl.ds(c, lines, stride=per), :] for j in range(blocks)]
+        sent_ref[:, c * LANES:(c + 1) * LANES] = jnp.concatenate(piece, axis=0).astype(BF16)
     for copy in copies[5:]:
         copy.wait()
 
@@ -120,7 +124,8 @@
             pltpu.VMEM(out_basis.shape, F32),
             pltpu.VMEM(in_basis.shape, F32),
             pltpu.VMEM(eigenvalues.shape, F32),
-            rows, rows, rows,
+            pltpu.VMEM((blocks, qdev * chunks, LANES), F32),
+            rows, rows,
             pltpu.VMEM((side, LANES), F32),
             pltpu.VMEM((side, LANES), F32),
             pltpu.SemaphoreType.DMA((7,)),

time: 19 us -> 19.2 us (1.011)
  no operation moved by 1% of the time
where the time goes in v14:
time: 19.2 us; the launch traced here: 19 us
  starting transfers between devices  11.6 us (60%)
  Pallas kernels  3.95 us (21%)
  waiting for transfers between devices  2.79 us (15%)
  other arithmetic  0.6 us (3%)
    ppermute x7, starting transfers between devices, swap(): return lax.ppermute(x, 'row', [(r, r ^ mask) for r in range(n_row)])  11.6 us
    pallas_call x1, Pallas kernels, precondition(): pl.pallas_call(precondition_kernel, out_shape=(jax.ShapeDtypeStruct((coun...  1.95 us
    ppermute x7, waiting for transfers between devices, swap(): return lax.ppermute(x, 'row', [(r, r ^ mask) for r in range(n_row)])  1.61 us
    ppermute x1, waiting for transfers between devices, body(): got = lax.ppermute(other, 'layer', [(0, 1), (1, 0)])  1.18 us
    pallas_call x1, Pallas kernels, scores(): pl.pallas_call(functools.partial(late_kernel, masks[early:] + masks[:earl...  1.01 us
    pallas_call x1, Pallas kernels, scores(): pl.pallas_call(functools.partial(early_kernel, masks), out_shape=(jax.Sha...  0.99 us
    transpose x1, other arithmetic, body(): return total.reshape(blocks, -1, rows).transpose(0, 2, 1)  0.6 us
  transfers between devices with their start and end apart: 8, of which 3 were waited for; matrix products, arithmetic and copies ran while one was open for 0% of the time, Pallas kernels for 5%

profile of v14, /device:TPU:0, one launch (start us, length us, event | category | flops | bytes accessed | tf_op | source)
XLA Modules:
  0.0 19.0 jit_solution(6477455732490233360)
XLA Ops:
  0.0 1.9 %precondition.1 = (bf16[24,1024]{1,0:T(8,128)(2,1)S(1)}, s32[1,256]{1,0:T(1,128)S(1)}, bf16[256,4096]{1,0:T(8,128)(2,1)S(1)}) custom-call(s32[3]{0:T(128)} %order_hbm.1, bf16[3,64,128]{2,1,0:T(8,128)(2,1)} %bitcast.12, f32[1,64,64]{2,1,0:T(8,128)} %out_basis_hbm.1, f32[1,64,64]{2,1,0:T(8,128)} %in_basis_hbm.1, f32[32,128]{1,0:T(8,128)} %bitcast.13, ...), custom_call_target="tpu_custom_call" | custom-call | tf_op jit(solution)/shard_map/precondition/pallas_call | solution.py:112
  2.0 5.1 %collective-permute-start.2 = (bf16[24,1024]{1,0:T(8,128)(2,1)S(1)}, bf16[24,1024]{1,0:T(8,128)(2,1)S(1)}, u32[]{:S(2)}, u32[]{:S(2)}) collective-permute-start(bf16[24,1024]{1,0:T(8,128)(2,1)S(1)} %get-tuple-element.14.refs_0_), channel_id=1, source_target_pairs={{0,12},{2,14},{4,8},{6,10},{8,4},{10,6},{12,0},{14,2},{1,13},{3,15... | collective-permute-start | bytes 147464 | tf_op jit(solution)/shard_map/ppermute | solution.py:243
  7.1 0.0 collective-permute-start.3
  7.1 0.6 %collective-permute-start = (bf16[24,1024]{1,0:T(8,128)(2,1)S(1)}, bf16[24,1024]{1,0:T(8,128)(2,1)S(1)}, u32[]{:S(2)}, u32[]{:S(2)}) collective-permute-start(bf16[24,1024]{1,0:T(8,128)(2,1)S(1)} %get-tuple-element.14.refs_0_), channel_id=1, source_target_pairs={{0,4},{2,6},{4,0},{6,2},{8,12},{10,14},{12,8},{14,10},{1,5},{3,7},... | collective-permute-start | bytes 147464 | tf_op jit(solution)/shard_map/ppermute | solution.py:243
  7.7 1.6 %collective-permute-start.1 = (bf16[24,1024]{1,0:T(8,128)(2,1)S(1)}, bf16[24,1024]{1,0:T(8,128)(2,1)S(1)}, u32[]{:S(2)}, u32[]{:S(2)}) collective-permute-start(bf16[24,1024]{1,0:T(8,128)(2,1)S(1)} %get-tuple-element.14.refs_0_), channel_id=1, source_target_pairs={{0,2},{2,0},{4,6},{6,4},{8,10},{10,8},{12,14},{14,12},{1,3},{3,1},... | collective-permute-start | bytes 147464 | tf_op jit(solution)/shard_map/ppermute | solution.py:243
  9.3 1.2 %collective-permute-start.4 = (bf16[24,1024]{1,0:T(8,128)(2,1)S(1)}, bf16[24,1024]{1,0:T(8,128)(2,1)S(1)}, u32[]{:S(2)}, u32[]{:S(2)}) collective-permute-start(bf16[24,1024]{1,0:T(8,128)(2,1)S(1)} %get-tuple-element.14.refs_0_), channel_id=1, source_target_pairs={{0,6},{2,4},{4,2},{6,0},{8,14},{10,12},{12,10},{14,8},{1,7},{3,5},... | collective-permute-start | bytes 147464 | tf_op jit(solution)/shard_map/ppermute | solution.py:243
  10.6 0.0 collective-permute-done.2.refs_3_
  10.6 1.5 %collective-permute-start.5 = (bf16[24,1024]{1,0:T(8,128)(2,1)S(1)}, bf16[24,1024]{1,0:T(8,128)(2,1)S(1)}, u32[]{:S(2)}, u32[]{:S(2)}) collective-permute-start(bf16[24,1024]{1,0:T(8,128)(2,1)S(1)} %collective-permute-done.2.refs_3_), channel_id=1, source_target_pairs={{0,2},{2,0},{4,6},{6,4},{8,10},{10,8},{12,14},{14,12},{1,3},{3,1},... | collective-permute-start | bytes 147464 | tf_op jit(solution)/shard_map/ppermute | solution.py:243
  12.1 0.0 collective-permute-done.3.refs_4_
  12.1 1.5 %collective-permute-start.6 = (bf16[24,1024]{1,0:T(8,128)(2,1)S(1)}, bf16[24,1024]{1,0:T(8,128)(2,1)S(1)}, u32[]{:S(2)}, u32[]{:S(2)}) collective-permute-start(bf16[24,1024]{1,0:T(8,128)(2,1)S(1)} %collective-permute-done.3.refs_4_), channel_id=1, source_target_pairs={{0,2},{2,0},{4,6},{6,4},{8,10},{10,8},{12,14},{14,12},{1,3},{3,1},... | collective-permute-start | bytes 147464 | tf_op jit(solution)/shard_map/ppermute | solution.py:243
  13.5 0.0 collective-permute-done.refs_1_
  13.6 0.0 collective-permute-done.1.refs_2_
  13.6 1.0 %scores_early.1 = (f32[48,256]{1,0:T(8,128)S(1)}, bf16[256,256]{1,0:T(8,128)(2,1)S(1)}) custom-call(bf16[256,4096]{1,0:T(8,128)(2,1)S(1)} %get-tuple-element.12.train_ref, s32[1,256]{1,0:T(1,128)S(1)} %get-tuple-element.13.ids_ref, bf16[24,1024]{1,0:T(8,128)(2,1)S(1)} %get-tuple-element.14.refs_0_, bf16[24,1024]{1,0:T(8,128)(2,1)S(1)} %collective-permute-done.refs_1_, ...), custom_call_target="tpu_custom_call" | custom-call | flops 100663296 | bytes 2293760 | tf_op jit(solution)/shard_map/scores_early/pallas_call | solution.py:215
  14.5 0.0 collective-permute-done.4.refs_0_
  14.6 0.7 %collective-permute-done.5.refs_1_ = bf16[24,1024]{1,0:T(8,128)(2,1)S(1)} collective-permute-done((bf16[24,1024]{1,0:T(8,128)(2,1)S(1)}, bf16[24,1024]{1,0:T(8,128)(2,1)S(1)}, u32[]{:S(2)}, u32[]{:S(2)}) %collective-permute-start.5) | collective-permute-done | bytes 49184 | tf_op jit(solution)/shard_map/ppermute | solution.py:243
  15.3 0.9 %collective-permute-done.6.refs_2_ = bf16[24,1024]{1,0:T(8,128)(2,1)S(1)} collective-permute-done((bf16[24,1024]{1,0:T(8,128)(2,1)S(1)}, bf16[24,1024]{1,0:T(8,128)(2,1)S(1)}, u32[]{:S(2)}, u32[]{:S(2)}) %collective-permute-start.6) | collective-permute-done | bytes 49184 | tf_op jit(solution)/shard_map/ppermute | solution.py:243
  16.2 1.0 %scores_late.1 = (f32[24,256]{1,0:T(8,128)S(1)}, f32[24,256]{1,0:T(8,128)S(1)}) custom-call(bf16[256,4096]{1,0:T(8,128)(2,1)S(1)} %get-tuple-element.12.train_ref, bf16[256,256]{1,0:T(8,128)(2,1)S(1)} %get-tuple-element.15.place_ref, f32[48,256]{1,0:T(8,128)S(1)} %get-tuple-element.16.early_ref, bf16[24,1024]{1,0:T(8,128)(2,1)S(1)} %collective-permute-done.4.refs_0_, ...), custom_call_target="tpu_custom_call" | custom-call | flops 100663296 | bytes 2293760 | tf_op jit(solution)/shard_map/scores_late/pallas_call | solution.py:229
  17.2 0.1 collective-permute-start.7
  17.2 1.2 %collective-permute-done.7 = f32[24,256]{1,0:T(8,128)S(1)} collective-permute-done((f32[24,256]{1,0:T(8,128)S(1)}, f32[24,256]{1,0:T(8,128)S(1)}, u32[]{:S(2)}, u32[]{:S(2)}) %collective-permute-start.7) | collective-permute-done | bytes 24608 | tf_op jit(solution)/shard_map/ppermute | solution.py:263
  18.4 0.6 %fusion = bf16[3,256,8]{1,2,0:T(8,128)(2,1)} fusion(f32[24,256]{1,0:T(8,128)S(1)} %get-tuple-element.17, f32[24,256]{1,0:T(8,128)S(1)} %collective-permute-done.7), kind=kLoop, calls=%fused_computation.1 | loop fusion | flops 12288 | bytes 61440 | tf_op jit(solution)/shard_map/transpose | solution.py:265
Async XLA Ops:
  2.0 8.6 %collective-permute-start.2 = (bf16[24,1024]{1,0:T(8,128)(2,1)S(1)}, bf16[24,1024]{1,0:T(8,128)(2,1)S(1)}, u32[]{:S(2)}, u32[]{:S(2)}) collective-permute-start(bf16[24,1024]{1,0:T(8,128)(2,1)S(1)} %get-tuple-element.14.refs_0_), channel_id=1, source_target_pairs={{0,12},{2,14},{4,8},{6,10},{8,4},{10,6},{12,0},{14,2},{1,13},{3,15... | collective-permute-start | bytes 147464 | tf_op jit(solution)/shard_map/ppermute | solution.py:243
  7.1 5.0 %collective-permute-start.3 = (bf16[24,1024]{1,0:T(8,128)(2,1)S(1)}, bf16[24,1024]{1,0:T(8,128)(2,1)S(1)}, u32[]{:S(2)}, u32[]{:S(2)}) collective-permute-start(bf16[24,1024]{1,0:T(8,128)(2,1)S(1)} %get-tuple-element.14.refs_0_), channel_id=1, source_target_pairs={{0,8},{2,10},{4,12},{6,14},{8,0},{10,2},{12,4},{14,6},{1,9},{3,11}... | collective-permute-start | bytes 147464 | tf_op jit(solution)/shard_map/ppermute | solution.py:243
  7.1 6.5 %collective-permute-start = (bf16[24,1024]{1,0:T(8,128)(2,1)S(1)}, bf16[24,1024]{1,0:T(8,128)(2,1)S(1)}, u32[]{:S(2)}, u32[]{:S(2)}) collective-permute-start(bf16[24,1024]{1,0:T(8,128)(2,1)S(1)} %get-tuple-element.14.refs_0_), channel_id=1, source_target_pairs={{0,4},{2,6},{4,0},{6,2},{8,12},{10,14},{12,8},{14,10},{1,5},{3,7},... | collective-permute-start | bytes 147464 | tf_op jit(solution)/shard_map/ppermute | solution.py:243
  7.7 5.8 %collective-permute-start.1 = (bf16[24,1024]{1,0:T(8,128)(2,1)S(1)}, bf16[24,1024]{1,0:T(8,128)(2,1)S(1)}, u32[]{:S(2)}, u32[]{:S(2)}) collective-permute-start(bf16[24,1024]{1,0:T(8,128)(2,1)S(1)} %get-tuple-element.14.refs_0_), channel_id=1, source_target_pairs={{0,2},{2,0},{4,6},{6,4},{8,10},{10,8},{12,14},{14,12},{1,3},{3,1},... | collective-permute-start | bytes 147464 | tf_op jit(solution)/shard_map/ppermute | solution.py:243
  9.3 5.2 %collective-permute-start.4 = (bf16[24,1024]{1,0:T(8,128)(2,1)S(1)}, bf16[24,1024]{1,0:T(8,128)(2,1)S(1)}, u32[]{:S(2)}, u32[]{:S(2)}) collective-permute-start(bf16[24,1024]{1,0:T(8,128)(2,1)S(1)} %get-tuple-element.14.refs_0_), channel_id=1, source_target_pairs={{0,6},{2,4},{4,2},{6,0},{8,14},{10,12},{12,10},{14,8},{1,7},{3,5},... | collective-permute-start | bytes 147464 | tf_op jit(solution)/shard_map/ppermute | solution.py:243
  10.6 4.7 %collective-permute-start.5 = (bf16[24,1024]{1,0:T(8,128)(2,1)S(1)}, bf16[24,1024]{1,0:T(8,128)(2,1)S(1)}, u32[]{:S(2)}, u32[]{:S(2)}) collective-permute-start(bf16[24,1024]{1,0:T(8,128)(2,1)S(1)} %collective-permute-done.2.refs_3_), channel_id=1, source_target_pairs={{0,2},{2,0},{4,6},{6,4},{8,10},{10,8},{12,14},{14,12},{1,3},{3,1},... | collective-permute-start | bytes 147464 | tf_op jit(solution)/shard_map/ppermute | solution.py:243
  12.1 4.1 %collective-permute-start.6 = (bf16[24,1024]{1,0:T(8,128)(2,1)S(1)}, bf16[24,1024]{1,0:T(8,128)(2,1)S(1)}, u32[]{:S(2)}, u32[]{:S(2)}) collective-permute-start(bf16[24,1024]{1,0:T(8,128)(2,1)S(1)} %collective-permute-done.3.refs_4_), channel_id=1, source_target_pairs={{0,2},{2,0},{4,6},{6,4},{8,10},{10,8},{12,14},{14,12},{1,3},{3,1},... | collective-permute-start | bytes 147464 | tf_op jit(solution)/shard_map/ppermute | solution.py:243
  17.2 1.3 %collective-permute-start.7 = (f32[24,256]{1,0:T(8,128)S(1)}, f32[24,256]{1,0:T(8,128)S(1)}, u32[]{:S(2)}, u32[]{:S(2)}) collective-permute-start(f32[24,256]{1,0:T(8,128)S(1)} %get-tuple-element.18), channel_id=1, source_target_pairs={{0,1},{1,0},{2,3},{3,2},{4,5},{5,4},{6,7},{7,6},{8,9},{9,8},{10,11... | collective-permute-start | bytes 73736 | tf_op jit(solution)/shard_map/ppermute | solution.py:263

commit v15 on v12

--- a/solution.py
+++ b/solution.py
@@ -47,12 +47,17 @@
     chunks = eig_ref.shape[0]
     side = out_basis_ref.shape[1]
     half = side // 2
-    qdev = lines // chunks
-    count = blocks * qdev
+    count = blocks * (lines // chunks)
+    left_lanes = lax.broadcasted_iota(jnp.int32, (half, LANES), 1) < side
+
+    def swapped(x):
+        return jnp.concatenate([x[:, side:], x[:, :side]], axis=1)
+
     scale = 1.0 / (eig_ref[...] + DAMPING)
-    eig_scr[pl.ds(0, half, stride=2), :side] = scale[:, :side]
-    eig_scr[pl.ds(1, half, stride=2), :side] = scale[:, side:]
-    scale = eig_scr[:, :side]
+    turned = swapped(scale)
+    eig_scr[pl.ds(0, half, stride=2), :] = jnp.where(left_lanes, scale, turned)
+    eig_scr[pl.ds(1, half, stride=2), :] = jnp.where(left_lanes, turned, scale)
+    scale = jnp.concatenate([eig_scr[...]] * blocks, axis=1)
     o_scr[:, :side] = out_basis_ref[0]
     basis = jnp.concatenate(
         [o_scr[pl.ds(0, half, stride=2), :side], o_scr[pl.ds(1, half, stride=2), :side]], axis=0
@@ -61,31 +66,46 @@
     t_hi, t_lo = split2(basis.T)
     left = jnp.concatenate([t_hi, t_hi, t_lo], axis=1)
     back = jnp.concatenate([b_hi, b_hi, b_lo], axis=1)
-    i_hi, i_lo = split2(in_basis_ref[0])
-    none = jnp.zeros_like(i_hi)
+    twice_hi, twice_lo = split2(jnp.concatenate([in_basis_ref[0]] * 2, axis=1))
+    none = jnp.zeros_like(twice_hi)
     raw = jnp.concatenate([q_ref[order_ref[j]] for j in range(blocks)], axis=0)
-    raw2 = jnp.concatenate([raw, raw], axis=1)
-    even = mm(raw2, jnp.concatenate([i_hi, none, i_lo, none], axis=0))
-    odd = mm(raw2, jnp.concatenate([none, i_hi, none, i_lo], axis=0))
-    even_scr[:, :side] = even
-    odd_scr[:, :side] = odd
-    evens, odds = [], []
-    for q in range(count):
-        rows = pl.ds(q // qdev * lines + q % qdev, half, stride=qdev)
-        hi, lo = split2(jnp.concatenate([even_scr[rows, :side], odd_scr[rows, :side]], axis=0))
-        rotated = mm(left, jnp.concatenate([hi, lo, hi], axis=0))
-        hi, lo = split2(rotated * scale)
-        again = mm(back, jnp.concatenate([hi, lo, hi], axis=0))
-        evens.append(again[:half])
-        odds.append(again[half:])
-    total = None
-    for rows, lower in ((evens, False), (odds, True)):
-        hi, lo = split2(jnp.concatenate(rows, axis=0))
-        w_hi = jnp.concatenate([none, i_hi] if lower else [i_hi, none], axis=0)
-        w_lo = jnp.concatenate([none, i_lo] if lower else [i_lo, none], axis=0)
-        term = mm_nt(hi, w_hi) + mm_nt(lo, w_hi) + mm_nt(hi, w_lo)
-        total = term if total is None else total + term
-    x_scr[...] = total
+    rotated = mm(jnp.concatenate([raw, raw], axis=1), jnp.concatenate([
+        jnp.concatenate([twice_hi, none, twice_lo, none], axis=0),
+        jnp.concatenate([none, twice_hi, none, twice_lo], axis=0),
+    ], axis=1))
+    even_scr[...] = rotated[:, :LANES]
+    odd_scr[...] = rotated[:, LANES:]
+    pairs = []
+    for j in range(blocks):
+        first, second = pl.ds(j * lines, half, stride=2), pl.ds(j * lines + 1, half, stride=2)
+        pairs.append(jnp.concatenate(
+            [jnp.where(left_lanes, scr[first, :], scr[second, :]) for scr in (even_scr, odd_scr)], axis=0
+        ))
+    hi, lo = split2(jnp.concatenate(pairs, axis=1))
+    rotated = mm(left, jnp.concatenate([hi, lo, hi], axis=0))
+    hi, lo = split2(rotated * scale)
+    again = mm(back, jnp.concatenate([hi, lo, hi], axis=0))
+    rows = jnp.concatenate([
+        jnp.concatenate([again[at:at + half, j * LANES:(j + 1) * LANES] for j in range(blocks)], axis=0)
+        for at in (0, half)
+    ], axis=1)
+    hi, lo = split2(rows)
+    left_side = lax.broadcasted_iota(jnp.int32, (side, LANES), 1) < side
+
+    def placed(twice):
+        one, two = jnp.where(left_side, twice, 0), jnp.where(left_side, 0, twice)
+        zero = jnp.zeros_like(one)
+        return jnp.concatenate([
+            jnp.concatenate([one, zero], axis=1), jnp.concatenate([zero, one], axis=1),
+            jnp.concatenate([two, zero], axis=1), jnp.concatenate([zero, two], axis=1),
+        ], axis=0).astype(BF16)
+
+    w_hi, w_lo = placed(twice_hi.astype(F32)), placed(twice_lo.astype(F32))
+    total = mm_nt(hi, w_hi) + mm_nt(lo, w_hi) + mm_nt(hi, w_lo)
+    for j in range(blocks):
+        for e in range(2):
+            at = (2 * j + e) * chunks
+            x_scr[at:at + chunks, :] = total[j * half:(j + 1) * half, e * LANES:(e + 1) * LANES]
     per = chunks // SEGMENTS
     for c in range(per):
         piece = x_scr[pl.ds(c, count * SEGMENTS, stride=per), :].astype(BF16)

time: 19 us -> 19 us (level)
  no operation moved by 1% of the time
where the time goes in v15:
time: 19 us; the launch traced here: 18.8 us
  starting transfers between devices  11.7 us (62%)
  Pallas kernels  3.75 us (20%)
  waiting for transfers between devices  2.78 us (15%)
  other arithmetic  0.6 us (3%)
    ppermute x7, starting transfers between devices, swap(): return lax.ppermute(x, 'row', [(r, r ^ mask) for r in range(n_row)])  11.6 us
    pallas_call x1, Pallas kernels, precondition(): pl.pallas_call(precondition_kernel, out_shape=(jax.ShapeDtypeStruct((coun...  1.75 us
    ppermute x7, waiting for transfers between devices, swap(): return lax.ppermute(x, 'row', [(r, r ^ mask) for r in range(n_row)])  1.6 us
    ppermute x1, waiting for transfers between devices, body(): got = lax.ppermute(other, 'layer', [(0, 1), (1, 0)])  1.18 us
    pallas_call x1, Pallas kernels, scores(): pl.pallas_call(functools.partial(late_kernel, masks[early:] + masks[:earl...  1 us
    pallas_call x1, Pallas kernels, scores(): pl.pallas_call(functools.partial(early_kernel, masks), out_shape=(jax.Sha...  0.99 us
    transpose x1, other arithmetic, body(): return total.reshape(blocks, -1, rows).transpose(0, 2, 1)  0.6 us
  transfers between devices with their start and end apart: 8, of which 3 were waited for; matrix products, arithmetic and copies ran while one was open for 0% of the time, Pallas kernels for 5%

profile of v15, /device:TPU:0, one launch (start us, length us, event | category | flops | bytes accessed | tf_op | source)
XLA Modules:
  0.0 18.8 jit_solution(1680627997196143712)
XLA Ops:
  0.0 1.8 %precondition.1 = (bf16[24,1024]{1,0:T(8,128)(2,1)S(1)}, s32[1,256]{1,0:T(1,128)S(1)}, bf16[256,4096]{1,0:T(8,128)(2,1)S(1)}) custom-call(s32[3]{0:T(128)} %order_hbm.1, bf16[3,64,128]{2,1,0:T(8,128)(2,1)} %bitcast.12, f32[1,64,64]{2,1,0:T(8,128)} %out_basis_hbm.1, f32[1,64,64]{2,1,0:T(8,128)} %in_basis_hbm.1, f32[32,128]{1,0:T(8,128)} %bitcast.13, ...), custom_call_target="tpu_custom_call" | custom-call | tf_op jit(solution)/shard_map/precondition/pallas_call | solution.py:128
  1.8 5.1 %collective-permute-start.2 = (bf16[24,1024]{1,0:T(8,128)(2,1)S(1)}, bf16[24,1024]{1,0:T(8,128)(2,1)S(1)}, u32[]{:S(2)}, u32[]{:S(2)}) collective-permute-start(bf16[24,1024]{1,0:T(8,128)(2,1)S(1)} %get-tuple-element.14.refs_0_), channel_id=1, source_target_pairs={{0,12},{2,14},{4,8},{6,10},{8,4},{10,6},{12,0},{14,2},{1,13},{3,15... | collective-permute-start | bytes 147464 | tf_op jit(solution)/shard_map/ppermute | solution.py:258
  6.9 0.0 collective-permute-start.3
  6.9 0.6 %collective-permute-start = (bf16[24,1024]{1,0:T(8,128)(2,1)S(1)}, bf16[24,1024]{1,0:T(8,128)(2,1)S(1)}, u32[]{:S(2)}, u32[]{:S(2)}) collective-permute-start(bf16[24,1024]{1,0:T(8,128)(2,1)S(1)} %get-tuple-element.14.refs_0_), channel_id=1, source_target_pairs={{0,4},{2,6},{4,0},{6,2},{8,12},{10,14},{12,8},{14,10},{1,5},{3,7},... | collective-permute-start | bytes 147464 | tf_op jit(solution)/shard_map/ppermute | solution.py:258
  7.5 1.6 %collective-permute-start.1 = (bf16[24,1024]{1,0:T(8,128)(2,1)S(1)}, bf16[24,1024]{1,0:T(8,128)(2,1)S(1)}, u32[]{:S(2)}, u32[]{:S(2)}) collective-permute-start(bf16[24,1024]{1,0:T(8,128)(2,1)S(1)} %get-tuple-element.14.refs_0_), channel_id=1, source_target_pairs={{0,2},{2,0},{4,6},{6,4},{8,10},{10,8},{12,14},{14,12},{1,3},{3,1},... | collective-permute-start | bytes 147464 | tf_op jit(solution)/shard_map/ppermute | solution.py:258
  9.2 1.2 %collective-permute-start.4 = (bf16[24,1024]{1,0:T(8,128)(2,1)S(1)}, bf16[24,1024]{1,0:T(8,128)(2,1)S(1)}, u32[]{:S(2)}, u32[]{:S(2)}) collective-permute-start(bf16[24,1024]{1,0:T(8,128)(2,1)S(1)} %get-tuple-element.14.refs_0_), channel_id=1, source_target_pairs={{0,6},{2,4},{4,2},{6,0},{8,14},{10,12},{12,10},{14,8},{1,7},{3,5},... | collective-permute-start | bytes 147464 | tf_op jit(solution)/shard_map/ppermute | solution.py:258
  10.4 0.0 collective-permute-done.2.refs_3_
  10.4 1.5 %collective-permute-start.5 = (bf16[24,1024]{1,0:T(8,128)(2,1)S(1)}, bf16[24,1024]{1,0:T(8,128)(2,1)S(1)}, u32[]{:S(2)}, u32[]{:S(2)}) collective-permute-start(bf16[24,1024]{1,0:T(8,128)(2,1)S(1)} %collective-permute-done.2.refs_3_), channel_id=1, source_target_pairs={{0,2},{2,0},{4,6},{6,4},{8,10},{10,8},{12,14},{14,12},{1,3},{3,1},... | collective-permute-start | bytes 147464 | tf_op jit(solution)/shard_map/ppermute | solution.py:258
  11.9 0.0 collective-permute-done.3.refs_4_
  11.9 1.5 %collective-permute-start.6 = (bf16[24,1024]{1,0:T(8,128)(2,1)S(1)}, bf16[24,1024]{1,0:T(8,128)(2,1)S(1)}, u32[]{:S(2)}, u32[]{:S(2)}) collective-permute-start(bf16[24,1024]{1,0:T(8,128)(2,1)S(1)} %collective-permute-done.3.refs_4_), channel_id=1, source_target_pairs={{0,2},{2,0},{4,6},{6,4},{8,10},{10,8},{12,14},{14,12},{1,3},{3,1},... | collective-permute-start | bytes 147464 | tf_op jit(solution)/shard_map/ppermute | solution.py:258
  13.4 0.0 collective-permute-done.refs_1_
  13.4 0.0 collective-permute-done.1.refs_2_
  13.4 1.0 %scores_early.1 = (f32[48,256]{1,0:T(8,128)S(1)}, bf16[256,256]{1,0:T(8,128)(2,1)S(1)}) custom-call(bf16[256,4096]{1,0:T(8,128)(2,1)S(1)} %get-tuple-element.12.train_ref, s32[1,256]{1,0:T(1,128)S(1)} %get-tuple-element.13.ids_ref, bf16[24,1024]{1,0:T(8,128)(2,1)S(1)} %get-tuple-element.14.refs_0_, bf16[24,1024]{1,0:T(8,128)(2,1)S(1)} %collective-permute-done.refs_1_, ...), custom_call_target="tpu_custom_call" | custom-call | flops 100663296 | bytes 2293760 | tf_op jit(solution)/shard_map/scores_early/pallas_call | solution.py:230
  14.4 0.0 collective-permute-done.4.refs_0_
  14.4 0.7 %collective-permute-done.5.refs_1_ = bf16[24,1024]{1,0:T(8,128)(2,1)S(1)} collective-permute-done((bf16[24,1024]{1,0:T(8,128)(2,1)S(1)}, bf16[24,1024]{1,0:T(8,128)(2,1)S(1)}, u32[]{:S(2)}, u32[]{:S(2)}) %collective-permute-start.5) | collective-permute-done | bytes 49184 | tf_op jit(solution)/shard_map/ppermute | solution.py:258
  15.1 0.9 %collective-permute-done.6.refs_2_ = bf16[24,1024]{1,0:T(8,128)(2,1)S(1)} collective-permute-done((bf16[24,1024]{1,0:T(8,128)(2,1)S(1)}, bf16[24,1024]{1,0:T(8,128)(2,1)S(1)}, u32[]{:S(2)}, u32[]{:S(2)}) %collective-permute-start.6) | collective-permute-done | bytes 49184 | tf_op jit(solution)/shard_map/ppermute | solution.py:258
  16.0 1.0 %scores_late.1 = (f32[24,256]{1,0:T(8,128)S(1)}, f32[24,256]{1,0:T(8,128)S(1)}) custom-call(bf16[256,4096]{1,0:T(8,128)(2,1)S(1)} %get-tuple-element.12.train_ref, bf16[256,256]{1,0:T(8,128)(2,1)S(1)} %get-tuple-element.15.place_ref, f32[48,256]{1,0:T(8,128)S(1)} %get-tuple-element.16.early_ref, bf16[24,1024]{1,0:T(8,128)(2,1)S(1)} %collective-permute-done.4.refs_0_, ...), custom_call_target="tpu_custom_call" | custom-call | flops 100663296 | bytes 2293760 | tf_op jit(solution)/shard_map/scores_late/pallas_call | solution.py:244
  17.0 0.1 collective-permute-start.7
  17.0 1.2 %collective-permute-done.7 = f32[24,256]{1,0:T(8,128)S(1)} collective-permute-done((f32[24,256]{1,0:T(8,128)S(1)}, f32[24,256]{1,0:T(8,128)S(1)}, u32[]{:S(2)}, u32[]{:S(2)}) %collective-permute-start.7) | collective-permute-done | bytes 24608 | tf_op jit(solution)/shard_map/ppermute | solution.py:278
  18.2 0.6 %fusion = bf16[3,256,8]{1,2,0:T(8,128)(2,1)} fusion(f32[24,256]{1,0:T(8,128)S(1)} %get-tuple-element.17, f32[24,256]{1,0:T(8,128)S(1)} %collective-permute-done.7), kind=kLoop, calls=%fused_computation.1 | loop fusion | flops 12288 | bytes 61440 | tf_op jit(solution)/shard_map/transpose | solution.py:280
Async XLA Ops:
  1.8 8.6 %collective-permute-start.2 = (bf16[24,1024]{1,0:T(8,128)(2,1)S(1)}, bf16[24,1024]{1,0:T(8,128)(2,1)S(1)}, u32[]{:S(2)}, u32[]{:S(2)}) collective-permute-start(bf16[24,1024]{1,0:T(8,128)(2,1)S(1)} %get-tuple-element.14.refs_0_), channel_id=1, source_target_pairs={{0,12},{2,14},{4,8},{6,10},{8,4},{10,6},{12,0},{14,2},{1,13},{3,15... | collective-permute-start | bytes 147464 | tf_op jit(solution)/shard_map/ppermute | solution.py:258
  6.9 5.0 %collective-permute-start.3 = (bf16[24,1024]{1,0:T(8,128)(2,1)S(1)}, bf16[24,1024]{1,0:T(8,128)(2,1)S(1)}, u32[]{:S(2)}, u32[]{:S(2)}) collective-permute-start(bf16[24,1024]{1,0:T(8,128)(2,1)S(1)} %get-tuple-element.14.refs_0_), channel_id=1, source_target_pairs={{0,8},{2,10},{4,12},{6,14},{8,0},{10,2},{12,4},{14,6},{1,9},{3,11}... | collective-permute-start | bytes 147464 | tf_op jit(solution)/shard_map/ppermute | solution.py:258
  6.9 6.5 %collective-permute-start = (bf16[24,1024]{1,0:T(8,128)(2,1)S(1)}, bf16[24,1024]{1,0:T(8,128)(2,1)S(1)}, u32[]{:S(2)}, u32[]{:S(2)}) collective-permute-start(bf16[24,1024]{1,0:T(8,128)(2,1)S(1)} %get-tuple-element.14.refs_0_), channel_id=1, source_target_pairs={{0,4},{2,6},{4,0},{6,2},{8,12},{10,14},{12,8},{14,10},{1,5},{3,7},... | collective-permute-start | bytes 147464 | tf_op jit(solution)/shard_map/ppermute | solution.py:258
  7.5 5.8 %collective-permute-start.1 = (bf16[24,1024]{1,0:T(8,128)(2,1)S(1)}, bf16[24,1024]{1,0:T(8,128)(2,1)S(1)}, u32[]{:S(2)}, u32[]{:S(2)}) collective-permute-start(bf16[24,1024]{1,0:T(8,128)(2,1)S(1)} %get-tuple-element.14.refs_0_), channel_id=1, source_target_pairs={{0,2},{2,0},{4,6},{6,4},{8,10},{10,8},{12,14},{14,12},{1,3},{3,1},... | collective-permute-start | bytes 147464 | tf_op jit(solution)/shard_map/ppermute | solution.py:258
  9.2 5.2 %collective-permute-start.4 = (bf16[24,1024]{1,0:T(8,128)(2,1)S(1)}, bf16[24,1024]{1,0:T(8,128)(2,1)S(1)}, u32[]{:S(2)}, u32[]{:S(2)}) collective-permute-start(bf16[24,1024]{1,0:T(8,128)(2,1)S(1)} %get-tuple-element.14.refs_0_), channel_id=1, source_target_pairs={{0,6},{2,4},{4,2},{6,0},{8,14},{10,12},{12,10},{14,8},{1,7},{3,5},... | collective-permute-start | bytes 147464 | tf_op jit(solution)/shard_map/ppermute | solution.py:258
  10.4 4.7 %collective-permute-start.5 = (bf16[24,1024]{1,0:T(8,128)(2,1)S(1)}, bf16[24,1024]{1,0:T(8,128)(2,1)S(1)}, u32[]{:S(2)}, u32[]{:S(2)}) collective-permute-start(bf16[24,1024]{1,0:T(8,128)(2,1)S(1)} %collective-permute-done.2.refs_3_), channel_id=1, source_target_pairs={{0,2},{2,0},{4,6},{6,4},{8,10},{10,8},{12,14},{14,12},{1,3},{3,1},... | collective-permute-start | bytes 147464 | tf_op jit(solution)/shard_map/ppermute | solution.py:258
  11.9 4.1 %collective-permute-start.6 = (bf16[24,1024]{1,0:T(8,128)(2,1)S(1)}, bf16[24,1024]{1,0:T(8,128)(2,1)S(1)}, u32[]{:S(2)}, u32[]{:S(2)}) collective-permute-start(bf16[24,1024]{1,0:T(8,128)(2,1)S(1)} %collective-permute-done.3.refs_4_), channel_id=1, source_target_pairs={{0,2},{2,0},{4,6},{6,4},{8,10},{10,8},{12,14},{14,12},{1,3},{3,1},... | collective-permute-start | bytes 147464 | tf_op jit(solution)/shard_map/ppermute | solution.py:258
  17.0 1.3 %collective-permute-start.7 = (f32[24,256]{1,0:T(8,128)S(1)}, f32[24,256]{1,0:T(8,128)S(1)}, u32[]{:S(2)}, u32[]{:S(2)}) collective-permute-start(f32[24,256]{1,0:T(8,128)S(1)} %get-tuple-element.18), channel_id=1, source_target_pairs={{0,1},{1,0},{2,3},{3,2},{4,5},{5,4},{6,7},{7,6},{8,9},{9,8},{10,11... | collective-permute-start | bytes 73736 | tf_op jit(solution)/shard_map/ppermute | solution.py:278

commit v16 on v15

--- a/solution.py
+++ b/solution.py
@@ -35,19 +35,18 @@
     copies = [
         pltpu.make_async_copy(src, dst, sems.at[n])
         for n, (src, dst) in enumerate((
-            (order_hbm, order_ref), (q_hbm, q_ref), (in_basis_hbm, in_basis_ref), (out_basis_hbm, out_basis_ref), (eig_hbm, eig_ref),
-            (ids_hbm, ids_out_ref), (train_hbm, train_out_ref),
+            (q_hbm, q_ref), (in_basis_hbm, in_basis_ref), (out_basis_hbm, out_basis_ref), (eig_hbm, eig_ref),
+            (order_hbm, order_ref), (ids_hbm, ids_out_ref), (train_hbm, train_out_ref),
         ))
     ]
     for copy in copies:
         copy.start()
-    for copy in copies[:5]:
+    for copy in copies[:4]:
         copy.wait()
     blocks, lines, _ = q_ref.shape
     chunks = eig_ref.shape[0]
     side = out_basis_ref.shape[1]
     half = side // 2
-    count = blocks * (lines // chunks)
     left_lanes = lax.broadcasted_iota(jnp.int32, (half, LANES), 1) < side
 
     def swapped(x):
@@ -68,7 +67,7 @@
     back = jnp.concatenate([b_hi, b_hi, b_lo], axis=1)
     twice_hi, twice_lo = split2(jnp.concatenate([in_basis_ref[0]] * 2, axis=1))
     none = jnp.zeros_like(twice_hi)
-    raw = jnp.concatenate([q_ref[order_ref[j]] for j in range(blocks)], axis=0)
+    raw = jnp.concatenate([q_ref[j] for j in range(blocks)], axis=0)
     rotated = mm(jnp.concatenate([raw, raw], axis=1), jnp.concatenate([
         jnp.concatenate([twice_hi, none, twice_lo, none], axis=0),
         jnp.concatenate([none, twice_hi, none, twice_lo], axis=0),
@@ -104,12 +103,12 @@
     total = mm_nt(hi, w_hi) + mm_nt(lo, w_hi) + mm_nt(hi, w_lo)
     for j in range(blocks):
         for e in range(2):
-            at = (2 * j + e) * chunks
-            x_scr[at:at + chunks, :] = total[j * half:(j + 1) * half, e * LANES:(e + 1) * LANES]
+            x_scr[j, e * chunks:(e + 1) * chunks, :] = total[j * half:(j + 1) * half, e * LANES:(e + 1) * LANES]
+    copies[4].wait()
     per = chunks // SEGMENTS
     for c in range(per):
-        piece = x_scr[pl.ds(c, count * SEGMENTS, stride=per), :].astype(BF16)
-        sent_ref[:, c * LANES:(c + 1) * LANES] = piece
+        piece = [x_scr[order_ref[j], pl.ds(c, 2 * SEGMENTS, stride=per), :] for j in range(blocks)]
+        sent_ref[:, c * LANES:(c + 1) * LANES] = jnp.concatenate(piece, axis=0).astype(BF16)
     for copy in copies[5:]:
         copy.wait()
 
@@ -140,7 +139,8 @@
             pltpu.VMEM(out_basis.shape, F32),
             pltpu.VMEM(in_basis.shape, F32),
             pltpu.VMEM(eigenvalues.shape, F32),
-            rows, rows, rows,
+            pltpu.VMEM((blocks, qdev * chunks, LANES), F32),
+            rows, rows,
             pltpu.VMEM((side, LANES), F32),
             pltpu.VMEM((side, LANES), F32),
             pltpu.SemaphoreType.DMA((7,)),
@@ -151,13 +151,6 @@
         pltpu.with_memory_space_constraint(x, pltpu.HBM)
         for x in (block_order, query_grads, out_basis, in_basis, eigenvalues, row_ids, train)
     ))
-
-
-def split3(x):
-    hi = x.astype(BF16)
-    rest = x - hi.astype(F32)
-    mid = rest.astype(BF16)
-    return hi, mid, (rest - mid.astype(F32)).astype(BF16)
 
 
 def slot_of(n_row, mask):
@@ -184,8 +177,8 @@
         ], axis=1)
         term = mm_nt(queries.astype(BF16), train_ref[:, j * seg:(j + 1) * seg])
         terms = term if terms is None else terms + term
-    a, b, c = split3(terms)
-    return mm(a, place) + mm(b, place) + mm(c, place)
+    hi, lo = split2(terms)
+    return mm(hi, place) + mm(lo, place)
 
 
 def early_kernel(masks, train_ref, ids_ref, *refs):
@@ -212,7 +205,7 @@
                 out_scr[h, pl.ds(first, per, stride=qdev), :] = terms[at:at + per, h * LANES:(h + 1) * LANES]
     for h in range(halves):
         mine_ref[:, h * LANES:(h + 1) * LANES] = out_scr[h, :half_rows]
-        other_ref[:, h * LANES:(h + 1) * LANES] = out_scr[h, half_rows:]
+        other_ref[:, h * LANES:(h + 1) * LANES] = out_scr[h, half_rows:].astype(BF16)
 
 
 def scores(masks, early, train, row_ids, parts, blocks, qdev):
@@ -240,10 +233,10 @@
         cost_estimate=cost,
         name="scores_early",
     )(train, row_ids, *parts[:early])
-    out = jax.ShapeDtypeStruct((queries // 2, rows), F32)
+    half = (queries // 2, rows)
     return pl.pallas_call(
         functools.partial(late_kernel, masks[early:] + masks[:early], blocks, qdev),
-        out_shape=(out, out),
+        out_shape=(jax.ShapeDtypeStruct(half, F32), jax.ShapeDtypeStruct(half, BF16)),
         in_specs=[vmem] * (3 + n_row - early),
         out_specs=(vmem, vmem),
         scratch_shapes=[flat_scr, pltpu.VMEM((rows // LANES, queries, LANES), F32)],
@@ -276,7 +269,7 @@
         parts, early = gather(own)
         mine, other = scores(tuple(parts), early, train, row_ids, tuple(parts.values()), blocks, qdev)
         got = lax.ppermute(other, "layer", [(0, 1), (1, 0)])
-        total = (mine + got).astype(BF16)
+        total = (mine + got.astype(F32)).astype(BF16)
         return total.reshape(blocks, -1, rows).transpose(0, 2, 1)
 
     return body

time: 19 us -> 18.9 us (level)
  no operation moved by 1% of the time
where the time goes in v16:
time: 18.9 us; the launch traced here: 18.8 us
  starting transfers between devices  11.7 us (62%)
  Pallas kernels  3.69 us (20%)
  waiting for transfers between devices  2.8 us (15%)
  other arithmetic  0.61 us (3%)
    ppermute x7, starting transfers between devices, swap(): return lax.ppermute(x, 'row', [(r, r ^ mask) for r in range(n_row)])  11.6 us
    pallas_call x1, Pallas kernels, precondition(): pl.pallas_call(precondition_kernel, out_shape=(jax.ShapeDtypeStruct((coun...  1.75 us
    ppermute x7, waiting for transfers between devices, swap(): return lax.ppermute(x, 'row', [(r, r ^ mask) for r in range(n_row)])  1.63 us
    ppermute x1, waiting for transfers between devices, body(): got = lax.ppermute(other, 'layer', [(0, 1), (1, 0)])  1.16 us
    pallas_call x1, Pallas kernels, scores(): pl.pallas_call(functools.partial(late_kernel, masks[early:] + masks[:earl...  0.97 us
    pallas_call x1, Pallas kernels, scores(): pl.pallas_call(functools.partial(early_kernel, masks), out_shape=(jax.Sha...  0.96 us
    transpose x1, other arithmetic, body(): return total.reshape(blocks, -1, rows).transpose(0, 2, 1)  0.61 us
  transfers between devices with their start and end apart: 8, of which 3 were waited for; matrix products, arithmetic and copies ran while one was open for 0% of the time, Pallas kernels for 5%

profile of v16, /device:TPU:0, one launch (start us, length us, event | category | flops | bytes accessed | tf_op | source)
XLA Modules:
  0.0 18.8 jit_solution(2797187970218171855)
XLA Ops:
  0.0 1.8 %precondition.1 = (bf16[24,1024]{1,0:T(8,128)(2,1)S(1)}, s32[1,256]{1,0:T(1,128)S(1)}, bf16[256,4096]{1,0:T(8,128)(2,1)S(1)}) custom-call(s32[3]{0:T(128)} %order_hbm.1, bf16[3,64,128]{2,1,0:T(8,128)(2,1)} %bitcast.12, f32[1,64,64]{2,1,0:T(8,128)} %out_basis_hbm.1, f32[1,64,64]{2,1,0:T(8,128)} %in_basis_hbm.1, f32[32,128]{1,0:T(8,128)} %bitcast.13, ...), custom_call_target="tpu_custom_call" | custom-call | tf_op jit(solution)/shard_map/precondition/pallas_call | solution.py:127
  1.8 5.1 %collective-permute-start.2 = (bf16[24,1024]{1,0:T(8,128)(2,1)S(1)}, bf16[24,1024]{1,0:T(8,128)(2,1)S(1)}, u32[]{:S(2)}, u32[]{:S(2)}) collective-permute-start(bf16[24,1024]{1,0:T(8,128)(2,1)S(1)} %get-tuple-element.14.refs_0_), channel_id=1, source_target_pairs={{0,12},{2,14},{4,8},{6,10},{8,4},{10,6},{12,0},{14,2},{1,13},{3,15... | collective-permute-start | bytes 147464 | tf_op jit(solution)/shard_map/ppermute | solution.py:251
  6.9 0.0 collective-permute-start.3
  6.9 0.6 %collective-permute-start = (bf16[24,1024]{1,0:T(8,128)(2,1)S(1)}, bf16[24,1024]{1,0:T(8,128)(2,1)S(1)}, u32[]{:S(2)}, u32[]{:S(2)}) collective-permute-start(bf16[24,1024]{1,0:T(8,128)(2,1)S(1)} %get-tuple-element.14.refs_0_), channel_id=1, source_target_pairs={{0,4},{2,6},{4,0},{6,2},{8,12},{10,14},{12,8},{14,10},{1,5},{3,7},... | collective-permute-start | bytes 147464 | tf_op jit(solution)/shard_map/ppermute | solution.py:251
  7.5 1.6 %collective-permute-start.1 = (bf16[24,1024]{1,0:T(8,128)(2,1)S(1)}, bf16[24,1024]{1,0:T(8,128)(2,1)S(1)}, u32[]{:S(2)}, u32[]{:S(2)}) collective-permute-start(bf16[24,1024]{1,0:T(8,128)(2,1)S(1)} %get-tuple-element.14.refs_0_), channel_id=1, source_target_pairs={{0,2},{2,0},{4,6},{6,4},{8,10},{10,8},{12,14},{14,12},{1,3},{3,1},... | collective-permute-start | bytes 147464 | tf_op jit(solution)/shard_map/ppermute | solution.py:251
  9.2 1.2 %collective-permute-start.4 = (bf16[24,1024]{1,0:T(8,128)(2,1)S(1)}, bf16[24,1024]{1,0:T(8,128)(2,1)S(1)}, u32[]{:S(2)}, u32[]{:S(2)}) collective-permute-start(bf16[24,1024]{1,0:T(8,128)(2,1)S(1)} %get-tuple-element.14.refs_0_), channel_id=1, source_target_pairs={{0,6},{2,4},{4,2},{6,0},{8,14},{10,12},{12,10},{14,8},{1,7},{3,5},... | collective-permute-start | bytes 147464 | tf_op jit(solution)/shard_map/ppermute | solution.py:251
  10.4 0.0 collective-permute-done.2.refs_3_
  10.4 1.5 %collective-permute-start.5 = (bf16[24,1024]{1,0:T(8,128)(2,1)S(1)}, bf16[24,1024]{1,0:T(8,128)(2,1)S(1)}, u32[]{:S(2)}, u32[]{:S(2)}) collective-permute-start(bf16[24,1024]{1,0:T(8,128)(2,1)S(1)} %collective-permute-done.2.refs_3_), channel_id=1, source_target_pairs={{0,2},{2,0},{4,6},{6,4},{8,10},{10,8},{12,14},{14,12},{1,3},{3,1},... | collective-permute-start | bytes 147464 | tf_op jit(solution)/shard_map/ppermute | solution.py:251
  11.9 0.0 collective-permute-done.3.refs_4_
  11.9 1.5 %collective-permute-start.6 = (bf16[24,1024]{1,0:T(8,128)(2,1)S(1)}, bf16[24,1024]{1,0:T(8,128)(2,1)S(1)}, u32[]{:S(2)}, u32[]{:S(2)}) collective-permute-start(bf16[24,1024]{1,0:T(8,128)(2,1)S(1)} %collective-permute-done.3.refs_4_), channel_id=1, source_target_pairs={{0,2},{2,0},{4,6},{6,4},{8,10},{10,8},{12,14},{14,12},{1,3},{3,1},... | collective-permute-start | bytes 147464 | tf_op jit(solution)/shard_map/ppermute | solution.py:251
  13.4 0.0 collective-permute-done.refs_1_
  13.4 0.0 collective-permute-done.1.refs_2_
  13.4 1.0 %scores_early.1 = (f32[48,256]{1,0:T(8,128)S(1)}, bf16[256,256]{1,0:T(8,128)(2,1)S(1)}) custom-call(bf16[256,4096]{1,0:T(8,128)(2,1)S(1)} %get-tuple-element.12.train_ref, s32[1,256]{1,0:T(1,128)S(1)} %get-tuple-element.13.ids_ref, bf16[24,1024]{1,0:T(8,128)(2,1)S(1)} %get-tuple-element.14.refs_0_, bf16[24,1024]{1,0:T(8,128)(2,1)S(1)} %collective-permute-done.refs_1_, ...), custom_call_target="tpu_custom_call" | custom-call | flops 100663296 | bytes 2293760 | tf_op jit(solution)/shard_map/scores_early/pallas_call | solution.py:223
  14.3 0.0 collective-permute-done.4.refs_0_
  14.4 0.7 %collective-permute-done.5.refs_1_ = bf16[24,1024]{1,0:T(8,128)(2,1)S(1)} collective-permute-done((bf16[24,1024]{1,0:T(8,128)(2,1)S(1)}, bf16[24,1024]{1,0:T(8,128)(2,1)S(1)}, u32[]{:S(2)}, u32[]{:S(2)}) %collective-permute-start.5) | collective-permute-done | bytes 49184 | tf_op jit(solution)/shard_map/ppermute | solution.py:251
  15.1 0.9 %collective-permute-done.6.refs_2_ = bf16[24,1024]{1,0:T(8,128)(2,1)S(1)} collective-permute-done((bf16[24,1024]{1,0:T(8,128)(2,1)S(1)}, bf16[24,1024]{1,0:T(8,128)(2,1)S(1)}, u32[]{:S(2)}, u32[]{:S(2)}) %collective-permute-start.6) | collective-permute-done | bytes 49184 | tf_op jit(solution)/shard_map/ppermute | solution.py:251
  16.0 1.0 %scores_late.1 = (f32[24,256]{1,0:T(8,128)S(1)}, bf16[24,256]{1,0:T(8,128)(2,1)S(1)}) custom-call(bf16[256,4096]{1,0:T(8,128)(2,1)S(1)} %get-tuple-element.12.train_ref, bf16[256,256]{1,0:T(8,128)(2,1)S(1)} %get-tuple-element.15.place_ref, f32[48,256]{1,0:T(8,128)S(1)} %get-tuple-element.16.early_ref, bf16[24,1024]{1,0:T(8,128)(2,1)S(1)} %collective-permute-done.4.refs_0_, ...), custom_call_target="tpu_custom_call" | custom-call | flops 100663296 | bytes 2293760 | tf_op jit(solution)/shard_map/scores_late/pallas_call | solution.py:237
  16.9 0.1 collective-permute-start.7
  17.0 1.2 %collective-permute-done.7 = bf16[24,256]{1,0:T(8,128)(2,1)S(1)} collective-permute-done((bf16[24,256]{1,0:T(8,128)(2,1)S(1)}, bf16[24,256]{1,0:T(8,128)(2,1)S(1)}, u32[]{:S(2)}, u32[]{:S(2)}) %collective-permute-start.7) | collective-permute-done | bytes 12320 | tf_op jit(solution)/shard_map/ppermute | solution.py:271
  18.2 0.6 %fusion = bf16[3,256,8]{1,2,0:T(8,128)(2,1)} fusion(f32[24,256]{1,0:T(8,128)S(1)} %get-tuple-element.17, bf16[24,256]{1,0:T(8,128)(2,1)S(1)} %collective-permute-done.7), kind=kLoop, calls=%fused_computation.1 | loop fusion | flops 18432 | bytes 49152 | tf_op jit(solution)/shard_map/transpose | solution.py:273
Async XLA Ops:
  1.8 8.6 %collective-permute-start.2 = (bf16[24,1024]{1,0:T(8,128)(2,1)S(1)}, bf16[24,1024]{1,0:T(8,128)(2,1)S(1)}, u32[]{:S(2)}, u32[]{:S(2)}) collective-permute-start(bf16[24,1024]{1,0:T(8,128)(2,1)S(1)} %get-tuple-element.14.refs_0_), channel_id=1, source_target_pairs={{0,12},{2,14},{4,8},{6,10},{8,4},{10,6},{12,0},{14,2},{1,13},{3,15... | collective-permute-start | bytes 147464 | tf_op jit(solution)/shard_map/ppermute | solution.py:251
  6.9 5.0 %collective-permute-start.3 = (bf16[24,1024]{1,0:T(8,128)(2,1)S(1)}, bf16[24,1024]{1,0:T(8,128)(2,1)S(1)}, u32[]{:S(2)}, u32[]{:S(2)}) collective-permute-start(bf16[24,1024]{1,0:T(8,128)(2,1)S(1)} %get-tuple-element.14.refs_0_), channel_id=1, source_target_pairs={{0,8},{2,10},{4,12},{6,14},{8,0},{10,2},{12,4},{14,6},{1,9},{3,11}... | collective-permute-start | bytes 147464 | tf_op jit(solution)/shard_map/ppermute | solution.py:251
  6.9 6.5 %collective-permute-start = (bf16[24,1024]{1,0:T(8,128)(2,1)S(1)}, bf16[24,1024]{1,0:T(8,128)(2,1)S(1)}, u32[]{:S(2)}, u32[]{:S(2)}) collective-permute-start(bf16[24,1024]{1,0:T(8,128)(2,1)S(1)} %get-tuple-element.14.refs_0_), channel_id=1, source_target_pairs={{0,4},{2,6},{4,0},{6,2},{8,12},{10,14},{12,8},{14,10},{1,5},{3,7},... | collective-permute-start | bytes 147464 | tf_op jit(solution)/shard_map/ppermute | solution.py:251
  7.5 5.8 %collective-permute-start.1 = (bf16[24,1024]{1,0:T(8,128)(2,1)S(1)}, bf16[24,1024]{1,0:T(8,128)(2,1)S(1)}, u32[]{:S(2)}, u32[]{:S(2)}) collective-permute-start(bf16[24,1024]{1,0:T(8,128)(2,1)S(1)} %get-tuple-element.14.refs_0_), channel_id=1, source_target_pairs={{0,2},{2,0},{4,6},{6,4},{8,10},{10,8},{12,14},{14,12},{1,3},{3,1},... | collective-permute-start | bytes 147464 | tf_op jit(solution)/shard_map/ppermute | solution.py:251
  9.2 5.2 %collective-permute-start.4 = (bf16[24,1024]{1,0:T(8,128)(2,1)S(1)}, bf16[24,1024]{1,0:T(8,128)(2,1)S(1)}, u32[]{:S(2)}, u32[]{:S(2)}) collective-permute-start(bf16[24,1024]{1,0:T(8,128)(2,1)S(1)} %get-tuple-element.14.refs_0_), channel_id=1, source_target_pairs={{0,6},{2,4},{4,2},{6,0},{8,14},{10,12},{12,10},{14,8},{1,7},{3,5},... | collective-permute-start | bytes 147464 | tf_op jit(solution)/shard_map/ppermute | solution.py:251
  10.4 4.7 %collective-permute-start.5 = (bf16[24,1024]{1,0:T(8,128)(2,1)S(1)}, bf16[24,1024]{1,0:T(8,128)(2,1)S(1)}, u32[]{:S(2)}, u32[]{:S(2)}) collective-permute-start(bf16[24,1024]{1,0:T(8,128)(2,1)S(1)} %collective-permute-done.2.refs_3_), channel_id=1, source_target_pairs={{0,2},{2,0},{4,6},{6,4},{8,10},{10,8},{12,14},{14,12},{1,3},{3,1},... | collective-permute-start | bytes 147464 | tf_op jit(solution)/shard_map/ppermute | solution.py:251
  11.9 4.1 %collective-permute-start.6 = (bf16[24,1024]{1,0:T(8,128)(2,1)S(1)}, bf16[24,1024]{1,0:T(8,128)(2,1)S(1)}, u32[]{:S(2)}, u32[]{:S(2)}) collective-permute-start(bf16[24,1024]{1,0:T(8,128)(2,1)S(1)} %collective-permute-done.3.refs_4_), channel_id=1, source_target_pairs={{0,2},{2,0},{4,6},{6,4},{8,10},{10,8},{12,14},{14,12},{1,3},{3,1},... | collective-permute-start | bytes 147464 | tf_op jit(solution)/shard_map/ppermute | solution.py:251
  16.9 1.2 %collective-permute-start.7 = (bf16[24,256]{1,0:T(8,128)(2,1)S(1)}, bf16[24,256]{1,0:T(8,128)(2,1)S(1)}, u32[]{:S(2)}, u32[]{:S(2)}) collective-permute-start(bf16[24,256]{1,0:T(8,128)(2,1)S(1)} %get-tuple-element.18), channel_id=1, source_target_pairs={{0,1},{1,0},{2,3},{3,2},{4,5},{5,4},{6,7},{7,6},{8,9},{9,8},{10,11... | collective-permute-start | bytes 36872 | tf_op jit(solution)/shard_map/ppermute | solution.py:271

commit v17 on v15

--- a/solution.py
+++ b/solution.py
@@ -161,7 +161,8 @@
 
 
 def slot_of(n_row, mask):
-    source, per = lax.axis_index("row") ^ mask, n_row // 2
+    mask, flip = mask
+    source, per = lax.axis_index("row") ^ mask ^ (lax.axis_index("grp") * flip), n_row // 2
     return source ^ (lax.axis_index("layer") * per)
 
 
@@ -253,18 +254,24 @@
     )(train, place, terms, *parts[early:])
 
 
-def make_body(n_row):
-    def swap(x, mask):
-        return lax.ppermute(x, "row", [(r, r ^ mask) for r in range(n_row)])
+def make_body(n_grp, n_row):
+    def swap(x, mask, flip=0, cross=0):
+        pairs = [
+            (g * n_row + r, (g ^ cross) * n_row + (r ^ mask ^ (g * flip))) for g in range(n_grp) for r in range(n_row)
+        ]
+        return lax.ppermute(x, ("grp", "row"), pairs)
 
     def gather(own):
-        if n_row != 8:
+        if (n_grp, n_row) != (2, 8):
             near = {0: own, **{m: swap(own, m) for m in range(2, n_row, 2)}}
-            return {**near, **{m ^ 1: swap(x, 1) for m, x in near.items()}}, n_row // 2
-        far = {m: swap(own, m) for m in (6, 4)}
-        diagonal = {3: swap(own, 3)}
-        near = {m: swap(own, m) for m in (2, 1)}
-        return {0: own, **near, **far, **diagonal, **{m ^ 1: swap(x, 1) for m, x in far.items()}}, 5
+            parts = {**near, **{m ^ 1: swap(x, 1) for m, x in near.items()}}
+            return {(m, 0): x for m, x in parts.items()}, n_row // 2
+        far = swap(own, 4, 2)
+        near = swap(own, 2)
+        return {
+            (0, 0): own, (1, 0): swap(own, 1), (2, 0): near, (4, 2): far,
+            (7, 2): swap(own, 7, 2), (3, 0): swap(near, 1), (5, 2): swap(far, 1), (6, 2): swap(far, 0, cross=1),
+        }, 4
 
     def body(train_grads, query_grads, out_basis, in_basis, eigenvalues, block_order, row_ids):
         blocks, qdev, _, width = query_grads.shape
@@ -293,5 +300,5 @@
         P(("grp", "row"), None),
     )
     out_specs = P(None, ("grp", "row"), "layer")
-    body = make_body(mesh.shape["row"])
+    body = make_body(mesh.shape["grp"], mesh.shape["row"])
     return jax.shard_map(body, mesh=mesh, in_specs=in_specs, out_specs=out_specs, check_vma=False)

time: 19 us -> 19.3 us (1.016)
  waiting for transfers between devices: 2.78 us -> 3.76 us
  starting transfers between devices: 11.7 us -> 11 us
    ppermute x7, waiting for transfers between devices: 1.6 us -> 2.58 us  [swap(): return lax.ppermute(x, ('grp', 'row'), pairs)]
    ppermute x7, starting transfers between devices: 11.6 us -> 11 us  [swap(): return lax.ppermute(x, ('grp', 'row'), pairs)]
where the time goes in v17:
time: 19.3 us; the launch traced here: 19.2 us
  starting transfers between devices  11 us (57%)
  waiting for transfers between devices  3.76 us (19%)
  Pallas kernels  3.74 us (19%)
  other arithmetic  0.6 us (3%)
    ppermute x7, starting transfers between devices, swap(): return lax.ppermute(x, ('grp', 'row'), pairs)  11 us
    ppermute x7, waiting for transfers between devices, swap(): return lax.ppermute(x, ('grp', 'row'), pairs)  2.58 us
    pallas_call x1, Pallas kernels, precondition(): pl.pallas_call(precondition_kernel, out_shape=(jax.ShapeDtypeStruct((coun...  1.75 us
    ppermute x1, waiting for transfers between devices, body(): got = lax.ppermute(other, 'layer', [(0, 1), (1, 0)])  1.18 us
    pallas_call x1, Pallas kernels, scores(): pl.pallas_call(functools.partial(late_kernel, masks[early:] + masks[:earl...  1 us
    pallas_call x1, Pallas kernels, scores(): pl.pallas_call(functools.partial(early_kernel, masks), out_shape=(jax.Sha...  0.98 us
    transpose x1, other arithmetic, body(): return total.reshape(blocks, -1, rows).transpose(0, 2, 1)  0.6 us
  transfers between devices with their start and end apart: 8, of which 3 were waited for; matrix products, arithmetic and copies ran while one was open for 0% of the time, Pallas kernels for 5%

profile of v17, /device:TPU:0, one launch (start us, length us, event | category | flops | bytes accessed | tf_op | source)
XLA Modules:
  0.0 19.2 jit_solution(17079148703584660217)
XLA Ops:
  0.0 1.8 %precondition.1 = (bf16[24,1024]{1,0:T(8,128)(2,1)S(1)}, s32[1,256]{1,0:T(1,128)S(1)}, bf16[256,4096]{1,0:T(8,128)(2,1)S(1)}) custom-call(s32[3]{0:T(128)} %order_hbm.1, bf16[3,64,128]{2,1,0:T(8,128)(2,1)} %bitcast.12, f32[1,64,64]{2,1,0:T(8,128)} %out_basis_hbm.1, f32[1,64,64]{2,1,0:T(8,128)} %in_basis_hbm.1, f32[32,128]{1,0:T(8,128)} %bitcast.13, ...), custom_call_target="tpu_custom_call" | custom-call | tf_op jit(solution)/shard_map/precondition/pallas_call | solution.py:128
  1.8 4.1 %collective-permute-start.2 = (bf16[24,1024]{1,0:T(8,128)(2,1)S(1)}, bf16[24,1024]{1,0:T(8,128)(2,1)S(1)}, u32[]{:S(2)}, u32[]{:S(2)}) collective-permute-start(bf16[24,1024]{1,0:T(8,128)(2,1)S(1)} %get-tuple-element.14.refs_0_), channel_id=1, source_target_pairs={{0,8},{2,10},{4,12},{6,14},{8,0},{10,2},{12,4},{14,6},{16,28},{18,... | collective-permute-start | bytes 147464 | tf_op jit(solution)/shard_map/ppermute | solution.py:262
  5.9 1.6 %collective-permute-start.1 = (bf16[24,1024]{1,0:T(8,128)(2,1)S(1)}, bf16[24,1024]{1,0:T(8,128)(2,1)S(1)}, u32[]{:S(2)}, u32[]{:S(2)}) collective-permute-start(bf16[24,1024]{1,0:T(8,128)(2,1)S(1)} %get-tuple-element.14.refs_0_), channel_id=1, source_target_pairs={{0,4},{2,6},{4,0},{6,2},{8,12},{10,14},{12,8},{14,10},{16,20},{18,... | collective-permute-start | bytes 147464 | tf_op jit(solution)/shard_map/ppermute | solution.py:262
  7.4 1.5 %collective-permute-start = (bf16[24,1024]{1,0:T(8,128)(2,1)S(1)}, bf16[24,1024]{1,0:T(8,128)(2,1)S(1)}, u32[]{:S(2)}, u32[]{:S(2)}) collective-permute-start(bf16[24,1024]{1,0:T(8,128)(2,1)S(1)} %get-tuple-element.14.refs_0_), channel_id=1, source_target_pairs={{0,2},{2,0},{4,6},{6,4},{8,10},{10,8},{12,14},{14,12},{16,18},{18,... | collective-permute-start | bytes 147464 | tf_op jit(solution)/shard_map/ppermute | solution.py:262
  8.9 0.0 collective-permute-start.3
  8.9 0.0 collective-permute-done.2.refs_3_
  8.9 1.7 %collective-permute-start.5 = (bf16[24,1024]{1,0:T(8,128)(2,1)S(1)}, bf16[24,1024]{1,0:T(8,128)(2,1)S(1)}, u32[]{:S(2)}, u32[]{:S(2)}) collective-permute-start(bf16[24,1024]{1,0:T(8,128)(2,1)S(1)} %collective-permute-done.2.refs_3_), channel_id=1, source_target_pairs={{0,2},{2,0},{4,6},{6,4},{8,10},{10,8},{12,14},{14,12},{16,18},{18,... | collective-permute-start | bytes 147464 | tf_op jit(solution)/shard_map/ppermute | solution.py:262
  10.6 1.6 %collective-permute-start.6 = (bf16[24,1024]{1,0:T(8,128)(2,1)S(1)}, bf16[24,1024]{1,0:T(8,128)(2,1)S(1)}, u32[]{:S(2)}, u32[]{:S(2)}) collective-permute-start(bf16[24,1024]{1,0:T(8,128)(2,1)S(1)} %collective-permute-done.2.refs_3_), channel_id=1, source_target_pairs={{0,16},{2,18},{4,20},{6,22},{8,24},{10,26},{12,28},{14,30},{16,0},... | collective-permute-start | bytes 147464 | tf_op jit(solution)/shard_map/ppermute | solution.py:262
  12.2 0.0 collective-permute-done.1.refs_2_
  12.2 0.5 %collective-permute-start.4 = (bf16[24,1024]{1,0:T(8,128)(2,1)S(1)}, bf16[24,1024]{1,0:T(8,128)(2,1)S(1)}, u32[]{:S(2)}, u32[]{:S(2)}) collective-permute-start(bf16[24,1024]{1,0:T(8,128)(2,1)S(1)} %collective-permute-done.1.refs_2_), channel_id=1, source_target_pairs={{0,2},{2,0},{4,6},{6,4},{8,10},{10,8},{12,14},{14,12},{16,18},{18,... | collective-permute-start | bytes 147464 | tf_op jit(solution)/shard_map/ppermute | solution.py:262
  12.7 0.0 collective-permute-done.refs_1_
  12.7 1.0 %scores_early.1 = (f32[48,256]{1,0:T(8,128)S(1)}, bf16[256,256]{1,0:T(8,128)(2,1)S(1)}) custom-call(bf16[256,4096]{1,0:T(8,128)(2,1)S(1)} %get-tuple-element.12.train_ref, s32[1,256]{1,0:T(1,128)S(1)} %get-tuple-element.13.ids_ref, bf16[24,1024]{1,0:T(8,128)(2,1)S(1)} %get-tuple-element.14.refs_0_, bf16[24,1024]{1,0:T(8,128)(2,1)S(1)} %collective-permute-done.refs_1_, ...), custom_call_target="tpu_custom_call" | custom-call | flops 100663296 | bytes 2293760 | tf_op jit(solution)/shard_map/scores_early/pallas_call | solution.py:231
  13.7 2.0 %collective-permute-done.3.refs_0_ = bf16[24,1024]{1,0:T(8,128)(2,1)S(1)} collective-permute-done((bf16[24,1024]{1,0:T(8,128)(2,1)S(1)}, bf16[24,1024]{1,0:T(8,128)(2,1)S(1)}, u32[]{:S(2)}, u32[]{:S(2)}) %collective-permute-start.3) | collective-permute-done | bytes 49184 | tf_op jit(solution)/shard_map/ppermute | solution.py:262
  15.7 0.0 collective-permute-done.5.refs_2_
  15.7 0.0 collective-permute-done.6.refs_3_
  15.7 0.6 %collective-permute-done.4.refs_1_ = bf16[24,1024]{1,0:T(8,128)(2,1)S(1)} collective-permute-done((bf16[24,1024]{1,0:T(8,128)(2,1)S(1)}, bf16[24,1024]{1,0:T(8,128)(2,1)S(1)}, u32[]{:S(2)}, u32[]{:S(2)}) %collective-permute-start.4) | collective-permute-done | bytes 49184 | tf_op jit(solution)/shard_map/ppermute | solution.py:262
  16.3 1.0 %scores_late.1 = (f32[24,256]{1,0:T(8,128)S(1)}, f32[24,256]{1,0:T(8,128)S(1)}) custom-call(bf16[256,4096]{1,0:T(8,128)(2,1)S(1)} %get-tuple-element.12.train_ref, bf16[256,256]{1,0:T(8,128)(2,1)S(1)} %get-tuple-element.15.place_ref, f32[48,256]{1,0:T(8,128)S(1)} %get-tuple-element.16.early_ref, bf16[24,1024]{1,0:T(8,128)(2,1)S(1)} %collective-permute-done.3.refs_0_, ...), custom_call_target="tpu_custom_call" | custom-call | flops 100663296 | bytes 2293760 | tf_op jit(solution)/shard_map/scores_late/pallas_call | solution.py:245
  17.3 0.1 collective-permute-start.7
  17.4 1.2 %collective-permute-done.7 = f32[24,256]{1,0:T(8,128)S(1)} collective-permute-done((f32[24,256]{1,0:T(8,128)S(1)}, f32[24,256]{1,0:T(8,128)S(1)}, u32[]{:S(2)}, u32[]{:S(2)}) %collective-permute-start.7) | collective-permute-done | bytes 24608 | tf_op jit(solution)/shard_map/ppermute | solution.py:285
  18.6 0.6 %fusion = bf16[3,256,8]{1,2,0:T(8,128)(2,1)} fusion(f32[24,256]{1,0:T(8,128)S(1)} %get-tuple-element.17, f32[24,256]{1,0:T(8,128)S(1)} %collective-permute-done.7), kind=kLoop, calls=%fused_computation.1 | loop fusion | flops 12288 | bytes 61440 | tf_op jit(solution)/shard_map/transpose | solution.py:287
Async XLA Ops:
  1.8 7.2 %collective-permute-start.2 = (bf16[24,1024]{1,0:T(8,128)(2,1)S(1)}, bf16[24,1024]{1,0:T(8,128)(2,1)S(1)}, u32[]{:S(2)}, u32[]{:S(2)}) collective-permute-start(bf16[24,1024]{1,0:T(8,128)(2,1)S(1)} %get-tuple-element.14.refs_0_), channel_id=1, source_target_pairs={{0,8},{2,10},{4,12},{6,14},{8,0},{10,2},{12,4},{14,6},{16,28},{18,... | collective-permute-start | bytes 147464 | tf_op jit(solution)/shard_map/ppermute | solution.py:262
  5.9 6.3 %collective-permute-start.1 = (bf16[24,1024]{1,0:T(8,128)(2,1)S(1)}, bf16[24,1024]{1,0:T(8,128)(2,1)S(1)}, u32[]{:S(2)}, u32[]{:S(2)}) collective-permute-start(bf16[24,1024]{1,0:T(8,128)(2,1)S(1)} %get-tuple-element.14.refs_0_), channel_id=1, source_target_pairs={{0,4},{2,6},{4,0},{6,2},{8,12},{10,14},{12,8},{14,10},{16,20},{18,... | collective-permute-start | bytes 147464 | tf_op jit(solution)/shard_map/ppermute | solution.py:262
  7.4 5.3 %collective-permute-start = (bf16[24,1024]{1,0:T(8,128)(2,1)S(1)}, bf16[24,1024]{1,0:T(8,128)(2,1)S(1)}, u32[]{:S(2)}, u32[]{:S(2)}) collective-permute-start(bf16[24,1024]{1,0:T(8,128)(2,1)S(1)} %get-tuple-element.14.refs_0_), channel_id=1, source_target_pairs={{0,2},{2,0},{4,6},{6,4},{8,10},{10,8},{12,14},{14,12},{16,18},{18,... | collective-permute-start | bytes 147464 | tf_op jit(solution)/shard_map/ppermute | solution.py:262
  8.9 6.8 %collective-permute-start.3 = (bf16[24,1024]{1,0:T(8,128)(2,1)S(1)}, bf16[24,1024]{1,0:T(8,128)(2,1)S(1)}, u32[]{:S(2)}, u32[]{:S(2)}) collective-permute-start(bf16[24,1024]{1,0:T(8,128)(2,1)S(1)} %get-tuple-element.14.refs_0_), channel_id=1, source_target_pairs={{0,14},{2,12},{4,10},{6,8},{8,6},{10,4},{12,2},{14,0},{16,26},{18,... | collective-permute-start | bytes 147464 | tf_op jit(solution)/shard_map/ppermute | solution.py:262
  8.9 6.8 %collective-permute-start.5 = (bf16[24,1024]{1,0:T(8,128)(2,1)S(1)}, bf16[24,1024]{1,0:T(8,128)(2,1)S(1)}, u32[]{:S(2)}, u32[]{:S(2)}) collective-permute-start(bf16[24,1024]{1,0:T(8,128)(2,1)S(1)} %collective-permute-done.2.refs_3_), channel_id=1, source_target_pairs={{0,2},{2,0},{4,6},{6,4},{8,10},{10,8},{12,14},{14,12},{16,18},{18,... | collective-permute-start | bytes 147464 | tf_op jit(solution)/shard_map/ppermute | solution.py:262
  10.6 5.1 %collective-permute-start.6 = (bf16[24,1024]{1,0:T(8,128)(2,1)S(1)}, bf16[24,1024]{1,0:T(8,128)(2,1)S(1)}, u32[]{:S(2)}, u32[]{:S(2)}) collective-permute-start(bf16[24,1024]{1,0:T(8,128)(2,1)S(1)} %collective-permute-done.2.refs_3_), channel_id=1, source_target_pairs={{0,16},{2,18},{4,20},{6,22},{8,24},{10,26},{12,28},{14,30},{16,0},... | collective-permute-start | bytes 147464 | tf_op jit(solution)/shard_map/ppermute | solution.py:262
  12.2 4.1 %collective-permute-start.4 = (bf16[24,1024]{1,0:T(8,128)(2,1)S(1)}, bf16[24,1024]{1,0:T(8,128)(2,1)S(1)}, u32[]{:S(2)}, u32[]{:S(2)}) collective-permute-start(bf16[24,1024]{1,0:T(8,128)(2,1)S(1)} %collective-permute-done.1.refs_2_), channel_id=1, source_target_pairs={{0,2},{2,0},{4,6},{6,4},{8,10},{10,8},{12,14},{14,12},{16,18},{18,... | collective-permute-start | bytes 147464 | tf_op jit(solution)/shard_map/ppermute | solution.py:262
  17.3 1.3 %collective-permute-start.7 = (f32[24,256]{1,0:T(8,128)S(1)}, f32[24,256]{1,0:T(8,128)S(1)}, u32[]{:S(2)}, u32[]{:S(2)}) collective-permute-start(f32[24,256]{1,0:T(8,128)S(1)} %get-tuple-element.18), channel_id=1, source_target_pairs={{0,1},{1,0},{2,3},{3,2},{4,5},{5,4},{6,7},{7,6},{8,9},{9,8},{10,11... | collective-permute-start | bytes 73736 | tf_op jit(solution)/shard_map/ppermute | solution.py:285

commit v18 on v17

--- a/solution.py
+++ b/solution.py
@@ -266,11 +266,11 @@
             near = {0: own, **{m: swap(own, m) for m in range(2, n_row, 2)}}
             parts = {**near, **{m ^ 1: swap(x, 1) for m, x in near.items()}}
             return {(m, 0): x for m, x in parts.items()}, n_row // 2
-        far = swap(own, 4, 2)
+        far = swap(own, 6, 2)
         near = swap(own, 2)
         return {
-            (0, 0): own, (1, 0): swap(own, 1), (2, 0): near, (4, 2): far,
-            (7, 2): swap(own, 7, 2), (3, 0): swap(near, 1), (5, 2): swap(far, 1), (6, 2): swap(far, 0, cross=1),
+            (0, 0): own, (1, 0): swap(own, 1), (2, 0): near, (6, 2): far,
+            (5, 2): swap(own, 5, 2), (3, 0): swap(near, 1), (7, 2): swap(far, 1), (4, 2): swap(far, 0, cross=1),
         }, 4
 
     def body(train_grads, query_grads, out_basis, in_basis, eigenvalues, block_order, row_ids):

time: 19.3 us -> 19.3 us (level)
  starting transfers between devices: 11 us -> 10.8 us
    ppermute x7, starting transfers between devices: 11 us -> 10.7 us  [swap(): return lax.ppermute(x, ('grp', 'row'), pairs)]
  transfers between devices with their start and end apart: 8 -> 8, of which waited for: 3 -> 5; matrix products, arithmetic and copies ran while one was open for 0% -> 0% of each run, Pallas kernels for 5% -> 5%
where the time goes in v18:
time: 19.3 us; the launch traced here: 19.1 us
  starting transfers between devices  10.8 us (56%)
  waiting for transfers between devices  3.93 us (20%)
  Pallas kernels  3.73 us (19%)
  other arithmetic  0.6 us (3%)
    ppermute x7, starting transfers between devices, swap(): return lax.ppermute(x, ('grp', 'row'), pairs)  10.7 us
    ppermute x7, waiting for transfers between devices, swap(): return lax.ppermute(x, ('grp', 'row'), pairs)  2.75 us
    pallas_call x1, Pallas kernels, precondition(): pl.pallas_call(precondition_kernel, out_shape=(jax.ShapeDtypeStruct((coun...  1.75 us
    ppermute x1, waiting for transfers between devices, body(): got = lax.ppermute(other, 'layer', [(0, 1), (1, 0)])  1.18 us
    pallas_call x1, Pallas kernels, scores(): pl.pallas_call(functools.partial(late_kernel, masks[early:] + masks[:earl...  1.01 us
    pallas_call x1, Pallas kernels, scores(): pl.pallas_call(functools.partial(early_kernel, masks), out_shape=(jax.Sha...  0.98 us
    transpose x1, other arithmetic, body(): return total.reshape(blocks, -1, rows).transpose(0, 2, 1)  0.6 us
  transfers between devices with their start and end apart: 8, of which 5 were waited for; matrix products, arithmetic and copies ran while one was open for 0% of the time, Pallas kernels for 5%

profile of v18, /device:TPU:0, one launch (start us, length us, event | category | flops | bytes accessed | tf_op | source)
XLA Modules:
  0.0 19.1 jit_solution(10672253036014347870)
XLA Ops:
  0.0 1.8 %precondition.1 = (bf16[24,1024]{1,0:T(8,128)(2,1)S(1)}, s32[1,256]{1,0:T(1,128)S(1)}, bf16[256,4096]{1,0:T(8,128)(2,1)S(1)}) custom-call(s32[3]{0:T(128)} %order_hbm.1, bf16[3,64,128]{2,1,0:T(8,128)(2,1)} %bitcast.12, f32[1,64,64]{2,1,0:T(8,128)} %out_basis_hbm.1, f32[1,64,64]{2,1,0:T(8,128)} %in_basis_hbm.1, f32[32,128]{1,0:T(8,128)} %bitcast.13, ...), custom_call_target="tpu_custom_call" | custom-call | tf_op jit(solution)/shard_map/precondition/pallas_call | solution.py:128
  1.8 5.1 %collective-permute-start.2 = (bf16[24,1024]{1,0:T(8,128)(2,1)S(1)}, bf16[24,1024]{1,0:T(8,128)(2,1)S(1)}, u32[]{:S(2)}, u32[]{:S(2)}) collective-permute-start(bf16[24,1024]{1,0:T(8,128)(2,1)S(1)} %get-tuple-element.14.refs_0_), channel_id=1, source_target_pairs={{0,12},{2,14},{4,8},{6,10},{8,4},{10,6},{12,0},{14,2},{16,24},{18,... | collective-permute-start | bytes 147464 | tf_op jit(solution)/shard_map/ppermute | solution.py:262
  6.9 0.0 collective-permute-start.1
  6.9 1.5 %collective-permute-start = (bf16[24,1024]{1,0:T(8,128)(2,1)S(1)}, bf16[24,1024]{1,0:T(8,128)(2,1)S(1)}, u32[]{:S(2)}, u32[]{:S(2)}) collective-permute-start(bf16[24,1024]{1,0:T(8,128)(2,1)S(1)} %get-tuple-element.14.refs_0_), channel_id=1, source_target_pairs={{0,2},{2,0},{4,6},{6,4},{8,10},{10,8},{12,14},{14,12},{16,18},{18,... | collective-permute-start | bytes 147464 | tf_op jit(solution)/shard_map/ppermute | solution.py:262
  8.4 0.6 %collective-permute-start.3 = (bf16[24,1024]{1,0:T(8,128)(2,1)S(1)}, bf16[24,1024]{1,0:T(8,128)(2,1)S(1)}, u32[]{:S(2)}, u32[]{:S(2)}) collective-permute-start(bf16[24,1024]{1,0:T(8,128)(2,1)S(1)} %get-tuple-element.14.refs_0_), channel_id=1, source_target_pairs={{0,10},{2,8},{4,14},{6,12},{8,2},{10,0},{12,6},{14,4},{16,30},{18,... | collective-permute-start | bytes 147464 | tf_op jit(solution)/shard_map/ppermute | solution.py:262
  9.0 0.2 collective-permute-done.2.refs_3_
  9.2 1.5 %collective-permute-start.5 = (bf16[24,1024]{1,0:T(8,128)(2,1)S(1)}, bf16[24,1024]{1,0:T(8,128)(2,1)S(1)}, u32[]{:S(2)}, u32[]{:S(2)}) collective-permute-start(bf16[24,1024]{1,0:T(8,128)(2,1)S(1)} %collective-permute-done.2.refs_3_), channel_id=1, source_target_pairs={{0,2},{2,0},{4,6},{6,4},{8,10},{10,8},{12,14},{14,12},{16,18},{18,... | collective-permute-start | bytes 147464 | tf_op jit(solution)/shard_map/ppermute | solution.py:262
  10.7 1.5 %collective-permute-start.6 = (bf16[24,1024]{1,0:T(8,128)(2,1)S(1)}, bf16[24,1024]{1,0:T(8,128)(2,1)S(1)}, u32[]{:S(2)}, u32[]{:S(2)}) collective-permute-start(bf16[24,1024]{1,0:T(8,128)(2,1)S(1)} %collective-permute-done.2.refs_3_), channel_id=1, source_target_pairs={{0,16},{2,18},{4,20},{6,22},{8,24},{10,26},{12,28},{14,30},{16,0},... | collective-permute-start | bytes 147464 | tf_op jit(solution)/shard_map/ppermute | solution.py:262
  12.1 0.0 collective-permute-done.1.refs_2_
  12.1 0.5 %collective-permute-start.4 = (bf16[24,1024]{1,0:T(8,128)(2,1)S(1)}, bf16[24,1024]{1,0:T(8,128)(2,1)S(1)}, u32[]{:S(2)}, u32[]{:S(2)}) collective-permute-start(bf16[24,1024]{1,0:T(8,128)(2,1)S(1)} %collective-permute-done.1.refs_2_), channel_id=1, source_target_pairs={{0,2},{2,0},{4,6},{6,4},{8,10},{10,8},{12,14},{14,12},{16,18},{18,... | collective-permute-start | bytes 147464 | tf_op jit(solution)/shard_map/ppermute | solution.py:262
  12.7 0.0 collective-permute-done.refs_1_
  12.7 1.0 %scores_early.1 = (f32[48,256]{1,0:T(8,128)S(1)}, bf16[256,256]{1,0:T(8,128)(2,1)S(1)}) custom-call(bf16[256,4096]{1,0:T(8,128)(2,1)S(1)} %get-tuple-element.12.train_ref, s32[1,256]{1,0:T(1,128)S(1)} %get-tuple-element.13.ids_ref, bf16[24,1024]{1,0:T(8,128)(2,1)S(1)} %get-tuple-element.14.refs_0_, bf16[24,1024]{1,0:T(8,128)(2,1)S(1)} %collective-permute-done.refs_1_, ...), custom_call_target="tpu_custom_call" | custom-call | flops 100663296 | bytes 2293760 | tf_op jit(solution)/shard_map/scores_early/pallas_call | solution.py:231
  13.7 0.6 %collective-permute-done.3.refs_0_ = bf16[24,1024]{1,0:T(8,128)(2,1)S(1)} collective-permute-done((bf16[24,1024]{1,0:T(8,128)(2,1)S(1)}, bf16[24,1024]{1,0:T(8,128)(2,1)S(1)}, u32[]{:S(2)}, u32[]{:S(2)}) %collective-permute-start.3) | collective-permute-done | bytes 49184 | tf_op jit(solution)/shard_map/ppermute | solution.py:262
  14.3 0.0 collective-permute-done.5.refs_2_
  14.3 0.5 %collective-permute-done.6.refs_3_ = bf16[24,1024]{1,0:T(8,128)(2,1)S(1)} collective-permute-done((bf16[24,1024]{1,0:T(8,128)(2,1)S(1)}, bf16[24,1024]{1,0:T(8,128)(2,1)S(1)}, u32[]{:S(2)}, u32[]{:S(2)}) %collective-permute-start.6) | collective-permute-done | bytes 49184 | tf_op jit(solution)/shard_map/ppermute | solution.py:262
  14.8 1.5 %collective-permute-done.4.refs_1_ = bf16[24,1024]{1,0:T(8,128)(2,1)S(1)} collective-permute-done((bf16[24,1024]{1,0:T(8,128)(2,1)S(1)}, bf16[24,1024]{1,0:T(8,128)(2,1)S(1)}, u32[]{:S(2)}, u32[]{:S(2)}) %collective-permute-start.4) | collective-permute-done | bytes 49184 | tf_op jit(solution)/shard_map/ppermute | solution.py:262
  16.2 1.0 %scores_late.1 = (f32[24,256]{1,0:T(8,128)S(1)}, f32[24,256]{1,0:T(8,128)S(1)}) custom-call(bf16[256,4096]{1,0:T(8,128)(2,1)S(1)} %get-tuple-element.12.train_ref, bf16[256,256]{1,0:T(8,128)(2,1)S(1)} %get-tuple-element.15.place_ref, f32[48,256]{1,0:T(8,128)S(1)} %get-tuple-element.16.early_ref, bf16[24,1024]{1,0:T(8,128)(2,1)S(1)} %collective-permute-done.3.refs_0_, ...), custom_call_target="tpu_custom_call" | custom-call | flops 100663296 | bytes 2293760 | tf_op jit(solution)/shard_map/scores_late/pallas_call | solution.py:245
  17.2 0.1 collective-permute-start.7
  17.3 1.2 %collective-permute-done.7 = f32[24,256]{1,0:T(8,128)S(1)} collective-permute-done((f32[24,256]{1,0:T(8,128)S(1)}, f32[24,256]{1,0:T(8,128)S(1)}, u32[]{:S(2)}, u32[]{:S(2)}) %collective-permute-start.7) | collective-permute-done | bytes 24608 | tf_op jit(solution)/shard_map/ppermute | solution.py:285
  18.5 0.6 %fusion = bf16[3,256,8]{1,2,0:T(8,128)(2,1)} fusion(f32[24,256]{1,0:T(8,128)S(1)} %get-tuple-element.17, f32[24,256]{1,0:T(8,128)S(1)} %collective-permute-done.7), kind=kLoop, calls=%fused_computation.1 | loop fusion | flops 12288 | bytes 61440 | tf_op jit(solution)/shard_map/transpose | solution.py:287
Async XLA Ops:
  1.8 7.4 %collective-permute-start.2 = (bf16[24,1024]{1,0:T(8,128)(2,1)S(1)}, bf16[24,1024]{1,0:T(8,128)(2,1)S(1)}, u32[]{:S(2)}, u32[]{:S(2)}) collective-permute-start(bf16[24,1024]{1,0:T(8,128)(2,1)S(1)} %get-tuple-element.14.refs_0_), channel_id=1, source_target_pairs={{0,12},{2,14},{4,8},{6,10},{8,4},{10,6},{12,0},{14,2},{16,24},{18,... | collective-permute-start | bytes 147464 | tf_op jit(solution)/shard_map/ppermute | solution.py:262
  6.9 5.3 %collective-permute-start.1 = (bf16[24,1024]{1,0:T(8,128)(2,1)S(1)}, bf16[24,1024]{1,0:T(8,128)(2,1)S(1)}, u32[]{:S(2)}, u32[]{:S(2)}) collective-permute-start(bf16[24,1024]{1,0:T(8,128)(2,1)S(1)} %get-tuple-element.14.refs_0_), channel_id=1, source_target_pairs={{0,4},{2,6},{4,0},{6,2},{8,12},{10,14},{12,8},{14,10},{16,20},{18,... | collective-permute-start | bytes 147464 | tf_op jit(solution)/shard_map/ppermute | solution.py:262
  6.9 5.8 %collective-permute-start = (bf16[24,1024]{1,0:T(8,128)(2,1)S(1)}, bf16[24,1024]{1,0:T(8,128)(2,1)S(1)}, u32[]{:S(2)}, u32[]{:S(2)}) collective-permute-start(bf16[24,1024]{1,0:T(8,128)(2,1)S(1)} %get-tuple-element.14.refs_0_), channel_id=1, source_target_pairs={{0,2},{2,0},{4,6},{6,4},{8,10},{10,8},{12,14},{14,12},{16,18},{18,... | collective-permute-start | bytes 147464 | tf_op jit(solution)/shard_map/ppermute | solution.py:262
  8.4 5.9 %collective-permute-start.3 = (bf16[24,1024]{1,0:T(8,128)(2,1)S(1)}, bf16[24,1024]{1,0:T(8,128)(2,1)S(1)}, u32[]{:S(2)}, u32[]{:S(2)}) collective-permute-start(bf16[24,1024]{1,0:T(8,128)(2,1)S(1)} %get-tuple-element.14.refs_0_), channel_id=1, source_target_pairs={{0,10},{2,8},{4,14},{6,12},{8,2},{10,0},{12,6},{14,4},{16,30},{18,... | collective-permute-start | bytes 147464 | tf_op jit(solution)/shard_map/ppermute | solution.py:262
  9.2 5.1 %collective-permute-start.5 = (bf16[24,1024]{1,0:T(8,128)(2,1)S(1)}, bf16[24,1024]{1,0:T(8,128)(2,1)S(1)}, u32[]{:S(2)}, u32[]{:S(2)}) collective-permute-start(bf16[24,1024]{1,0:T(8,128)(2,1)S(1)} %collective-permute-done.2.refs_3_), channel_id=1, source_target_pairs={{0,2},{2,0},{4,6},{6,4},{8,10},{10,8},{12,14},{14,12},{16,18},{18,... | collective-permute-start | bytes 147464 | tf_op jit(solution)/shard_map/ppermute | solution.py:262
  10.7 4.1 %collective-permute-start.6 = (bf16[24,1024]{1,0:T(8,128)(2,1)S(1)}, bf16[24,1024]{1,0:T(8,128)(2,1)S(1)}, u32[]{:S(2)}, u32[]{:S(2)}) collective-permute-start(bf16[24,1024]{1,0:T(8,128)(2,1)S(1)} %collective-permute-done.2.refs_3_), channel_id=1, source_target_pairs={{0,16},{2,18},{4,20},{6,22},{8,24},{10,26},{12,28},{14,30},{16,0},... | collective-permute-start | bytes 147464 | tf_op jit(solution)/shard_map/ppermute | solution.py:262
  12.1 4.1 %collective-permute-start.4 = (bf16[24,1024]{1,0:T(8,128)(2,1)S(1)}, bf16[24,1024]{1,0:T(8,128)(2,1)S(1)}, u32[]{:S(2)}, u32[]{:S(2)}) collective-permute-start(bf16[24,1024]{1,0:T(8,128)(2,1)S(1)} %collective-permute-done.1.refs_2_), channel_id=1, source_target_pairs={{0,2},{2,0},{4,6},{6,4},{8,10},{10,8},{12,14},{14,12},{16,18},{18,... | collective-permute-start | bytes 147464 | tf_op jit(solution)/shard_map/ppermute | solution.py:262
  17.2 1.3 %collective-permute-start.7 = (f32[24,256]{1,0:T(8,128)S(1)}, f32[24,256]{1,0:T(8,128)S(1)}, u32[]{:S(2)}, u32[]{:S(2)}) collective-permute-start(f32[24,256]{1,0:T(8,128)S(1)} %get-tuple-element.18), channel_id=1, source_target_pairs={{0,1},{1,0},{2,3},{3,2},{4,5},{5,4},{6,7},{7,6},{8,9},{9,8},{10,11... | collective-permute-start | bytes 73736 | tf_op jit(solution)/shard_map/ppermute | solution.py:285

commit v19 on v15

--- a/solution.py
+++ b/solution.py
@@ -261,7 +261,7 @@
         if n_row != 8:
             near = {0: own, **{m: swap(own, m) for m in range(2, n_row, 2)}}
             return {**near, **{m ^ 1: swap(x, 1) for m, x in near.items()}}, n_row // 2
-        far = {m: swap(own, m) for m in (6, 4)}
+        far = {m: swap(own, m) for m in (4, 6)}
         diagonal = {3: swap(own, 3)}
         near = {m: swap(own, m) for m in (2, 1)}
         return {0: own, **near, **far, **diagonal, **{m ^ 1: swap(x, 1) for m, x in far.items()}}, 5

time: 19 us -> 19.3 us (1.016)
  waiting for transfers between devices: 2.78 us -> 3.12 us
    ppermute x7, waiting for transfers between devices: 1.6 us -> 1.94 us  [swap(): return lax.ppermute(x, 'row', [(r, r ^ mask) for r in range(n_row)])]
where the time goes in v19:
time: 19.3 us; the launch traced here: 19.2 us
  starting transfers between devices  11.7 us (61%)
  Pallas kernels  3.74 us (19%)
  waiting for transfers between devices  3.12 us (16%)
  other arithmetic  0.6 us (3%)
    ppermute x7, starting transfers between devices, swap(): return lax.ppermute(x, 'row', [(r, r ^ mask) for r in range(n_row)])  11.6 us
    ppermute x7, waiting for transfers between devices, swap(): return lax.ppermute(x, 'row', [(r, r ^ mask) for r in range(n_row)])  1.94 us
    pallas_call x1, Pallas kernels, precondition(): pl.pallas_call(precondition_kernel, out_shape=(jax.ShapeDtypeStruct((coun...  1.75 us
    ppermute x1, waiting for transfers between devices, body(): got = lax.ppermute(other, 'layer', [(0, 1), (1, 0)])  1.18 us
    pallas_call x1, Pallas kernels, scores(): pl.pallas_call(functools.partial(late_kernel, masks[early:] + masks[:earl...  1 us
    pallas_call x1, Pallas kernels, scores(): pl.pallas_call(functools.partial(early_kernel, masks), out_shape=(jax.Sha...  0.99 us
    transpose x1, other arithmetic, body(): return total.reshape(blocks, -1, rows).transpose(0, 2, 1)  0.6 us
  transfers between devices with their start and end apart: 8, of which 3 were waited for; matrix products, arithmetic and copies ran while one was open for 0% of the time, Pallas kernels for 5%

profile of v19, /device:TPU:0, one launch (start us, length us, event | category | flops | bytes accessed | tf_op | source)
XLA Modules:
  0.0 19.2 jit_solution(10823369830191188172)
XLA Ops:
  0.0 1.8 %precondition.1 = (bf16[24,1024]{1,0:T(8,128)(2,1)S(1)}, s32[1,256]{1,0:T(1,128)S(1)}, bf16[256,4096]{1,0:T(8,128)(2,1)S(1)}) custom-call(s32[3]{0:T(128)} %order_hbm.1, bf16[3,64,128]{2,1,0:T(8,128)(2,1)} %bitcast.12, f32[1,64,64]{2,1,0:T(8,128)} %out_basis_hbm.1, f32[1,64,64]{2,1,0:T(8,128)} %in_basis_hbm.1, f32[32,128]{1,0:T(8,128)} %bitcast.13, ...), custom_call_target="tpu_custom_call" | custom-call | tf_op jit(solution)/shard_map/precondition/pallas_call | solution.py:128
  1.8 4.1 %collective-permute-start.2 = (bf16[24,1024]{1,0:T(8,128)(2,1)S(1)}, bf16[24,1024]{1,0:T(8,128)(2,1)S(1)}, u32[]{:S(2)}, u32[]{:S(2)}) collective-permute-start(bf16[24,1024]{1,0:T(8,128)(2,1)S(1)} %get-tuple-element.14.refs_0_), channel_id=1, source_target_pairs={{0,8},{2,10},{4,12},{6,14},{8,0},{10,2},{12,4},{14,6},{1,9},{3,11}... | collective-permute-start | bytes 147464 | tf_op jit(solution)/shard_map/ppermute | solution.py:258
  5.9 1.3 %collective-permute-start.3 = (bf16[24,1024]{1,0:T(8,128)(2,1)S(1)}, bf16[24,1024]{1,0:T(8,128)(2,1)S(1)}, u32[]{:S(2)}, u32[]{:S(2)}) collective-permute-start(bf16[24,1024]{1,0:T(8,128)(2,1)S(1)} %get-tuple-element.14.refs_0_), channel_id=1, source_target_pairs={{0,12},{2,14},{4,8},{6,10},{8,4},{10,6},{12,0},{14,2},{1,13},{3,15... | collective-permute-start | bytes 147464 | tf_op jit(solution)/shard_map/ppermute | solution.py:258
  7.2 0.2 %collective-permute-start = (bf16[24,1024]{1,0:T(8,128)(2,1)S(1)}, bf16[24,1024]{1,0:T(8,128)(2,1)S(1)}, u32[]{:S(2)}, u32[]{:S(2)}) collective-permute-start(bf16[24,1024]{1,0:T(8,128)(2,1)S(1)} %get-tuple-element.14.refs_0_), channel_id=1, source_target_pairs={{0,4},{2,6},{4,0},{6,2},{8,12},{10,14},{12,8},{14,10},{1,5},{3,7},... | collective-permute-start | bytes 147464 | tf_op jit(solution)/shard_map/ppermute | solution.py:258
  7.4 1.5 %collective-permute-start.1 = (bf16[24,1024]{1,0:T(8,128)(2,1)S(1)}, bf16[24,1024]{1,0:T(8,128)(2,1)S(1)}, u32[]{:S(2)}, u32[]{:S(2)}) collective-permute-start(bf16[24,1024]{1,0:T(8,128)(2,1)S(1)} %get-tuple-element.14.refs_0_), channel_id=1, source_target_pairs={{0,2},{2,0},{4,6},{6,4},{8,10},{10,8},{12,14},{14,12},{1,3},{3,1},... | collective-permute-start | bytes 147464 | tf_op jit(solution)/shard_map/ppermute | solution.py:258
  8.9 1.8 %collective-permute-start.4 = (bf16[24,1024]{1,0:T(8,128)(2,1)S(1)}, bf16[24,1024]{1,0:T(8,128)(2,1)S(1)}, u32[]{:S(2)}, u32[]{:S(2)}) collective-permute-start(bf16[24,1024]{1,0:T(8,128)(2,1)S(1)} %get-tuple-element.14.refs_0_), channel_id=1, source_target_pairs={{0,6},{2,4},{4,2},{6,0},{8,14},{10,12},{12,10},{14,8},{1,7},{3,5},... | collective-permute-start | bytes 147464 | tf_op jit(solution)/shard_map/ppermute | solution.py:258
  10.7 0.0 collective-permute-done.2.refs_3_
  10.7 1.5 %collective-permute-start.5 = (bf16[24,1024]{1,0:T(8,128)(2,1)S(1)}, bf16[24,1024]{1,0:T(8,128)(2,1)S(1)}, u32[]{:S(2)}, u32[]{:S(2)}) collective-permute-start(bf16[24,1024]{1,0:T(8,128)(2,1)S(1)} %collective-permute-done.2.refs_3_), channel_id=1, source_target_pairs={{0,2},{2,0},{4,6},{6,4},{8,10},{10,8},{12,14},{14,12},{1,3},{3,1},... | collective-permute-start | bytes 147464 | tf_op jit(solution)/shard_map/ppermute | solution.py:258
  12.2 0.0 collective-permute-done.3.refs_4_
  12.2 1.2 %collective-permute-start.6 = (bf16[24,1024]{1,0:T(8,128)(2,1)S(1)}, bf16[24,1024]{1,0:T(8,128)(2,1)S(1)}, u32[]{:S(2)}, u32[]{:S(2)}) collective-permute-start(bf16[24,1024]{1,0:T(8,128)(2,1)S(1)} %collective-permute-done.3.refs_4_), channel_id=1, source_target_pairs={{0,2},{2,0},{4,6},{6,4},{8,10},{10,8},{12,14},{14,12},{1,3},{3,1},... | collective-permute-start | bytes 147464 | tf_op jit(solution)/shard_map/ppermute | solution.py:258
  13.4 0.0 collective-permute-done.refs_1_
  13.4 0.0 collective-permute-done.1.refs_2_
  13.4 1.0 %scores_early.1 = (f32[48,256]{1,0:T(8,128)S(1)}, bf16[256,256]{1,0:T(8,128)(2,1)S(1)}) custom-call(bf16[256,4096]{1,0:T(8,128)(2,1)S(1)} %get-tuple-element.12.train_ref, s32[1,256]{1,0:T(1,128)S(1)} %get-tuple-element.13.ids_ref, bf16[24,1024]{1,0:T(8,128)(2,1)S(1)} %get-tuple-element.14.refs_0_, bf16[24,1024]{1,0:T(8,128)(2,1)S(1)} %collective-permute-done.refs_1_, ...), custom_call_target="tpu_custom_call" | custom-call | flops 100663296 | bytes 2293760 | tf_op jit(solution)/shard_map/scores_early/pallas_call | solution.py:230
  14.4 0.0 collective-permute-done.4.refs_0_
  14.4 0.4 %collective-permute-done.5.refs_1_ = bf16[24,1024]{1,0:T(8,128)(2,1)S(1)} collective-permute-done((bf16[24,1024]{1,0:T(8,128)(2,1)S(1)}, bf16[24,1024]{1,0:T(8,128)(2,1)S(1)}, u32[]{:S(2)}, u32[]{:S(2)}) %collective-permute-start.5) | collective-permute-done | bytes 49184 | tf_op jit(solution)/shard_map/ppermute | solution.py:258
  14.8 1.5 %collective-permute-done.6.refs_2_ = bf16[24,1024]{1,0:T(8,128)(2,1)S(1)} collective-permute-done((bf16[24,1024]{1,0:T(8,128)(2,1)S(1)}, bf16[24,1024]{1,0:T(8,128)(2,1)S(1)}, u32[]{:S(2)}, u32[]{:S(2)}) %collective-permute-start.6) | collective-permute-done | bytes 49184 | tf_op jit(solution)/shard_map/ppermute | solution.py:258
  16.3 1.0 %scores_late.1 = (f32[24,256]{1,0:T(8,128)S(1)}, f32[24,256]{1,0:T(8,128)S(1)}) custom-call(bf16[256,4096]{1,0:T(8,128)(2,1)S(1)} %get-tuple-element.12.train_ref, bf16[256,256]{1,0:T(8,128)(2,1)S(1)} %get-tuple-element.15.place_ref, f32[48,256]{1,0:T(8,128)S(1)} %get-tuple-element.16.early_ref, bf16[24,1024]{1,0:T(8,128)(2,1)S(1)} %collective-permute-done.4.refs_0_, ...), custom_call_target="tpu_custom_call" | custom-call | flops 100663296 | bytes 2293760 | tf_op jit(solution)/shard_map/scores_late/pallas_call | solution.py:244
  17.3 0.1 collective-permute-start.7
  17.4 1.2 %collective-permute-done.7 = f32[24,256]{1,0:T(8,128)S(1)} collective-permute-done((f32[24,256]{1,0:T(8,128)S(1)}, f32[24,256]{1,0:T(8,128)S(1)}, u32[]{:S(2)}, u32[]{:S(2)}) %collective-permute-start.7) | collective-permute-done | bytes 24608 | tf_op jit(solution)/shard_map/ppermute | solution.py:278
  18.6 0.6 %fusion = bf16[3,256,8]{1,2,0:T(8,128)(2,1)} fusion(f32[24,256]{1,0:T(8,128)S(1)} %get-tuple-element.17, f32[24,256]{1,0:T(8,128)S(1)} %collective-permute-done.7), kind=kLoop, calls=%fused_computation.1 | loop fusion | flops 12288 | bytes 61440 | tf_op jit(solution)/shard_map/transpose | solution.py:280
Async XLA Ops:
  1.8 8.9 %collective-permute-start.2 = (bf16[24,1024]{1,0:T(8,128)(2,1)S(1)}, bf16[24,1024]{1,0:T(8,128)(2,1)S(1)}, u32[]{:S(2)}, u32[]{:S(2)}) collective-permute-start(bf16[24,1024]{1,0:T(8,128)(2,1)S(1)} %get-tuple-element.14.refs_0_), channel_id=1, source_target_pairs={{0,8},{2,10},{4,12},{6,14},{8,0},{10,2},{12,4},{14,6},{1,9},{3,11}... | collective-permute-start | bytes 147464 | tf_op jit(solution)/shard_map/ppermute | solution.py:258
  5.9 6.3 %collective-permute-start.3 = (bf16[24,1024]{1,0:T(8,128)(2,1)S(1)}, bf16[24,1024]{1,0:T(8,128)(2,1)S(1)}, u32[]{:S(2)}, u32[]{:S(2)}) collective-permute-start(bf16[24,1024]{1,0:T(8,128)(2,1)S(1)} %get-tuple-element.14.refs_0_), channel_id=1, source_target_pairs={{0,12},{2,14},{4,8},{6,10},{8,4},{10,6},{12,0},{14,2},{1,13},{3,15... | collective-permute-start | bytes 147464 | tf_op jit(solution)/shard_map/ppermute | solution.py:258
  7.2 6.1 %collective-permute-start = (bf16[24,1024]{1,0:T(8,128)(2,1)S(1)}, bf16[24,1024]{1,0:T(8,128)(2,1)S(1)}, u32[]{:S(2)}, u32[]{:S(2)}) collective-permute-start(bf16[24,1024]{1,0:T(8,128)(2,1)S(1)} %get-tuple-element.14.refs_0_), channel_id=1, source_target_pairs={{0,4},{2,6},{4,0},{6,2},{8,12},{10,14},{12,8},{14,10},{1,5},{3,7},... | collective-permute-start | bytes 147464 | tf_op jit(solution)/shard_map/ppermute | solution.py:258
  7.4 5.9 %collective-permute-start.1 = (bf16[24,1024]{1,0:T(8,128)(2,1)S(1)}, bf16[24,1024]{1,0:T(8,128)(2,1)S(1)}, u32[]{:S(2)}, u32[]{:S(2)}) collective-permute-start(bf16[24,1024]{1,0:T(8,128)(2,1)S(1)} %get-tuple-element.14.refs_0_), channel_id=1, source_target_pairs={{0,2},{2,0},{4,6},{6,4},{8,10},{10,8},{12,14},{14,12},{1,3},{3,1},... | collective-permute-start | bytes 147464 | tf_op jit(solution)/shard_map/ppermute | solution.py:258
  8.9 5.4 %collective-permute-start.4 = (bf16[24,1024]{1,0:T(8,128)(2,1)S(1)}, bf16[24,1024]{1,0:T(8,128)(2,1)S(1)}, u32[]{:S(2)}, u32[]{:S(2)}) collective-permute-start(bf16[24,1024]{1,0:T(8,128)(2,1)S(1)} %get-tuple-element.14.refs_0_), channel_id=1, source_target_pairs={{0,6},{2,4},{4,2},{6,0},{8,14},{10,12},{12,10},{14,8},{1,7},{3,5},... | collective-permute-start | bytes 147464 | tf_op jit(solution)/shard_map/ppermute | solution.py:258
  10.7 4.1 %collective-permute-start.5 = (bf16[24,1024]{1,0:T(8,128)(2,1)S(1)}, bf16[24,1024]{1,0:T(8,128)(2,1)S(1)}, u32[]{:S(2)}, u32[]{:S(2)}) collective-permute-start(bf16[24,1024]{1,0:T(8,128)(2,1)S(1)} %collective-permute-done.2.refs_3_), channel_id=1, source_target_pairs={{0,2},{2,0},{4,6},{6,4},{8,10},{10,8},{12,14},{14,12},{1,3},{3,1},... | collective-permute-start | bytes 147464 | tf_op jit(solution)/shard_map/ppermute | solution.py:258
  12.2 4.1 %collective-permute-start.6 = (bf16[24,1024]{1,0:T(8,128)(2,1)S(1)}, bf16[24,1024]{1,0:T(8,128)(2,1)S(1)}, u32[]{:S(2)}, u32[]{:S(2)}) collective-permute-start(bf16[24,1024]{1,0:T(8,128)(2,1)S(1)} %collective-permute-done.3.refs_4_), channel_id=1, source_target_pairs={{0,2},{2,0},{4,6},{6,4},{8,10},{10,8},{12,14},{14,12},{1,3},{3,1},... | collective-permute-start | bytes 147464 | tf_op jit(solution)/shard_map/ppermute | solution.py:258
  17.3 1.3 %collective-permute-start.7 = (f32[24,256]{1,0:T(8,128)S(1)}, f32[24,256]{1,0:T(8,128)S(1)}, u32[]{:S(2)}, u32[]{:S(2)}) collective-permute-start(f32[24,256]{1,0:T(8,128)S(1)} %get-tuple-element.18), channel_id=1, source_target_pairs={{0,1},{1,0},{2,3},{3,2},{4,5},{5,4},{6,7},{7,6},{8,9},{9,8},{10,11... | collective-permute-start | bytes 73736 | tf_op jit(solution)/shard_map/ppermute | solution.py:278

commit v20 on v15

--- a/solution.py
+++ b/solution.py
@@ -153,13 +153,6 @@
     ))
 
 
-def split3(x):
-    hi = x.astype(BF16)
-    rest = x - hi.astype(F32)
-    mid = rest.astype(BF16)
-    return hi, mid, (rest - mid.astype(F32)).astype(BF16)
-
-
 def slot_of(n_row, mask):
     source, per = lax.axis_index("row") ^ mask, n_row // 2
     return source ^ (lax.axis_index("layer") * per)
@@ -184,8 +177,8 @@
         ], axis=1)
         term = mm_nt(queries.astype(BF16), train_ref[:, j * seg:(j + 1) * seg])
         terms = term if terms is None else terms + term
-    a, b, c = split3(terms)
-    return mm(a, place) + mm(b, place) + mm(c, place)
+    hi, lo = split2(terms)
+    return mm(hi, place) + mm(lo, place)
 
 
 def early_kernel(masks, train_ref, ids_ref, *refs):
@@ -263,7 +256,7 @@
             return {**near, **{m ^ 1: swap(x, 1) for m, x in near.items()}}, n_row // 2
         far = {m: swap(own, m) for m in (6, 4)}
         diagonal = {3: swap(own, 3)}
-        near = {m: swap(own, m) for m in (2, 1)}
+        near = {m: swap(own, m) for m in (1, 2)}
         return {0: own, **near, **far, **diagonal, **{m ^ 1: swap(x, 1) for m, x in far.items()}}, 5
 
     def body(train_grads, query_grads, out_basis, in_basis, eigenvalues, block_order, row_ids):

time: 19 us -> 19 us (level)
  no operation moved by 1% of the time
where the time goes in v20:
time: 19 us; the launch traced here: 18.8 us
  starting transfers between devices  11.7 us (62%)
  Pallas kernels  3.68 us (19%)
  waiting for transfers between devices  2.76 us (15%)
  other arithmetic  0.6 us (3%)
    ppermute x7, starting transfers between devices, swap(): return lax.ppermute(x, 'row', [(r, r ^ mask) for r in range(n_row)])  11.6 us
    pallas_call x1, Pallas kernels, precondition(): pl.pallas_call(precondition_kernel, out_shape=(jax.ShapeDtypeStruct((coun...  1.75 us
    ppermute x7, waiting for transfers between devices, swap(): return lax.ppermute(x, 'row', [(r, r ^ mask) for r in range(n_row)])  1.58 us
    ppermute x1, waiting for transfers between devices, body(): got = lax.ppermute(other, 'layer', [(0, 1), (1, 0)])  1.18 us
    pallas_call x1, Pallas kernels, scores(): pl.pallas_call(functools.partial(late_kernel, masks[early:] + masks[:earl...  0.97 us
    pallas_call x1, Pallas kernels, scores(): pl.pallas_call(functools.partial(early_kernel, masks), out_shape=(jax.Sha...  0.96 us
    transpose x1, other arithmetic, body(): return total.reshape(blocks, -1, rows).transpose(0, 2, 1)  0.6 us
  transfers between devices with their start and end apart: 8, of which 3 were waited for; matrix products, arithmetic and copies ran while one was open for 0% of the time, Pallas kernels for 5%

profile of v20, /device:TPU:0, one launch (start us, length us, event | category | flops | bytes accessed | tf_op | source)
XLA Modules:
  0.0 18.8 jit_solution(299512909428348935)
XLA Ops:
  0.0 1.8 %precondition.1 = (bf16[24,1024]{1,0:T(8,128)(2,1)S(1)}, s32[1,256]{1,0:T(1,128)S(1)}, bf16[256,4096]{1,0:T(8,128)(2,1)S(1)}) custom-call(s32[3]{0:T(128)} %order_hbm.1, bf16[3,64,128]{2,1,0:T(8,128)(2,1)} %bitcast.12, f32[1,64,64]{2,1,0:T(8,128)} %out_basis_hbm.1, f32[1,64,64]{2,1,0:T(8,128)} %in_basis_hbm.1, f32[32,128]{1,0:T(8,128)} %bitcast.13, ...), custom_call_target="tpu_custom_call" | custom-call | tf_op jit(solution)/shard_map/precondition/pallas_call | solution.py:128
  1.8 5.1 %collective-permute-start.2 = (bf16[24,1024]{1,0:T(8,128)(2,1)S(1)}, bf16[24,1024]{1,0:T(8,128)(2,1)S(1)}, u32[]{:S(2)}, u32[]{:S(2)}) collective-permute-start(bf16[24,1024]{1,0:T(8,128)(2,1)S(1)} %get-tuple-element.14.refs_0_), channel_id=1, source_target_pairs={{0,12},{2,14},{4,8},{6,10},{8,4},{10,6},{12,0},{14,2},{1,13},{3,15... | collective-permute-start | bytes 147464 | tf_op jit(solution)/shard_map/ppermute | solution.py:251
  6.9 0.0 collective-permute-start.3
  6.9 1.5 %collective-permute-start = (bf16[24,1024]{1,0:T(8,128)(2,1)S(1)}, bf16[24,1024]{1,0:T(8,128)(2,1)S(1)}, u32[]{:S(2)}, u32[]{:S(2)}) collective-permute-start(bf16[24,1024]{1,0:T(8,128)(2,1)S(1)} %get-tuple-element.14.refs_0_), channel_id=1, source_target_pairs={{0,2},{2,0},{4,6},{6,4},{8,10},{10,8},{12,14},{14,12},{1,3},{3,1},... | collective-permute-start | bytes 147464 | tf_op jit(solution)/shard_map/ppermute | solution.py:251
  8.4 0.8 %collective-permute-start.1 = (bf16[24,1024]{1,0:T(8,128)(2,1)S(1)}, bf16[24,1024]{1,0:T(8,128)(2,1)S(1)}, u32[]{:S(2)}, u32[]{:S(2)}) collective-permute-start(bf16[24,1024]{1,0:T(8,128)(2,1)S(1)} %get-tuple-element.14.refs_0_), channel_id=1, source_target_pairs={{0,4},{2,6},{4,0},{6,2},{8,12},{10,14},{12,8},{14,10},{1,5},{3,7},... | collective-permute-start | bytes 147464 | tf_op jit(solution)/shard_map/ppermute | solution.py:251
  9.2 1.2 %collective-permute-start.4 = (bf16[24,1024]{1,0:T(8,128)(2,1)S(1)}, bf16[24,1024]{1,0:T(8,128)(2,1)S(1)}, u32[]{:S(2)}, u32[]{:S(2)}) collective-permute-start(bf16[24,1024]{1,0:T(8,128)(2,1)S(1)} %get-tuple-element.14.refs_0_), channel_id=1, source_target_pairs={{0,6},{2,4},{4,2},{6,0},{8,14},{10,12},{12,10},{14,8},{1,7},{3,5},... | collective-permute-start | bytes 147464 | tf_op jit(solution)/shard_map/ppermute | solution.py:251
  10.4 0.0 collective-permute-done.2.refs_3_
  10.4 1.5 %collective-permute-start.5 = (bf16[24,1024]{1,0:T(8,128)(2,1)S(1)}, bf16[24,1024]{1,0:T(8,128)(2,1)S(1)}, u32[]{:S(2)}, u32[]{:S(2)}) collective-permute-start(bf16[24,1024]{1,0:T(8,128)(2,1)S(1)} %collective-permute-done.2.refs_3_), channel_id=1, source_target_pairs={{0,2},{2,0},{4,6},{6,4},{8,10},{10,8},{12,14},{14,12},{1,3},{3,1},... | collective-permute-start | bytes 147464 | tf_op jit(solution)/shard_map/ppermute | solution.py:251
  11.9 0.0 collective-permute-done.3.refs_4_
  11.9 1.5 %collective-permute-start.6 = (bf16[24,1024]{1,0:T(8,128)(2,1)S(1)}, bf16[24,1024]{1,0:T(8,128)(2,1)S(1)}, u32[]{:S(2)}, u32[]{:S(2)}) collective-permute-start(bf16[24,1024]{1,0:T(8,128)(2,1)S(1)} %collective-permute-done.3.refs_4_), channel_id=1, source_target_pairs={{0,2},{2,0},{4,6},{6,4},{8,10},{10,8},{12,14},{14,12},{1,3},{3,1},... | collective-permute-start | bytes 147464 | tf_op jit(solution)/shard_map/ppermute | solution.py:251
  13.4 0.0 collective-permute-done.refs_1_
  13.4 0.0 collective-permute-done.1.refs_2_
  13.4 1.0 %scores_early.1 = (f32[48,256]{1,0:T(8,128)S(1)}, bf16[256,256]{1,0:T(8,128)(2,1)S(1)}) custom-call(bf16[256,4096]{1,0:T(8,128)(2,1)S(1)} %get-tuple-element.12.train_ref, s32[1,256]{1,0:T(1,128)S(1)} %get-tuple-element.13.ids_ref, bf16[24,1024]{1,0:T(8,128)(2,1)S(1)} %get-tuple-element.14.refs_0_, bf16[24,1024]{1,0:T(8,128)(2,1)S(1)} %collective-permute-done.refs_1_, ...), custom_call_target="tpu_custom_call" | custom-call | flops 100663296 | bytes 2293760 | tf_op jit(solution)/shard_map/scores_early/pallas_call | solution.py:223
  14.4 0.0 collective-permute-done.4.refs_0_
  14.4 0.7 %collective-permute-done.5.refs_1_ = bf16[24,1024]{1,0:T(8,128)(2,1)S(1)} collective-permute-done((bf16[24,1024]{1,0:T(8,128)(2,1)S(1)}, bf16[24,1024]{1,0:T(8,128)(2,1)S(1)}, u32[]{:S(2)}, u32[]{:S(2)}) %collective-permute-start.5) | collective-permute-done | bytes 49184 | tf_op jit(solution)/shard_map/ppermute | solution.py:251
  15.1 0.9 %collective-permute-done.6.refs_2_ = bf16[24,1024]{1,0:T(8,128)(2,1)S(1)} collective-permute-done((bf16[24,1024]{1,0:T(8,128)(2,1)S(1)}, bf16[24,1024]{1,0:T(8,128)(2,1)S(1)}, u32[]{:S(2)}, u32[]{:S(2)}) %collective-permute-start.6) | collective-permute-done | bytes 49184 | tf_op jit(solution)/shard_map/ppermute | solution.py:251
  16.0 1.0 %scores_late.1 = (f32[24,256]{1,0:T(8,128)S(1)}, f32[24,256]{1,0:T(8,128)S(1)}) custom-call(bf16[256,4096]{1,0:T(8,128)(2,1)S(1)} %get-tuple-element.12.train_ref, bf16[256,256]{1,0:T(8,128)(2,1)S(1)} %get-tuple-element.15.place_ref, f32[48,256]{1,0:T(8,128)S(1)} %get-tuple-element.16.early_ref, bf16[24,1024]{1,0:T(8,128)(2,1)S(1)} %collective-permute-done.4.refs_0_, ...), custom_call_target="tpu_custom_call" | custom-call | flops 100663296 | bytes 2293760 | tf_op jit(solution)/shard_map/scores_late/pallas_call | solution.py:237
  16.9 0.1 collective-permute-start.7
  17.0 1.2 %collective-permute-done.7 = f32[24,256]{1,0:T(8,128)S(1)} collective-permute-done((f32[24,256]{1,0:T(8,128)S(1)}, f32[24,256]{1,0:T(8,128)S(1)}, u32[]{:S(2)}, u32[]{:S(2)}) %collective-permute-start.7) | collective-permute-done | bytes 24608 | tf_op jit(solution)/shard_map/ppermute | solution.py:271
  18.2 0.6 %fusion = bf16[3,256,8]{1,2,0:T(8,128)(2,1)} fusion(f32[24,256]{1,0:T(8,128)S(1)} %get-tuple-element.17, f32[24,256]{1,0:T(8,128)S(1)} %collective-permute-done.7), kind=kLoop, calls=%fused_computation.1 | loop fusion | flops 12288 | bytes 61440 | tf_op jit(solution)/shard_map/transpose | solution.py:273
Async XLA Ops:
  1.8 8.6 %collective-permute-start.2 = (bf16[24,1024]{1,0:T(8,128)(2,1)S(1)}, bf16[24,1024]{1,0:T(8,128)(2,1)S(1)}, u32[]{:S(2)}, u32[]{:S(2)}) collective-permute-start(bf16[24,1024]{1,0:T(8,128)(2,1)S(1)} %get-tuple-element.14.refs_0_), channel_id=1, source_target_pairs={{0,12},{2,14},{4,8},{6,10},{8,4},{10,6},{12,0},{14,2},{1,13},{3,15... | collective-permute-start | bytes 147464 | tf_op jit(solution)/shard_map/ppermute | solution.py:251
  6.9 5.0 %collective-permute-start.3 = (bf16[24,1024]{1,0:T(8,128)(2,1)S(1)}, bf16[24,1024]{1,0:T(8,128)(2,1)S(1)}, u32[]{:S(2)}, u32[]{:S(2)}) collective-permute-start(bf16[24,1024]{1,0:T(8,128)(2,1)S(1)} %get-tuple-element.14.refs_0_), channel_id=1, source_target_pairs={{0,8},{2,10},{4,12},{6,14},{8,0},{10,2},{12,4},{14,6},{1,9},{3,11}... | collective-permute-start | bytes 147464 | tf_op jit(solution)/shard_map/ppermute | solution.py:251
  6.9 6.5 %collective-permute-start = (bf16[24,1024]{1,0:T(8,128)(2,1)S(1)}, bf16[24,1024]{1,0:T(8,128)(2,1)S(1)}, u32[]{:S(2)}, u32[]{:S(2)}) collective-permute-start(bf16[24,1024]{1,0:T(8,128)(2,1)S(1)} %get-tuple-element.14.refs_0_), channel_id=1, source_target_pairs={{0,2},{2,0},{4,6},{6,4},{8,10},{10,8},{12,14},{14,12},{1,3},{3,1},... | collective-permute-start | bytes 147464 | tf_op jit(solution)/shard_map/ppermute | solution.py:251
  8.4 5.0 %collective-permute-start.1 = (bf16[24,1024]{1,0:T(8,128)(2,1)S(1)}, bf16[24,1024]{1,0:T(8,128)(2,1)S(1)}, u32[]{:S(2)}, u32[]{:S(2)}) collective-permute-start(bf16[24,1024]{1,0:T(8,128)(2,1)S(1)} %get-tuple-element.14.refs_0_), channel_id=1, source_target_pairs={{0,4},{2,6},{4,0},{6,2},{8,12},{10,14},{12,8},{14,10},{1,5},{3,7},... | collective-permute-start | bytes 147464 | tf_op jit(solution)/shard_map/ppermute | solution.py:251
  9.2 5.2 %collective-permute-start.4 = (bf16[24,1024]{1,0:T(8,128)(2,1)S(1)}, bf16[24,1024]{1,0:T(8,128)(2,1)S(1)}, u32[]{:S(2)}, u32[]{:S(2)}) collective-permute-start(bf16[24,1024]{1,0:T(8,128)(2,1)S(1)} %get-tuple-element.14.refs_0_), channel_id=1, source_target_pairs={{0,6},{2,4},{4,2},{6,0},{8,14},{10,12},{12,10},{14,8},{1,7},{3,5},... | collective-permute-start | bytes 147464 | tf_op jit(solution)/shard_map/ppermute | solution.py:251
  10.4 4.7 %collective-permute-start.5 = (bf16[24,1024]{1,0:T(8,128)(2,1)S(1)}, bf16[24,1024]{1,0:T(8,128)(2,1)S(1)}, u32[]{:S(2)}, u32[]{:S(2)}) collective-permute-start(bf16[24,1024]{1,0:T(8,128)(2,1)S(1)} %collective-permute-done.2.refs_3_), channel_id=1, source_target_pairs={{0,2},{2,0},{4,6},{6,4},{8,10},{10,8},{12,14},{14,12},{1,3},{3,1},... | collective-permute-start | bytes 147464 | tf_op jit(solution)/shard_map/ppermute | solution.py:251
  11.9 4.1 %collective-permute-start.6 = (bf16[24,1024]{1,0:T(8,128)(2,1)S(1)}, bf16[24,1024]{1,0:T(8,128)(2,1)S(1)}, u32[]{:S(2)}, u32[]{:S(2)}) collective-permute-start(bf16[24,1024]{1,0:T(8,128)(2,1)S(1)} %collective-permute-done.3.refs_4_), channel_id=1, source_target_pairs={{0,2},{2,0},{4,6},{6,4},{8,10},{10,8},{12,14},{14,12},{1,3},{3,1},... | collective-permute-start | bytes 147464 | tf_op jit(solution)/shard_map/ppermute | solution.py:251
  16.9 1.3 %collective-permute-start.7 = (f32[24,256]{1,0:T(8,128)S(1)}, f32[24,256]{1,0:T(8,128)S(1)}, u32[]{:S(2)}, u32[]{:S(2)}) collective-permute-start(f32[24,256]{1,0:T(8,128)S(1)} %get-tuple-element.18), channel_id=1, source_target_pairs={{0,1},{1,0},{2,3},{3,2},{4,5},{5,4},{6,7},{7,6},{8,9},{9,8},{10,11... | collective-permute-start | bytes 73736 | tf_op jit(solution)/shard_map/ppermute | solution.py:271
